TPU v7x, 32 devices: a whole 2x2x4 slice. The times are simulated.
32 devices in a mesh: gx: 4 (over x, core), gy: 4 (over z), gz: 2 (over y).
Axes of the slice: x: 2, y: 2, z: 4, core: 2. Of those that a mesh axis runs over, the one named last changes fastest.
Arguments:
- cells: bfloat16 [4, 16, 256, 256], P(None, 'gx', 'gy', 'gz'), may hold values from -6 to 6
- weight: bfloat16 [32, 4, 3, 3, 3], replicated, may hold values from -0.625 to 0.625
- bias: float32 [32], replicated, may hold values from -3 to 3
- cotangent: bfloat16 [32, 8, 128, 128], P(None, 'gx', 'gy', 'gz'), may hold values from -6 to 6
Outputs:
- pooled: bfloat16 [32, 8, 128, 128], P(None, 'gx', 'gy', 'gz')
- weight_grad: float32 [32, 4, 3, 3, 3], replicated
- bias_grad: float32 [32], replicated
- input_grad: float32 [4, 16, 256, 256], P(None, 'gx', 'gy', 'gz')
All inputs are finite; a program needn't handle non-finite values.
Results may differ from a plain program's by a relative error of at most 0.0029.
Values may be sent and summed in bfloat16 or wider, within the bound.
No kernel may reach another device: no remote copies, remote signals or barrier semaphores. Data moves between devices by JAX's collectives and lax.ppermute only.
A program may use at most 128 MiB of HBM per device.

v0:
```python
import functools

import jax
import jax.numpy as jnp
import numpy as np
from jax import lax
from jax.experimental import pallas as pl
from jax.experimental.pallas import tpu as pltpu
from jax.sharding import PartitionSpec as P

axes = ("gx", "gy", "gz")
f32, bf16 = jnp.float32, jnp.bfloat16
log_scale = 0.07
lanes = 128
limit = 48 * 1024 * 1024


def dot(a, b, contract=((1,), (0,))):
    return lax.dot_general(a, b, (contract, ((), ())), preferred_element_type=f32)


def iota(shape, dim):
    return lax.broadcasted_iota(jnp.int32, shape, dim)


def taken_from(array, offset):
    sizes = [lax.axis_size(axis) for axis in axes]
    pairs = []
    for place in np.ndindex(*sizes):
        source = [(p + o) % n for p, o, n in zip(place, offset, sizes)]
        pairs.append(
            (int(np.ravel_multi_index(source, sizes)), int(np.ravel_multi_index(place, sizes)))
        )
    return lax.ppermute(array, axes, pairs)


def pack_kernel(cells, edges, first, last, low, high, rows):
    chan, count_x, count_y, _ = cells.shape
    count = chan * count_x
    planes = [cells[c, x] for x in range(count_x) for c in range(chan)]
    wide = jnp.concatenate(planes, axis=1)
    row = iota((2 * count, count * lanes), 0)
    lane = iota((2 * count, count * lanes), 1)
    want = jnp.where(row < count, row * lanes, (row - count) * lanes + lanes - 1)
    pick = (lane == want).astype(f32).astype(bf16)
    found = dot(pick, wide, ((1,), (1,)))
    found = jnp.concatenate([found, jnp.zeros((2 * count, lanes - count_y), f32)], axis=1)
    edges[...] = pltpu.roll(found, 1, 1).astype(bf16)
    for at, plane in enumerate(planes):
        wide_plane = plane.astype(f32)
        rows[at : at + 1, :] = wide_plane[0:1]
        rows[count + at : count + at + 1, :] = wide_plane[count_y - 1 : count_y]
    first[...] = rows[0:count, :].astype(bf16)
    last[...] = rows[count : 2 * count, :].astype(bf16)
    low[...] = cells[:, 0]
    high[...] = cells[:, count_x - 1]


def main_kernel(
    cells, low, high, above, below, edges, cot, wbig, wback,
    pooled, wsum, grad, face_low, face_high, row_low, row_high, cols,
    stage, patches, left, right, spread, sums, field, outer, carry, gram,
):
    chan, count_x, count_y, _ = cells.shape
    chan_out = cot.shape[0]
    own = chan * count_x
    wide = own + 2 * chan
    depth = 3 * wide + 8
    lane = iota((wide, lanes), 1)

    for x in range(count_x + 2):
        for c in range(chan):
            if x == 0:
                plane = low[c]
            elif x == count_x + 1:
                plane = high[c]
            else:
                plane = cells[c, x - 1]
            stage[pl.ds(wide + x * chan + c, count_y, stride=wide), :] = plane.astype(f32)
    for ref, base in ((above, 0), (below, (count_y + 1) * wide)):
        stage[base : base + chan, :] = ref[0].astype(f32)[own - chan : own]
        stage[base + chan : base + chan + own, :] = ref[1].astype(f32)
        stage[base + chan + own : base + wide, :] = ref[2].astype(f32)[0:chan]
    for side, ref in ((1, left), (0, right)):
        at = slice(side * own, side * own + own)
        spot = iota((own, lanes), 1)
        whole = []
        for dx in range(3):
            mid = edges[dx, 1].astype(f32)[at]
            before = pltpu.roll(edges[dx, 0].astype(f32)[at], count_y, 1)
            after = pltpu.roll(edges[dx, 2].astype(f32)[at], lanes - count_y, 1)
            whole.append(jnp.where(spot == 0, before, jnp.where(spot == count_y + 1, after, mid)))
        ref[0:chan, :] = whole[0][own - chan : own]
        ref[chan : chan + own, :] = whole[1]
        ref[chan + own : wide, :] = whole[2][0:chan]
    left_cols, right_cols = left[...], right[...]
    for y in range(count_y + 2):
        mid = stage[y * wide : (y + 1) * wide, :]
        low_col = pltpu.roll(left_cols, (lanes - y) % lanes, 1)
        high_col = pltpu.roll(right_cols, (lanes - 1 - y) % lanes, 1)
        before = jnp.where(lane == 0, low_col, pltpu.roll(mid, 1, 1))
        after = jnp.where(lane == lanes - 1, high_col, pltpu.roll(mid, lanes - 1, 1))
        whole = jnp.concatenate([before, mid, after, jnp.ones((8, lanes), f32)], axis=0)
        patches[y * depth : (y + 1) * depth, :] = whole.astype(bf16)

    pool_x, pool_y, pool_z = cot.shape[1:]
    twice = jnp.where(
        iota((pool_z, lanes), 1) // 2 == iota((pool_z, lanes), 0), 0.125, 0.0
    ).astype(bf16)
    for o in range(chan_out):
        part = dot(cot[o].reshape(pool_x * pool_y, pool_z), twice)
        for x in range(pool_x):
            spread[pl.ds(x * chan_out + o, pool_y, stride=pool_x * chan_out), :] = part[
                x * pool_y : (x + 1) * pool_y
            ]

    carry[...] = jnp.zeros_like(carry)
    gram[...] = jnp.zeros_like(gram)
    pairs = 4

    def finish(y, whole):
        before = pltpu.roll(whole[0:wide], lanes - 1, 1)
        after = pltpu.roll(whole[2 * wide : 3 * wide], 1, 1)
        zero = jnp.zeros_like(before)
        inner = (
            whole[wide : 2 * wide]
            + jnp.where(lane == lanes - 1, zero, before)
            + jnp.where(lane == 0, zero, after)
        )
        rest = jnp.where(lane == lanes - 1, before, jnp.where(lane == 0, after, zero))
        place = pl.ds(pl.multiple_of(y * wide, 8), wide)
        field[place, :] = inner
        outer[place, :] = rest

    def step(i, _):
        deltas, blocks = [], []
        weights = wbig[...]
        for k in range(pairs):
            j = i * pairs + k
            block = jnp.concatenate(
                [
                    patches[pl.ds(pl.multiple_of((2 * j + h) * depth, 16), 3 * depth), :]
                    for h in range(2)
                ],
                axis=1,
            )
            preact = dot(weights, block)
            slope = jnp.tanh(5.0 * preact)
            linear = jnp.maximum(preact, 0.3 * preact)
            factor = 1.0 + jnp.abs(slope)
            here = spread[pl.ds(pl.multiple_of(j * pool_x * chan_out, 8), pool_x * chan_out), :]
            slope = 0.65 + 0.35 * slope
            delta = []
            for x in range(pool_x):
                top, mid = 2 * x * chan_out, (2 * x + 1) * chan_out
                end = mid + chan_out
                times = here[x * chan_out : (x + 1) * chan_out]
                times = jnp.concatenate([times, times], axis=1)
                delta.append((slope[top:mid] * times).astype(bf16))
                delta.append((slope[mid:end] * times).astype(bf16))
                total = linear[top:mid] + linear[mid:end]
                total = total[:, :lanes] + total[:, lanes:]
                prod = factor[top:mid] * factor[mid:end]
                prod = prod[:, :lanes] * prod[:, lanes:]
                total = total - log_scale * jnp.log(prod)
                sums[pl.ds(x * pool_y + j, chan_out, stride=pool_x * pool_y), :] = total
            deltas.append(jnp.concatenate(delta, axis=0))
            blocks.append(block)
        gram[...] += dot(
            jnp.concatenate(deltas, axis=1), jnp.concatenate(blocks, axis=1), ((1,), (1,))
        )
        back = wback[...]
        size = 3 * wide
        carry_a, carry_b = carry[0:size, :], carry[size : 2 * size, :]
        for k in range(pairs):
            j = i * pairs + k
            parts = dot(back, deltas[k])
            part = lambda b, h: parts[b * size : (b + 1) * size, h * lanes : (h + 1) * lanes]
            finish(2 * j, carry_a + part(0, 0))
            finish(2 * j + 1, carry_b + part(1, 0) + part(0, 1))
            carry_a = part(2, 0) + part(1, 1)
            carry_b = part(2, 1)
        carry[0:size, :] = carry_a
        carry[size : 2 * size, :] = carry_b
        return 0

    lax.fori_loop(0, count_y // (2 * pairs), step, 0)
    size = 3 * wide
    finish(count_y, carry[0:size, :])
    finish(count_y + 1, carry[size : 2 * size, :])

    span = gram.shape[1]
    straight, turned = 0.0, 0.0
    for x in range(count_x):
        part = gram[x * chan_out : (x + 1) * chan_out, :]
        part = jnp.concatenate([part, jnp.zeros((chan_out, 2 * lanes - span), f32)], axis=1)
        straight = straight + part
        turned = turned + (pltpu.roll(part, 2 * lanes - chan * x, 1) if x else part)
    wsum[...] = jnp.where(iota((chan_out, 2 * lanes), 1) == 3 * wide, straight, turned)

    halves = jnp.where(
        iota((2 * lanes, pool_z), 0) % lanes // 2 == iota((2 * lanes, pool_z), 1), 0.125, 0.0
    ).astype(bf16)
    for o in range(0, chan_out, 4):
        rows = 4 * pool_x * pool_y
        part = sums[o * pool_x * pool_y : o * pool_x * pool_y + rows, :]
        coarse = part.astype(bf16)
        fine = (part - coarse.astype(f32)).astype(bf16)
        mean = dot(jnp.concatenate([coarse, fine], axis=1), halves) + log_scale * float(np.log(2.0))
        pooled[o : o + 4] = mean.astype(bf16).reshape(4, pool_x, pool_y, pool_z)

    for x in range(count_x + 2):
        for c in range(chan):
            plane = field[pl.ds(wide + x * chan + c, count_y, stride=wide), :]
            if x == 0:
                face_low[c] = plane.astype(bf16)
            elif x == count_x + 1:
                face_high[c] = plane.astype(bf16)
            else:
                grad[c, x - 1] = plane
    row_low[...] = field[0:wide, :]
    row_high[...] = field[(count_y + 1) * wide : (count_y + 2) * wide, :]
    tall = cols.shape[0]
    outer[(count_y + 2) * wide :, :] = jnp.zeros((outer.shape[0] - (count_y + 2) * wide, lanes), f32)
    planes = [outer[pl.ds(r, tall, stride=wide), :].astype(bf16) for r in range(wide)]
    row = iota((wide * lanes, lanes), 0)
    spot = iota((wide * lanes, lanes), 1)
    want = jnp.where(spot < wide, spot * lanes + lanes - 1, (spot - wide) * lanes)
    pick = ((row == want) & (spot < 2 * wide)).astype(f32).astype(bf16)
    cols[...] = dot(jnp.concatenate(planes, axis=1), pick).astype(bf16)


def final_kernel(grad, low, high, above, below, cols, out):
    chan, count_x, count_y, _ = grad.shape
    own = chan * count_x
    wide = own + 2 * chan
    spot = iota((count_y, lanes), 1)
    row = iota((count_y, lanes), 0)
    total = 0.0
    for dx, turn, start in ((1, 0, chan), (0, lanes - own, chan), (2, own, own)):
        mid = cols[dx, 1].astype(f32)
        mid = mid[1 : count_y + 1]
        before = cols[dx, 0].astype(f32)[count_y + 1 : count_y + 2]
        after = cols[dx, 2].astype(f32)[0:1]
        mid = mid + jnp.where(row == 0, before, 0.0) + jnp.where(row == count_y - 1, after, 0.0)
        if turn:
            mid = pltpu.roll(mid, turn, 1)
            near = (spot >= start) & (spot < start + chan)
            near = near | ((spot >= wide + start) & (spot < wide + start + chan))
            mid = jnp.where(near, mid, 0.0)
        total = total + mid
    for x in range(count_x):
        for c in range(chan):
            r = chan + x * chan + c
            plane = grad[c, x]
            first = above[1][r : r + 1]
            final = below[1][r : r + 1]
            if x == 0:
                plane = plane + low[c].astype(f32)
                first = first + above[0][chan + own + c : chan + own + c + 1]
                final = final + below[0][chan + own + c : chan + own + c + 1]
            if x == count_x - 1:
                plane = plane + high[c].astype(f32)
                first = first + above[2][c : c + 1]
                final = final + below[2][c : c + 1]
            plane = plane + jnp.where(row == 0, first, 0.0)
            plane = plane + jnp.where(row == count_y - 1, final, 0.0)
            plane = plane + jnp.where(spot == lanes - 1, total[:, r : r + 1], 0.0)
            plane = plane + jnp.where(spot == 0, total[:, wide + r : wide + r + 1], 0.0)
            out[c, x] = plane


def call(kernel, outs, scratch=()):
    return pl.pallas_call(
        kernel,
        out_shape=outs,
        scratch_shapes=list(scratch),
        compiler_params=pltpu.CompilerParams(vmem_limit_bytes=limit),
    )


def summed(array, axis):
    count = lax.axis_size(axis)
    if count > 4:
        return lax.psum(array, axis)
    moved = [array] + [
        lax.ppermute(array, axis, [((i + k) % count, i) for i in range(count)])
        for k in range(1, count)
    ]
    if count == 4:
        return (moved[0] + moved[2]) + (moved[1] + moved[3])
    return sum(moved[1:], moved[0])


def on_device(cells, weight, bias, cotangent):
    chan, count_x, count_y, count_z = cells.shape
    chan_out = weight.shape[0]
    own = chan * count_x
    wide = own + 2 * chan
    depth = 3 * wide + 8
    shape = jax.ShapeDtypeStruct

    kernel = weight.transpose(0, 3, 4, 2, 1)
    placed = jnp.stack(
        [
            jnp.pad(kernel, ((0, 0), (0, 0), (0, 0), (x, count_x - 1 - x), (0, 0)))
            for x in range(count_x)
        ]
    ).reshape(count_x * chan_out, 3, 3 * wide)
    coarse = lax.reduce_precision(bias, 8, 7)
    middle = lax.reduce_precision(bias - coarse, 8, 7)
    fine = bias - coarse - middle
    pieces = jnp.stack([coarse, middle, fine], axis=1).astype(bf16)
    pieces = jnp.pad(jnp.tile(pieces, (count_x, 1))[:, None], ((0, 0), (0, 2), (0, 5)))
    wbig = jnp.concatenate([placed, pieces], axis=2).reshape(count_x * chan_out, 3 * depth)
    wback = placed.reshape(count_x * chan_out, 9 * wide).T

    edges, first, last, low, high = call(
        pack_kernel,
        [
            shape((2 * own, lanes), bf16),
            shape((own, lanes), bf16),
            shape((own, lanes), bf16),
            shape((chan, count_y, lanes), bf16),
            shape((chan, count_y, lanes), bf16),
        ],
        [pltpu.VMEM((2 * own, lanes), f32)],
    )(cells)
    steps = (-1, 0, 1)
    edges_in = jnp.stack(
        [jnp.stack([taken_from(edges, (dx, dy, 1)) for dy in steps]) for dx in steps]
    )
    above = jnp.stack([taken_from(last, (dx, -1, 0)) for dx in steps])
    below = jnp.stack([taken_from(first, (dx, 1, 0)) for dx in steps])
    low_in = taken_from(high, (-1, 0, 0))
    high_in = taken_from(low, (1, 0, 0))

    pool_x, pool_y, pool_z = cotangent.shape[1:]
    tall = 80
    pooled, wsum, grad, face_low, face_high, row_low, row_high, cols = call(
        main_kernel,
        [
            shape(cotangent.shape, bf16),
            shape((chan_out, 2 * lanes), f32),
            shape(cells.shape, f32),
            shape((chan, count_y, lanes), bf16),
            shape((chan, count_y, lanes), bf16),
            shape((wide, lanes), f32),
            shape((wide, lanes), f32),
            shape((tall, lanes), bf16),
        ],
        [
            pltpu.VMEM(((count_y + 2) * wide, lanes), f32),
            pltpu.VMEM(((count_y + 2) * depth, lanes), bf16),
            pltpu.VMEM((wide, lanes), f32),
            pltpu.VMEM((wide, lanes), f32),
            pltpu.VMEM((pool_y * pool_x * chan_out, lanes), f32),
            pltpu.VMEM((pool_y * pool_x * chan_out, lanes), f32),
            pltpu.VMEM(((count_y + 2) * wide, lanes), f32),
            pltpu.VMEM((tall * wide, lanes), f32),
            pltpu.VMEM((6 * wide, lanes), f32),
            pltpu.VMEM((count_x * chan_out, 3 * depth), f32),
        ],
    )(cells, low_in, high_in, above, below, edges_in, cotangent, wbig, wback)

    low_back = taken_from(face_high, (-1, 0, 0))
    high_back = taken_from(face_low, (1, 0, 0))
    above_back = jnp.stack([taken_from(row_high, (dx, -1, 0)) for dx in steps])
    below_back = jnp.stack([taken_from(row_low, (dx, 1, 0)) for dx in steps])
    cols_back = jnp.stack(
        [jnp.stack([taken_from(cols, (dx, dy, 1)) for dy in steps]) for dx in steps]
    )
    input_grad = call(final_kernel, shape(cells.shape, f32))(
        grad, low_back, high_back, above_back, below_back, cols_back
    )

    for axis in axes:
        wsum = summed(wsum, axis)
    bias_grad = wsum[:, 3 * wide]
    weight_grad = wsum[:, : 3 * depth].reshape(chan_out, 3, depth)[:, :, : 3 * wide]
    weight_grad = weight_grad.reshape(chan_out, 3, 3, count_x + 2, chan)[:, :, :, :3]
    return (pooled, weight_grad.transpose(0, 4, 3, 1, 2), bias_grad, input_grad)


def solution(mesh):
    in_specs = (P(None, "gx", "gy", "gz"), P(), P(), P(None, "gx", "gy", "gz"))
    out_specs = (P(None, "gx", "gy", "gz"), P(), P(), P(None, "gx", "gy", "gz"))
    return jax.shard_map(
        on_device, mesh=mesh, in_specs=in_specs, out_specs=out_specs, check_vma=False
    )
```

profile of v0, /device:TPU:0, one launch (start us, length us, event | category | flops | bytes accessed | tf_op | source)
XLA Modules:
  0.0 86.2 jit_solution(6943963403099089398)
XLA Ops:
  1.8 3.4 %collective-permute-start.8 = (bf16[32,128]{1,0:T(8,128)(2,1)S(1)}, bf16[32,128]{1,0:T(8,128)(2,1)S(1)}, u32[]{:S(2)}, u32[]{:S(2)}) collective-permute-start(bf16[32,128]{1,0:T(8,128)(2,1)S(1)} %get-tuple-element.21), channel_id=1, source_target_pairs={{31,0},{30,1},{25,2},{24,3},{27,4},{26,5},{29,6},{28,7},{7,8},{6,9... | collective-permute-start | bytes 24584 | tf_op jit(solution)/shard_map/ppermute | solution.py:34
  5.3 1.7 %collective-permute-start.9 = (bf16[32,128]{1,0:T(8,128)(2,1)S(1)}, bf16[32,128]{1,0:T(8,128)(2,1)S(1)}, u32[]{:S(2)}, u32[]{:S(2)}) collective-permute-start(bf16[32,128]{1,0:T(8,128)(2,1)S(1)} %get-tuple-element.21), channel_id=1, source_target_pairs={{25,0},{24,1},{27,2},{26,3},{29,4},{28,5},{31,6},{30,7},{1,8},{0,9... | collective-permute-start | bytes 24584 | tf_op jit(solution)/shard_map/ppermute | solution.py:34
  7.0 2.1 %collective-permute-start.5 = (bf16[16,128]{1,0:T(8,128)(2,1)S(1)}, bf16[16,128]{1,0:T(8,128)(2,1)S(1)}, u32[]{:S(2)}, u32[]{:S(2)}) collective-permute-start(bf16[16,128]{1,0:T(8,128)(2,1)S(1)} %get-tuple-element.20), channel_id=1, source_target_pairs={{26,0},{27,1},{28,2},{29,3},{30,4},{31,5},{24,6},{25,7},{2,8},{3,9... | collective-permute-start | bytes 12296 | tf_op jit(solution)/shard_map/ppermute | solution.py:34
  9.1 1.4 %collective-permute-start.6 = (bf16[16,128]{1,0:T(8,128)(2,1)S(1)}, bf16[16,128]{1,0:T(8,128)(2,1)S(1)}, u32[]{:S(2)}, u32[]{:S(2)}) collective-permute-start(bf16[16,128]{1,0:T(8,128)(2,1)S(1)} %get-tuple-element.20), channel_id=1, source_target_pairs={{2,0},{3,1},{4,2},{5,3},{6,4},{7,5},{0,6},{1,7},{10,8},{11,9},{12,... | collective-permute-start | bytes 12296 | tf_op jit(solution)/shard_map/ppermute | solution.py:34
  15.0 1.4 %collective-permute-start.4 = (bf16[16,128]{1,0:T(8,128)(2,1)S(1)}, bf16[16,128]{1,0:T(8,128)(2,1)S(1)}, u32[]{:S(2)}, u32[]{:S(2)}) collective-permute-start(bf16[16,128]{1,0:T(8,128)(2,1)S(1)} %get-tuple-element.19), channel_id=1, source_target_pairs={{14,0},{15,1},{8,2},{9,3},{10,4},{11,5},{12,6},{13,7},{22,8},{23,9... | collective-permute-start | bytes 12296 | tf_op jit(solution)/shard_map/ppermute | solution.py:34
  16.5 2.6 %collective-permute-done.2 = bf16[16,128]{1,0:T(8,128)(2,1)S(1)} collective-permute-done((bf16[16,128]{1,0:T(8,128)(2,1)S(1)}, bf16[16,128]{1,0:T(8,128)(2,1)S(1)}, u32[]{:S(2)}, u32[]{:S(2)}) %collective-permute-start.2) | collective-permute-done | bytes 4128 | tf_op jit(solution)/shard_map/ppermute | solution.py:34
  20.1 1.5 %collective-permute-start.12 = (bf16[32,128]{1,0:T(8,128)(2,1)S(1)}, bf16[32,128]{1,0:T(8,128)(2,1)S(1)}, u32[]{:S(2)}, u32[]{:S(2)}) collective-permute-start(bf16[32,128]{1,0:T(8,128)(2,1)S(1)} %get-tuple-element.21), channel_id=1, source_target_pairs={{1,0},{0,1},{3,2},{2,3},{5,4},{4,5},{7,6},{6,7},{9,8},{8,9},{11,10... | collective-permute-start | bytes 24584 | tf_op jit(solution)/shard_map/ppermute | solution.py:34
  21.6 3.9 %collective-permute-start.13 = (bf16[32,128]{1,0:T(8,128)(2,1)S(1)}, bf16[32,128]{1,0:T(8,128)(2,1)S(1)}, u32[]{:S(2)}, u32[]{:S(2)}) collective-permute-start(bf16[32,128]{1,0:T(8,128)(2,1)S(1)} %get-tuple-element.21), channel_id=1, source_target_pairs={{3,0},{2,1},{5,2},{4,3},{7,4},{6,5},{1,6},{0,7},{11,8},{10,9},{13,... | collective-permute-start | bytes 24584 | tf_op jit(solution)/shard_map/ppermute | solution.py:34
  27.1 4.4 %collective-permute-start.16 = (bf16[32,128]{1,0:T(8,128)(2,1)S(1)}, bf16[32,128]{1,0:T(8,128)(2,1)S(1)}, u32[]{:S(2)}, u32[]{:S(2)}) collective-permute-start(bf16[32,128]{1,0:T(8,128)(2,1)S(1)} %get-tuple-element.21), channel_id=1, source_target_pairs={{11,0},{10,1},{13,2},{12,3},{15,4},{14,5},{9,6},{8,7},{19,8},{18,9... | collective-permute-start | bytes 24584 | tf_op jit(solution)/shard_map/ppermute | solution.py:34
  31.6 1.7 %collective-permute-start.1 = (bf16[4,64,128]{2,1,0:T(8,128)(2,1)S(1)}, bf16[4,64,128]{2,1,0:T(8,128)(2,1)S(1)}, u32[]{:S(2)}, u32[]{:S(2)}) collective-permute-start(bf16[4,64,128]{2,1,0:T(8,128)(2,1)S(1)} %get-tuple-element.18), channel_id=1, source_target_pairs={{8,0},{9,1},{10,2},{11,3},{12,4},{13,5},{14,6},{15,7},{16,8},{17,9... | collective-permute-start | bytes 196616 | tf_op jit(solution)/shard_map/ppermute | solution.py:34
  33.4 1.9 %collective-permute-done.low = bf16[4,64,128]{2,1,0:T(8,128)(2,1)S(1)} collective-permute-done((bf16[4,64,128]{2,1,0:T(8,128)(2,1)S(1)}, bf16[4,64,128]{2,1,0:T(8,128)(2,1)S(1)}, u32[]{:S(2)}, u32[]{:S(2)}) %collective-permute-start) | collective-permute-done | bytes 65568 | tf_op jit(solution)/shard_map/ppermute | solution.py:34
  35.3 8.7 %shard_map.76 = (bf16[32,2,32,64]{3,2,1,0:T(8,128)(2,1)}, f32[32,256]{1,0:T(8,128)S(1)}, f32[4,4,64,128]{3,2,1,0:T(8,128)S(1)}, bf16[4,64,128]{2,1,0:T(8,128)(2,...) custom-call(bf16[4,4,64,128]{3,2,1,0:T(8,128)(2,1)S(1)} %copy-done.1, ...), custom_call_target="tpu_custom_call" | custom-call | tf_op jit(solution)/shard_map/pallas_call | solution.py:340
  44.0 2.1 %collective-permute-start.29 = (f32[24,128]{1,0:T(8,128)S(1)}, f32[24,128]{1,0:T(8,128)S(1)}, u32[]{:S(2)}, u32[]{:S(2)}) collective-permute-start(f32[24,128]{1,0:T(8,128)S(1)} %get-tuple-element.28), channel_id=1, source_target_pairs={{26,0},{27,1},{28,2},{29,3},{30,4},{31,5},{24,6},{25,7},{2,8},{3,9... | collective-permute-start | bytes 36872 | tf_op jit(solution)/shard_map/ppermute | solution.py:34
  46.1 2.7 %collective-permute-start.32 = (bf16[80,128]{1,0:T(8,128)(2,1)S(1)}, bf16[80,128]{1,0:T(8,128)(2,1)S(1)}, u32[]{:S(2)}, u32[]{:S(2)}) collective-permute-start(bf16[80,128]{1,0:T(8,128)(2,1)S(1)} %get-tuple-element.29), channel_id=1, source_target_pairs={{31,0},{30,1},{25,2},{24,3},{27,4},{26,5},{29,6},{28,7},{7,8},{6,9... | collective-permute-start | bytes 61448 | tf_op jit(solution)/shard_map/ppermute | solution.py:34
  53.5 2.3 %collective-permute-done.26 = f32[24,128]{1,0:T(8,128)S(1)} collective-permute-done((f32[24,128]{1,0:T(8,128)S(1)}, f32[24,128]{1,0:T(8,128)S(1)}, u32[]{:S(2)}, u32[]{:S(2)}) %collective-permute-start.26) | collective-permute-done | bytes 12320 | tf_op jit(solution)/shard_map/ppermute | solution.py:34
  58.4 4.4 %collective-permute-start.37 = (bf16[80,128]{1,0:T(8,128)(2,1)S(1)}, bf16[80,128]{1,0:T(8,128)(2,1)S(1)}, u32[]{:S(2)}, u32[]{:S(2)}) collective-permute-start(bf16[80,128]{1,0:T(8,128)(2,1)S(1)} %get-tuple-element.29), channel_id=1, source_target_pairs={{3,0},{2,1},{5,2},{4,3},{7,4},{6,5},{1,6},{0,7},{11,8},{10,9},{13,... | collective-permute-start | bytes 61448 | tf_op jit(solution)/shard_map/ppermute | solution.py:34
  65.0 2.5 %collective-permute-done.17 = f32[32,256]{1,0:T(8,128)S(1)} collective-permute-done((f32[32,256]{1,0:T(8,128)S(1)}, f32[32,256]{1,0:T(8,128)S(1)}, u32[]{:S(2)}, u32[]{:S(2)}) %collective-permute-start.17) | collective-permute-done | bytes 32800 | tf_op jit(solution)/shard_map/ppermute | solution.py:287
  67.6 3.5 %collective-permute-start.40 = (bf16[80,128]{1,0:T(8,128)(2,1)S(1)}, bf16[80,128]{1,0:T(8,128)(2,1)S(1)}, u32[]{:S(2)}, u32[]{:S(2)}) collective-permute-start(bf16[80,128]{1,0:T(8,128)(2,1)S(1)} %get-tuple-element.29), channel_id=1, source_target_pairs={{11,0},{10,1},{13,2},{12,3},{15,4},{14,5},{9,6},{8,7},{19,8},{18,9... | collective-permute-start | bytes 61448 | tf_op jit(solution)/shard_map/ppermute | solution.py:34
  71.1 1.7 %collective-permute-start.24 = (bf16[4,64,128]{2,1,0:T(8,128)(2,1)S(1)}, bf16[4,64,128]{2,1,0:T(8,128)(2,1)S(1)}, u32[]{:S(2)}, u32[]{:S(2)}) collective-permute-start(bf16[4,64,128]{2,1,0:T(8,128)(2,1)S(1)} %get-tuple-element.25), channel_id=1, source_target_pairs={{24,0},{25,1},{26,2},{27,3},{28,4},{29,5},{30,6},{31,7},{0,8},{1,9... | collective-permute-start | bytes 196616 | tf_op jit(solution)/shard_map/ppermute | solution.py:34
  73.1 1.7 %collective-permute-start.21 = (f32[32,256]{1,0:T(8,128)S(1)}, f32[32,256]{1,0:T(8,128)S(1)}, u32[]{:S(2)}, u32[]{:S(2)}) collective-permute-start(f32[32,256]{1,0:T(8,128)S(1)} %add_add_fusion.1), channel_id=1, source_target_pairs={{2,0},{4,2},{6,4},{0,6},{3,1},{5,3},{7,5},{1,7},{10,8},{12,10},{14... | collective-permute-start | bytes 98312 | tf_op jit(solution)/shard_map/ppermute | solution.py:287
  75.4 2.5 %collective-permute-done.20 = f32[32,256]{1,0:T(8,128)S(1)} collective-permute-done((f32[32,256]{1,0:T(8,128)S(1)}, f32[32,256]{1,0:T(8,128)S(1)}, u32[]{:S(2)}, u32[]{:S(2)}) %collective-permute-start.20) | collective-permute-done | bytes 32800 | tf_op jit(solution)/shard_map/ppermute | solution.py:287
  77.9 2.8 %collective-permute-done.22 = f32[32,256]{1,0:T(8,128)S(1)} collective-permute-done((f32[32,256]{1,0:T(8,128)S(1)}, f32[32,256]{1,0:T(8,128)S(1)}, u32[]{:S(2)}, u32[]{:S(2)}) %collective-permute-start.22) | collective-permute-done | bytes 32800 | tf_op jit(solution)/shard_map/ppermute | solution.py:287
  81.3 1.3 %shard_map.77 = f32[4,4,64,128]{3,2,1,0:T(8,128)} custom-call(f32[4,4,64,128]{3,2,1,0:T(8,128)S(1)} %get-tuple-element.24.grad, bf16[4,64,128]{2,1,0:T(8,128)(2,1)S(1)} %collective-permute-done.24.low, bf16[4,64,128]{2,1,0:T(8,128)(2,1)S(1)} %collective-permute-done.25.high, f32[3,24,128]{2,1,0:T(8,128)S(1)} %pad_maximum_fusion.3.above, ...), custom_call_target="tpu_custom_call" | custom-call | tf_op jit(solution)/shard_map/pallas_call | solution.py:373
  82.7 2.0 %collective-permute-done.23 = f32[32,256]{1,0:T(8,128)S(1)} collective-permute-done((f32[32,256]{1,0:T(8,128)S(1)}, f32[32,256]{1,0:T(8,128)S(1)}, u32[]{:S(2)}, u32[]{:S(2)}) %collective-permute-start.23) | collective-permute-done | bytes 32800 | tf_op jit(solution)/shard_map/ppermute | solution.py:287
  (102 shorter events, 20.9 us)
Async XLA Ops:
  1.8 19.7 %collective-permute-start.8 = (bf16[32,128]{1,0:T(8,128)(2,1)S(1)}, bf16[32,128]{1,0:T(8,128)(2,1)S(1)}, u32[]{:S(2)}, u32[]{:S(2)}) collective-permute-start(bf16[32,128]{1,0:T(8,128)(2,1)S(1)} %get-tuple-element.21), channel_id=1, source_target_pairs={{31,0},{30,1},{25,2},{24,3},{27,4},{26,5},{29,6},{28,7},{7,8},{6,9... | collective-permute-start | bytes 24584 | tf_op jit(solution)/shard_map/ppermute | solution.py:34
  5.3 20.2 %collective-permute-start.9 = (bf16[32,128]{1,0:T(8,128)(2,1)S(1)}, bf16[32,128]{1,0:T(8,128)(2,1)S(1)}, u32[]{:S(2)}, u32[]{:S(2)}) collective-permute-start(bf16[32,128]{1,0:T(8,128)(2,1)S(1)} %get-tuple-element.21), channel_id=1, source_target_pairs={{25,0},{24,1},{27,2},{26,3},{29,4},{28,5},{31,6},{30,7},{1,8},{0,9... | collective-permute-start | bytes 24584 | tf_op jit(solution)/shard_map/ppermute | solution.py:34
  7.0 6.3 %collective-permute-start.5 = (bf16[16,128]{1,0:T(8,128)(2,1)S(1)}, bf16[16,128]{1,0:T(8,128)(2,1)S(1)}, u32[]{:S(2)}, u32[]{:S(2)}) collective-permute-start(bf16[16,128]{1,0:T(8,128)(2,1)S(1)} %get-tuple-element.20), channel_id=1, source_target_pairs={{26,0},{27,1},{28,2},{29,3},{30,4},{31,5},{24,6},{25,7},{2,8},{3,9... | collective-permute-start | bytes 12296 | tf_op jit(solution)/shard_map/ppermute | solution.py:34
  19.1 7.2 %collective-permute-start.10 = (bf16[32,128]{1,0:T(8,128)(2,1)S(1)}, bf16[32,128]{1,0:T(8,128)(2,1)S(1)}, u32[]{:S(2)}, u32[]{:S(2)}) collective-permute-start(bf16[32,128]{1,0:T(8,128)(2,1)S(1)} %get-tuple-element.21), channel_id=1, source_target_pairs={{27,0},{26,1},{29,2},{28,3},{31,4},{30,5},{25,6},{24,7},{3,8},{2,9... | collective-permute-start | bytes 24584 | tf_op jit(solution)/shard_map/ppermute | solution.py:34
  19.6 7.6 %collective-permute-start.11 = (bf16[32,128]{1,0:T(8,128)(2,1)S(1)}, bf16[32,128]{1,0:T(8,128)(2,1)S(1)}, u32[]{:S(2)}, u32[]{:S(2)}) collective-permute-start(bf16[32,128]{1,0:T(8,128)(2,1)S(1)} %get-tuple-element.21), channel_id=1, source_target_pairs={{7,0},{6,1},{1,2},{0,3},{3,4},{2,5},{5,6},{4,7},{15,8},{14,9},{9,1... | collective-permute-start | bytes 24584 | tf_op jit(solution)/shard_map/ppermute | solution.py:34
  20.1 11.5 %collective-permute-start.12 = (bf16[32,128]{1,0:T(8,128)(2,1)S(1)}, bf16[32,128]{1,0:T(8,128)(2,1)S(1)}, u32[]{:S(2)}, u32[]{:S(2)}) collective-permute-start(bf16[32,128]{1,0:T(8,128)(2,1)S(1)} %get-tuple-element.21), channel_id=1, source_target_pairs={{1,0},{0,1},{3,2},{2,3},{5,4},{4,5},{7,6},{6,7},{9,8},{8,9},{11,10... | collective-permute-start | bytes 24584 | tf_op jit(solution)/shard_map/ppermute | solution.py:34
  21.6 10.0 %collective-permute-start.13 = (bf16[32,128]{1,0:T(8,128)(2,1)S(1)}, bf16[32,128]{1,0:T(8,128)(2,1)S(1)}, u32[]{:S(2)}, u32[]{:S(2)}) collective-permute-start(bf16[32,128]{1,0:T(8,128)(2,1)S(1)} %get-tuple-element.21), channel_id=1, source_target_pairs={{3,0},{2,1},{5,2},{4,3},{7,4},{6,5},{1,6},{0,7},{11,8},{10,9},{13,... | collective-permute-start | bytes 24584 | tf_op jit(solution)/shard_map/ppermute | solution.py:34
  25.5 7.8 %collective-permute-start.14 = (bf16[32,128]{1,0:T(8,128)(2,1)S(1)}, bf16[32,128]{1,0:T(8,128)(2,1)S(1)}, u32[]{:S(2)}, u32[]{:S(2)}) collective-permute-start(bf16[32,128]{1,0:T(8,128)(2,1)S(1)} %get-tuple-element.21), channel_id=1, source_target_pairs={{15,0},{14,1},{9,2},{8,3},{11,4},{10,5},{13,6},{12,7},{23,8},{22,9... | collective-permute-start | bytes 24584 | tf_op jit(solution)/shard_map/ppermute | solution.py:34
  26.3 7.0 %collective-permute-start.15 = (bf16[32,128]{1,0:T(8,128)(2,1)S(1)}, bf16[32,128]{1,0:T(8,128)(2,1)S(1)}, u32[]{:S(2)}, u32[]{:S(2)}) collective-permute-start(bf16[32,128]{1,0:T(8,128)(2,1)S(1)} %get-tuple-element.21), channel_id=1, source_target_pairs={{9,0},{8,1},{11,2},{10,3},{13,4},{12,5},{15,6},{14,7},{17,8},{16,9... | collective-permute-start | bytes 24584 | tf_op jit(solution)/shard_map/ppermute | solution.py:34
  27.1 6.2 %collective-permute-start.16 = (bf16[32,128]{1,0:T(8,128)(2,1)S(1)}, bf16[32,128]{1,0:T(8,128)(2,1)S(1)}, u32[]{:S(2)}, u32[]{:S(2)}) collective-permute-start(bf16[32,128]{1,0:T(8,128)(2,1)S(1)} %get-tuple-element.21), channel_id=1, source_target_pairs={{11,0},{10,1},{13,2},{12,3},{15,4},{14,5},{9,6},{8,7},{19,8},{18,9... | collective-permute-start | bytes 24584 | tf_op jit(solution)/shard_map/ppermute | solution.py:34
  46.1 6.1 %collective-permute-start.31 = (f32[24,128]{1,0:T(8,128)S(1)}, f32[24,128]{1,0:T(8,128)S(1)}, u32[]{:S(2)}, u32[]{:S(2)}) collective-permute-start(f32[24,128]{1,0:T(8,128)S(1)} %get-tuple-element.28), channel_id=1, source_target_pairs={{10,0},{11,1},{12,2},{13,3},{14,4},{15,5},{8,6},{9,7},{18,8},{19,9... | collective-permute-start | bytes 36872 | tf_op jit(solution)/shard_map/ppermute | solution.py:34
  46.1 12.3 %collective-permute-start.32 = (bf16[80,128]{1,0:T(8,128)(2,1)S(1)}, bf16[80,128]{1,0:T(8,128)(2,1)S(1)}, u32[]{:S(2)}, u32[]{:S(2)}) collective-permute-start(bf16[80,128]{1,0:T(8,128)(2,1)S(1)} %get-tuple-element.29), channel_id=1, source_target_pairs={{31,0},{30,1},{25,2},{24,3},{27,4},{26,5},{29,6},{28,7},{7,8},{6,9... | collective-permute-start | bytes 61448 | tf_op jit(solution)/shard_map/ppermute | solution.py:34
  48.8 14.0 %collective-permute-start.33 = (bf16[80,128]{1,0:T(8,128)(2,1)S(1)}, bf16[80,128]{1,0:T(8,128)(2,1)S(1)}, u32[]{:S(2)}, u32[]{:S(2)}) collective-permute-start(bf16[80,128]{1,0:T(8,128)(2,1)S(1)} %get-tuple-element.29), channel_id=1, source_target_pairs={{25,0},{24,1},{27,2},{26,3},{29,4},{28,5},{31,6},{30,7},{1,8},{0,9... | collective-permute-start | bytes 61448 | tf_op jit(solution)/shard_map/ppermute | solution.py:34
  55.7 7.2 %collective-permute-start.34 = (bf16[80,128]{1,0:T(8,128)(2,1)S(1)}, bf16[80,128]{1,0:T(8,128)(2,1)S(1)}, u32[]{:S(2)}, u32[]{:S(2)}) collective-permute-start(bf16[80,128]{1,0:T(8,128)(2,1)S(1)} %get-tuple-element.29), channel_id=1, source_target_pairs={{27,0},{26,1},{29,2},{28,3},{31,4},{30,5},{25,6},{24,7},{3,8},{2,9... | collective-permute-start | bytes 61448 | tf_op jit(solution)/shard_map/ppermute | solution.py:34
  56.5 7.1 %collective-permute-start.35 = (bf16[80,128]{1,0:T(8,128)(2,1)S(1)}, bf16[80,128]{1,0:T(8,128)(2,1)S(1)}, u32[]{:S(2)}, u32[]{:S(2)}) collective-permute-start(bf16[80,128]{1,0:T(8,128)(2,1)S(1)} %get-tuple-element.29), channel_id=1, source_target_pairs={{7,0},{6,1},{1,2},{0,3},{3,4},{2,5},{5,6},{4,7},{15,8},{14,9},{9,1... | collective-permute-start | bytes 61448 | tf_op jit(solution)/shard_map/ppermute | solution.py:34
  57.3 7.2 %collective-permute-start.36 = (bf16[80,128]{1,0:T(8,128)(2,1)S(1)}, bf16[80,128]{1,0:T(8,128)(2,1)S(1)}, u32[]{:S(2)}, u32[]{:S(2)}) collective-permute-start(bf16[80,128]{1,0:T(8,128)(2,1)S(1)} %get-tuple-element.29), channel_id=1, source_target_pairs={{1,0},{0,1},{3,2},{2,3},{5,4},{4,5},{7,6},{6,7},{9,8},{8,9},{11,10... | collective-permute-start | bytes 61448 | tf_op jit(solution)/shard_map/ppermute | solution.py:34
  58.4 6.6 %collective-permute-start.37 = (bf16[80,128]{1,0:T(8,128)(2,1)S(1)}, bf16[80,128]{1,0:T(8,128)(2,1)S(1)}, u32[]{:S(2)}, u32[]{:S(2)}) collective-permute-start(bf16[80,128]{1,0:T(8,128)(2,1)S(1)} %get-tuple-element.29), channel_id=1, source_target_pairs={{3,0},{2,1},{5,2},{4,3},{7,4},{6,5},{1,6},{0,7},{11,8},{10,9},{13,... | collective-permute-start | bytes 61448 | tf_op jit(solution)/shard_map/ppermute | solution.py:34
  62.8 10.2 %collective-permute-start.38 = (bf16[80,128]{1,0:T(8,128)(2,1)S(1)}, bf16[80,128]{1,0:T(8,128)(2,1)S(1)}, u32[]{:S(2)}, u32[]{:S(2)}) collective-permute-start(bf16[80,128]{1,0:T(8,128)(2,1)S(1)} %get-tuple-element.29), channel_id=1, source_target_pairs={{15,0},{14,1},{9,2},{8,3},{11,4},{10,5},{13,6},{12,7},{23,8},{22,9... | collective-permute-start | bytes 61448 | tf_op jit(solution)/shard_map/ppermute | solution.py:34
  62.9 10.2 %collective-permute-start.39 = (bf16[80,128]{1,0:T(8,128)(2,1)S(1)}, bf16[80,128]{1,0:T(8,128)(2,1)S(1)}, u32[]{:S(2)}, u32[]{:S(2)}) collective-permute-start(bf16[80,128]{1,0:T(8,128)(2,1)S(1)} %get-tuple-element.29), channel_id=1, source_target_pairs={{9,0},{8,1},{11,2},{10,3},{13,4},{12,5},{15,6},{14,7},{17,8},{16,9... | collective-permute-start | bytes 61448 | tf_op jit(solution)/shard_map/ppermute | solution.py:34
  64.5 6.6 %collective-permute-start.18 = (f32[32,256]{1,0:T(8,128)S(1)}, f32[32,256]{1,0:T(8,128)S(1)}, u32[]{:S(2)}, u32[]{:S(2)}) collective-permute-start(f32[32,256]{1,0:T(8,128)S(1)} %get-tuple-element.23), channel_id=1, source_target_pairs={{8,0},{16,8},{24,16},{0,24},{9,1},{17,9},{25,17},{1,25},{10,2},{18... | collective-permute-start | bytes 98312 | tf_op jit(solution)/shard_map/ppermute | solution.py:287
  65.0 7.8 %collective-permute-start.19 = (f32[32,256]{1,0:T(8,128)S(1)}, f32[32,256]{1,0:T(8,128)S(1)}, u32[]{:S(2)}, u32[]{:S(2)}) collective-permute-start(f32[32,256]{1,0:T(8,128)S(1)} %get-tuple-element.23), channel_id=1, source_target_pairs={{24,0},{0,8},{8,16},{16,24},{25,1},{1,9},{9,17},{17,25},{26,2},{2,... | collective-permute-start | bytes 98312 | tf_op jit(solution)/shard_map/ppermute | solution.py:287
  67.6 7.2 %collective-permute-start.40 = (bf16[80,128]{1,0:T(8,128)(2,1)S(1)}, bf16[80,128]{1,0:T(8,128)(2,1)S(1)}, u32[]{:S(2)}, u32[]{:S(2)}) collective-permute-start(bf16[80,128]{1,0:T(8,128)(2,1)S(1)} %get-tuple-element.29), channel_id=1, source_target_pairs={{11,0},{10,1},{13,2},{12,3},{15,4},{14,5},{9,6},{8,7},{19,8},{18,9... | collective-permute-start | bytes 61448 | tf_op jit(solution)/shard_map/ppermute | solution.py:34
  71.1 10.3 %collective-permute-start.24 = (bf16[4,64,128]{2,1,0:T(8,128)(2,1)S(1)}, bf16[4,64,128]{2,1,0:T(8,128)(2,1)S(1)}, u32[]{:S(2)}, u32[]{:S(2)}) collective-permute-start(bf16[4,64,128]{2,1,0:T(8,128)(2,1)S(1)} %get-tuple-element.25), channel_id=1, source_target_pairs={{24,0},{25,1},{26,2},{27,3},{28,4},{29,5},{30,6},{31,7},{0,8},{1,9... | collective-permute-start | bytes 196616 | tf_op jit(solution)/shard_map/ppermute | solution.py:34
  72.8 8.6 %collective-permute-start.25 = (bf16[4,64,128]{2,1,0:T(8,128)(2,1)S(1)}, bf16[4,64,128]{2,1,0:T(8,128)(2,1)S(1)}, u32[]{:S(2)}, u32[]{:S(2)}) collective-permute-start(bf16[4,64,128]{2,1,0:T(8,128)(2,1)S(1)} %get-tuple-element.26), channel_id=1, source_target_pairs={{8,0},{9,1},{10,2},{11,3},{12,4},{13,5},{14,6},{15,7},{16,8},{17,9... | collective-permute-start | bytes 196616 | tf_op jit(solution)/shard_map/ppermute | solution.py:34
  (22 other events, 140.4 us)
where the time goes:
time: 86.4 us; the launch traced here: 86.2 us
  starting transfers between devices  53.6 us (62%)
  waiting for transfers between devices  17.4 us (20%)
  Pallas kernels  10.3 us (12%)
  local copies, waits for them, and re-layouts  3.63 us (4%)
  between operations  0.88 us (1%)
    ppermute x34, starting transfers between devices, taken_from(): return lax.ppermute(array, axes, pairs)  49.3 us
    ppermute x7, waiting for transfers between devices, summed(): lax.ppermute(array, axis, [((i + k) % count, i) for i in range(count)])  9.88 us
    pallas_call x1, Pallas kernels, on_device(): call(main_kernel, [shape(cotangent.shape, bf16), shape((chan_out, 2 * lan...  8.69 us
    ppermute x34, waiting for transfers between devices, taken_from(): return lax.ppermute(array, axes, pairs)  7.55 us
    ppermute x7, starting transfers between devices, summed(): lax.ppermute(array, axis, [((i + k) % count, i) for i in range(count)])  4.36 us
    unnamed x11, local copies, waits for them, and re-layouts  2.08 us
  transfers between devices with their start and end apart: 41, of which 8 were waited for; matrix products, arithmetic and copies ran while one was open for 1% of the time, Pallas kernels for 2%

commit v1 on v0

--- a/solution.py
+++ b/solution.py
@@ -34,7 +34,14 @@
     return lax.ppermute(array, axes, pairs)
 
 
-def pack_kernel(cells, edges, first, last, low, high, rows):
+def place_of(offset, sizes):
+    at = 0
+    for axis, step, size in zip(axes, offset, sizes):
+        at = at * size + lax.rem(lax.axis_index(axis) + step + size, size)
+    return at
+
+
+def pack_kernel(cells, frame, low, high, rows):
     chan, count_x, count_y, _ = cells.shape
     count = chan * count_x
     planes = [cells[c, x] for x in range(count_x) for c in range(chan)]
@@ -45,20 +52,20 @@
     pick = (lane == want).astype(f32).astype(bf16)
     found = dot(pick, wide, ((1,), (1,)))
     found = jnp.concatenate([found, jnp.zeros((2 * count, lanes - count_y), f32)], axis=1)
-    edges[...] = pltpu.roll(found, 1, 1).astype(bf16)
+    frame[0 : 2 * count, :] = pltpu.roll(found, 1, 1).astype(bf16)
     for at, plane in enumerate(planes):
         wide_plane = plane.astype(f32)
         rows[at : at + 1, :] = wide_plane[0:1]
         rows[count + at : count + at + 1, :] = wide_plane[count_y - 1 : count_y]
-    first[...] = rows[0:count, :].astype(bf16)
-    last[...] = rows[count : 2 * count, :].astype(bf16)
+    frame[2 * count :, :] = rows[...].astype(bf16)
     low[...] = cells[:, 0]
     high[...] = cells[:, count_x - 1]
 
 
 def main_kernel(
-    cells, low, high, above, below, edges, cot, wbig, wback,
-    pooled, wsum, grad, face_low, face_high, row_low, row_high, cols,
+    sizes,
+    cells, low, high, frames, cot, wbig, wback,
+    pooled, grad, face_low, face_high, frame_out,
     stage, patches, left, right, spread, sums, field, outer, carry, gram,
 ):
     chan, count_x, count_y, _ = cells.shape
@@ -77,18 +84,25 @@
             else:
                 plane = cells[c, x - 1]
             stage[pl.ds(wide + x * chan + c, count_y, stride=wide), :] = plane.astype(f32)
-    for ref, base in ((above, 0), (below, (count_y + 1) * wide)):
-        stage[base : base + chan, :] = ref[0].astype(f32)[own - chan : own]
-        stage[base + chan : base + chan + own, :] = ref[1].astype(f32)
-        stage[base + chan + own : base + wide, :] = ref[2].astype(f32)[0:chan]
+    for dy, base in ((-1, 0), (1, (count_y + 1) * wide)):
+        top = (3 if dy < 0 else 2) * own
+        rows = [
+            frames[place_of((dx, dy, 0), sizes), top : top + own, :].astype(f32)
+            for dx in (-1, 0, 1)
+        ]
+        stage[base : base + chan, :] = rows[0][own - chan : own]
+        stage[base + chan : base + chan + own, :] = rows[1]
+        stage[base + chan + own : base + wide, :] = rows[2][0:chan]
     for side, ref in ((1, left), (0, right)):
         at = slice(side * own, side * own + own)
         spot = iota((own, lanes), 1)
         whole = []
         for dx in range(3):
-            mid = edges[dx, 1].astype(f32)[at]
-            before = pltpu.roll(edges[dx, 0].astype(f32)[at], count_y, 1)
-            after = pltpu.roll(edges[dx, 2].astype(f32)[at], lanes - count_y, 1)
+            before, mid, after = [
+                frames[place_of((dx - 1, dy, 1), sizes), at, :].astype(f32) for dy in (-1, 0, 1)
+            ]
+            before = pltpu.roll(before, count_y, 1)
+            after = pltpu.roll(after, lanes - count_y, 1)
             whole.append(jnp.where(spot == 0, before, jnp.where(spot == count_y + 1, after, mid)))
         ref[0:chan, :] = whole[0][own - chan : own]
         ref[chan : chan + own, :] = whole[1]
@@ -196,7 +210,19 @@
         part = jnp.concatenate([part, jnp.zeros((chan_out, 2 * lanes - span), f32)], axis=1)
         straight = straight + part
         turned = turned + (pltpu.roll(part, 2 * lanes - chan * x, 1) if x else part)
-    wsum[...] = jnp.where(iota((chan_out, 2 * lanes), 1) == 3 * wide, straight, turned)
+    spot = iota((chan_out, lanes), 1)
+    tight = 0.0
+    group = 3 * chan
+    for b in range(3):
+        for e in range(3):
+            shift = (b * depth + e * wide) - (b * 3 + e) * group
+            part = pltpu.roll(turned, 2 * lanes - shift, 1)[:, :lanes] if shift else turned[:, :lanes]
+            tight = jnp.where(spot // group == b * 3 + e, part, tight)
+    part = pltpu.roll(straight, 2 * lanes + 9 * group - 3 * wide, 1)[:, :lanes]
+    tight = jnp.where(spot == 9 * group, part, tight)
+    coarse = tight.astype(bf16)
+    frame_out[0:chan_out, :] = coarse
+    frame_out[chan_out : 2 * chan_out, :] = (tight - coarse.astype(f32)).astype(bf16)
 
     halves = jnp.where(
         iota((2 * lanes, pool_z), 0) % lanes // 2 == iota((2 * lanes, pool_z), 1), 0.125, 0.0
@@ -218,30 +244,48 @@
                 face_high[c] = plane.astype(bf16)
             else:
                 grad[c, x - 1] = plane
-    row_low[...] = field[0:wide, :]
-    row_high[...] = field[(count_y + 1) * wide : (count_y + 2) * wide, :]
-    tall = cols.shape[0]
+    top = 2 * chan_out
+    ends = [field[0:wide, :], field[(count_y + 1) * wide : (count_y + 2) * wide, :]]
+    frame_out[top : top + 2 * wide, :] = jnp.concatenate(ends, axis=0).astype(bf16)
+    top = top + 2 * wide
+    tall = frame_out.shape[0] - top
     outer[(count_y + 2) * wide :, :] = jnp.zeros((outer.shape[0] - (count_y + 2) * wide, lanes), f32)
     planes = [outer[pl.ds(r, tall, stride=wide), :].astype(bf16) for r in range(wide)]
     row = iota((wide * lanes, lanes), 0)
     spot = iota((wide * lanes, lanes), 1)
     want = jnp.where(spot < wide, spot * lanes + lanes - 1, (spot - wide) * lanes)
     pick = ((row == want) & (spot < 2 * wide)).astype(f32).astype(bf16)
-    cols[...] = dot(jnp.concatenate(planes, axis=1), pick).astype(bf16)
-
-
-def final_kernel(grad, low, high, above, below, cols, out):
+    frame_out[top:, :] = dot(jnp.concatenate(planes, axis=1), pick).astype(bf16)
+
+
+def final_kernel(sizes, grad, low, high, frames, out, wout):
     chan, count_x, count_y, _ = grad.shape
+    chan_out = wout.shape[0]
     own = chan * count_x
     wide = own + 2 * chan
+    coarse, fine = 0.0, 0.0
+    for at in range(frames.shape[0]):
+        coarse = coarse + frames[at, 0:chan_out, :].astype(f32)
+        fine = fine + frames[at, chan_out : 2 * chan_out, :].astype(f32)
+    wout[...] = coarse + fine
+    top = 2 * chan_out
+    above, below = [], []
+    for dx in (-1, 0, 1):
+        rows = frames[place_of((dx, -1, 0), sizes), top : top + 2 * wide, :]
+        above.append(rows.astype(f32)[wide:])
+        rows = frames[place_of((dx, 1, 0), sizes), top : top + 2 * wide, :]
+        below.append(rows.astype(f32)[:wide])
+    top = top + 2 * wide
     spot = iota((count_y, lanes), 1)
     row = iota((count_y, lanes), 0)
     total = 0.0
     for dx, turn, start in ((1, 0, chan), (0, lanes - own, chan), (2, own, own)):
-        mid = cols[dx, 1].astype(f32)
+        before, mid, after = [
+            frames[place_of((dx - 1, dy, 1), sizes), top:, :].astype(f32) for dy in (-1, 0, 1)
+        ]
         mid = mid[1 : count_y + 1]
-        before = cols[dx, 0].astype(f32)[count_y + 1 : count_y + 2]
-        after = cols[dx, 2].astype(f32)[0:1]
+        before = before[count_y + 1 : count_y + 2]
+        after = after[0:1]
         mid = mid + jnp.where(row == 0, before, 0.0) + jnp.where(row == count_y - 1, after, 0.0)
         if turn:
             mid = pltpu.roll(mid, turn, 1)
@@ -279,19 +323,6 @@
     )
 
 
-def summed(array, axis):
-    count = lax.axis_size(axis)
-    if count > 4:
-        return lax.psum(array, axis)
-    moved = [array] + [
-        lax.ppermute(array, axis, [((i + k) % count, i) for i in range(count)])
-        for k in range(1, count)
-    ]
-    if count == 4:
-        return (moved[0] + moved[2]) + (moved[1] + moved[3])
-    return sum(moved[1:], moved[0])
-
-
 def on_device(cells, weight, bias, cotangent):
     chan, count_x, count_y, count_z = cells.shape
     chan_out = weight.shape[0]
@@ -315,39 +346,30 @@
     wbig = jnp.concatenate([placed, pieces], axis=2).reshape(count_x * chan_out, 3 * depth)
     wback = placed.reshape(count_x * chan_out, 9 * wide).T
 
-    edges, first, last, low, high = call(
+    sizes = [lax.axis_size(axis) for axis in axes]
+    frame, low, high = call(
         pack_kernel,
         [
-            shape((2 * own, lanes), bf16),
-            shape((own, lanes), bf16),
-            shape((own, lanes), bf16),
+            shape((4 * own, lanes), bf16),
             shape((chan, count_y, lanes), bf16),
             shape((chan, count_y, lanes), bf16),
         ],
         [pltpu.VMEM((2 * own, lanes), f32)],
     )(cells)
-    steps = (-1, 0, 1)
-    edges_in = jnp.stack(
-        [jnp.stack([taken_from(edges, (dx, dy, 1)) for dy in steps]) for dx in steps]
-    )
-    above = jnp.stack([taken_from(last, (dx, -1, 0)) for dx in steps])
-    below = jnp.stack([taken_from(first, (dx, 1, 0)) for dx in steps])
+    frames = lax.all_gather(frame, axes)
     low_in = taken_from(high, (-1, 0, 0))
     high_in = taken_from(low, (1, 0, 0))
 
     pool_x, pool_y, pool_z = cotangent.shape[1:]
     tall = 80
-    pooled, wsum, grad, face_low, face_high, row_low, row_high, cols = call(
-        main_kernel,
+    pooled, grad, face_low, face_high, frame = call(
+        functools.partial(main_kernel, sizes),
         [
             shape(cotangent.shape, bf16),
-            shape((chan_out, 2 * lanes), f32),
             shape(cells.shape, f32),
             shape((chan, count_y, lanes), bf16),
             shape((chan, count_y, lanes), bf16),
-            shape((wide, lanes), f32),
-            shape((wide, lanes), f32),
-            shape((tall, lanes), bf16),
+            shape((2 * chan_out + 2 * wide + tall, lanes), bf16),
         ],
         [
             pltpu.VMEM(((count_y + 2) * wide, lanes), f32),
@@ -361,24 +383,18 @@
             pltpu.VMEM((6 * wide, lanes), f32),
             pltpu.VMEM((count_x * chan_out, 3 * depth), f32),
         ],
-    )(cells, low_in, high_in, above, below, edges_in, cotangent, wbig, wback)
-
+    )(cells, low_in, high_in, frames, cotangent, wbig, wback)
+
+    frames = lax.all_gather(frame, axes)
     low_back = taken_from(face_high, (-1, 0, 0))
     high_back = taken_from(face_low, (1, 0, 0))
-    above_back = jnp.stack([taken_from(row_high, (dx, -1, 0)) for dx in steps])
-    below_back = jnp.stack([taken_from(row_low, (dx, 1, 0)) for dx in steps])
-    cols_back = jnp.stack(
-        [jnp.stack([taken_from(cols, (dx, dy, 1)) for dy in steps]) for dx in steps]
-    )
-    input_grad = call(final_kernel, shape(cells.shape, f32))(
-        grad, low_back, high_back, above_back, below_back, cols_back
-    )
-
-    for axis in axes:
-        wsum = summed(wsum, axis)
-    bias_grad = wsum[:, 3 * wide]
-    weight_grad = wsum[:, : 3 * depth].reshape(chan_out, 3, depth)[:, :, : 3 * wide]
-    weight_grad = weight_grad.reshape(chan_out, 3, 3, count_x + 2, chan)[:, :, :, :3]
+    input_grad, wsum = call(
+        functools.partial(final_kernel, sizes),
+        [shape(cells.shape, f32), shape((chan_out, lanes), f32)],
+    )(grad, low_back, high_back, frames)
+    group = 3 * chan
+    bias_grad = wsum[:, 9 * group]
+    weight_grad = wsum[:, : 9 * group].reshape(chan_out, 3, 3, 3, chan)
     return (pooled, weight_grad.transpose(0, 4, 3, 1, 2), bias_grad, input_grad)
 
 

time: 86.4 us -> 157 us (1.82)
  blocking collectives: 0 us -> 71.1 us
  starting transfers between devices: 53.6 us -> 4.29 us
  waiting for transfers between devices: 17.4 us -> 50.9 us
  between operations: 0.88 us -> 14.2 us
  local copies, waits for them, and re-layouts: 3.63 us -> 5.38 us
    all_gather x0 -> x1, blocking collectives: none -> 71.1 us  [on_device(): frames = lax.all_gather(frame, axes)]
    all_gather x0 -> x1, waiting for transfers between devices: none -> 49 us  [on_device(): frames = lax.all_gather(frame, axes)]
    ppermute x34 -> x4, starting transfers between devices: 49.3 us -> 4.25 us  [taken_from(): return lax.ppermute(array, axes, pairs)]
    ppermute x7 -> x0, waiting for transfers between devices: 9.88 us -> none  [summed(): lax.ppermute(array, axis, [((i + k) % count, i) for i in range(count)])]
    ppermute x34 -> x4, waiting for transfers between devices: 7.55 us -> 1.94 us  [taken_from(): return lax.ppermute(array, axes, pairs)]
    ppermute x7 -> x0, starting transfers between devices: 4.36 us -> none  [summed(): lax.ppermute(array, axis, [((i + k) % count, i) for i in range(count)])]
  transfers between devices with their start and end apart: 41 -> 5, of which waited for: 8 -> 2; matrix products, arithmetic and copies ran while one was open for 1% -> 1% of each run, Pallas kernels for 2% -> 0%
where the time goes in v1:
time: 157 us; the launch traced here: 156 us
  blocking collectives  71.1 us (45%)
  waiting for transfers between devices  50.9 us (32%)
  between operations  14.2 us (9%)
  Pallas kernels  10.4 us (7%)
  local copies, waits for them, and re-layouts  5.38 us (3%)
  starting transfers between devices  4.29 us (3%)
    all_gather x1, blocking collectives, on_device(): frames = lax.all_gather(frame, axes)  71.1 us
    all_gather x1, waiting for transfers between devices, on_device(): frames = lax.all_gather(frame, axes)  49 us
    pallas_call x1, Pallas kernels, on_device(): call(functools.partial(main_kernel, sizes), [shape(cotangent.shape, bf16)...  8.77 us
    ppermute x4, starting transfers between devices, taken_from(): return lax.ppermute(array, axes, pairs)  4.25 us
  transfers between devices with their start and end apart: 5, of which 2 were waited for; matrix products, arithmetic and copies ran while one was open for 1% of the time, Pallas kernels for 0%

profile of v1, /device:TPU:0, one launch (start us, length us, event | category | flops | bytes accessed | tf_op | source)
XLA Modules:
  0.0 156.5 jit_solution(10928291238019390772)
XLA Ops:
  7.2 0.0 all-gather.4.cloned.1.call-start
  7.2 0.9 copy-done.1
  8.2 0.3 shard_map.75
  8.4 0.5 collective-permute-start
  8.9 2.0 %collective-permute-start.1 = (bf16[4,64,128]{2,1,0:T(8,128)(2,1)S(1)}, bf16[4,64,128]{2,1,0:T(8,128)(2,1)S(1)}, u32[]{:S(2)}, u32[]{:S(2)}) collective-permute-start(bf16[4,64,128]{2,1,0:T(8,128)(2,1)S(1)} %get-tuple-element.15), channel_id=1, source_target_pairs={{8,0},{9,1},{10,2},{11,3},{12,4},{13,5},{14,6},{15,7},{16,8},{17,9... | collective-permute-start | bytes 196616 | tf_op jit(solution)/shard_map/ppermute | solution.py:34
  10.9 1.0 pad_bitcast_fusion.3
  11.9 0.2 pad_maximum_fusion
  12.1 0.1 copy.11
  12.2 0.2 reshape_reshape.3
  12.3 0.2 reshape.50
  12.6 0.1 tile.9
  12.6 71.1 %all-gather = bf16[2048,128]{1,0:T(8,128)(2,1)S(1)} all-gather(bf16[64,128]{1,0:T(8,128)(2,1)S(1)} %get-tuple-element.16), channel_id=2, replica_groups=mesh['gx'=4,'gy'=4,'gz'=2] {'gx','gy','gz'}, dimensions={0}, use_global_device_ids=true | all-gather | bytes 540672 | tf_op jit(solution)/shard_map/all_gather | solution.py:359
  83.8 0.1 copy.13.wbig
  83.9 8.8 %shard_map.76 = (bf16[32,2,32,64]{3,2,1,0:T(8,128)(2,1)}, f32[4,4,64,128]{3,2,1,0:T(8,128)S(1)}, bf16[4,64,128]{2,1,0:T(8,128)(2,1)S(1)}, bf16[4,64,128]{2,1,0:T(8,128)(2,1)S(1)}, bf16[192,128]{1,0:T(8,128)(2,1)}) custom-call(bf16[4,4,64,128]{3,2,1,0:T(8,128)(2,1)S(1)} %copy-done.2, bf16[4,64,128]{2,1,0:T(8,128)(2,1)S(1)} %collective-permute-done.low, ...), custom_call_target="tpu_custom_call" | custom-call | tf_op jit(solution)/shard_map/pallas_call | solution.py:365
  92.7 0.0 all-gather.4.cloned.1.call-update
  92.7 0.1 collective-permute-start.2
  92.8 1.7 %collective-permute-start.3 = (bf16[4,64,128]{2,1,0:T(8,128)(2,1)S(1)}, bf16[4,64,128]{2,1,0:T(8,128)(2,1)S(1)}, u32[]{:S(2)}, u32[]{:S(2)}) collective-permute-start(bf16[4,64,128]{2,1,0:T(8,128)(2,1)S(1)} %get-tuple-element.20), channel_id=1, source_target_pairs={{8,0},{9,1},{10,2},{11,3},{12,4},{13,5},{14,6},{15,7},{16,8},{17,9... | collective-permute-start | bytes 196616 | tf_op jit(solution)/shard_map/ppermute | solution.py:34
  94.5 1.9 %collective-permute-done.2.low = bf16[4,64,128]{2,1,0:T(8,128)(2,1)S(1)} collective-permute-done((bf16[4,64,128]{2,1,0:T(8,128)(2,1)S(1)}, bf16[4,64,128]{2,1,0:T(8,128)(2,1)S(1)}, u32[]{:S(2)}, u32[]{:S(2)}) %collective-permute-start.2) | collective-permute-done | bytes 65568 | tf_op jit(solution)/shard_map/ppermute | solution.py:34
  96.5 49.0 %all-gather.4.cloned.1.call-done = bf16[6144,128]{1,0:T(8,128)(2,1)} async-done(((bf16[192,128]{1,0:T(8,128)(2,1)}), bf16[6144,128]{1,0:T(8,128)(2,1)}) %all-gather.4.cloned.1.call-update) | async-done | bytes 1572880 | tf_op jit(solution)/shard_map/all_gather | solution.py:388
  145.5 1.4 copy-done
  146.9 1.3 shard_map.77
  148.2 0.7 slice_reduce_fusion
  148.9 0.1 copy.14
  149.0 0.6 copy.15
  (16 shorter events, 0.1 us)
Async XLA Ops:
  7.2 138.3 %all-gather.4.cloned.1.call-start = ((), (), s32[]{:S(2)}) async-start(), calls=%async_computation | async-start | bytes 1622016 | tf_op jit(solution)/shard_map/all_gather | solution.py:388
  7.2 1.0 copy-start.1
  8.2 4.3 %copy-start.4 = (f32[32]{0:T(128)S(1)}, f32[32]{0:T(128)}, u32[]{:S(2)}) copy-start(f32[32]{0:T(128)} %param.6) | copy-start | bytes 388
  8.2 75.7 %copy-start.2 = (bf16[4,4,64,128]{3,2,1,0:T(8,128)(2,1)S(1)}, bf16[4,4,64,128]{3,2,1,0:T(8,128)(2,1)}, u32[]{:S(2)}) copy-start(bf16[4,4,64,128]{3,2,1,0:T(8,128)(2,1)} %cells.3) | copy-start | bytes 786436
  8.2 75.7 %copy-start.3 = (bf16[32,2,32,64]{3,2,1,0:T(8,128)(2,1)S(1)}, bf16[32,2,32,64]{3,2,1,0:T(8,128)(2,1)}, u32[]{:S(2)}) copy-start(bf16[32,2,32,64]{3,2,1,0:T(8,128)(2,1)} %cot.1) | copy-start | bytes 786436
  8.4 75.4 %collective-permute-start = (bf16[4,64,128]{2,1,0:T(8,128)(2,1)S(1)}, bf16[4,64,128]{2,1,0:T(8,128)(2,1)S(1)}, u32[]{:S(2)}, u32[]{:S(2)}) collective-permute-start(bf16[4,64,128]{2,1,0:T(8,128)(2,1)S(1)} %get-tuple-element.14), channel_id=1, source_target_pairs={{24,0},{25,1},{26,2},{27,3},{28,4},{29,5},{30,6},{31,7},{0,8},{1,9... | collective-permute-start | bytes 196616 | tf_op jit(solution)/shard_map/ppermute | solution.py:34
  8.9 75.0 %collective-permute-start.1 = (bf16[4,64,128]{2,1,0:T(8,128)(2,1)S(1)}, bf16[4,64,128]{2,1,0:T(8,128)(2,1)S(1)}, u32[]{:S(2)}, u32[]{:S(2)}) collective-permute-start(bf16[4,64,128]{2,1,0:T(8,128)(2,1)S(1)} %get-tuple-element.15), channel_id=1, source_target_pairs={{8,0},{9,1},{10,2},{11,3},{12,4},{13,5},{14,6},{15,7},{16,8},{17,9... | collective-permute-start | bytes 196616 | tf_op jit(solution)/shard_map/ppermute | solution.py:34
  92.7 3.7 %collective-permute-start.2 = (bf16[4,64,128]{2,1,0:T(8,128)(2,1)S(1)}, bf16[4,64,128]{2,1,0:T(8,128)(2,1)S(1)}, u32[]{:S(2)}, u32[]{:S(2)}) collective-permute-start(bf16[4,64,128]{2,1,0:T(8,128)(2,1)S(1)} %get-tuple-element.19), channel_id=1, source_target_pairs={{24,0},{25,1},{26,2},{27,3},{28,4},{29,5},{30,6},{31,7},{0,8},{1,9... | collective-permute-start | bytes 196616 | tf_op jit(solution)/shard_map/ppermute | solution.py:34
  92.8 3.7 %collective-permute-start.3 = (bf16[4,64,128]{2,1,0:T(8,128)(2,1)S(1)}, bf16[4,64,128]{2,1,0:T(8,128)(2,1)S(1)}, u32[]{:S(2)}, u32[]{:S(2)}) collective-permute-start(bf16[4,64,128]{2,1,0:T(8,128)(2,1)S(1)} %get-tuple-element.20), channel_id=1, source_target_pairs={{8,0},{9,1},{10,2},{11,3},{12,4},{13,5},{14,6},{15,7},{16,8},{17,9... | collective-permute-start | bytes 196616 | tf_op jit(solution)/shard_map/ppermute | solution.py:34
  145.4 1.4 copy-start
Sparse Core Ops, SparseCore 0:
  92.8 52.5 all-gather.3

commit v2 on v0

v2 whole, which is shorter than its diff:
```python
import functools

import jax
import jax.numpy as jnp
import numpy as np
from jax import lax
from jax.experimental import pallas as pl
from jax.experimental.pallas import tpu as pltpu
from jax.sharding import PartitionSpec as P

axes = ("gx", "gy", "gz")
f32, bf16 = jnp.float32, jnp.bfloat16
log_scale = 0.07
lanes = 128
limit = 48 * 1024 * 1024


def dot(a, b, contract=((1,), (0,))):
    return lax.dot_general(a, b, (contract, ((), ())), preferred_element_type=f32)


def iota(shape, dim):
    return lax.broadcasted_iota(jnp.int32, shape, dim)


def taken_from(array, offset):
    sizes = [lax.axis_size(axis) for axis in axes]
    pairs = []
    for place in np.ndindex(*sizes):
        source = [(p + o) % n for p, o, n in zip(place, offset, sizes)]
        pairs.append(
            (int(np.ravel_multi_index(source, sizes)), int(np.ravel_multi_index(place, sizes)))
        )
    return lax.ppermute(array, axes, pairs)


def split(value):
    coarse = value.astype(bf16)
    return coarse, (value - coarse.astype(f32)).astype(bf16)


def joined(pair):
    half = pair.shape[0] // 2
    return pair[:half].astype(f32) + pair[half:].astype(f32)


def pack_kernel(cells, edges, first, last, rows):
    chan, count_x, count_y, _ = cells.shape
    count = chan * count_x
    planes = [cells[c, x] for x in range(count_x) for c in range(chan)]
    wide = jnp.concatenate(planes, axis=1)
    row = iota((2 * count, count * lanes), 0)
    lane = iota((2 * count, count * lanes), 1)
    want = jnp.where(row < count, row * lanes, (row - count) * lanes + lanes - 1)
    pick = (lane == want).astype(f32).astype(bf16)
    found = dot(pick, wide, ((1,), (1,)))
    found = jnp.concatenate([found, jnp.zeros((2 * count, lanes - count_y), f32)], axis=1)
    edges[...] = pltpu.roll(found, 1, 1).astype(bf16)
    for at, plane in enumerate(planes):
        wide_plane = plane.astype(f32)
        rows[at : at + 1, :] = wide_plane[0:1]
        rows[count + at : count + at + 1, :] = wide_plane[count_y - 1 : count_y]
    first[...] = rows[0:count, :].astype(bf16)
    last[...] = rows[count : 2 * count, :].astype(bf16)


def bundle_kernel(cells, edges, above, below, low, high, left, right):
    chan, count_x, count_y, _ = cells.shape
    own = chan * count_x
    spot = iota((2 * own, lanes), 1)
    before = pltpu.roll(above[own:, :].astype(f32), count_y, 1)
    after = pltpu.roll(below[own:, :].astype(f32), lanes - count_y, 1)
    whole = jnp.where(
        spot == 0, before, jnp.where(spot == count_y + 1, after, edges[...].astype(f32))
    )
    right[...] = whole[0:own]
    left[...] = whole[own : 2 * own]
    rows_above = above[0:own, :].astype(f32)
    rows_below = below[0:own, :].astype(f32)
    zero = jnp.zeros((8, lanes), f32)
    body = chan * count_y
    for ref, x in ((low, 0), (high, count_x - 1)):
        for c in range(chan):
            ref[c * count_y : (c + 1) * count_y, :] = cells[c, x]
        at = slice(x * chan, x * chan + chan)
        frame = [rows_above[at], rows_below[at], zero]
        frame += [whole[own + x * chan : own + (x + 1) * chan], whole[at], zero]
        ref[body : body + 32, :] = jnp.concatenate(frame, axis=0).astype(bf16)


def spread_kernel(cot, spread):
    chan_out, pool_x, pool_y, pool_z = cot.shape
    twice = jnp.where(
        iota((pool_z, lanes), 1) // 2 == iota((pool_z, lanes), 0), 0.125, 0.0
    ).astype(bf16)
    for o in range(chan_out):
        part = dot(cot[o].reshape(pool_x * pool_y, pool_z), twice)
        for x in range(pool_x):
            spread[pl.ds(x * chan_out + o, pool_y, stride=pool_x * chan_out), :] = part[
                x * pool_y : (x + 1) * pool_y
            ]


def pool_kernel(sums, pooled):
    chan_out, pool_x, pool_y, pool_z = pooled.shape
    halves = jnp.where(
        iota((2 * lanes, pool_z), 0) % lanes // 2 == iota((2 * lanes, pool_z), 1), 0.125, 0.0
    ).astype(bf16)
    for o in range(0, chan_out, 4):
        rows = 4 * pool_x * pool_y
        part = sums[o * pool_x * pool_y : o * pool_x * pool_y + rows, :]
        mean = dot(jnp.concatenate(split(part), axis=1), halves) + log_scale * float(np.log(2.0))
        pooled[o : o + 4] = mean.astype(bf16).reshape(4, pool_x, pool_y, pool_z)


def main_kernel(
    cells, low, high, above, below, left_in, right_in, spread, wbig, wback,
    sums, field, bundle_low, bundle_high, wpart, wframe, rows_out, cols,
    stage, patches, left, right, outer, carry, gram,
):
    chan, count_x, count_y, _ = cells.shape
    pool_x, pool_y = count_x // 2, count_y // 2
    chan_out = wbig.shape[0] // count_x
    own = chan * count_x
    wide = own + 2 * chan
    depth = 3 * wide + 8
    body = chan * count_y
    lane = iota((wide, lanes), 1)

    for x in range(count_x + 2):
        for c in range(chan):
            if x == 0:
                plane = low[c * count_y : (c + 1) * count_y, :]
            elif x == count_x + 1:
                plane = high[c * count_y : (c + 1) * count_y, :]
            else:
                plane = cells[c, x - 1]
            stage[pl.ds(wide + x * chan + c, count_y, stride=wide), :] = plane.astype(f32)
    rest_low = low[body : body + 32, :].astype(f32)
    rest_high = high[body : body + 32, :].astype(f32)
    for base, ref, at in ((0, above, 0), ((count_y + 1) * wide, below, chan)):
        stage[base : base + chan, :] = rest_low[at : at + chan]
        stage[base + chan : base + chan + own, :] = ref[0:own, :].astype(f32)
        stage[base + chan + own : base + wide, :] = rest_high[at : at + chan]
    for ref, mine, at in ((left, left_in, 16), (right, right_in, 16 + chan)):
        ref[0:chan, :] = rest_low[at : at + chan]
        ref[chan : chan + own, :] = mine[...]
        ref[chan + own : wide, :] = rest_high[at : at + chan]
    left_cols, right_cols = left[...], right[...]
    for y in range(count_y + 2):
        mid = stage[y * wide : (y + 1) * wide, :]
        low_col = pltpu.roll(left_cols, (lanes - y) % lanes, 1)
        high_col = pltpu.roll(right_cols, (lanes - 1 - y) % lanes, 1)
        before = jnp.where(lane == 0, low_col, pltpu.roll(mid, 1, 1))
        after = jnp.where(lane == lanes - 1, high_col, pltpu.roll(mid, lanes - 1, 1))
        whole = jnp.concatenate([before, mid, after, jnp.ones((8, lanes), f32)], axis=0)
        patches[y * depth : (y + 1) * depth, :] = whole.astype(bf16)

    carry[...] = jnp.zeros_like(carry)
    gram[...] = jnp.zeros_like(gram)
    pairs = 4

    def finish(y, whole):
        before = pltpu.roll(whole[0:wide], lanes - 1, 1)
        after = pltpu.roll(whole[2 * wide : 3 * wide], 1, 1)
        zero = jnp.zeros_like(before)
        inner = (
            whole[wide : 2 * wide]
            + jnp.where(lane == lanes - 1, zero, before)
            + jnp.where(lane == 0, zero, after)
        )
        rest = jnp.where(lane == lanes - 1, before, jnp.where(lane == 0, after, zero))
        place = pl.ds(pl.multiple_of(y * wide, 8), wide)
        field[place, :] = inner
        outer[place, :] = rest

    def step(i, _):
        deltas, blocks = [], []
        weights = wbig[...]
        for k in range(pairs):
            j = i * pairs + k
            block = jnp.concatenate(
                [
                    patches[pl.ds(pl.multiple_of((2 * j + h) * depth, 16), 3 * depth), :]
                    for h in range(2)
                ],
                axis=1,
            )
            preact = dot(weights, block)
            slope = jnp.tanh(5.0 * preact)
            linear = jnp.maximum(preact, 0.3 * preact)
            factor = 1.0 + jnp.abs(slope)
            here = spread[pl.ds(pl.multiple_of(j * pool_x * chan_out, 8), pool_x * chan_out), :]
            slope = 0.65 + 0.35 * slope
            delta = []
            for x in range(pool_x):
                top, mid = 2 * x * chan_out, (2 * x + 1) * chan_out
                end = mid + chan_out
                times = here[x * chan_out : (x + 1) * chan_out]
                times = jnp.concatenate([times, times], axis=1)
                delta.append((slope[top:mid] * times).astype(bf16))
                delta.append((slope[mid:end] * times).astype(bf16))
                total = linear[top:mid] + linear[mid:end]
                total = total[:, :lanes] + total[:, lanes:]
                prod = factor[top:mid] * factor[mid:end]
                prod = prod[:, :lanes] * prod[:, lanes:]
                total = total - log_scale * jnp.log(prod)
                sums[pl.ds(x * pool_y + j, chan_out, stride=pool_x * pool_y), :] = total
            deltas.append(jnp.concatenate(delta, axis=0))
            blocks.append(block)
        gram[...] += dot(
            jnp.concatenate(deltas, axis=1), jnp.concatenate(blocks, axis=1), ((1,), (1,))
        )
        back = wback[...]
        size = 3 * wide
        carry_a, carry_b = carry[0:size, :], carry[size : 2 * size, :]
        for k in range(pairs):
            j = i * pairs + k
            parts = dot(back, deltas[k])
            part = lambda b, h: parts[b * size : (b + 1) * size, h * lanes : (h + 1) * lanes]
            finish(2 * j, carry_a + part(0, 0))
            finish(2 * j + 1, carry_b + part(1, 0) + part(0, 1))
            carry_a = part(2, 0) + part(1, 1)
            carry_b = part(2, 1)
        carry[0:size, :] = carry_a
        carry[size : 2 * size, :] = carry_b
        return 0

    lax.fori_loop(0, count_y // (2 * pairs), step, 0)
    size = 3 * wide
    finish(count_y, carry[0:size, :])
    finish(count_y + 1, carry[size : 2 * size, :])

    span = gram.shape[1]
    straight, turned = 0.0, 0.0
    for x in range(count_x):
        part = gram[x * chan_out : (x + 1) * chan_out, :]
        part = jnp.concatenate([part, jnp.zeros((chan_out, 2 * lanes - span), f32)], axis=1)
        straight = straight + part
        turned = turned + (pltpu.roll(part, 2 * lanes - chan * x, 1) if x else part)
    spot = iota((chan_out, lanes), 1)
    tight = 0.0
    group = 3 * chan
    for b in range(3):
        for e in range(3):
            shift = (b * depth + e * wide) - (b * 3 + e) * group
            part = pltpu.roll(turned, 2 * lanes - shift, 1)[:, :lanes] if shift else turned[:, :lanes]
            tight = jnp.where(spot // group == b * 3 + e, part, tight)
    part = pltpu.roll(straight, 2 * lanes + 9 * group - 3 * wide, 1)[:, :lanes]
    tight = jnp.where(spot == 9 * group, part, tight)
    coarse = tight.astype(bf16)
    wpart[...] = tight
    sides = jnp.concatenate(split(tight), axis=0)
    wframe[...] = sides

    ends = [field[0:wide, :], field[(count_y + 1) * wide : (count_y + 2) * wide, :]]
    rows_out[...] = jnp.concatenate([end[chan : chan + own] for end in ends], axis=0)
    tall = cols.shape[0]
    outer[(count_y + 2) * wide :, :] = jnp.zeros((outer.shape[0] - (count_y + 2) * wide, lanes), f32)
    planes = [outer[pl.ds(r, tall, stride=wide), :].astype(bf16) for r in range(wide)]
    row = iota((wide * lanes, lanes), 0)
    spot = iota((wide * lanes, lanes), 1)
    want = jnp.where(spot < wide, spot * lanes + lanes - 1, (spot - wide) * lanes)
    pick = ((row == want) & (spot < 2 * wide)).astype(f32).astype(bf16)
    found = dot(jnp.concatenate(planes, axis=1), pick)
    cols[...] = found
    found = found.astype(bf16)
    zero = jnp.zeros((8, lanes), f32)
    for ref, x in ((bundle_low, 0), (bundle_high, count_x + 1)):
        for c in range(chan):
            plane = field[pl.ds(wide + x * chan + c, count_y, stride=wide), :]
            ref[c * count_y : (c + 1) * count_y, :] = plane.astype(bf16)
        frame = [end[x * chan : (x + 1) * chan] for end in ends] + [zero]
        ref[body : body + 16, :] = jnp.concatenate(frame, axis=0).astype(bf16)
        ref[body + 16 : body + 16 + tall, :] = found
        ref[body + 16 + tall :, :] = sides


def x_kernel(alone, wpart, wframe, rows, cols, from_low, from_high, far, wsum, up, down, cols_out):
    tall = cols.shape[0]
    chan_out = wpart.shape[0]
    own = rows.shape[0] // 2
    body = from_low.shape[0] - 16 - tall - 2 * chan_out
    chan = 4
    wide = own + 2 * chan
    if alone:
        total = joined(jnp.concatenate(split(wpart[...]), axis=0))
    else:
        total = joined(wframe[...]) + joined(far[...])
        sides = [ref[body + 16 + tall :, :] for ref in (from_low, from_high)]
        total = total + (joined(sides[0]) + joined(sides[1]))
    wsum[...] = total
    sides = jnp.concatenate(split(total), axis=0)
    spot = iota((tall, lanes), 1)
    found = cols[...]
    for ref, turn, start in ((from_low, lanes - own, chan), (from_high, own, own)):
        part = pltpu.roll(ref[body + 16 : body + 16 + tall, :].astype(f32), turn, 1)
        near = (spot >= start) & (spot < start + chan)
        near = near | ((spot >= wide + start) & (spot < wide + start + chan))
        found = found + jnp.where(near, part, 0.0)
    cols_out[...] = found
    low_rows = from_low[body : body + 16, :].astype(f32)
    high_rows = from_high[body : body + 16, :].astype(f32)
    count_y = body // chan
    mid = jnp.zeros((own - 2 * chan, lanes), f32)
    for ref, at, line in ((down, 0, 0), (up, 1, count_y + 1)):
        more = [low_rows[at * chan : (at + 1) * chan], mid, high_rows[at * chan : (at + 1) * chan]]
        total = rows[at * own : (at + 1) * own, :] + jnp.concatenate(more, axis=0)
        extra = jnp.broadcast_to(found[line : line + 1], (16, lanes))
        ref[0 : own + 16, :] = jnp.concatenate([total, extra], axis=0).astype(bf16)
        ref[own + 16 :, :] = sides


def y_kernel(alone, count_y, wsum, cols, above, below, far, wout, frame):
    tall = cols.shape[0]
    chan_out = wsum.shape[0]
    top = above.shape[0] - 2 * chan_out
    if alone:
        total = joined(jnp.concatenate(split(wsum[...]), axis=0))
    else:
        total = joined(jnp.concatenate(split(wsum[...]), axis=0)) + joined(far[...])
        total = total + (joined(above[top:, :]) + joined(below[top:, :]))
    wout[...] = total
    frame[tall:, :] = jnp.concatenate(split(total), axis=0)
    row = iota((tall, lanes), 0)
    found = cols[...]
    found = found + jnp.where(row == 1, above[top - 16 : top, :].astype(f32)[0:1], 0.0)
    found = found + jnp.where(row == count_y, below[top - 16 : top, :].astype(f32)[0:1], 0.0)
    frame[0:tall, :] = found.astype(bf16)


def grad_kernel(field, from_low, from_high, grad):
    chan, count_x, count_y, _ = grad.shape
    wide = chan * (count_x + 2)
    for x in range(count_x):
        for c in range(chan):
            plane = field[pl.ds(wide + (x + 1) * chan + c, count_y, stride=wide), :]
            if x == 0:
                plane = plane + from_low[c * count_y : (c + 1) * count_y, :].astype(f32)
            if x == count_x - 1:
                plane = plane + from_high[c * count_y : (c + 1) * count_y, :].astype(f32)
            grad[c, x] = plane


def final_kernel(grad, wsum, above, below, frame, out, wout, bout):
    chan, count_x, count_y, _ = grad.shape
    chan_out = wsum.shape[0]
    own = chan * count_x
    wide = own + 2 * chan
    tall = frame.shape[0] - 2 * chan_out
    total = joined(jnp.concatenate(split(wsum[...]), axis=0)) + joined(frame[tall:, :])
    total = jnp.concatenate([total, jnp.zeros((lanes - chan_out, lanes), f32)], axis=0)
    total = total.T
    for a in range(3):
        for be in range(9):
            at = (be * 3 + a) * chan
            wout[a * 9 + be] = total[at : at + chan, :chan_out]
    bout[...] = total[27 * chan : 27 * chan + 1, :chan_out]
    spot = iota((count_y, lanes), 1)
    row = iota((count_y, lanes), 0)
    cols = frame[0:tall, :].astype(f32)[1 : count_y + 1]
    first = above[0:own, :].astype(f32)
    final = below[0:own, :].astype(f32)
    for x in range(count_x):
        for c in range(chan):
            at = x * chan + c
            r = chan + at
            more = jnp.where(spot == lanes - 1, cols[:, r : r + 1], 0.0)
            more = jnp.where(spot == 0, cols[:, wide + r : wide + r + 1], more)
            more = more + jnp.where(row == 0, first[at : at + 1], 0.0)
            more = more + jnp.where(row == count_y - 1, final[at : at + 1], 0.0)
            out[c, x] = grad[c, x] + more


def call(kernel, outs, scratch=(), cost=None):
    return pl.pallas_call(
        kernel,
        out_shape=outs,
        scratch_shapes=list(scratch),
        cost_estimate=cost,
        compiler_params=pltpu.CompilerParams(vmem_limit_bytes=limit),
    )


def on_device(cells, weight, bias, cotangent):
    chan, count_x, count_y, count_z = cells.shape
    chan_out = weight.shape[0]
    own = chan * count_x
    wide = own + 2 * chan
    depth = 3 * wide + 8
    shape = jax.ShapeDtypeStruct

    kernel = weight.transpose(0, 3, 4, 2, 1)
    placed = jnp.stack(
        [
            jnp.pad(kernel, ((0, 0), (0, 0), (0, 0), (x, count_x - 1 - x), (0, 0)))
            for x in range(count_x)
        ]
    ).reshape(count_x * chan_out, 3, 3 * wide)
    coarse = lax.reduce_precision(bias, 8, 7)
    middle = lax.reduce_precision(bias - coarse, 8, 7)
    fine = bias - coarse - middle
    pieces = jnp.stack([coarse, middle, fine], axis=1).astype(bf16)
    pieces = jnp.pad(jnp.tile(pieces, (count_x, 1))[:, None], ((0, 0), (0, 2), (0, 5)))
    wbig = jnp.concatenate([placed, pieces], axis=2).reshape(count_x * chan_out, 3 * depth)
    wback = placed.reshape(count_x * chan_out, 9 * wide).T

    own_block = shape((own, lanes), bf16)
    edges, first, last = call(
        pack_kernel,
        [shape((2 * own, lanes), bf16), own_block, own_block],
        [pltpu.VMEM((2 * own, lanes), f32)],
    )(cells)
    pool_x, pool_y, pool_z = cotangent.shape[1:]
    pooled_rows = shape((pool_y * pool_x * chan_out, lanes), f32)
    spread = call(spread_kernel, pooled_rows)(cotangent)
    edges = taken_from(edges, (0, 0, 1))
    above = taken_from(jnp.concatenate([last, edges]), (0, -1, 0))
    below = taken_from(jnp.concatenate([first, edges]), (0, 1, 0))
    body = chan * count_y
    bundle = shape((body + 32, lanes), bf16)
    low, high, left, right = call(
        bundle_kernel, [bundle, bundle, shape((own, lanes), f32), shape((own, lanes), f32)]
    )(cells, edges, above, below)
    low, high = taken_from(high, (-1, 0, 0)), taken_from(low, (1, 0, 0))

    tall = 80
    bundle = shape((body + 16 + tall + 2 * chan_out, lanes), bf16)
    sums, field, low, high, wpart, wframe, rows, cols = call(
        main_kernel,
        [
            pooled_rows,
            shape(((count_y + 2) * wide, lanes), f32),
            bundle,
            bundle,
            shape((chan_out, lanes), f32),
            shape((2 * chan_out, lanes), bf16),
            shape((2 * own, lanes), f32),
            shape((tall, lanes), f32),
        ],
        [
            pltpu.VMEM(((count_y + 2) * wide, lanes), f32),
            pltpu.VMEM(((count_y + 2) * depth, lanes), bf16),
            pltpu.VMEM((wide, lanes), f32),
            pltpu.VMEM((wide, lanes), f32),
            pltpu.VMEM((tall * wide, lanes), f32),
            pltpu.VMEM((6 * wide, lanes), f32),
            pltpu.VMEM((count_x * chan_out, 3 * depth), f32),
        ],
    )(cells, low, high, above, below, left, right, spread, wbig, wback)

    alone_x = lax.axis_size("gx") != 4
    alone_y = lax.axis_size("gy") != 4
    if alone_x:
        wpart, far = lax.psum(wpart, "gx"), wframe
    else:
        far = taken_from(wframe, (2, 0, 0))
    low, high = taken_from(high, (-1, 0, 0)), taken_from(low, (1, 0, 0))
    pooled = call(pool_kernel, shape(cotangent.shape, bf16))(sums)
    rows_out = shape((own + 16 + 2 * chan_out, lanes), bf16)
    wsum, up, down, cols = call(
        functools.partial(x_kernel, alone_x),
        [shape((chan_out, lanes), f32), rows_out, rows_out, shape((tall, lanes), f32)],
    )(wpart, wframe, rows, cols, low, high, far)
    grad = call(grad_kernel, shape(cells.shape, f32))(field, low, high)
    if alone_y:
        far, wsum = wframe, lax.psum(wsum, "gy")
    else:
        far = taken_from(up[own + 16 :], (0, 2, 0))
    above, below = taken_from(up, (0, -1, 0)), taken_from(down, (0, 1, 0))
    wsum, frame = call(
        functools.partial(y_kernel, alone_y, count_y),
        [shape((chan_out, lanes), f32), shape((tall + 2 * chan_out, lanes), bf16)],
    )(wsum, cols, above, below, far)
    frame = taken_from(frame, (0, 0, 1))
    input_grad, wsum, bias_grad = call(
        final_kernel,
        [
            shape(cells.shape, f32),
            shape((27, chan, chan_out), f32),
            shape((1, chan_out), f32),
        ],
    )(grad, wsum, above, below, frame)
    weight_grad = wsum.reshape(3, 3, 3, chan, chan_out).transpose(4, 3, 0, 1, 2)
    return (pooled, weight_grad, bias_grad.reshape(chan_out), input_grad)


def solution(mesh):
    in_specs = (P(None, "gx", "gy", "gz"), P(), P(), P(None, "gx", "gy", "gz"))
    out_specs = (P(None, "gx", "gy", "gz"), P(), P(), P(None, "gx", "gy", "gz"))
    return jax.shard_map(
        on_device, mesh=mesh, in_specs=in_specs, out_specs=out_specs, check_vma=False
    )
```

time: 86.4 us -> 45.3 us (0.52)
  starting transfers between devices: 53.6 us -> 15.9 us
  local copies, waits for them, and re-layouts: 3.63 us -> 1.62 us
  waiting for transfers between devices: 17.4 us -> 15.9 us
    ppermute x34 -> x12, starting transfers between devices: 49.3 us -> 15.9 us  [taken_from(): return lax.ppermute(array, axes, pairs)]
    ppermute x7 -> x0, waiting for transfers between devices: 9.88 us -> none  [summed(): lax.ppermute(array, axis, [((i + k) % count, i) for i in range(count)])]
    ppermute x34 -> x12, waiting for transfers between devices: 7.55 us -> 15.9 us  [taken_from(): return lax.ppermute(array, axes, pairs)]
    ppermute x7 -> x0, starting transfers between devices: 4.36 us -> none  [summed(): lax.ppermute(array, axis, [((i + k) % count, i) for i in range(count)])]
    unnamed x11 -> x10, local copies, waits for them, and re-layouts: 2.08 us -> 0.97 us
    pallas_call x3 -> x9, Pallas kernels: 10.3 us -> 10.7 us  [the longest x1 6.92 us: on_device(): call(main_kernel, [pooled_rows, shape(((count_y + 2) * wide, lanes), f32)...]
  transfers between devices with their start and end apart: 41 -> 12, of which waited for: 8 -> 7; matrix products, arithmetic and copies ran while one was open for 1% -> 2% of each run, Pallas kernels for 2% -> 5%
where the time goes in v2:
time: 45.3 us; the launch traced here: 45.1 us
  starting transfers between devices  15.9 us (35%)
  waiting for transfers between devices  15.9 us (35%)
  Pallas kernels  10.7 us (24%)
  local copies, waits for them, and re-layouts  1.62 us (4%)
  between operations  0.77 us (2%)
    ppermute x12, waiting for transfers between devices, taken_from(): return lax.ppermute(array, axes, pairs)  15.9 us
    ppermute x12, starting transfers between devices, taken_from(): return lax.ppermute(array, axes, pairs)  15.9 us
    pallas_call x1, Pallas kernels, on_device(): call(main_kernel, [pooled_rows, shape(((count_y + 2) * wide, lanes), f32)...  6.92 us
    pallas_call x1, Pallas kernels, on_device(): pooled = call(pool_kernel, shape(cotangent.shape, bf16))(sums)  1.24 us
    pallas_call x1, Pallas kernels, on_device(): call(final_kernel, [shape(cells.shape, f32), shape((27, chan, chan_out),...  1.13 us
    unnamed x10, local copies, waits for them, and re-layouts  0.97 us
  transfers between devices with their start and end apart: 12, of which 7 were waited for; matrix products, arithmetic and copies ran while one was open for 2% of the time, Pallas kernels for 5%

profile of v2, /device:TPU:0, one launch (start us, length us, event | category | flops | bytes accessed | tf_op | source)
XLA Modules:
  0.0 45.1 jit_solution(16209132686153575740)
XLA Ops:
  0.6 0.9 %copy-done = bf16[4,4,64,128]{3,2,1,0:T(8,128)(2,1)S(1)} copy-done((bf16[4,4,64,128]{3,2,1,0:T(8,128)(2,1)S(1)}, bf16[4,4,64,128]{3,2,1,0:T(8,128)(2,1)}, u32[]{:S(2)}) %copy-start) | copy-done | bytes 262168
  1.6 0.3 shard_map.75
  1.8 3.0 %collective-permute-start = (bf16[32,128]{1,0:T(8,128)(2,1)S(1)}, bf16[32,128]{1,0:T(8,128)(2,1)S(1)}, u32[]{:S(2)}, u32[]{:S(2)}) collective-permute-start(bf16[32,128]{1,0:T(8,128)(2,1)S(1)} %get-tuple-element.28), channel_id=1, source_target_pairs={{1,0},{0,1},{3,2},{2,3},{5,4},{4,5},{7,6},{6,7},{9,8},{8,9},{11,10... | collective-permute-start | bytes 24584 | tf_op jit(solution)/shard_map/ppermute | solution.py:34
  4.9 0.2 pad_maximum_fusion
  5.2 1.3 %collective-permute-done.edges = bf16[32,128]{1,0:T(8,128)(2,1)S(1)} collective-permute-done((bf16[32,128]{1,0:T(8,128)(2,1)S(1)}, bf16[32,128]{1,0:T(8,128)(2,1)S(1)}, u32[]{:S(2)}, u32[]{:S(2)}) %collective-permute-start) | collective-permute-done | bytes 8224 | tf_op jit(solution)/shard_map/ppermute | solution.py:34
  6.5 4.1 %collective-permute-start.2 = (bf16[48,128]{1,0:T(8,128)(2,1)S(1)}, bf16[48,128]{1,0:T(8,128)(2,1)S(1)}, u32[]{:S(2)}, u32[]{:S(2)}) collective-permute-start(bf16[48,128]{1,0:T(8,128)(2,1)S(1)} %get-tuple-element.56), channel_id=1, source_target_pairs={{2,0},{3,1},{4,2},{5,3},{6,4},{7,5},{0,6},{1,7},{10,8},{11,9},{12,... | collective-permute-start | bytes 36872 | tf_op jit(solution)/shard_map/ppermute | solution.py:34
  10.7 0.2 reshape_reshape.3
  10.9 0.2 reshape.53
  11.1 0.9 %collective-permute-done.2.below = bf16[48,128]{1,0:T(8,128)(2,1)S(1)} collective-permute-done((bf16[48,128]{1,0:T(8,128)(2,1)S(1)}, bf16[48,128]{1,0:T(8,128)(2,1)S(1)}, u32[]{:S(2)}, u32[]{:S(2)}) %collective-permute-start.2) | collective-permute-done | bytes 12320 | tf_op jit(solution)/shard_map/ppermute | solution.py:34
  12.0 4.1 %collective-permute-done.1.above = bf16[48,128]{1,0:T(8,128)(2,1)S(1)} collective-permute-done((bf16[48,128]{1,0:T(8,128)(2,1)S(1)}, bf16[48,128]{1,0:T(8,128)(2,1)S(1)}, u32[]{:S(2)}, u32[]{:S(2)}) %collective-permute-start.1) | collective-permute-done | bytes 12320 | tf_op jit(solution)/shard_map/ppermute | solution.py:34
  16.2 1.7 %collective-permute-start.4 = (bf16[288,128]{1,0:T(8,128)(2,1)S(1)}, bf16[288,128]{1,0:T(8,128)(2,1)S(1)}, u32[]{:S(2)}, u32[]{:S(2)}) collective-permute-start(bf16[288,128]{1,0:T(8,128)(2,1)S(1)} %get-tuple-element.32), channel_id=1, source_target_pairs={{8,0},{9,1},{10,2},{11,3},{12,4},{13,5},{14,6},{15,7},{16,8},{17,9... | collective-permute-start | bytes 221192 | tf_op jit(solution)/shard_map/ppermute | solution.py:34
  18.0 0.9 %shard_map.77.spread = f32[2048,128]{1,0:T(8,128)S(1)} custom-call(bf16[32,2,32,64]{3,2,1,0:T(8,128)(2,1)S(1)} %copy-done.2), custom_call_target="tpu_custom_call" | custom-call | tf_op jit(solution)/shard_map/pallas_call | solution.py:416
  18.9 1.0 %collective-permute-done.3.low = bf16[288,128]{1,0:T(8,128)(2,1)S(1)} collective-permute-done((bf16[288,128]{1,0:T(8,128)(2,1)S(1)}, bf16[288,128]{1,0:T(8,128)(2,1)S(1)}, u32[]{:S(2)}, u32[]{:S(2)}) %collective-permute-start.3) | collective-permute-done | bytes 73760 | tf_op jit(solution)/shard_map/ppermute | solution.py:34
  19.9 6.9 %shard_map.78 = (f32[2048,128]{1,0:T(8,128)S(1)}, f32[1584,128]{1,0:T(8,128)S(1)}, bf16[416,128]{1,0:T(8,128)(2,1)S(1)}, bf16[416,128]{1,0:T(8,128)(2,1)S(1)}, f...) custom-call(bf16[4,4,64,128]{3,2,1,0:T(8,128)(2,1)S(1)} %copy-done.1, ...), custom_call_target="tpu_custom_call" | custom-call | tf_op jit(solution)/shard_map/pallas_call | solution.py:429
  26.9 1.6 %collective-permute-start.5 = (bf16[416,128]{1,0:T(8,128)(2,1)S(1)}, bf16[416,128]{1,0:T(8,128)(2,1)S(1)}, u32[]{:S(2)}, u32[]{:S(2)}) collective-permute-start(bf16[416,128]{1,0:T(8,128)(2,1)S(1)} %get-tuple-element.37), channel_id=1, source_target_pairs={{24,0},{25,1},{26,2},{27,3},{28,4},{29,5},{30,6},{31,7},{0,8},{1,9... | collective-permute-start | bytes 319496 | tf_op jit(solution)/shard_map/ppermute | solution.py:34
  28.5 0.2 collective-permute-start.6
  28.7 1.5 %collective-permute-start.7 = (bf16[64,128]{1,0:T(8,128)(2,1)S(1)}, bf16[64,128]{1,0:T(8,128)(2,1)S(1)}, u32[]{:S(2)}, u32[]{:S(2)}) collective-permute-start(bf16[64,128]{1,0:T(8,128)(2,1)S(1)} %get-tuple-element.40.wframe), channel_id=1, source_target_pairs={{16,0},{17,1},{18,2},{19,3},{20,4},{21,5},{22,6},{23,7},{24,8},{25... | collective-permute-start | bytes 49160 | tf_op jit(solution)/shard_map/ppermute | solution.py:34
  30.2 2.9 %collective-permute-done.7.far = bf16[64,128]{1,0:T(8,128)(2,1)S(1)} collective-permute-done((bf16[64,128]{1,0:T(8,128)(2,1)S(1)}, bf16[64,128]{1,0:T(8,128)(2,1)S(1)}, u32[]{:S(2)}, u32[]{:S(2)}) %collective-permute-start.7) | collective-permute-done | bytes 16416 | tf_op jit(solution)/shard_map/ppermute | solution.py:34
  33.3 2.0 %collective-permute-start.8 = (bf16[96,128]{1,0:T(8,128)(2,1)S(1)}, bf16[96,128]{1,0:T(8,128)(2,1)S(1)}, u32[]{:S(2)}, u32[]{:S(2)}) collective-permute-start(bf16[96,128]{1,0:T(8,128)(2,1)S(1)} %get-tuple-element.45), channel_id=1, source_target_pairs={{6,0},{7,1},{0,2},{1,3},{2,4},{3,5},{4,6},{5,7},{14,8},{15,9},{8,1... | collective-permute-start | bytes 73736 | tf_op jit(solution)/shard_map/ppermute | solution.py:34
  35.3 4.6 %collective-permute-done.10.far = bf16[64,128]{1,0:T(8,128)(2,1)S(1)} collective-permute-done((bf16[64,128]{1,0:T(8,128)(2,1)S(1)}, bf16[64,128]{1,0:T(8,128)(2,1)S(1)}, u32[]{:S(2)}, u32[]{:S(2)}) %collective-permute-start.10) | collective-permute-done | bytes 16416 | tf_op jit(solution)/shard_map/ppermute | solution.py:34
  40.0 1.6 %collective-permute-start.11 = (bf16[144,128]{1,0:T(8,128)(2,1)S(1)}, bf16[144,128]{1,0:T(8,128)(2,1)S(1)}, u32[]{:S(2)}, u32[]{:S(2)}) collective-permute-start(bf16[144,128]{1,0:T(8,128)(2,1)S(1)} %get-tuple-element.48), channel_id=1, source_target_pairs={{1,0},{0,1},{3,2},{2,3},{5,4},{4,5},{7,6},{6,7},{9,8},{8,9},{11,10... | collective-permute-start | bytes 110600 | tf_op jit(solution)/shard_map/ppermute | solution.py:34
  41.6 1.2 %shard_map.79 = bf16[32,2,32,64]{3,2,1,0:T(8,128)(2,1)} custom-call(f32[2048,128]{1,0:T(8,128)S(1)} %get-tuple-element.35.sums), custom_call_target="tpu_custom_call" | custom-call | tf_op jit(solution)/shard_map/pallas_call | solution.py:459
  42.9 1.1 %collective-permute-done.11.frame = bf16[144,128]{1,0:T(8,128)(2,1)S(1)} collective-permute-done((bf16[144,128]{1,0:T(8,128)(2,1)S(1)}, bf16[144,128]{1,0:T(8,128)(2,1)S(1)}, u32[]{:S(2)}, u32[]{:S(2)}) %collective-permute-start.11) | collective-permute-done | bytes 36896 | tf_op jit(solution)/shard_map/ppermute | solution.py:34
  44.0 1.1 %shard_map.83 = (f32[4,4,64,128]{3,2,1,0:T(8,128)}, f32[27,4,32]{2,1,0:T(4,128)}, f32[1,32]{1,0:T(1,128)}) custom-call(f32[4,4,64,128]{3,2,1,0:T(8,128)S(1)} %shard_map.80.grad, f32[32,128]{1,0:T(8,128)S(1)} %get-tuple-element.47.wsum, bf16[96,128]{1,0:T(8,128)(2,1)S(1)} %collective-permute-done.8.above, bf16[96,128]{1,0:T(8,128)(2,1)S(1)} %collective-permute-done.9.below, ...), custom_call_target="tpu_custom_call" | custom-call | tf_op jit(solution)/shard_map/pallas_call | solution.py:476
  (32 shorter events, 0.8 us)
Async XLA Ops:
  0.6 1.0 %copy-start = (bf16[4,4,64,128]{3,2,1,0:T(8,128)(2,1)S(1)}, bf16[4,4,64,128]{3,2,1,0:T(8,128)(2,1)}, u32[]{:S(2)}) copy-start(bf16[4,4,64,128]{3,2,1,0:T(8,128)(2,1)} %cells.5) | copy-start | bytes 786436
  1.6 3.3 %copy-start.3 = (bf16[32,4,3,3,3]{0,1,4,3,2:T(4,128)(2,1)S(1)}, bf16[32,4,3,3,3]{0,1,4,3,2:T(4,128)(2,1)}, u32[]{:S(2)}) copy-start(bf16[32,4,3,3,3]{0,1,4,3,2:T(4,128)(2,1)} %param.5) | copy-start | bytes 20740
  1.8 3.0 %copy-start.4 = (f32[32]{0:T(128)S(1)}, f32[32]{0:T(128)}, u32[]{:S(2)}) copy-start(f32[32]{0:T(128)} %param.6) | copy-start | bytes 388
  1.8 4.6 %collective-permute-start = (bf16[32,128]{1,0:T(8,128)(2,1)S(1)}, bf16[32,128]{1,0:T(8,128)(2,1)S(1)}, u32[]{:S(2)}, u32[]{:S(2)}) collective-permute-start(bf16[32,128]{1,0:T(8,128)(2,1)S(1)} %get-tuple-element.28), channel_id=1, source_target_pairs={{1,0},{0,1},{3,2},{2,3},{5,4},{4,5},{7,6},{6,7},{9,8},{8,9},{11,10... | collective-permute-start | bytes 24584 | tf_op jit(solution)/shard_map/ppermute | solution.py:34
  6.5 5.5 %collective-permute-start.2 = (bf16[48,128]{1,0:T(8,128)(2,1)S(1)}, bf16[48,128]{1,0:T(8,128)(2,1)S(1)}, u32[]{:S(2)}, u32[]{:S(2)}) collective-permute-start(bf16[48,128]{1,0:T(8,128)(2,1)S(1)} %get-tuple-element.56), channel_id=1, source_target_pairs={{2,0},{3,1},{4,2},{5,3},{6,4},{7,5},{0,6},{1,7},{10,8},{11,9},{12,... | collective-permute-start | bytes 36872 | tf_op jit(solution)/shard_map/ppermute | solution.py:34
  10.6 5.5 %collective-permute-start.1 = (bf16[48,128]{1,0:T(8,128)(2,1)S(1)}, bf16[48,128]{1,0:T(8,128)(2,1)S(1)}, u32[]{:S(2)}, u32[]{:S(2)}) collective-permute-start(bf16[48,128]{1,0:T(8,128)(2,1)S(1)} %get-tuple-element.57), channel_id=1, source_target_pairs={{6,0},{7,1},{0,2},{1,3},{2,4},{3,5},{4,6},{5,7},{14,8},{15,9},{8,1... | collective-permute-start | bytes 36872 | tf_op jit(solution)/shard_map/ppermute | solution.py:34
  10.7 5.4 %copy-start.1 = (bf16[4,4,64,128]{3,2,1,0:T(8,128)(2,1)S(1)}, bf16[4,4,64,128]{3,2,1,0:T(8,128)(2,1)}, u32[]{:S(2)}) copy-start(bf16[4,4,64,128]{3,2,1,0:T(8,128)(2,1)} %cells.5) | copy-start | bytes 786436
  10.7 7.3 %copy-start.2 = (bf16[32,2,32,64]{3,2,1,0:T(8,128)(2,1)S(1)}, bf16[32,2,32,64]{3,2,1,0:T(8,128)(2,1)}, u32[]{:S(2)}) copy-start(bf16[32,2,32,64]{3,2,1,0:T(8,128)(2,1)} %cot.1) | copy-start | bytes 786436
  16.2 3.8 %collective-permute-start.3 = (bf16[288,128]{1,0:T(8,128)(2,1)S(1)}, bf16[288,128]{1,0:T(8,128)(2,1)S(1)}, u32[]{:S(2)}, u32[]{:S(2)}) collective-permute-start(bf16[288,128]{1,0:T(8,128)(2,1)S(1)} %get-tuple-element.31), channel_id=1, source_target_pairs={{24,0},{25,1},{26,2},{27,3},{28,4},{29,5},{30,6},{31,7},{0,8},{1,9... | collective-permute-start | bytes 221192 | tf_op jit(solution)/shard_map/ppermute | solution.py:34
  16.2 3.8 %collective-permute-start.4 = (bf16[288,128]{1,0:T(8,128)(2,1)S(1)}, bf16[288,128]{1,0:T(8,128)(2,1)S(1)}, u32[]{:S(2)}, u32[]{:S(2)}) collective-permute-start(bf16[288,128]{1,0:T(8,128)(2,1)S(1)} %get-tuple-element.32), channel_id=1, source_target_pairs={{8,0},{9,1},{10,2},{11,3},{12,4},{13,5},{14,6},{15,7},{16,8},{17,9... | collective-permute-start | bytes 221192 | tf_op jit(solution)/shard_map/ppermute | solution.py:34
  26.9 6.2 %collective-permute-start.5 = (bf16[416,128]{1,0:T(8,128)(2,1)S(1)}, bf16[416,128]{1,0:T(8,128)(2,1)S(1)}, u32[]{:S(2)}, u32[]{:S(2)}) collective-permute-start(bf16[416,128]{1,0:T(8,128)(2,1)S(1)} %get-tuple-element.37), channel_id=1, source_target_pairs={{24,0},{25,1},{26,2},{27,3},{28,4},{29,5},{30,6},{31,7},{0,8},{1,9... | collective-permute-start | bytes 319496 | tf_op jit(solution)/shard_map/ppermute | solution.py:34
  28.5 4.6 %collective-permute-start.6 = (bf16[416,128]{1,0:T(8,128)(2,1)S(1)}, bf16[416,128]{1,0:T(8,128)(2,1)S(1)}, u32[]{:S(2)}, u32[]{:S(2)}) collective-permute-start(bf16[416,128]{1,0:T(8,128)(2,1)S(1)} %get-tuple-element.38), channel_id=1, source_target_pairs={{8,0},{9,1},{10,2},{11,3},{12,4},{13,5},{14,6},{15,7},{16,8},{17,9... | collective-permute-start | bytes 319496 | tf_op jit(solution)/shard_map/ppermute | solution.py:34
  28.7 4.4 %collective-permute-start.7 = (bf16[64,128]{1,0:T(8,128)(2,1)S(1)}, bf16[64,128]{1,0:T(8,128)(2,1)S(1)}, u32[]{:S(2)}, u32[]{:S(2)}) collective-permute-start(bf16[64,128]{1,0:T(8,128)(2,1)S(1)} %get-tuple-element.40.wframe), channel_id=1, source_target_pairs={{16,0},{17,1},{18,2},{19,3},{20,4},{21,5},{22,6},{23,7},{24,8},{25... | collective-permute-start | bytes 49160 | tf_op jit(solution)/shard_map/ppermute | solution.py:34
  33.2 6.7 %collective-permute-start.9 = (bf16[96,128]{1,0:T(8,128)(2,1)S(1)}, bf16[96,128]{1,0:T(8,128)(2,1)S(1)}, u32[]{:S(2)}, u32[]{:S(2)}) collective-permute-start(bf16[96,128]{1,0:T(8,128)(2,1)S(1)} %get-tuple-element.46), channel_id=1, source_target_pairs={{2,0},{3,1},{4,2},{5,3},{6,4},{7,5},{0,6},{1,7},{10,8},{11,9},{12,... | collective-permute-start | bytes 73736 | tf_op jit(solution)/shard_map/ppermute | solution.py:34
  33.3 6.7 %collective-permute-start.8 = (bf16[96,128]{1,0:T(8,128)(2,1)S(1)}, bf16[96,128]{1,0:T(8,128)(2,1)S(1)}, u32[]{:S(2)}, u32[]{:S(2)}) collective-permute-start(bf16[96,128]{1,0:T(8,128)(2,1)S(1)} %get-tuple-element.45), channel_id=1, source_target_pairs={{6,0},{7,1},{0,2},{1,3},{2,4},{3,5},{4,6},{5,7},{14,8},{15,9},{8,1... | collective-permute-start | bytes 73736 | tf_op jit(solution)/shard_map/ppermute | solution.py:34
  35.3 4.6 %collective-permute-start.10 = (bf16[64,128]{1,0:T(8,128)(2,1)S(1)}, bf16[64,128]{1,0:T(8,128)(2,1)S(1)}, u32[]{:S(2)}, u32[]{:S(2)}) collective-permute-start(bf16[64,128]{1,0:T(8,128)(2,1)S(1)} %slice.3), channel_id=1, source_target_pairs={{4,0},{5,1},{6,2},{7,3},{0,4},{1,5},{2,6},{3,7},{12,8},{13,9},{14,... | collective-permute-start | bytes 49160 | tf_op jit(solution)/shard_map/ppermute | solution.py:34
  40.0 4.0 %collective-permute-start.11 = (bf16[144,128]{1,0:T(8,128)(2,1)S(1)}, bf16[144,128]{1,0:T(8,128)(2,1)S(1)}, u32[]{:S(2)}, u32[]{:S(2)}) collective-permute-start(bf16[144,128]{1,0:T(8,128)(2,1)S(1)} %get-tuple-element.48), channel_id=1, source_target_pairs={{1,0},{0,1},{3,2},{2,3},{5,4},{4,5},{7,6},{6,7},{9,8},{8,9},{11,10... | collective-permute-start | bytes 110600 | tf_op jit(solution)/shard_map/ppermute | solution.py:34

commit v3 on v2

--- a/solution.py
+++ b/solution.py
@@ -64,8 +64,25 @@
     last[...] = rows[count : 2 * count, :].astype(bf16)
 
 
-def bundle_kernel(cells, edges, above, below, low, high, left, right):
+def beside(axis, step, count):
+    return lax.rem(lax.axis_index(axis) + (step + count), count)
+
+
+def send_kernel(first, last, edges, blocks):
+    count = blocks.shape[0]
+    own = first.shape[0]
+    blocks[...] = jnp.zeros_like(blocks)
+    for step, ref in ((1, last), (-1, first)):
+        to = beside("gy", step, count)
+        blocks[to, 0:own, :] = ref[...]
+        blocks[to, own : 3 * own, :] = edges[...]
+
+
+def bundle_kernel(cells, edges, blocks, low, high, left, right, rows):
     chan, count_x, count_y, _ = cells.shape
+    count = blocks.shape[0]
+    above = blocks.at[beside("gy", -1, count)]
+    below = blocks.at[beside("gy", 1, count)]
     own = chan * count_x
     spot = iota((2 * own, lanes), 1)
     before = pltpu.roll(above[own:, :].astype(f32), count_y, 1)
@@ -77,6 +94,8 @@
     left[...] = whole[own : 2 * own]
     rows_above = above[0:own, :].astype(f32)
     rows_below = below[0:own, :].astype(f32)
+    rows[0:own, :] = rows_above
+    rows[own : 2 * own, :] = rows_below
     zero = jnp.zeros((8, lanes), f32)
     body = chan * count_y
     for ref, x in ((low, 0), (high, count_x - 1)):
@@ -114,7 +133,7 @@
 
 
 def main_kernel(
-    cells, low, high, above, below, left_in, right_in, spread, wbig, wback,
+    cells, low, high, rows_in, left_in, right_in, spread, wbig, wback,
     sums, field, bundle_low, bundle_high, wpart, wframe, rows_out, cols,
     stage, patches, left, right, outer, carry, gram,
 ):
@@ -138,9 +157,9 @@
             stage[pl.ds(wide + x * chan + c, count_y, stride=wide), :] = plane.astype(f32)
     rest_low = low[body : body + 32, :].astype(f32)
     rest_high = high[body : body + 32, :].astype(f32)
-    for base, ref, at in ((0, above, 0), ((count_y + 1) * wide, below, chan)):
+    for base, top, at in ((0, 0, 0), ((count_y + 1) * wide, own, chan)):
         stage[base : base + chan, :] = rest_low[at : at + chan]
-        stage[base + chan : base + chan + own, :] = ref[0:own, :].astype(f32)
+        stage[base + chan : base + chan + own, :] = rows_in[top : top + own, :]
         stage[base + chan + own : base + wide, :] = rest_high[at : at + chan]
     for ref, mine, at in ((left, left_in, 16), (right, right_in, 16 + chan)):
         ref[0:chan, :] = rest_low[at : at + chan]
@@ -276,7 +295,7 @@
         ref[body + 16 + tall :, :] = sides
 
 
-def x_kernel(alone, wpart, wframe, rows, cols, from_low, from_high, far, wsum, up, down, cols_out):
+def x_kernel(alone, wpart, wframe, rows, cols, from_low, from_high, far, blocks, cols_out):
     tall = cols.shape[0]
     chan_out = wpart.shape[0]
     own = rows.shape[0] // 2
@@ -289,7 +308,6 @@
         total = joined(wframe[...]) + joined(far[...])
         sides = [ref[body + 16 + tall :, :] for ref in (from_low, from_high)]
         total = total + (joined(sides[0]) + joined(sides[1]))
-    wsum[...] = total
     sides = jnp.concatenate(split(total), axis=0)
     spot = iota((tall, lanes), 1)
     found = cols[...]
@@ -303,23 +321,29 @@
     high_rows = from_high[body : body + 16, :].astype(f32)
     count_y = body // chan
     mid = jnp.zeros((own - 2 * chan, lanes), f32)
-    for ref, at, line in ((down, 0, 0), (up, 1, count_y + 1)):
+    count = blocks.shape[0]
+    for to in range(count):
+        blocks[to, 0 : own + 16, :] = jnp.zeros((own + 16, lanes), bf16)
+        blocks[to, own + 16 :, :] = sides
+    for step, at, line in ((-1, 0, 0), (1, 1, count_y + 1)):
         more = [low_rows[at * chan : (at + 1) * chan], mid, high_rows[at * chan : (at + 1) * chan]]
         total = rows[at * own : (at + 1) * own, :] + jnp.concatenate(more, axis=0)
         extra = jnp.broadcast_to(found[line : line + 1], (16, lanes))
-        ref[0 : own + 16, :] = jnp.concatenate([total, extra], axis=0).astype(bf16)
-        ref[own + 16 :, :] = sides
-
-
-def y_kernel(alone, count_y, wsum, cols, above, below, far, wout, frame):
+        to = beside("gy", step, count)
+        blocks[to, 0 : own + 16, :] = jnp.concatenate([total, extra], axis=0).astype(bf16)
+
+
+def y_kernel(count_y, cols, blocks, wout, rows, frame):
     tall = cols.shape[0]
-    chan_out = wsum.shape[0]
-    top = above.shape[0] - 2 * chan_out
-    if alone:
-        total = joined(jnp.concatenate(split(wsum[...]), axis=0))
-    else:
-        total = joined(jnp.concatenate(split(wsum[...]), axis=0)) + joined(far[...])
-        total = total + (joined(above[top:, :]) + joined(below[top:, :]))
+    chan_out = wout.shape[0]
+    count = blocks.shape[0]
+    top = blocks.shape[1] - 2 * chan_out
+    above = blocks.at[beside("gy", -1, count)]
+    below = blocks.at[beside("gy", 1, count)]
+    rows[...] = jnp.concatenate([above[0:16, :], below[0:16, :]], axis=0).astype(f32)
+    total = joined(blocks[0, top:, :])
+    for at in range(1, count):
+        total = total + joined(blocks[at, top:, :])
     wout[...] = total
     frame[tall:, :] = jnp.concatenate(split(total), axis=0)
     row = iota((tall, lanes), 0)
@@ -342,7 +366,7 @@
             grad[c, x] = plane
 
 
-def final_kernel(grad, wsum, above, below, frame, out, wout, bout):
+def final_kernel(grad, wsum, rows, frame, out, wout, bout):
     chan, count_x, count_y, _ = grad.shape
     chan_out = wsum.shape[0]
     own = chan * count_x
@@ -359,8 +383,8 @@
     spot = iota((count_y, lanes), 1)
     row = iota((count_y, lanes), 0)
     cols = frame[0:tall, :].astype(f32)[1 : count_y + 1]
-    first = above[0:own, :].astype(f32)
-    final = below[0:own, :].astype(f32)
+    first = rows[0:own, :]
+    final = rows[own : 2 * own, :]
     for x in range(count_x):
         for c in range(chan):
             at = x * chan + c
@@ -415,13 +439,15 @@
     pooled_rows = shape((pool_y * pool_x * chan_out, lanes), f32)
     spread = call(spread_kernel, pooled_rows)(cotangent)
     edges = taken_from(edges, (0, 0, 1))
-    above = taken_from(jnp.concatenate([last, edges]), (0, -1, 0))
-    below = taken_from(jnp.concatenate([first, edges]), (0, 1, 0))
+    count_gy = lax.axis_size("gy")
+    blocks = call(send_kernel, shape((count_gy, 3 * own, lanes), bf16))(first, last, edges)
+    blocks = lax.all_to_all(blocks, "gy", 0, 0)
     body = chan * count_y
     bundle = shape((body + 32, lanes), bf16)
-    low, high, left, right = call(
-        bundle_kernel, [bundle, bundle, shape((own, lanes), f32), shape((own, lanes), f32)]
-    )(cells, edges, above, below)
+    side = shape((own, lanes), f32)
+    low, high, left, right, rows = call(
+        bundle_kernel, [bundle, bundle, side, side, shape((2 * own, lanes), f32)]
+    )(cells, edges, blocks)
     low, high = taken_from(high, (-1, 0, 0)), taken_from(low, (1, 0, 0))
 
     tall = 80
@@ -447,31 +473,32 @@
             pltpu.VMEM((6 * wide, lanes), f32),
             pltpu.VMEM((count_x * chan_out, 3 * depth), f32),
         ],
-    )(cells, low, high, above, below, left, right, spread, wbig, wback)
+    )(cells, low, high, rows, left, right, spread, wbig, wback)
 
     alone_x = lax.axis_size("gx") != 4
-    alone_y = lax.axis_size("gy") != 4
     if alone_x:
         wpart, far = lax.psum(wpart, "gx"), wframe
     else:
         far = taken_from(wframe, (2, 0, 0))
     low, high = taken_from(high, (-1, 0, 0)), taken_from(low, (1, 0, 0))
     pooled = call(pool_kernel, shape(cotangent.shape, bf16))(sums)
-    rows_out = shape((own + 16 + 2 * chan_out, lanes), bf16)
-    wsum, up, down, cols = call(
+    blocks, cols = call(
         functools.partial(x_kernel, alone_x),
-        [shape((chan_out, lanes), f32), rows_out, rows_out, shape((tall, lanes), f32)],
+        [
+            shape((count_gy, own + 16 + 2 * chan_out, lanes), bf16),
+            shape((tall, lanes), f32),
+        ],
     )(wpart, wframe, rows, cols, low, high, far)
     grad = call(grad_kernel, shape(cells.shape, f32))(field, low, high)
-    if alone_y:
-        far, wsum = wframe, lax.psum(wsum, "gy")
-    else:
-        far = taken_from(up[own + 16 :], (0, 2, 0))
-    above, below = taken_from(up, (0, -1, 0)), taken_from(down, (0, 1, 0))
-    wsum, frame = call(
-        functools.partial(y_kernel, alone_y, count_y),
-        [shape((chan_out, lanes), f32), shape((tall + 2 * chan_out, lanes), bf16)],
-    )(wsum, cols, above, below, far)
+    blocks = lax.all_to_all(blocks, "gy", 0, 0)
+    wsum, rows, frame = call(
+        functools.partial(y_kernel, count_y),
+        [
+            shape((chan_out, lanes), f32),
+            shape((2 * own, lanes), f32),
+            shape((tall + 2 * chan_out, lanes), bf16),
+        ],
+    )(cols, blocks)
     frame = taken_from(frame, (0, 0, 1))
     input_grad, wsum, bias_grad = call(
         final_kernel,
@@ -480,7 +507,7 @@
             shape((27, chan, chan_out), f32),
             shape((1, chan_out), f32),
         ],
-    )(grad, wsum, above, below, frame)
+    )(grad, wsum, rows, frame)
     weight_grad = wsum.reshape(3, 3, 3, chan, chan_out).transpose(4, 3, 0, 1, 2)
     return (pooled, weight_grad, bias_grad.reshape(chan_out), input_grad)
 

time: 45.3 us -> 49 us (1.082)
  blocking collectives: 0 us -> 8.21 us
  waiting for transfers between devices: 15.9 us -> 11.5 us
  starting transfers between devices: 15.9 us -> 15 us
  Pallas kernels: 10.7 us -> 11.4 us
    ppermute x12 -> x7, waiting for transfers between devices: 15.9 us -> 5.89 us  [taken_from(): return lax.ppermute(array, axes, pairs)]
    all_to_all x0 -> x1, blocking collectives: none -> 8.21 us  [on_device(): blocks = lax.all_to_all(blocks, 'gy', 0, 0)]
    ppermute x12 -> x7, starting transfers between devices: 15.9 us -> 9.67 us  [taken_from(): return lax.ppermute(array, axes, pairs)]
    all_to_all x0 -> x1, waiting for transfers between devices: none -> 5.59 us  [on_device(): blocks = lax.all_to_all(blocks, 'gy', 0, 0)]
    all_to_all x0 -> x1, starting transfers between devices: none -> 5.37 us  [on_device(): blocks = lax.all_to_all(blocks, 'gy', 0, 0)]
    pallas_call x3 -> x4, Pallas kernels: 0.19 us -> 0.83 us  [the longest x1 0.64 us: on_device(): call(send_kernel, shape((count_gy, 3 * own, lanes), bf16))]
  transfers between devices with their start and end apart: 12 -> 8, of which waited for: 7 -> 5; matrix products, arithmetic and copies ran while one was open for 2% -> 2% of each run, Pallas kernels for 5% -> 5%
where the time goes in v3:
time: 49 us; the launch traced here: 48.7 us
  starting transfers between devices  15 us (31%)
  waiting for transfers between devices  11.5 us (23%)
  Pallas kernels  11.4 us (23%)
  blocking collectives  8.21 us (17%)
  local copies, waits for them, and re-layouts  1.63 us (3%)
  between operations  0.75 us (2%)
    ppermute x7, starting transfers between devices, taken_from(): return lax.ppermute(array, axes, pairs)  9.67 us
    all_to_all x1, blocking collectives, on_device(): blocks = lax.all_to_all(blocks, 'gy', 0, 0)  8.21 us
    pallas_call x1, Pallas kernels, on_device(): call(main_kernel, [pooled_rows, shape(((count_y + 2) * wide, lanes), f32)...  6.94 us
    ppermute x7, waiting for transfers between devices, taken_from(): return lax.ppermute(array, axes, pairs)  5.89 us
    all_to_all x1, waiting for transfers between devices, on_device(): blocks = lax.all_to_all(blocks, 'gy', 0, 0)  5.59 us
    all_to_all x1, starting transfers between devices, on_device(): blocks = lax.all_to_all(blocks, 'gy', 0, 0)  5.37 us
    pallas_call x1, Pallas kernels, on_device(): pooled = call(pool_kernel, shape(cotangent.shape, bf16))(sums)  1.24 us
    pallas_call x1, Pallas kernels, on_device(): call(final_kernel, [shape(cells.shape, f32), shape((27, chan, chan_out),...  1.13 us
  transfers between devices with their start and end apart: 8, of which 5 were waited for; matrix products, arithmetic and copies ran while one was open for 2% of the time, Pallas kernels for 5%

profile of v3, /device:TPU:0, one launch (start us, length us, event | category | flops | bytes accessed | tf_op | source)
XLA Modules:
  0.0 48.7 jit_solution(3559974200235650117)
XLA Ops:
  0.6 0.9 %copy-done = bf16[4,4,64,128]{3,2,1,0:T(8,128)(2,1)S(1)} copy-done((bf16[4,4,64,128]{3,2,1,0:T(8,128)(2,1)S(1)}, bf16[4,4,64,128]{3,2,1,0:T(8,128)(2,1)}, u32[]{:S(2)}) %copy-start) | copy-done | bytes 262168
  1.6 0.3 shard_map.75
  1.8 3.0 %collective-permute-start = (bf16[32,128]{1,0:T(8,128)(2,1)S(1)}, bf16[32,128]{1,0:T(8,128)(2,1)S(1)}, u32[]{:S(2)}, u32[]{:S(2)}) collective-permute-start(bf16[32,128]{1,0:T(8,128)(2,1)S(1)} %get-tuple-element.28), channel_id=1, source_target_pairs={{1,0},{0,1},{3,2},{2,3},{5,4},{4,5},{7,6},{6,7},{9,8},{8,9},{11,10... | collective-permute-start | bytes 24584 | tf_op jit(solution)/shard_map/ppermute | solution.py:34
  4.9 0.2 pad_maximum_fusion
  5.2 0.2 reshape_reshape.3
  5.4 0.2 reshape.53
  5.6 0.9 %collective-permute-done.edges = bf16[32,128]{1,0:T(8,128)(2,1)S(1)} collective-permute-done((bf16[32,128]{1,0:T(8,128)(2,1)S(1)}, bf16[32,128]{1,0:T(8,128)(2,1)S(1)}, u32[]{:S(2)}, u32[]{:S(2)}) %collective-permute-start) | collective-permute-done | bytes 8224 | tf_op jit(solution)/shard_map/ppermute | solution.py:34
  6.5 0.6 %shard_map.76 = bf16[4,48,128]{2,1,0:T(8,128)(2,1)} custom-call(bf16[16,128]{1,0:T(8,128)(2,1)S(1)} %get-tuple-element.29.first, bf16[16,128]{1,0:T(8,128)(2,1)S(1)} %get-tuple-element.30.last, bf16[32,128]{1,0:T(8,128)(2,1)S(1)} %collective-permute-done.edges), custom_call_target="tpu_custom_call" | custom-call | tf_op jit(solution)/shard_map/pallas_call | solution.py:443
  7.1 5.4 %all-to-all-start = ((bf16[4,48,128]{2,1,0:T(8,128)(2,1)}), bf16[4,48,128]{2,1,0:T(8,128)(2,1)S(1)}, u32[]{:S(2)}, u32[]{:S(2)}) async-start(bf16[4,48,128]{2,1,0:T(8,128)(2,1)} %shard_map.76), calls=%async_computation | async-start | bytes 98304 | tf_op jit(solution)/shard_map/all_to_all | solution.py:444
  12.6 5.6 %all-to-all-done.blocks = bf16[4,48,128]{2,1,0:T(8,128)(2,1)S(1)} async-done(((bf16[4,48,128]{2,1,0:T(8,128)(2,1)}), bf16[4,48,128]{2,1,0:T(8,128)(2,1)S(1)}, u32[]{:S(2)}, u32[]{:S(2)}) %all-to-all-start) | async-done | bytes 49184 | tf_op jit(solution)/shard_map/all_to_all | solution.py:444
  18.3 1.7 %collective-permute-start.2 = (bf16[288,128]{1,0:T(8,128)(2,1)S(1)}, bf16[288,128]{1,0:T(8,128)(2,1)S(1)}, u32[]{:S(2)}, u32[]{:S(2)}) collective-permute-start(bf16[288,128]{1,0:T(8,128)(2,1)S(1)} %get-tuple-element.32), channel_id=1, source_target_pairs={{8,0},{9,1},{10,2},{11,3},{12,4},{13,5},{14,6},{15,7},{16,8},{17,9... | collective-permute-start | bytes 221192 | tf_op jit(solution)/shard_map/ppermute | solution.py:34
  20.0 0.1 copy.12.wbig
  20.2 0.9 %shard_map.78.spread = f32[2048,128]{1,0:T(8,128)S(1)} custom-call(bf16[32,2,32,64]{3,2,1,0:T(8,128)(2,1)S(1)} %copy-done.2), custom_call_target="tpu_custom_call" | custom-call | tf_op jit(solution)/shard_map/pallas_call | solution.py:440
  21.0 1.0 %collective-permute-done.1.low = bf16[288,128]{1,0:T(8,128)(2,1)S(1)} collective-permute-done((bf16[288,128]{1,0:T(8,128)(2,1)S(1)}, bf16[288,128]{1,0:T(8,128)(2,1)S(1)}, u32[]{:S(2)}, u32[]{:S(2)}) %collective-permute-start.1) | collective-permute-done | bytes 73760 | tf_op jit(solution)/shard_map/ppermute | solution.py:34
  22.1 6.9 %shard_map.79 = (f32[2048,128]{1,0:T(8,128)S(1)}, f32[1584,128]{1,0:T(8,128)S(1)}, bf16[416,128]{1,0:T(8,128)(2,1)S(1)}, bf16[416,128]{1,0:T(8,128)(2,1)S(1)}, f...) custom-call(bf16[4,4,64,128]{3,2,1,0:T(8,128)(2,1)S(1)} %copy-done.1, ...), custom_call_target="tpu_custom_call" | custom-call | tf_op jit(solution)/shard_map/pallas_call | solution.py:455
  29.0 1.7 %collective-permute-start.3 = (bf16[416,128]{1,0:T(8,128)(2,1)S(1)}, bf16[416,128]{1,0:T(8,128)(2,1)S(1)}, u32[]{:S(2)}, u32[]{:S(2)}) collective-permute-start(bf16[416,128]{1,0:T(8,128)(2,1)S(1)} %get-tuple-element.38), channel_id=1, source_target_pairs={{24,0},{25,1},{26,2},{27,3},{28,4},{29,5},{30,6},{31,7},{0,8},{1,9... | collective-permute-start | bytes 319496 | tf_op jit(solution)/shard_map/ppermute | solution.py:34
  30.6 0.2 collective-permute-start.4
  30.9 1.5 %collective-permute-start.5 = (bf16[64,128]{1,0:T(8,128)(2,1)S(1)}, bf16[64,128]{1,0:T(8,128)(2,1)S(1)}, u32[]{:S(2)}, u32[]{:S(2)}) collective-permute-start(bf16[64,128]{1,0:T(8,128)(2,1)S(1)} %get-tuple-element.41.wframe), channel_id=1, source_target_pairs={{16,0},{17,1},{18,2},{19,3},{20,4},{21,5},{22,6},{23,7},{24,8},{25... | collective-permute-start | bytes 49160 | tf_op jit(solution)/shard_map/ppermute | solution.py:34
  32.3 2.9 %collective-permute-done.5.far = bf16[64,128]{1,0:T(8,128)(2,1)S(1)} collective-permute-done((bf16[64,128]{1,0:T(8,128)(2,1)S(1)}, bf16[64,128]{1,0:T(8,128)(2,1)S(1)}, u32[]{:S(2)}, u32[]{:S(2)}) %collective-permute-start.5) | collective-permute-done | bytes 16416 | tf_op jit(solution)/shard_map/ppermute | solution.py:34
  35.3 8.2 %all_to_all.10.blocks = bf16[4,96,128]{2,1,0:T(8,128)(2,1)S(1)} all-to-all(bf16[4,96,128]{2,1,0:T(8,128)(2,1)S(1)} %get-tuple-element.45), channel_id=1, replica_groups=mesh['gx'=4,'gy'=4,'gz'=2] {'gy'}, dimensions={0} | all-to-all | bytes 196608 | tf_op jit(solution)/shard_map/all_to_all | solution.py:493
  43.6 1.6 %collective-permute-start.6 = (bf16[144,128]{1,0:T(8,128)(2,1)S(1)}, bf16[144,128]{1,0:T(8,128)(2,1)S(1)}, u32[]{:S(2)}, u32[]{:S(2)}) collective-permute-start(bf16[144,128]{1,0:T(8,128)(2,1)S(1)} %get-tuple-element.48), channel_id=1, source_target_pairs={{1,0},{0,1},{3,2},{2,3},{5,4},{4,5},{7,6},{6,7},{9,8},{8,9},{11,10... | collective-permute-start | bytes 110600 | tf_op jit(solution)/shard_map/ppermute | solution.py:34
  45.2 1.2 %shard_map.80 = bf16[32,2,32,64]{3,2,1,0:T(8,128)(2,1)} custom-call(f32[2048,128]{1,0:T(8,128)S(1)} %get-tuple-element.36.sums), custom_call_target="tpu_custom_call" | custom-call | tf_op jit(solution)/shard_map/pallas_call | solution.py:484
  46.5 1.1 %collective-permute-done.6.frame = bf16[144,128]{1,0:T(8,128)(2,1)S(1)} collective-permute-done((bf16[144,128]{1,0:T(8,128)(2,1)S(1)}, bf16[144,128]{1,0:T(8,128)(2,1)S(1)}, u32[]{:S(2)}, u32[]{:S(2)}) %collective-permute-start.6) | collective-permute-done | bytes 36896 | tf_op jit(solution)/shard_map/ppermute | solution.py:34
  47.6 1.1 %shard_map.84 = (f32[4,4,64,128]{3,2,1,0:T(8,128)}, f32[27,4,32]{2,1,0:T(4,128)}, f32[1,32]{1,0:T(1,128)}) custom-call(f32[4,4,64,128]{3,2,1,0:T(8,128)S(1)} %shard_map.81.grad, f32[32,128]{1,0:T(8,128)S(1)} %get-tuple-element.46.wsum, f32[32,128]{1,0:T(8,128)S(1)} %get-tuple-element.47.rows, bf16[144,128]{1,0:T(8,128)(2,1)S(1)} %collective-permute-done.6.frame), custom_call_target="tpu_custom_call" | custom-call | tf_op jit(solution)/shard_map/pallas_call | solution.py:503
  (24 shorter events, 0.6 us)
Async XLA Ops:
  0.6 1.0 %copy-start = (bf16[4,4,64,128]{3,2,1,0:T(8,128)(2,1)S(1)}, bf16[4,4,64,128]{3,2,1,0:T(8,128)(2,1)}, u32[]{:S(2)}) copy-start(bf16[4,4,64,128]{3,2,1,0:T(8,128)(2,1)} %cells.5) | copy-start | bytes 786436
  1.6 3.3 %copy-start.3 = (bf16[32,4,3,3,3]{0,1,4,3,2:T(4,128)(2,1)S(1)}, bf16[32,4,3,3,3]{0,1,4,3,2:T(4,128)(2,1)}, u32[]{:S(2)}) copy-start(bf16[32,4,3,3,3]{0,1,4,3,2:T(4,128)(2,1)} %param.5) | copy-start | bytes 20740
  1.8 3.0 %copy-start.4 = (f32[32]{0:T(128)S(1)}, f32[32]{0:T(128)}, u32[]{:S(2)}) copy-start(f32[32]{0:T(128)} %param.6) | copy-start | bytes 388
  1.8 4.6 %collective-permute-start = (bf16[32,128]{1,0:T(8,128)(2,1)S(1)}, bf16[32,128]{1,0:T(8,128)(2,1)S(1)}, u32[]{:S(2)}, u32[]{:S(2)}) collective-permute-start(bf16[32,128]{1,0:T(8,128)(2,1)S(1)} %get-tuple-element.28), channel_id=1, source_target_pairs={{1,0},{0,1},{3,2},{2,3},{5,4},{4,5},{7,6},{6,7},{9,8},{8,9},{11,10... | collective-permute-start | bytes 24584 | tf_op jit(solution)/shard_map/ppermute | solution.py:34
  5.4 12.8 %copy-start.1 = (bf16[4,4,64,128]{3,2,1,0:T(8,128)(2,1)S(1)}, bf16[4,4,64,128]{3,2,1,0:T(8,128)(2,1)}, u32[]{:S(2)}) copy-start(bf16[4,4,64,128]{3,2,1,0:T(8,128)(2,1)} %cells.5) | copy-start | bytes 786436
  5.4 14.7 %copy-start.2 = (bf16[32,2,32,64]{3,2,1,0:T(8,128)(2,1)S(1)}, bf16[32,2,32,64]{3,2,1,0:T(8,128)(2,1)}, u32[]{:S(2)}) copy-start(bf16[32,2,32,64]{3,2,1,0:T(8,128)(2,1)} %cot.1) | copy-start | bytes 786436
  7.1 11.1 %all-to-all-start = ((bf16[4,48,128]{2,1,0:T(8,128)(2,1)}), bf16[4,48,128]{2,1,0:T(8,128)(2,1)S(1)}, u32[]{:S(2)}, u32[]{:S(2)}) async-start(bf16[4,48,128]{2,1,0:T(8,128)(2,1)} %shard_map.76), calls=%async_computation | async-start | bytes 98304 | tf_op jit(solution)/shard_map/all_to_all | solution.py:444
  18.3 3.8 %collective-permute-start.1 = (bf16[288,128]{1,0:T(8,128)(2,1)S(1)}, bf16[288,128]{1,0:T(8,128)(2,1)S(1)}, u32[]{:S(2)}, u32[]{:S(2)}) collective-permute-start(bf16[288,128]{1,0:T(8,128)(2,1)S(1)} %get-tuple-element.31), channel_id=1, source_target_pairs={{24,0},{25,1},{26,2},{27,3},{28,4},{29,5},{30,6},{31,7},{0,8},{1,9... | collective-permute-start | bytes 221192 | tf_op jit(solution)/shard_map/ppermute | solution.py:34
  18.3 3.8 %collective-permute-start.2 = (bf16[288,128]{1,0:T(8,128)(2,1)S(1)}, bf16[288,128]{1,0:T(8,128)(2,1)S(1)}, u32[]{:S(2)}, u32[]{:S(2)}) collective-permute-start(bf16[288,128]{1,0:T(8,128)(2,1)S(1)} %get-tuple-element.32), channel_id=1, source_target_pairs={{8,0},{9,1},{10,2},{11,3},{12,4},{13,5},{14,6},{15,7},{16,8},{17,9... | collective-permute-start | bytes 221192 | tf_op jit(solution)/shard_map/ppermute | solution.py:34
  29.0 6.3 %collective-permute-start.3 = (bf16[416,128]{1,0:T(8,128)(2,1)S(1)}, bf16[416,128]{1,0:T(8,128)(2,1)S(1)}, u32[]{:S(2)}, u32[]{:S(2)}) collective-permute-start(bf16[416,128]{1,0:T(8,128)(2,1)S(1)} %get-tuple-element.38), channel_id=1, source_target_pairs={{24,0},{25,1},{26,2},{27,3},{28,4},{29,5},{30,6},{31,7},{0,8},{1,9... | collective-permute-start | bytes 319496 | tf_op jit(solution)/shard_map/ppermute | solution.py:34
  30.6 4.6 %collective-permute-start.4 = (bf16[416,128]{1,0:T(8,128)(2,1)S(1)}, bf16[416,128]{1,0:T(8,128)(2,1)S(1)}, u32[]{:S(2)}, u32[]{:S(2)}) collective-permute-start(bf16[416,128]{1,0:T(8,128)(2,1)S(1)} %get-tuple-element.39), channel_id=1, source_target_pairs={{8,0},{9,1},{10,2},{11,3},{12,4},{13,5},{14,6},{15,7},{16,8},{17,9... | collective-permute-start | bytes 319496 | tf_op jit(solution)/shard_map/ppermute | solution.py:34
  30.9 4.4 %collective-permute-start.5 = (bf16[64,128]{1,0:T(8,128)(2,1)S(1)}, bf16[64,128]{1,0:T(8,128)(2,1)S(1)}, u32[]{:S(2)}, u32[]{:S(2)}) collective-permute-start(bf16[64,128]{1,0:T(8,128)(2,1)S(1)} %get-tuple-element.41.wframe), channel_id=1, source_target_pairs={{16,0},{17,1},{18,2},{19,3},{20,4},{21,5},{22,6},{23,7},{24,8},{25... | collective-permute-start | bytes 49160 | tf_op jit(solution)/shard_map/ppermute | solution.py:34
  43.6 4.0 %collective-permute-start.6 = (bf16[144,128]{1,0:T(8,128)(2,1)S(1)}, bf16[144,128]{1,0:T(8,128)(2,1)S(1)}, u32[]{:S(2)}, u32[]{:S(2)}) collective-permute-start(bf16[144,128]{1,0:T(8,128)(2,1)S(1)} %get-tuple-element.48), channel_id=1, source_target_pairs={{1,0},{0,1},{3,2},{2,3},{5,4},{4,5},{7,6},{6,7},{9,8},{8,9},{11,10... | collective-permute-start | bytes 110600 | tf_op jit(solution)/shard_map/ppermute | solution.py:34

commit v4 on v2

--- a/solution.py
+++ b/solution.py
@@ -23,15 +23,24 @@
     return lax.broadcasted_iota(jnp.int32, shape, dim)
 
 
-def taken_from(array, offset):
-    sizes = [lax.axis_size(axis) for axis in axes]
+def swapped(array, axis, pairing):
+    count = lax.axis_size(axis)
     pairs = []
-    for place in np.ndindex(*sizes):
-        source = [(p + o) % n for p, o, n in zip(place, offset, sizes)]
-        pairs.append(
-            (int(np.ravel_multi_index(source, sizes)), int(np.ravel_multi_index(place, sizes)))
-        )
-    return lax.ppermute(array, axes, pairs)
+    for i in range(count):
+        if pairing == 2:
+            partner = i + count // 2
+        else:
+            partner = i + 1 if i % 2 == pairing else i - 1
+        pairs.append((i, partner % count))
+    return lax.ppermute(array, axis, pairs)
+
+
+def is_even(axis):
+    return lax.rem(lax.axis_index(axis), 2) == 0
+
+
+def pick(axis, if_even, if_odd):
+    return jnp.where(is_even(axis), if_even, if_odd)
 
 
 def split(value):
@@ -44,7 +53,7 @@
     return pair[:half].astype(f32) + pair[half:].astype(f32)
 
 
-def pack_kernel(cells, edges, first, last, rows):
+def pack_kernel(cells, edges, sent_0, sent_1, rows):
     chan, count_x, count_y, _ = cells.shape
     count = chan * count_x
     planes = [cells[c, x] for x in range(count_x) for c in range(chan)]
@@ -52,40 +61,50 @@
     row = iota((2 * count, count * lanes), 0)
     lane = iota((2 * count, count * lanes), 1)
     want = jnp.where(row < count, row * lanes, (row - count) * lanes + lanes - 1)
-    pick = (lane == want).astype(f32).astype(bf16)
-    found = dot(pick, wide, ((1,), (1,)))
+    chosen = (lane == want).astype(f32).astype(bf16)
+    found = dot(chosen, wide, ((1,), (1,)))
     found = jnp.concatenate([found, jnp.zeros((2 * count, lanes - count_y), f32)], axis=1)
     edges[...] = pltpu.roll(found, 1, 1).astype(bf16)
     for at, plane in enumerate(planes):
         wide_plane = plane.astype(f32)
         rows[at : at + 1, :] = wide_plane[0:1]
         rows[count + at : count + at + 1, :] = wide_plane[count_y - 1 : count_y]
-    first[...] = rows[0:count, :].astype(bf16)
-    last[...] = rows[count : 2 * count, :].astype(bf16)
-
-
-def bundle_kernel(cells, edges, above, below, low, high, left, right):
+    first, last = rows[0:count, :], rows[count : 2 * count, :]
+    sent_0[...] = pick("gy", last, first).astype(bf16)
+    sent_1[...] = pick("gy", first, last).astype(bf16)
+
+
+def bundle_kernel(cells, edges, got_0, got_1, sent_0, sent_1, left, right, rows):
     chan, count_x, count_y, _ = cells.shape
     own = chan * count_x
+    above = pick("gy", got_1[...].astype(f32), got_0[...].astype(f32))
+    below = pick("gy", got_0[...].astype(f32), got_1[...].astype(f32))
     spot = iota((2 * own, lanes), 1)
-    before = pltpu.roll(above[own:, :].astype(f32), count_y, 1)
-    after = pltpu.roll(below[own:, :].astype(f32), lanes - count_y, 1)
+    before = pltpu.roll(above[own:], count_y, 1)
+    after = pltpu.roll(below[own:], lanes - count_y, 1)
     whole = jnp.where(
         spot == 0, before, jnp.where(spot == count_y + 1, after, edges[...].astype(f32))
     )
     right[...] = whole[0:own]
     left[...] = whole[own : 2 * own]
-    rows_above = above[0:own, :].astype(f32)
-    rows_below = below[0:own, :].astype(f32)
+    rows_above, rows_below = above[0:own], below[0:own]
+    rows[0:own, :] = rows_above
+    rows[own : 2 * own, :] = rows_below
     zero = jnp.zeros((8, lanes), f32)
     body = chan * count_y
-    for ref, x in ((low, 0), (high, count_x - 1)):
-        for c in range(chan):
-            ref[c * count_y : (c + 1) * count_y, :] = cells[c, x]
+    frames = []
+    for x in (0, count_x - 1):
         at = slice(x * chan, x * chan + chan)
         frame = [rows_above[at], rows_below[at], zero]
         frame += [whole[own + x * chan : own + (x + 1) * chan], whole[at], zero]
-        ref[body : body + 32, :] = jnp.concatenate(frame, axis=0).astype(bf16)
+        frames.append(jnp.concatenate(frame, axis=0))
+    even = is_even("gx")
+    for ref, odd in ((sent_0, 0), (sent_1, 1)):
+        high = even != (odd == 1)
+        x = jnp.where(high, count_x - 1, 0)
+        for c in range(chan):
+            ref[c * count_y : (c + 1) * count_y, :] = cells[c, x]
+        ref[body : body + 32, :] = jnp.where(high, frames[1], frames[0]).astype(bf16)
 
 
 def spread_kernel(cot, spread):
@@ -114,8 +133,8 @@
 
 
 def main_kernel(
-    cells, low, high, above, below, left_in, right_in, spread, wbig, wback,
-    sums, field, bundle_low, bundle_high, wpart, wframe, rows_out, cols,
+    cells, got_0, got_1, rows_in, left_in, right_in, spread, wbig, wback,
+    sums, field, sent_0, sent_1, wpart, wframe, rows_out, cols,
     stage, patches, left, right, outer, carry, gram,
 ):
     chan, count_x, count_y, _ = cells.shape
@@ -126,21 +145,26 @@
     depth = 3 * wide + 8
     body = chan * count_y
     lane = iota((wide, lanes), 1)
+    even = is_even("gx")
+
+    def got(up, start, size):
+        one = got_0[start : start + size, :].astype(f32)
+        two = got_1[start : start + size, :].astype(f32)
+        return jnp.where(even, one, two) if up else jnp.where(even, two, one)
 
     for x in range(count_x + 2):
         for c in range(chan):
             if x == 0:
-                plane = low[c * count_y : (c + 1) * count_y, :]
+                plane = got(False, c * count_y, count_y)
             elif x == count_x + 1:
-                plane = high[c * count_y : (c + 1) * count_y, :]
+                plane = got(True, c * count_y, count_y)
             else:
                 plane = cells[c, x - 1]
             stage[pl.ds(wide + x * chan + c, count_y, stride=wide), :] = plane.astype(f32)
-    rest_low = low[body : body + 32, :].astype(f32)
-    rest_high = high[body : body + 32, :].astype(f32)
-    for base, ref, at in ((0, above, 0), ((count_y + 1) * wide, below, chan)):
+    rest_low, rest_high = got(False, body, 32), got(True, body, 32)
+    for base, top, at in ((0, 0, 0), ((count_y + 1) * wide, own, chan)):
         stage[base : base + chan, :] = rest_low[at : at + chan]
-        stage[base + chan : base + chan + own, :] = ref[0:own, :].astype(f32)
+        stage[base + chan : base + chan + own, :] = rows_in[top : top + own, :]
         stage[base + chan + own : base + wide, :] = rest_high[at : at + chan]
     for ref, mine, at in ((left, left_in, 16), (right, right_in, 16 + chan)):
         ref[0:chan, :] = rest_low[at : at + chan]
@@ -261,88 +285,105 @@
     row = iota((wide * lanes, lanes), 0)
     spot = iota((wide * lanes, lanes), 1)
     want = jnp.where(spot < wide, spot * lanes + lanes - 1, (spot - wide) * lanes)
-    pick = ((row == want) & (spot < 2 * wide)).astype(f32).astype(bf16)
-    found = dot(jnp.concatenate(planes, axis=1), pick)
+    chosen = ((row == want) & (spot < 2 * wide)).astype(f32).astype(bf16)
+    found = dot(jnp.concatenate(planes, axis=1), chosen)
     cols[...] = found
     found = found.astype(bf16)
     zero = jnp.zeros((8, lanes), f32)
-    for ref, x in ((bundle_low, 0), (bundle_high, count_x + 1)):
+    for ref, odd in ((sent_0, 0), (sent_1, 1)):
+        high = even != (odd == 1)
         for c in range(chan):
-            plane = field[pl.ds(wide + x * chan + c, count_y, stride=wide), :]
+            low_plane, high_plane = [
+                field[pl.ds(wide + x * chan + c, count_y, stride=wide), :]
+                for x in (0, count_x + 1)
+            ]
+            plane = jnp.where(high, high_plane, low_plane)
             ref[c * count_y : (c + 1) * count_y, :] = plane.astype(bf16)
-        frame = [end[x * chan : (x + 1) * chan] for end in ends] + [zero]
-        ref[body : body + 16, :] = jnp.concatenate(frame, axis=0).astype(bf16)
+        low_frame, high_frame = [
+            jnp.concatenate([end[x * chan : (x + 1) * chan] for end in ends] + [zero], axis=0)
+            for x in (0, count_x + 1)
+        ]
+        ref[body : body + 16, :] = jnp.where(high, high_frame, low_frame).astype(bf16)
         ref[body + 16 : body + 16 + tall, :] = found
         ref[body + 16 + tall :, :] = sides
 
 
-def x_kernel(alone, wpart, wframe, rows, cols, from_low, from_high, far, wsum, up, down, cols_out):
+def x_kernel(alone, wpart, wframe, rows, cols, got_0, got_1, far, wsum, sent_0, sent_1, cols_out):
     tall = cols.shape[0]
     chan_out = wpart.shape[0]
     own = rows.shape[0] // 2
-    body = from_low.shape[0] - 16 - tall - 2 * chan_out
+    body = got_0.shape[0] - 16 - tall - 2 * chan_out
     chan = 4
     wide = own + 2 * chan
     if alone:
         total = joined(jnp.concatenate(split(wpart[...]), axis=0))
     else:
         total = joined(wframe[...]) + joined(far[...])
-        sides = [ref[body + 16 + tall :, :] for ref in (from_low, from_high)]
+        sides = [ref[body + 16 + tall :, :] for ref in (got_0, got_1)]
         total = total + (joined(sides[0]) + joined(sides[1]))
     wsum[...] = total
     sides = jnp.concatenate(split(total), axis=0)
     spot = iota((tall, lanes), 1)
     found = cols[...]
-    for ref, turn, start in ((from_low, lanes - own, chan), (from_high, own, own)):
-        part = pltpu.roll(ref[body + 16 : body + 16 + tall, :].astype(f32), turn, 1)
+    one = got_0[body : body + 16 + tall, :].astype(f32)
+    two = got_1[body : body + 16 + tall, :].astype(f32)
+    from_low, from_high = pick("gx", two, one), pick("gx", one, two)
+    for part, turn, start in ((from_low, lanes - own, chan), (from_high, own, own)):
+        part = pltpu.roll(part[16:], turn, 1)
         near = (spot >= start) & (spot < start + chan)
         near = near | ((spot >= wide + start) & (spot < wide + start + chan))
         found = found + jnp.where(near, part, 0.0)
     cols_out[...] = found
-    low_rows = from_low[body : body + 16, :].astype(f32)
-    high_rows = from_high[body : body + 16, :].astype(f32)
     count_y = body // chan
     mid = jnp.zeros((own - 2 * chan, lanes), f32)
-    for ref, at, line in ((down, 0, 0), (up, 1, count_y + 1)):
-        more = [low_rows[at * chan : (at + 1) * chan], mid, high_rows[at * chan : (at + 1) * chan]]
+    both = []
+    for at, line in ((0, 0), (1, count_y + 1)):
+        more = [from_low[at * chan : (at + 1) * chan], mid, from_high[at * chan : (at + 1) * chan]]
         total = rows[at * own : (at + 1) * own, :] + jnp.concatenate(more, axis=0)
         extra = jnp.broadcast_to(found[line : line + 1], (16, lanes))
-        ref[0 : own + 16, :] = jnp.concatenate([total, extra], axis=0).astype(bf16)
+        both.append(jnp.concatenate([total, extra], axis=0))
+    sent_0[0 : own + 16, :] = pick("gy", both[1], both[0]).astype(bf16)
+    sent_1[0 : own + 16, :] = pick("gy", both[0], both[1]).astype(bf16)
+    for ref in (sent_0, sent_1):
         ref[own + 16 :, :] = sides
 
 
-def y_kernel(alone, count_y, wsum, cols, above, below, far, wout, frame):
+def y_kernel(alone, count_y, wsum, cols, got_0, got_1, far, wout, frame, rows):
     tall = cols.shape[0]
     chan_out = wsum.shape[0]
-    top = above.shape[0] - 2 * chan_out
+    top = got_0.shape[0] - 2 * chan_out
+    one, two = got_0[0:top, :].astype(f32), got_1[0:top, :].astype(f32)
+    above, below = pick("gy", two, one), pick("gy", one, two)
+    rows[...] = jnp.concatenate([above[0 : top - 16], below[0 : top - 16]], axis=0)
     if alone:
         total = joined(jnp.concatenate(split(wsum[...]), axis=0))
     else:
         total = joined(jnp.concatenate(split(wsum[...]), axis=0)) + joined(far[...])
-        total = total + (joined(above[top:, :]) + joined(below[top:, :]))
+        total = total + (joined(got_0[top:, :]) + joined(got_1[top:, :]))
     wout[...] = total
     frame[tall:, :] = jnp.concatenate(split(total), axis=0)
     row = iota((tall, lanes), 0)
     found = cols[...]
-    found = found + jnp.where(row == 1, above[top - 16 : top, :].astype(f32)[0:1], 0.0)
-    found = found + jnp.where(row == count_y, below[top - 16 : top, :].astype(f32)[0:1], 0.0)
+    found = found + jnp.where(row == 1, above[top - 16 : top - 15], 0.0)
+    found = found + jnp.where(row == count_y, below[top - 16 : top - 15], 0.0)
     frame[0:tall, :] = found.astype(bf16)
 
 
-def grad_kernel(field, from_low, from_high, grad):
+def grad_kernel(field, got_0, got_1, grad):
     chan, count_x, count_y, _ = grad.shape
     wide = chan * (count_x + 2)
     for x in range(count_x):
         for c in range(chan):
             plane = field[pl.ds(wide + (x + 1) * chan + c, count_y, stride=wide), :]
+            place = slice(c * count_y, (c + 1) * count_y)
             if x == 0:
-                plane = plane + from_low[c * count_y : (c + 1) * count_y, :].astype(f32)
+                plane = plane + pick("gx", got_1[place, :].astype(f32), got_0[place, :].astype(f32))
             if x == count_x - 1:
-                plane = plane + from_high[c * count_y : (c + 1) * count_y, :].astype(f32)
+                plane = plane + pick("gx", got_0[place, :].astype(f32), got_1[place, :].astype(f32))
             grad[c, x] = plane
 
 
-def final_kernel(grad, wsum, above, below, frame, out, wout, bout):
+def final_kernel(grad, wsum, rows, frame, out, wout, bout):
     chan, count_x, count_y, _ = grad.shape
     chan_out = wsum.shape[0]
     own = chan * count_x
@@ -359,8 +400,7 @@
     spot = iota((count_y, lanes), 1)
     row = iota((count_y, lanes), 0)
     cols = frame[0:tall, :].astype(f32)[1 : count_y + 1]
-    first = above[0:own, :].astype(f32)
-    final = below[0:own, :].astype(f32)
+    first, final = rows[0:own, :], rows[own : 2 * own, :]
     for x in range(count_x):
         for c in range(chan):
             at = x * chan + c
@@ -406,7 +446,7 @@
     wback = placed.reshape(count_x * chan_out, 9 * wide).T
 
     own_block = shape((own, lanes), bf16)
-    edges, first, last = call(
+    edges, row_0, row_1 = call(
         pack_kernel,
         [shape((2 * own, lanes), bf16), own_block, own_block],
         [pltpu.VMEM((2 * own, lanes), f32)],
@@ -414,19 +454,20 @@
     pool_x, pool_y, pool_z = cotangent.shape[1:]
     pooled_rows = shape((pool_y * pool_x * chan_out, lanes), f32)
     spread = call(spread_kernel, pooled_rows)(cotangent)
-    edges = taken_from(edges, (0, 0, 1))
-    above = taken_from(jnp.concatenate([last, edges]), (0, -1, 0))
-    below = taken_from(jnp.concatenate([first, edges]), (0, 1, 0))
+    edges = swapped(edges, "gz", 0)
+    row_1 = swapped(jnp.concatenate([row_1, edges]), "gy", 1)
+    row_0 = swapped(jnp.concatenate([row_0, edges]), "gy", 0)
     body = chan * count_y
     bundle = shape((body + 32, lanes), bf16)
-    low, high, left, right = call(
-        bundle_kernel, [bundle, bundle, shape((own, lanes), f32), shape((own, lanes), f32)]
-    )(cells, edges, above, below)
-    low, high = taken_from(high, (-1, 0, 0)), taken_from(low, (1, 0, 0))
+    side = shape((own, lanes), f32)
+    face_0, face_1, left, right, rows = call(
+        bundle_kernel, [bundle, bundle, side, side, shape((2 * own, lanes), f32)]
+    )(cells, edges, row_0, row_1)
+    face_1, face_0 = swapped(face_1, "gx", 1), swapped(face_0, "gx", 0)
 
     tall = 80
     bundle = shape((body + 16 + tall + 2 * chan_out, lanes), bf16)
-    sums, field, low, high, wpart, wframe, rows, cols = call(
+    sums, field, face_0, face_1, wpart, wframe, rows, cols = call(
         main_kernel,
         [
             pooled_rows,
@@ -447,32 +488,36 @@
             pltpu.VMEM((6 * wide, lanes), f32),
             pltpu.VMEM((count_x * chan_out, 3 * depth), f32),
         ],
-    )(cells, low, high, above, below, left, right, spread, wbig, wback)
+    )(cells, face_0, face_1, rows, left, right, spread, wbig, wback)
 
     alone_x = lax.axis_size("gx") != 4
     alone_y = lax.axis_size("gy") != 4
     if alone_x:
         wpart, far = lax.psum(wpart, "gx"), wframe
     else:
-        far = taken_from(wframe, (2, 0, 0))
-    low, high = taken_from(high, (-1, 0, 0)), taken_from(low, (1, 0, 0))
+        far = swapped(wframe, "gx", 2)
+    face_1, face_0 = swapped(face_1, "gx", 1), swapped(face_0, "gx", 0)
     pooled = call(pool_kernel, shape(cotangent.shape, bf16))(sums)
     rows_out = shape((own + 16 + 2 * chan_out, lanes), bf16)
-    wsum, up, down, cols = call(
+    wsum, row_0, row_1, cols = call(
         functools.partial(x_kernel, alone_x),
         [shape((chan_out, lanes), f32), rows_out, rows_out, shape((tall, lanes), f32)],
-    )(wpart, wframe, rows, cols, low, high, far)
-    grad = call(grad_kernel, shape(cells.shape, f32))(field, low, high)
+    )(wpart, wframe, rows, cols, face_0, face_1, far)
+    grad = call(grad_kernel, shape(cells.shape, f32))(field, face_0, face_1)
     if alone_y:
         far, wsum = wframe, lax.psum(wsum, "gy")
     else:
-        far = taken_from(up[own + 16 :], (0, 2, 0))
-    above, below = taken_from(up, (0, -1, 0)), taken_from(down, (0, 1, 0))
-    wsum, frame = call(
+        far = swapped(row_0[own + 16 :], "gy", 2)
+    row_1, row_0 = swapped(row_1, "gy", 1), swapped(row_0, "gy", 0)
+    wsum, frame, rows = call(
         functools.partial(y_kernel, alone_y, count_y),
-        [shape((chan_out, lanes), f32), shape((tall + 2 * chan_out, lanes), bf16)],
-    )(wsum, cols, above, below, far)
-    frame = taken_from(frame, (0, 0, 1))
+        [
+            shape((chan_out, lanes), f32),
+            shape((tall + 2 * chan_out, lanes), bf16),
+            shape((2 * own, lanes), f32),
+        ],
+    )(wsum, cols, row_0, row_1, far)
+    frame = swapped(frame, "gz", 0)
     input_grad, wsum, bias_grad = call(
         final_kernel,
         [
@@ -480,7 +525,7 @@
             shape((27, chan, chan_out), f32),
             shape((1, chan_out), f32),
         ],
-    )(grad, wsum, above, below, frame)
+    )(grad, wsum, rows, frame)
     weight_grad = wsum.reshape(3, 3, 3, chan, chan_out).transpose(4, 3, 0, 1, 2)
     return (pooled, weight_grad, bias_grad.reshape(chan_out), input_grad)
 

time: 45.3 us -> 43.5 us (0.960)
  waiting for transfers between devices: 15.9 us -> 12.9 us
  starting transfers between devices: 15.9 us -> 17 us
    ppermute x12, waiting for transfers between devices: 15.9 us -> 12.9 us  [swapped(): return lax.ppermute(array, axis, pairs)]
    ppermute x12, starting transfers between devices: 15.9 us -> 17 us  [swapped(): return lax.ppermute(array, axis, pairs)]
where the time goes in v4:
time: 43.5 us; the launch traced here: 43.3 us
  starting transfers between devices  17 us (39%)
  waiting for transfers between devices  12.9 us (30%)
  Pallas kernels  10.8 us (25%)
  local copies, waits for them, and re-layouts  1.63 us (4%)
  between operations  0.77 us (2%)
    ppermute x12, starting transfers between devices, swapped(): return lax.ppermute(array, axis, pairs)  17 us
    ppermute x12, waiting for transfers between devices, swapped(): return lax.ppermute(array, axis, pairs)  12.9 us
    pallas_call x1, Pallas kernels, on_device(): call(main_kernel, [pooled_rows, shape(((count_y + 2) * wide, lanes), f32)...  6.94 us
    pallas_call x1, Pallas kernels, on_device(): pooled = call(pool_kernel, shape(cotangent.shape, bf16))(sums)  1.24 us
    pallas_call x1, Pallas kernels, on_device(): call(final_kernel, [shape(cells.shape, f32), shape((27, chan, chan_out),...  1.13 us
    unnamed x10, local copies, waits for them, and re-layouts  0.97 us
    pallas_call x1, Pallas kernels, on_device(): spread = call(spread_kernel, pooled_rows)(cotangent)  0.88 us
  transfers between devices with their start and end apart: 12, of which 7 were waited for; matrix products, arithmetic and copies ran while one was open for 2% of the time, Pallas kernels for 5%

profile of v4, /device:TPU:0, one launch (start us, length us, event | category | flops | bytes accessed | tf_op | source)
XLA Modules:
  0.0 43.3 jit_solution(9234959033514605698)
XLA Ops:
  0.6 0.9 %copy-done = bf16[4,4,64,128]{3,2,1,0:T(8,128)(2,1)S(1)} copy-done((bf16[4,4,64,128]{3,2,1,0:T(8,128)(2,1)S(1)}, bf16[4,4,64,128]{3,2,1,0:T(8,128)(2,1)}, u32[]{:S(2)}) %copy-start) | copy-done | bytes 262168
  1.6 0.3 shard_map.75
  1.9 3.0 %collective-permute-start = (bf16[32,128]{1,0:T(8,128)(2,1)S(1)}, bf16[32,128]{1,0:T(8,128)(2,1)S(1)}, u32[]{:S(2)}, u32[]{:S(2)}) collective-permute-start(bf16[32,128]{1,0:T(8,128)(2,1)S(1)} %get-tuple-element.30), channel_id=1, source_target_pairs={{0,1},{1,0},{2,3},{3,2},{4,5},{5,4},{6,7},{7,6},{8,9},{9,8},{10,11... | collective-permute-start | bytes 24584 | tf_op jit(solution)/shard_map/ppermute | solution.py:35
  4.9 0.2 pad_maximum_fusion
  5.2 1.3 %collective-permute-done.edges = bf16[32,128]{1,0:T(8,128)(2,1)S(1)} collective-permute-done((bf16[32,128]{1,0:T(8,128)(2,1)S(1)}, bf16[32,128]{1,0:T(8,128)(2,1)S(1)}, u32[]{:S(2)}, u32[]{:S(2)}) %collective-permute-start) | collective-permute-done | bytes 8224 | tf_op jit(solution)/shard_map/ppermute | solution.py:35
  6.5 4.1 %collective-permute-start.2 = (bf16[48,128]{1,0:T(8,128)(2,1)S(1)}, bf16[48,128]{1,0:T(8,128)(2,1)S(1)}, u32[]{:S(2)}, u32[]{:S(2)}) collective-permute-start(bf16[48,128]{1,0:T(8,128)(2,1)S(1)} %get-tuple-element.60), channel_id=1, source_target_pairs={{0,6},{2,4},{4,2},{6,0},{1,7},{3,5},{5,3},{7,1},{8,14},{10,12},{12... | collective-permute-start | bytes 36872 | tf_op jit(solution)/shard_map/ppermute | solution.py:35
  10.7 0.2 reshape_reshape.3
  11.1 1.1 %collective-permute-done.2.got_1 = bf16[48,128]{1,0:T(8,128)(2,1)S(1)} collective-permute-done((bf16[48,128]{1,0:T(8,128)(2,1)S(1)}, bf16[48,128]{1,0:T(8,128)(2,1)S(1)}, u32[]{:S(2)}, u32[]{:S(2)}) %collective-permute-start.2) | collective-permute-done | bytes 12320 | tf_op jit(solution)/shard_map/ppermute | solution.py:35
  12.3 2.0 %collective-permute-done.1.got_0 = bf16[48,128]{1,0:T(8,128)(2,1)S(1)} collective-permute-done((bf16[48,128]{1,0:T(8,128)(2,1)S(1)}, bf16[48,128]{1,0:T(8,128)(2,1)S(1)}, u32[]{:S(2)}, u32[]{:S(2)}) %collective-permute-start.1) | collective-permute-done | bytes 12320 | tf_op jit(solution)/shard_map/ppermute | solution.py:35
  14.4 1.6 %collective-permute-start.4 = (bf16[288,128]{1,0:T(8,128)(2,1)S(1)}, bf16[288,128]{1,0:T(8,128)(2,1)S(1)}, u32[]{:S(2)}, u32[]{:S(2)}) collective-permute-start(bf16[288,128]{1,0:T(8,128)(2,1)S(1)} %get-tuple-element.34), channel_id=1, source_target_pairs={{0,24},{8,16},{16,8},{24,0},{1,25},{9,17},{17,9},{25,1},{2,26},{10... | collective-permute-start | bytes 221192 | tf_op jit(solution)/shard_map/ppermute | solution.py:35
  16.1 0.9 %shard_map.77.spread = f32[2048,128]{1,0:T(8,128)S(1)} custom-call(bf16[32,2,32,64]{3,2,1,0:T(8,128)(2,1)S(1)} %copy-done.2), custom_call_target="tpu_custom_call" | custom-call | tf_op jit(solution)/shard_map/pallas_call | solution.py:456
  17.0 1.4 %collective-permute-done.4.got_1 = bf16[288,128]{1,0:T(8,128)(2,1)S(1)} collective-permute-done((bf16[288,128]{1,0:T(8,128)(2,1)S(1)}, bf16[288,128]{1,0:T(8,128)(2,1)S(1)}, u32[]{:S(2)}, u32[]{:S(2)}) %collective-permute-start.4) | collective-permute-done | bytes 73760 | tf_op jit(solution)/shard_map/ppermute | solution.py:35
  18.5 6.9 %shard_map.78 = (f32[2048,128]{1,0:T(8,128)S(1)}, f32[1584,128]{1,0:T(8,128)S(1)}, bf16[416,128]{1,0:T(8,128)(2,1)S(1)}, bf16[416,128]{1,0:T(8,128)(2,1)S(1)}, f...) custom-call(bf16[4,4,64,128]{3,2,1,0:T(8,128)(2,1)S(1)} %copy-done.1, ...), custom_call_target="tpu_custom_call" | custom-call | tf_op jit(solution)/shard_map/pallas_call | solution.py:470
  25.4 0.5 %collective-permute-start.5 = (bf16[416,128]{1,0:T(8,128)(2,1)S(1)}, bf16[416,128]{1,0:T(8,128)(2,1)S(1)}, u32[]{:S(2)}, u32[]{:S(2)}) collective-permute-start(bf16[416,128]{1,0:T(8,128)(2,1)S(1)} %get-tuple-element.40), channel_id=1, source_target_pairs={{0,8},{8,0},{16,24},{24,16},{1,9},{9,1},{17,25},{25,17},{2,10},{10... | collective-permute-start | bytes 319496 | tf_op jit(solution)/shard_map/ppermute | solution.py:35
  25.9 1.2 %collective-permute-start.6 = (bf16[416,128]{1,0:T(8,128)(2,1)S(1)}, bf16[416,128]{1,0:T(8,128)(2,1)S(1)}, u32[]{:S(2)}, u32[]{:S(2)}) collective-permute-start(bf16[416,128]{1,0:T(8,128)(2,1)S(1)} %get-tuple-element.41), channel_id=1, source_target_pairs={{0,24},{8,16},{16,8},{24,0},{1,25},{9,17},{17,9},{25,1},{2,26},{10... | collective-permute-start | bytes 319496 | tf_op jit(solution)/shard_map/ppermute | solution.py:35
  27.1 0.6 %collective-permute-start.7 = (bf16[64,128]{1,0:T(8,128)(2,1)S(1)}, bf16[64,128]{1,0:T(8,128)(2,1)S(1)}, u32[]{:S(2)}, u32[]{:S(2)}) collective-permute-start(bf16[64,128]{1,0:T(8,128)(2,1)S(1)} %get-tuple-element.43.wframe), channel_id=1, source_target_pairs={{0,16},{8,24},{16,0},{24,8},{1,17},{9,25},{17,1},{25,9},{2,18},{10... | collective-permute-start | bytes 49160 | tf_op jit(solution)/shard_map/ppermute | solution.py:35
  27.7 3.8 %collective-permute-done.7.far = bf16[64,128]{1,0:T(8,128)(2,1)S(1)} collective-permute-done((bf16[64,128]{1,0:T(8,128)(2,1)S(1)}, bf16[64,128]{1,0:T(8,128)(2,1)S(1)}, u32[]{:S(2)}, u32[]{:S(2)}) %collective-permute-start.7) | collective-permute-done | bytes 16416 | tf_op jit(solution)/shard_map/ppermute | solution.py:35
  31.6 1.9 %collective-permute-start.9 = (bf16[96,128]{1,0:T(8,128)(2,1)S(1)}, bf16[96,128]{1,0:T(8,128)(2,1)S(1)}, u32[]{:S(2)}, u32[]{:S(2)}) collective-permute-start(bf16[96,128]{1,0:T(8,128)(2,1)S(1)} %get-tuple-element.49), channel_id=1, source_target_pairs={{0,6},{2,4},{4,2},{6,0},{1,7},{3,5},{5,3},{7,1},{8,14},{10,12},{12... | collective-permute-start | bytes 73736 | tf_op jit(solution)/shard_map/ppermute | solution.py:35
  33.5 2.6 %collective-permute-start.10 = (bf16[64,128]{1,0:T(8,128)(2,1)S(1)}, bf16[64,128]{1,0:T(8,128)(2,1)S(1)}, u32[]{:S(2)}, u32[]{:S(2)}) collective-permute-start(bf16[64,128]{1,0:T(8,128)(2,1)S(1)} %slice.3), channel_id=1, source_target_pairs={{0,4},{2,6},{4,0},{6,2},{1,5},{3,7},{5,1},{7,3},{8,12},{10,14},{12... | collective-permute-start | bytes 49160 | tf_op jit(solution)/shard_map/ppermute | solution.py:35
  36.1 2.1 %collective-permute-done.10.far = bf16[64,128]{1,0:T(8,128)(2,1)S(1)} collective-permute-done((bf16[64,128]{1,0:T(8,128)(2,1)S(1)}, bf16[64,128]{1,0:T(8,128)(2,1)S(1)}, u32[]{:S(2)}, u32[]{:S(2)}) %collective-permute-start.10) | collective-permute-done | bytes 16416 | tf_op jit(solution)/shard_map/ppermute | solution.py:35
  38.2 1.6 %collective-permute-start.11 = (bf16[144,128]{1,0:T(8,128)(2,1)S(1)}, bf16[144,128]{1,0:T(8,128)(2,1)S(1)}, u32[]{:S(2)}, u32[]{:S(2)}) collective-permute-start(bf16[144,128]{1,0:T(8,128)(2,1)S(1)} %get-tuple-element.52), channel_id=1, source_target_pairs={{0,1},{1,0},{2,3},{3,2},{4,5},{5,4},{6,7},{7,6},{8,9},{9,8},{10,11... | collective-permute-start | bytes 110600 | tf_op jit(solution)/shard_map/ppermute | solution.py:35
  39.7 1.2 %shard_map.79 = bf16[32,2,32,64]{3,2,1,0:T(8,128)(2,1)} custom-call(f32[2048,128]{1,0:T(8,128)S(1)} %get-tuple-element.38.sums), custom_call_target="tpu_custom_call" | custom-call | tf_op jit(solution)/shard_map/pallas_call | solution.py:500
  41.1 1.1 %collective-permute-done.11.frame = bf16[144,128]{1,0:T(8,128)(2,1)S(1)} collective-permute-done((bf16[144,128]{1,0:T(8,128)(2,1)S(1)}, bf16[144,128]{1,0:T(8,128)(2,1)S(1)}, u32[]{:S(2)}, u32[]{:S(2)}) %collective-permute-start.11) | collective-permute-done | bytes 36896 | tf_op jit(solution)/shard_map/ppermute | solution.py:35
  42.2 1.1 %shard_map.83 = (f32[4,4,64,128]{3,2,1,0:T(8,128)}, f32[27,4,32]{2,1,0:T(4,128)}, f32[1,32]{1,0:T(1,128)}) custom-call(f32[4,4,64,128]{3,2,1,0:T(8,128)S(1)} %shard_map.80.grad, f32[32,128]{1,0:T(8,128)S(1)} %get-tuple-element.50.wsum, f32[32,128]{1,0:T(8,128)S(1)} %get-tuple-element.51.rows, bf16[144,128]{1,0:T(8,128)(2,1)S(1)} %collective-permute-done.11.frame), custom_call_target="tpu_custom_call" | custom-call | tf_op jit(solution)/shard_map/pallas_call | solution.py:521
  (32 shorter events, 0.9 us)
Async XLA Ops:
  0.6 1.0 %copy-start = (bf16[4,4,64,128]{3,2,1,0:T(8,128)(2,1)S(1)}, bf16[4,4,64,128]{3,2,1,0:T(8,128)(2,1)}, u32[]{:S(2)}) copy-start(bf16[4,4,64,128]{3,2,1,0:T(8,128)(2,1)} %cells.5) | copy-start | bytes 786436
  1.6 3.3 %copy-start.3 = (bf16[32,4,3,3,3]{0,1,4,3,2:T(4,128)(2,1)S(1)}, bf16[32,4,3,3,3]{0,1,4,3,2:T(4,128)(2,1)}, u32[]{:S(2)}) copy-start(bf16[32,4,3,3,3]{0,1,4,3,2:T(4,128)(2,1)} %param.5) | copy-start | bytes 20740
  1.9 3.0 %copy-start.4 = (f32[32]{0:T(128)S(1)}, f32[32]{0:T(128)}, u32[]{:S(2)}) copy-start(f32[32]{0:T(128)} %param.6) | copy-start | bytes 388
  1.9 4.6 %collective-permute-start = (bf16[32,128]{1,0:T(8,128)(2,1)S(1)}, bf16[32,128]{1,0:T(8,128)(2,1)S(1)}, u32[]{:S(2)}, u32[]{:S(2)}) collective-permute-start(bf16[32,128]{1,0:T(8,128)(2,1)S(1)} %get-tuple-element.30), channel_id=1, source_target_pairs={{0,1},{1,0},{2,3},{3,2},{4,5},{5,4},{6,7},{7,6},{8,9},{9,8},{10,11... | collective-permute-start | bytes 24584 | tf_op jit(solution)/shard_map/ppermute | solution.py:35
  6.5 5.8 %collective-permute-start.2 = (bf16[48,128]{1,0:T(8,128)(2,1)S(1)}, bf16[48,128]{1,0:T(8,128)(2,1)S(1)}, u32[]{:S(2)}, u32[]{:S(2)}) collective-permute-start(bf16[48,128]{1,0:T(8,128)(2,1)S(1)} %get-tuple-element.60), channel_id=1, source_target_pairs={{0,6},{2,4},{4,2},{6,0},{1,7},{3,5},{5,3},{7,1},{8,14},{10,12},{12... | collective-permute-start | bytes 36872 | tf_op jit(solution)/shard_map/ppermute | solution.py:35
  10.6 3.7 %collective-permute-start.1 = (bf16[48,128]{1,0:T(8,128)(2,1)S(1)}, bf16[48,128]{1,0:T(8,128)(2,1)S(1)}, u32[]{:S(2)}, u32[]{:S(2)}) collective-permute-start(bf16[48,128]{1,0:T(8,128)(2,1)S(1)} %get-tuple-element.61), channel_id=1, source_target_pairs={{0,2},{2,0},{4,6},{6,4},{1,3},{3,1},{5,7},{7,5},{8,10},{10,8},{12,... | collective-permute-start | bytes 36872 | tf_op jit(solution)/shard_map/ppermute | solution.py:35
  10.7 3.6 %copy-start.1 = (bf16[4,4,64,128]{3,2,1,0:T(8,128)(2,1)S(1)}, bf16[4,4,64,128]{3,2,1,0:T(8,128)(2,1)}, u32[]{:S(2)}) copy-start(bf16[4,4,64,128]{3,2,1,0:T(8,128)(2,1)} %cells.5) | copy-start | bytes 786436
  10.7 5.4 %copy-start.2 = (bf16[32,2,32,64]{3,2,1,0:T(8,128)(2,1)S(1)}, bf16[32,2,32,64]{3,2,1,0:T(8,128)(2,1)}, u32[]{:S(2)}) copy-start(bf16[32,2,32,64]{3,2,1,0:T(8,128)(2,1)} %cot.1) | copy-start | bytes 786436
  14.4 2.7 %collective-permute-start.3 = (bf16[288,128]{1,0:T(8,128)(2,1)S(1)}, bf16[288,128]{1,0:T(8,128)(2,1)S(1)}, u32[]{:S(2)}, u32[]{:S(2)}) collective-permute-start(bf16[288,128]{1,0:T(8,128)(2,1)S(1)} %get-tuple-element.33), channel_id=1, source_target_pairs={{0,8},{8,0},{16,24},{24,16},{1,9},{9,1},{17,25},{25,17},{2,10},{10... | collective-permute-start | bytes 221192 | tf_op jit(solution)/shard_map/ppermute | solution.py:35
  14.4 4.1 %collective-permute-start.4 = (bf16[288,128]{1,0:T(8,128)(2,1)S(1)}, bf16[288,128]{1,0:T(8,128)(2,1)S(1)}, u32[]{:S(2)}, u32[]{:S(2)}) collective-permute-start(bf16[288,128]{1,0:T(8,128)(2,1)S(1)} %get-tuple-element.34), channel_id=1, source_target_pairs={{0,24},{8,16},{16,8},{24,0},{1,25},{9,17},{17,9},{25,1},{2,26},{10... | collective-permute-start | bytes 221192 | tf_op jit(solution)/shard_map/ppermute | solution.py:35
  25.4 6.1 %collective-permute-start.5 = (bf16[416,128]{1,0:T(8,128)(2,1)S(1)}, bf16[416,128]{1,0:T(8,128)(2,1)S(1)}, u32[]{:S(2)}, u32[]{:S(2)}) collective-permute-start(bf16[416,128]{1,0:T(8,128)(2,1)S(1)} %get-tuple-element.40), channel_id=1, source_target_pairs={{0,8},{8,0},{16,24},{24,16},{1,9},{9,1},{17,25},{25,17},{2,10},{10... | collective-permute-start | bytes 319496 | tf_op jit(solution)/shard_map/ppermute | solution.py:35
  25.9 5.6 %collective-permute-start.6 = (bf16[416,128]{1,0:T(8,128)(2,1)S(1)}, bf16[416,128]{1,0:T(8,128)(2,1)S(1)}, u32[]{:S(2)}, u32[]{:S(2)}) collective-permute-start(bf16[416,128]{1,0:T(8,128)(2,1)S(1)} %get-tuple-element.41), channel_id=1, source_target_pairs={{0,24},{8,16},{16,8},{24,0},{1,25},{9,17},{17,9},{25,1},{2,26},{10... | collective-permute-start | bytes 319496 | tf_op jit(solution)/shard_map/ppermute | solution.py:35
  27.1 4.4 %collective-permute-start.7 = (bf16[64,128]{1,0:T(8,128)(2,1)S(1)}, bf16[64,128]{1,0:T(8,128)(2,1)S(1)}, u32[]{:S(2)}, u32[]{:S(2)}) collective-permute-start(bf16[64,128]{1,0:T(8,128)(2,1)S(1)} %get-tuple-element.43.wframe), channel_id=1, source_target_pairs={{0,16},{8,24},{16,0},{24,8},{1,17},{9,25},{17,1},{25,9},{2,18},{10... | collective-permute-start | bytes 49160 | tf_op jit(solution)/shard_map/ppermute | solution.py:35
  31.6 6.5 %collective-permute-start.9 = (bf16[96,128]{1,0:T(8,128)(2,1)S(1)}, bf16[96,128]{1,0:T(8,128)(2,1)S(1)}, u32[]{:S(2)}, u32[]{:S(2)}) collective-permute-start(bf16[96,128]{1,0:T(8,128)(2,1)S(1)} %get-tuple-element.49), channel_id=1, source_target_pairs={{0,6},{2,4},{4,2},{6,0},{1,7},{3,5},{5,3},{7,1},{8,14},{10,12},{12... | collective-permute-start | bytes 73736 | tf_op jit(solution)/shard_map/ppermute | solution.py:35
  33.5 4.7 %collective-permute-start.8 = (bf16[96,128]{1,0:T(8,128)(2,1)S(1)}, bf16[96,128]{1,0:T(8,128)(2,1)S(1)}, u32[]{:S(2)}, u32[]{:S(2)}) collective-permute-start(bf16[96,128]{1,0:T(8,128)(2,1)S(1)} %get-tuple-element.48), channel_id=1, source_target_pairs={{0,2},{2,0},{4,6},{6,4},{1,3},{3,1},{5,7},{7,5},{8,10},{10,8},{12,... | collective-permute-start | bytes 73736 | tf_op jit(solution)/shard_map/ppermute | solution.py:35
  33.5 4.6 %collective-permute-start.10 = (bf16[64,128]{1,0:T(8,128)(2,1)S(1)}, bf16[64,128]{1,0:T(8,128)(2,1)S(1)}, u32[]{:S(2)}, u32[]{:S(2)}) collective-permute-start(bf16[64,128]{1,0:T(8,128)(2,1)S(1)} %slice.3), channel_id=1, source_target_pairs={{0,4},{2,6},{4,0},{6,2},{1,5},{3,7},{5,1},{7,3},{8,12},{10,14},{12... | collective-permute-start | bytes 49160 | tf_op jit(solution)/shard_map/ppermute | solution.py:35
  38.2 4.0 %collective-permute-start.11 = (bf16[144,128]{1,0:T(8,128)(2,1)S(1)}, bf16[144,128]{1,0:T(8,128)(2,1)S(1)}, u32[]{:S(2)}, u32[]{:S(2)}) collective-permute-start(bf16[144,128]{1,0:T(8,128)(2,1)S(1)} %get-tuple-element.52), channel_id=1, source_target_pairs={{0,1},{1,0},{2,3},{3,2},{4,5},{5,4},{6,7},{7,6},{8,9},{9,8},{10,11... | collective-permute-start | bytes 110600 | tf_op jit(solution)/shard_map/ppermute | solution.py:35

commit v5 on v4

--- a/solution.py
+++ b/solution.py
@@ -135,7 +135,7 @@
 def main_kernel(
     cells, got_0, got_1, rows_in, left_in, right_in, spread, wbig, wback,
     sums, field, sent_0, sent_1, wpart, wframe, rows_out, cols,
-    stage, patches, left, right, outer, carry, gram,
+    stage, patches, left, right, carry, gram, deltas,
 ):
     chan, count_x, count_y, _ = cells.shape
     pool_x, pool_y = count_x // 2, count_y // 2
@@ -182,76 +182,87 @@
 
     carry[...] = jnp.zeros_like(carry)
     gram[...] = jnp.zeros_like(gram)
+    cols[...] = jnp.zeros_like(cols)
     pairs = 4
+    steps = count_y // (2 * pairs)
+    size = 3 * wide
+    inside, outside = lane != lanes - 1, lane != 0
 
     def finish(y, whole):
-        before = pltpu.roll(whole[0:wide], lanes - 1, 1)
-        after = pltpu.roll(whole[2 * wide : 3 * wide], 1, 1)
-        zero = jnp.zeros_like(before)
+        first, last = whole[0:wide], whole[2 * wide : 3 * wide]
         inner = (
             whole[wide : 2 * wide]
-            + jnp.where(lane == lanes - 1, zero, before)
-            + jnp.where(lane == 0, zero, after)
+            + jnp.where(inside, pltpu.roll(first, lanes - 1, 1), 0.0)
+            + jnp.where(outside, pltpu.roll(last, 1, 1), 0.0)
         )
-        rest = jnp.where(lane == lanes - 1, before, jnp.where(lane == 0, after, zero))
-        place = pl.ds(pl.multiple_of(y * wide, 8), wide)
-        field[place, :] = inner
-        outer[place, :] = rest
+        field[pl.ds(pl.multiple_of(y * wide, 8), wide), :] = inner
+        here = lane == y
+        cols[0:wide, :] = jnp.where(here, pltpu.roll(first, y, 1), cols[0:wide, :])
+        cols[wide : 2 * wide, :] = jnp.where(
+            here, pltpu.roll(last, y + 1, 1), cols[wide : 2 * wide, :]
+        )
+
+    def block_of(j):
+        return jnp.concatenate(
+            [
+                patches[pl.ds(pl.multiple_of((2 * j + h) * depth, 16), 3 * depth), :]
+                for h in range(2)
+            ],
+            axis=1,
+        )
+
+    def forward(i, k):
+        j = i * pairs + k
+        preact = dot(wbig[...], block_of(j))
+        slope = jnp.tanh(5.0 * preact)
+        linear = jnp.maximum(preact, 0.3 * preact)
+        factor = 1.0 + jnp.abs(slope)
+        here = spread[pl.ds(pl.multiple_of(j * pool_x * chan_out, 8), pool_x * chan_out), :]
+        slope = 0.65 + 0.35 * slope
+        delta = []
+        for x in range(pool_x):
+            top, mid = 2 * x * chan_out, (2 * x + 1) * chan_out
+            end = mid + chan_out
+            times = here[x * chan_out : (x + 1) * chan_out]
+            times = jnp.concatenate([times, times], axis=1)
+            delta.append((slope[top:mid] * times).astype(bf16))
+            delta.append((slope[mid:end] * times).astype(bf16))
+            total = linear[top:mid] + linear[mid:end]
+            total = total[:, :lanes] + total[:, lanes:]
+            prod = factor[top:mid] * factor[mid:end]
+            prod = prod[:, :lanes] * prod[:, lanes:]
+            total = total - log_scale * jnp.log(prod)
+            sums[pl.ds(x * pool_y + j, chan_out, stride=pool_x * pool_y), :] = total
+        slot = lax.rem(i, 2)
+        deltas[slot, :, 2 * k * lanes : 2 * (k + 1) * lanes] = jnp.concatenate(delta, axis=0)
+
+    def backward(i, k):
+        j = i * pairs + k
+        parts = dot(wback[...], deltas[lax.rem(i, 2), :, 2 * k * lanes : 2 * (k + 1) * lanes])
+        part = lambda b, h: parts[b * size : (b + 1) * size, h * lanes : (h + 1) * lanes]
+        finish(2 * j, carry[0:size, :] + part(0, 0))
+        finish(2 * j + 1, carry[size : 2 * size, :] + part(1, 0) + part(0, 1))
+        carry[0:size, :] = part(2, 0) + part(1, 1)
+        carry[size : 2 * size, :] = part(2, 1)
+
+    def weigh(i):
+        blocks = jnp.concatenate([block_of(i * pairs + k) for k in range(pairs)], axis=1)
+        gram[...] += dot(deltas[lax.rem(i, 2)], blocks, ((1,), (1,)))
 
     def step(i, _):
-        deltas, blocks = [], []
-        weights = wbig[...]
+        weigh(i - 1)
         for k in range(pairs):
-            j = i * pairs + k
-            block = jnp.concatenate(
-                [
-                    patches[pl.ds(pl.multiple_of((2 * j + h) * depth, 16), 3 * depth), :]
-                    for h in range(2)
-                ],
-                axis=1,
-            )
-            preact = dot(weights, block)
-            slope = jnp.tanh(5.0 * preact)
-            linear = jnp.maximum(preact, 0.3 * preact)
-            factor = 1.0 + jnp.abs(slope)
-            here = spread[pl.ds(pl.multiple_of(j * pool_x * chan_out, 8), pool_x * chan_out), :]
-            slope = 0.65 + 0.35 * slope
-            delta = []
-            for x in range(pool_x):
-                top, mid = 2 * x * chan_out, (2 * x + 1) * chan_out
-                end = mid + chan_out
-                times = here[x * chan_out : (x + 1) * chan_out]
-                times = jnp.concatenate([times, times], axis=1)
-                delta.append((slope[top:mid] * times).astype(bf16))
-                delta.append((slope[mid:end] * times).astype(bf16))
-                total = linear[top:mid] + linear[mid:end]
-                total = total[:, :lanes] + total[:, lanes:]
-                prod = factor[top:mid] * factor[mid:end]
-                prod = prod[:, :lanes] * prod[:, lanes:]
-                total = total - log_scale * jnp.log(prod)
-                sums[pl.ds(x * pool_y + j, chan_out, stride=pool_x * pool_y), :] = total
-            deltas.append(jnp.concatenate(delta, axis=0))
-            blocks.append(block)
-        gram[...] += dot(
-            jnp.concatenate(deltas, axis=1), jnp.concatenate(blocks, axis=1), ((1,), (1,))
-        )
-        back = wback[...]
-        size = 3 * wide
-        carry_a, carry_b = carry[0:size, :], carry[size : 2 * size, :]
-        for k in range(pairs):
-            j = i * pairs + k
-            parts = dot(back, deltas[k])
-            part = lambda b, h: parts[b * size : (b + 1) * size, h * lanes : (h + 1) * lanes]
-            finish(2 * j, carry_a + part(0, 0))
-            finish(2 * j + 1, carry_b + part(1, 0) + part(0, 1))
-            carry_a = part(2, 0) + part(1, 1)
-            carry_b = part(2, 1)
-        carry[0:size, :] = carry_a
-        carry[size : 2 * size, :] = carry_b
+            forward(i, k)
+            backward(i - 1, k)
         return 0
 
-    lax.fori_loop(0, count_y // (2 * pairs), step, 0)
-    size = 3 * wide
+    for k in range(pairs):
+        forward(jnp.int32(0), k)
+    lax.fori_loop(1, steps, step, 0)
+    last_step = jnp.int32(steps - 1)
+    weigh(last_step)
+    for k in range(pairs):
+        backward(last_step, k)
     finish(count_y, carry[0:size, :])
     finish(count_y + 1, carry[size : 2 * size, :])
 
@@ -280,15 +291,7 @@
     ends = [field[0:wide, :], field[(count_y + 1) * wide : (count_y + 2) * wide, :]]
     rows_out[...] = jnp.concatenate([end[chan : chan + own] for end in ends], axis=0)
     tall = cols.shape[0]
-    outer[(count_y + 2) * wide :, :] = jnp.zeros((outer.shape[0] - (count_y + 2) * wide, lanes), f32)
-    planes = [outer[pl.ds(r, tall, stride=wide), :].astype(bf16) for r in range(wide)]
-    row = iota((wide * lanes, lanes), 0)
-    spot = iota((wide * lanes, lanes), 1)
-    want = jnp.where(spot < wide, spot * lanes + lanes - 1, (spot - wide) * lanes)
-    chosen = ((row == want) & (spot < 2 * wide)).astype(f32).astype(bf16)
-    found = dot(jnp.concatenate(planes, axis=1), chosen)
-    cols[...] = found
-    found = found.astype(bf16)
+    found = cols[...].astype(bf16)
     zero = jnp.zeros((8, lanes), f32)
     for ref, odd in ((sent_0, 0), (sent_1, 1)):
         high = even != (odd == 1)
@@ -323,29 +326,27 @@
         total = total + (joined(sides[0]) + joined(sides[1]))
     wsum[...] = total
     sides = jnp.concatenate(split(total), axis=0)
-    spot = iota((tall, lanes), 1)
-    found = cols[...]
     one = got_0[body : body + 16 + tall, :].astype(f32)
     two = got_1[body : body + 16 + tall, :].astype(f32)
     from_low, from_high = pick("gx", two, one), pick("gx", one, two)
-    for part, turn, start in ((from_low, lanes - own, chan), (from_high, own, own)):
-        part = pltpu.roll(part[16:], turn, 1)
-        near = (spot >= start) & (spot < start + chan)
-        near = near | ((spot >= wide + start) & (spot < wide + start + chan))
-        found = found + jnp.where(near, part, 0.0)
+    mid = jnp.zeros((own - 2 * chan, lanes), f32)
+    found = []
+    for top in (0, wide):
+        more = [from_low[16 + top + chan + own : 16 + top + wide], mid]
+        more.append(from_high[16 + top : 16 + top + chan])
+        found.append(cols[top + chan : top + chan + own, :] + jnp.concatenate(more, axis=0))
+    found = jnp.concatenate(found, axis=0)
     cols_out[...] = found
-    count_y = body // chan
-    mid = jnp.zeros((own - 2 * chan, lanes), f32)
     both = []
-    for at, line in ((0, 0), (1, count_y + 1)):
+    for at in (0, 1):
         more = [from_low[at * chan : (at + 1) * chan], mid, from_high[at * chan : (at + 1) * chan]]
         total = rows[at * own : (at + 1) * own, :] + jnp.concatenate(more, axis=0)
-        extra = jnp.broadcast_to(found[line : line + 1], (16, lanes))
-        both.append(jnp.concatenate([total, extra], axis=0))
-    sent_0[0 : own + 16, :] = pick("gy", both[1], both[0]).astype(bf16)
-    sent_1[0 : own + 16, :] = pick("gy", both[0], both[1]).astype(bf16)
+        both.append(total)
+    sent_0[0:own, :] = pick("gy", both[1], both[0]).astype(bf16)
+    sent_1[0:own, :] = pick("gy", both[0], both[1]).astype(bf16)
     for ref in (sent_0, sent_1):
-        ref[own + 16 :, :] = sides
+        ref[own : 3 * own, :] = found.astype(bf16)
+        ref[3 * own :, :] = sides
 
 
 def y_kernel(alone, count_y, wsum, cols, got_0, got_1, far, wout, frame, rows):
@@ -354,7 +355,7 @@
     top = got_0.shape[0] - 2 * chan_out
     one, two = got_0[0:top, :].astype(f32), got_1[0:top, :].astype(f32)
     above, below = pick("gy", two, one), pick("gy", one, two)
-    rows[...] = jnp.concatenate([above[0 : top - 16], below[0 : top - 16]], axis=0)
+    rows[...] = jnp.concatenate([above[: top - tall], below[: top - tall]], axis=0)
     if alone:
         total = joined(jnp.concatenate(split(wsum[...]), axis=0))
     else:
@@ -362,10 +363,11 @@
         total = total + (joined(got_0[top:, :]) + joined(got_1[top:, :]))
     wout[...] = total
     frame[tall:, :] = jnp.concatenate(split(total), axis=0)
-    row = iota((tall, lanes), 0)
+    spot = iota((tall, lanes), 1)
+    above = pltpu.roll(above[top - tall :], lanes - count_y, 1)
+    below = pltpu.roll(below[top - tall :], count_y, 1)
     found = cols[...]
-    found = found + jnp.where(row == 1, above[top - 16 : top - 15], 0.0)
-    found = found + jnp.where(row == count_y, below[top - 16 : top - 15], 0.0)
+    found = found + jnp.where(spot == 1, above, jnp.where(spot == count_y, below, 0.0))
     frame[0:tall, :] = found.astype(bf16)
 
 
@@ -390,7 +392,9 @@
     wide = own + 2 * chan
     tall = frame.shape[0] - 2 * chan_out
     total = joined(jnp.concatenate(split(wsum[...]), axis=0)) + joined(frame[tall:, :])
-    total = jnp.concatenate([total, jnp.zeros((lanes - chan_out, lanes), f32)], axis=0)
+    columns = pltpu.roll(frame[0:tall, :].astype(f32), lanes - 1, 1)
+    rest = jnp.zeros((lanes - chan_out - tall, lanes), f32)
+    total = jnp.concatenate([total, columns, rest], axis=0)
     total = total.T
     for a in range(3):
         for be in range(9):
@@ -399,14 +403,14 @@
     bout[...] = total[27 * chan : 27 * chan + 1, :chan_out]
     spot = iota((count_y, lanes), 1)
     row = iota((count_y, lanes), 0)
-    cols = frame[0:tall, :].astype(f32)[1 : count_y + 1]
+    columns = total[0:count_y]
     first, final = rows[0:own, :], rows[own : 2 * own, :]
     for x in range(count_x):
         for c in range(chan):
             at = x * chan + c
-            r = chan + at
-            more = jnp.where(spot == lanes - 1, cols[:, r : r + 1], 0.0)
-            more = jnp.where(spot == 0, cols[:, wide + r : wide + r + 1], more)
+            r = chan_out + at
+            more = jnp.where(spot == lanes - 1, columns[:, r : r + 1], 0.0)
+            more = jnp.where(spot == 0, columns[:, own + r : own + r + 1], more)
             more = more + jnp.where(row == 0, first[at : at + 1], 0.0)
             more = more + jnp.where(row == count_y - 1, final[at : at + 1], 0.0)
             out[c, x] = grad[c, x] + more
@@ -465,7 +469,7 @@
     )(cells, edges, row_0, row_1)
     face_1, face_0 = swapped(face_1, "gx", 1), swapped(face_0, "gx", 0)
 
-    tall = 80
+    tall = 2 * wide
     bundle = shape((body + 16 + tall + 2 * chan_out, lanes), bf16)
     sums, field, face_0, face_1, wpart, wframe, rows, cols = call(
         main_kernel,
@@ -484,9 +488,9 @@
             pltpu.VMEM(((count_y + 2) * depth, lanes), bf16),
             pltpu.VMEM((wide, lanes), f32),
             pltpu.VMEM((wide, lanes), f32),
-            pltpu.VMEM((tall * wide, lanes), f32),
             pltpu.VMEM((6 * wide, lanes), f32),
             pltpu.VMEM((count_x * chan_out, 3 * depth), f32),
+            pltpu.VMEM((2, count_x * chan_out, 8 * lanes), bf16),
         ],
     )(cells, face_0, face_1, rows, left, right, spread, wbig, wback)
 
@@ -498,22 +502,22 @@
         far = swapped(wframe, "gx", 2)
     face_1, face_0 = swapped(face_1, "gx", 1), swapped(face_0, "gx", 0)
     pooled = call(pool_kernel, shape(cotangent.shape, bf16))(sums)
-    rows_out = shape((own + 16 + 2 * chan_out, lanes), bf16)
+    rows_out = shape((3 * own + 2 * chan_out, lanes), bf16)
     wsum, row_0, row_1, cols = call(
         functools.partial(x_kernel, alone_x),
-        [shape((chan_out, lanes), f32), rows_out, rows_out, shape((tall, lanes), f32)],
+        [shape((chan_out, lanes), f32), rows_out, rows_out, shape((2 * own, lanes), f32)],
     )(wpart, wframe, rows, cols, face_0, face_1, far)
     grad = call(grad_kernel, shape(cells.shape, f32))(field, face_0, face_1)
     if alone_y:
         far, wsum = wframe, lax.psum(wsum, "gy")
     else:
-        far = swapped(row_0[own + 16 :], "gy", 2)
+        far = swapped(row_0[3 * own :], "gy", 2)
     row_1, row_0 = swapped(row_1, "gy", 1), swapped(row_0, "gy", 0)
     wsum, frame, rows = call(
         functools.partial(y_kernel, alone_y, count_y),
         [
             shape((chan_out, lanes), f32),
-            shape((tall + 2 * chan_out, lanes), bf16),
+            shape((2 * own + 2 * chan_out, lanes), bf16),
             shape((2 * own, lanes), f32),
         ],
     )(wsum, cols, row_0, row_1, far)

time: 43.5 us -> 45.2 us (1.039)
  Pallas kernels: 10.8 us -> 12.9 us
    pallas_call x1, Pallas kernels: 6.94 us -> 8.86 us  [on_device(): call(main_kernel, [pooled_rows, shape(((count_y + 2) * wide, lanes), f32)...]
where the time goes in v5:
time: 45.2 us; the launch traced here: 45 us
  starting transfers between devices  17 us (38%)
  Pallas kernels  12.9 us (29%)
  waiting for transfers between devices  12.6 us (28%)
  local copies, waits for them, and re-layouts  1.63 us (4%)
  between operations  0.77 us (2%)
    ppermute x12, starting transfers between devices, swapped(): return lax.ppermute(array, axis, pairs)  17 us
    ppermute x12, waiting for transfers between devices, swapped(): return lax.ppermute(array, axis, pairs)  12.6 us
    pallas_call x1, Pallas kernels, on_device(): call(main_kernel, [pooled_rows, shape(((count_y + 2) * wide, lanes), f32)...  8.86 us
    pallas_call x1, Pallas kernels, on_device(): call(final_kernel, [shape(cells.shape, f32), shape((27, chan, chan_out),...  1.31 us
    pallas_call x1, Pallas kernels, on_device(): pooled = call(pool_kernel, shape(cotangent.shape, bf16))(sums)  1.24 us
    unnamed x10, local copies, waits for them, and re-layouts  0.97 us
  transfers between devices with their start and end apart: 12, of which 7 were waited for; matrix products, arithmetic and copies ran while one was open for 2% of the time, Pallas kernels for 5%

profile of v5, /device:TPU:0, one launch (start us, length us, event | category | flops | bytes accessed | tf_op | source)
XLA Modules:
  0.0 45.0 jit_solution(13133003170364153963)
XLA Ops:
  0.6 0.9 %copy-done = bf16[4,4,64,128]{3,2,1,0:T(8,128)(2,1)S(1)} copy-done((bf16[4,4,64,128]{3,2,1,0:T(8,128)(2,1)S(1)}, bf16[4,4,64,128]{3,2,1,0:T(8,128)(2,1)}, u32[]{:S(2)}) %copy-start) | copy-done | bytes 262168
  1.6 0.3 shard_map.75
  1.9 3.0 %collective-permute-start = (bf16[32,128]{1,0:T(8,128)(2,1)S(1)}, bf16[32,128]{1,0:T(8,128)(2,1)S(1)}, u32[]{:S(2)}, u32[]{:S(2)}) collective-permute-start(bf16[32,128]{1,0:T(8,128)(2,1)S(1)} %get-tuple-element.30), channel_id=1, source_target_pairs={{0,1},{1,0},{2,3},{3,2},{4,5},{5,4},{6,7},{7,6},{8,9},{9,8},{10,11... | collective-permute-start | bytes 24584 | tf_op jit(solution)/shard_map/ppermute | solution.py:35
  4.9 0.2 pad_maximum_fusion
  5.2 1.3 %collective-permute-done.edges = bf16[32,128]{1,0:T(8,128)(2,1)S(1)} collective-permute-done((bf16[32,128]{1,0:T(8,128)(2,1)S(1)}, bf16[32,128]{1,0:T(8,128)(2,1)S(1)}, u32[]{:S(2)}, u32[]{:S(2)}) %collective-permute-start) | collective-permute-done | bytes 8224 | tf_op jit(solution)/shard_map/ppermute | solution.py:35
  6.5 4.1 %collective-permute-start.2 = (bf16[48,128]{1,0:T(8,128)(2,1)S(1)}, bf16[48,128]{1,0:T(8,128)(2,1)S(1)}, u32[]{:S(2)}, u32[]{:S(2)}) collective-permute-start(bf16[48,128]{1,0:T(8,128)(2,1)S(1)} %get-tuple-element.60), channel_id=1, source_target_pairs={{0,6},{2,4},{4,2},{6,0},{1,7},{3,5},{5,3},{7,1},{8,14},{10,12},{12... | collective-permute-start | bytes 36872 | tf_op jit(solution)/shard_map/ppermute | solution.py:35
  10.7 0.2 reshape_reshape.3
  11.1 1.1 %collective-permute-done.2.got_1 = bf16[48,128]{1,0:T(8,128)(2,1)S(1)} collective-permute-done((bf16[48,128]{1,0:T(8,128)(2,1)S(1)}, bf16[48,128]{1,0:T(8,128)(2,1)S(1)}, u32[]{:S(2)}, u32[]{:S(2)}) %collective-permute-start.2) | collective-permute-done | bytes 12320 | tf_op jit(solution)/shard_map/ppermute | solution.py:35
  12.3 2.0 %collective-permute-done.1.got_0 = bf16[48,128]{1,0:T(8,128)(2,1)S(1)} collective-permute-done((bf16[48,128]{1,0:T(8,128)(2,1)S(1)}, bf16[48,128]{1,0:T(8,128)(2,1)S(1)}, u32[]{:S(2)}, u32[]{:S(2)}) %collective-permute-start.1) | collective-permute-done | bytes 12320 | tf_op jit(solution)/shard_map/ppermute | solution.py:35
  14.4 1.6 %collective-permute-start.4 = (bf16[288,128]{1,0:T(8,128)(2,1)S(1)}, bf16[288,128]{1,0:T(8,128)(2,1)S(1)}, u32[]{:S(2)}, u32[]{:S(2)}) collective-permute-start(bf16[288,128]{1,0:T(8,128)(2,1)S(1)} %get-tuple-element.34), channel_id=1, source_target_pairs={{0,24},{8,16},{16,8},{24,0},{1,25},{9,17},{17,9},{25,1},{2,26},{10... | collective-permute-start | bytes 221192 | tf_op jit(solution)/shard_map/ppermute | solution.py:35
  16.1 0.9 %shard_map.77.spread = f32[2048,128]{1,0:T(8,128)S(1)} custom-call(bf16[32,2,32,64]{3,2,1,0:T(8,128)(2,1)S(1)} %copy-done.2), custom_call_target="tpu_custom_call" | custom-call | tf_op jit(solution)/shard_map/pallas_call | solution.py:460
  17.0 1.4 %collective-permute-done.4.got_1 = bf16[288,128]{1,0:T(8,128)(2,1)S(1)} collective-permute-done((bf16[288,128]{1,0:T(8,128)(2,1)S(1)}, bf16[288,128]{1,0:T(8,128)(2,1)S(1)}, u32[]{:S(2)}, u32[]{:S(2)}) %collective-permute-start.4) | collective-permute-done | bytes 73760 | tf_op jit(solution)/shard_map/ppermute | solution.py:35
  18.5 8.9 %shard_map.78 = (f32[2048,128]{1,0:T(8,128)S(1)}, f32[1584,128]{1,0:T(8,128)S(1)}, bf16[384,128]{1,0:T(8,128)(2,1)S(1)}, bf16[384,128]{1,0:T(8,128)(2,1)S(1)}, f...) custom-call(bf16[4,4,64,128]{3,2,1,0:T(8,128)(2,1)S(1)} %copy-done.1, ...), custom_call_target="tpu_custom_call" | custom-call | tf_op jit(solution)/shard_map/pallas_call | solution.py:474
  27.3 0.5 %collective-permute-start.5 = (bf16[384,128]{1,0:T(8,128)(2,1)S(1)}, bf16[384,128]{1,0:T(8,128)(2,1)S(1)}, u32[]{:S(2)}, u32[]{:S(2)}) collective-permute-start(bf16[384,128]{1,0:T(8,128)(2,1)S(1)} %get-tuple-element.40), channel_id=1, source_target_pairs={{0,8},{8,0},{16,24},{24,16},{1,9},{9,1},{17,25},{25,17},{2,10},{10... | collective-permute-start | bytes 294920 | tf_op jit(solution)/shard_map/ppermute | solution.py:35
  27.8 1.2 %collective-permute-start.6 = (bf16[384,128]{1,0:T(8,128)(2,1)S(1)}, bf16[384,128]{1,0:T(8,128)(2,1)S(1)}, u32[]{:S(2)}, u32[]{:S(2)}) collective-permute-start(bf16[384,128]{1,0:T(8,128)(2,1)S(1)} %get-tuple-element.41), channel_id=1, source_target_pairs={{0,24},{8,16},{16,8},{24,0},{1,25},{9,17},{17,9},{25,1},{2,26},{10... | collective-permute-start | bytes 294920 | tf_op jit(solution)/shard_map/ppermute | solution.py:35
  29.0 0.6 %collective-permute-start.7 = (bf16[64,128]{1,0:T(8,128)(2,1)S(1)}, bf16[64,128]{1,0:T(8,128)(2,1)S(1)}, u32[]{:S(2)}, u32[]{:S(2)}) collective-permute-start(bf16[64,128]{1,0:T(8,128)(2,1)S(1)} %get-tuple-element.43.wframe), channel_id=1, source_target_pairs={{0,16},{8,24},{16,0},{24,8},{1,17},{9,25},{17,1},{25,9},{2,18},{10... | collective-permute-start | bytes 49160 | tf_op jit(solution)/shard_map/ppermute | solution.py:35
  29.6 3.7 %collective-permute-done.7.far = bf16[64,128]{1,0:T(8,128)(2,1)S(1)} collective-permute-done((bf16[64,128]{1,0:T(8,128)(2,1)S(1)}, bf16[64,128]{1,0:T(8,128)(2,1)S(1)}, u32[]{:S(2)}, u32[]{:S(2)}) %collective-permute-start.7) | collective-permute-done | bytes 16416 | tf_op jit(solution)/shard_map/ppermute | solution.py:35
  33.3 1.9 %collective-permute-start.9 = (bf16[112,128]{1,0:T(8,128)(2,1)S(1)}, bf16[112,128]{1,0:T(8,128)(2,1)S(1)}, u32[]{:S(2)}, u32[]{:S(2)}) collective-permute-start(bf16[112,128]{1,0:T(8,128)(2,1)S(1)} %get-tuple-element.49), channel_id=1, source_target_pairs={{0,6},{2,4},{4,2},{6,0},{1,7},{3,5},{5,3},{7,1},{8,14},{10,12},{12... | collective-permute-start | bytes 86024 | tf_op jit(solution)/shard_map/ppermute | solution.py:35
  35.1 2.6 %collective-permute-start.10 = (bf16[64,128]{1,0:T(8,128)(2,1)S(1)}, bf16[64,128]{1,0:T(8,128)(2,1)S(1)}, u32[]{:S(2)}, u32[]{:S(2)}) collective-permute-start(bf16[64,128]{1,0:T(8,128)(2,1)S(1)} %slice.3), channel_id=1, source_target_pairs={{0,4},{2,6},{4,0},{6,2},{1,5},{3,7},{5,1},{7,3},{8,12},{10,14},{12... | collective-permute-start | bytes 49160 | tf_op jit(solution)/shard_map/ppermute | solution.py:35
  37.7 2.1 %collective-permute-done.10.far = bf16[64,128]{1,0:T(8,128)(2,1)S(1)} collective-permute-done((bf16[64,128]{1,0:T(8,128)(2,1)S(1)}, bf16[64,128]{1,0:T(8,128)(2,1)S(1)}, u32[]{:S(2)}, u32[]{:S(2)}) %collective-permute-start.10) | collective-permute-done | bytes 16416 | tf_op jit(solution)/shard_map/ppermute | solution.py:35
  39.9 1.5 %collective-permute-start.11 = (bf16[96,128]{1,0:T(8,128)(2,1)S(1)}, bf16[96,128]{1,0:T(8,128)(2,1)S(1)}, u32[]{:S(2)}, u32[]{:S(2)}) collective-permute-start(bf16[96,128]{1,0:T(8,128)(2,1)S(1)} %get-tuple-element.52), channel_id=1, source_target_pairs={{0,1},{1,0},{2,3},{3,2},{4,5},{5,4},{6,7},{7,6},{8,9},{9,8},{10,11... | collective-permute-start | bytes 73736 | tf_op jit(solution)/shard_map/ppermute | solution.py:35
  41.4 1.2 %shard_map.79 = bf16[32,2,32,64]{3,2,1,0:T(8,128)(2,1)} custom-call(f32[2048,128]{1,0:T(8,128)S(1)} %get-tuple-element.38.sums), custom_call_target="tpu_custom_call" | custom-call | tf_op jit(solution)/shard_map/pallas_call | solution.py:504
  42.8 0.9 %collective-permute-done.11.frame = bf16[96,128]{1,0:T(8,128)(2,1)S(1)} collective-permute-done((bf16[96,128]{1,0:T(8,128)(2,1)S(1)}, bf16[96,128]{1,0:T(8,128)(2,1)S(1)}, u32[]{:S(2)}, u32[]{:S(2)}) %collective-permute-start.11) | collective-permute-done | bytes 24608 | tf_op jit(solution)/shard_map/ppermute | solution.py:35
  43.7 1.3 %shard_map.83 = (f32[4,4,64,128]{3,2,1,0:T(8,128)}, f32[27,4,32]{2,1,0:T(4,128)}, f32[1,32]{1,0:T(1,128)}) custom-call(f32[4,4,64,128]{3,2,1,0:T(8,128)S(1)} %shard_map.80.grad, f32[32,128]{1,0:T(8,128)S(1)} %get-tuple-element.50.wsum, f32[32,128]{1,0:T(8,128)S(1)} %get-tuple-element.51.rows, bf16[96,128]{1,0:T(8,128)(2,1)S(1)} %collective-permute-done.11.frame), custom_call_target="tpu_custom_call" | custom-call | tf_op jit(solution)/shard_map/pallas_call | solution.py:525
  (32 shorter events, 0.9 us)
Async XLA Ops:
  0.6 1.0 %copy-start = (bf16[4,4,64,128]{3,2,1,0:T(8,128)(2,1)S(1)}, bf16[4,4,64,128]{3,2,1,0:T(8,128)(2,1)}, u32[]{:S(2)}) copy-start(bf16[4,4,64,128]{3,2,1,0:T(8,128)(2,1)} %cells.5) | copy-start | bytes 786436
  1.6 3.3 %copy-start.3 = (bf16[32,4,3,3,3]{0,1,4,3,2:T(4,128)(2,1)S(1)}, bf16[32,4,3,3,3]{0,1,4,3,2:T(4,128)(2,1)}, u32[]{:S(2)}) copy-start(bf16[32,4,3,3,3]{0,1,4,3,2:T(4,128)(2,1)} %param.5) | copy-start | bytes 20740
  1.9 3.0 %copy-start.4 = (f32[32]{0:T(128)S(1)}, f32[32]{0:T(128)}, u32[]{:S(2)}) copy-start(f32[32]{0:T(128)} %param.6) | copy-start | bytes 388
  1.9 4.6 %collective-permute-start = (bf16[32,128]{1,0:T(8,128)(2,1)S(1)}, bf16[32,128]{1,0:T(8,128)(2,1)S(1)}, u32[]{:S(2)}, u32[]{:S(2)}) collective-permute-start(bf16[32,128]{1,0:T(8,128)(2,1)S(1)} %get-tuple-element.30), channel_id=1, source_target_pairs={{0,1},{1,0},{2,3},{3,2},{4,5},{5,4},{6,7},{7,6},{8,9},{9,8},{10,11... | collective-permute-start | bytes 24584 | tf_op jit(solution)/shard_map/ppermute | solution.py:35
  6.5 5.8 %collective-permute-start.2 = (bf16[48,128]{1,0:T(8,128)(2,1)S(1)}, bf16[48,128]{1,0:T(8,128)(2,1)S(1)}, u32[]{:S(2)}, u32[]{:S(2)}) collective-permute-start(bf16[48,128]{1,0:T(8,128)(2,1)S(1)} %get-tuple-element.60), channel_id=1, source_target_pairs={{0,6},{2,4},{4,2},{6,0},{1,7},{3,5},{5,3},{7,1},{8,14},{10,12},{12... | collective-permute-start | bytes 36872 | tf_op jit(solution)/shard_map/ppermute | solution.py:35
  10.6 3.7 %collective-permute-start.1 = (bf16[48,128]{1,0:T(8,128)(2,1)S(1)}, bf16[48,128]{1,0:T(8,128)(2,1)S(1)}, u32[]{:S(2)}, u32[]{:S(2)}) collective-permute-start(bf16[48,128]{1,0:T(8,128)(2,1)S(1)} %get-tuple-element.61), channel_id=1, source_target_pairs={{0,2},{2,0},{4,6},{6,4},{1,3},{3,1},{5,7},{7,5},{8,10},{10,8},{12,... | collective-permute-start | bytes 36872 | tf_op jit(solution)/shard_map/ppermute | solution.py:35
  10.7 3.6 %copy-start.1 = (bf16[4,4,64,128]{3,2,1,0:T(8,128)(2,1)S(1)}, bf16[4,4,64,128]{3,2,1,0:T(8,128)(2,1)}, u32[]{:S(2)}) copy-start(bf16[4,4,64,128]{3,2,1,0:T(8,128)(2,1)} %cells.5) | copy-start | bytes 786436
  10.7 5.4 %copy-start.2 = (bf16[32,2,32,64]{3,2,1,0:T(8,128)(2,1)S(1)}, bf16[32,2,32,64]{3,2,1,0:T(8,128)(2,1)}, u32[]{:S(2)}) copy-start(bf16[32,2,32,64]{3,2,1,0:T(8,128)(2,1)} %cot.1) | copy-start | bytes 786436
  14.4 2.7 %collective-permute-start.3 = (bf16[288,128]{1,0:T(8,128)(2,1)S(1)}, bf16[288,128]{1,0:T(8,128)(2,1)S(1)}, u32[]{:S(2)}, u32[]{:S(2)}) collective-permute-start(bf16[288,128]{1,0:T(8,128)(2,1)S(1)} %get-tuple-element.33), channel_id=1, source_target_pairs={{0,8},{8,0},{16,24},{24,16},{1,9},{9,1},{17,25},{25,17},{2,10},{10... | collective-permute-start | bytes 221192 | tf_op jit(solution)/shard_map/ppermute | solution.py:35
  14.4 4.1 %collective-permute-start.4 = (bf16[288,128]{1,0:T(8,128)(2,1)S(1)}, bf16[288,128]{1,0:T(8,128)(2,1)S(1)}, u32[]{:S(2)}, u32[]{:S(2)}) collective-permute-start(bf16[288,128]{1,0:T(8,128)(2,1)S(1)} %get-tuple-element.34), channel_id=1, source_target_pairs={{0,24},{8,16},{16,8},{24,0},{1,25},{9,17},{17,9},{25,1},{2,26},{10... | collective-permute-start | bytes 221192 | tf_op jit(solution)/shard_map/ppermute | solution.py:35
  27.3 5.9 %collective-permute-start.5 = (bf16[384,128]{1,0:T(8,128)(2,1)S(1)}, bf16[384,128]{1,0:T(8,128)(2,1)S(1)}, u32[]{:S(2)}, u32[]{:S(2)}) collective-permute-start(bf16[384,128]{1,0:T(8,128)(2,1)S(1)} %get-tuple-element.40), channel_id=1, source_target_pairs={{0,8},{8,0},{16,24},{24,16},{1,9},{9,1},{17,25},{25,17},{2,10},{10... | collective-permute-start | bytes 294920 | tf_op jit(solution)/shard_map/ppermute | solution.py:35
  27.8 5.5 %collective-permute-start.6 = (bf16[384,128]{1,0:T(8,128)(2,1)S(1)}, bf16[384,128]{1,0:T(8,128)(2,1)S(1)}, u32[]{:S(2)}, u32[]{:S(2)}) collective-permute-start(bf16[384,128]{1,0:T(8,128)(2,1)S(1)} %get-tuple-element.41), channel_id=1, source_target_pairs={{0,24},{8,16},{16,8},{24,0},{1,25},{9,17},{17,9},{25,1},{2,26},{10... | collective-permute-start | bytes 294920 | tf_op jit(solution)/shard_map/ppermute | solution.py:35
  29.0 4.2 %collective-permute-start.7 = (bf16[64,128]{1,0:T(8,128)(2,1)S(1)}, bf16[64,128]{1,0:T(8,128)(2,1)S(1)}, u32[]{:S(2)}, u32[]{:S(2)}) collective-permute-start(bf16[64,128]{1,0:T(8,128)(2,1)S(1)} %get-tuple-element.43.wframe), channel_id=1, source_target_pairs={{0,16},{8,24},{16,0},{24,8},{1,17},{9,25},{17,1},{25,9},{2,18},{10... | collective-permute-start | bytes 49160 | tf_op jit(solution)/shard_map/ppermute | solution.py:35
  33.3 6.5 %collective-permute-start.9 = (bf16[112,128]{1,0:T(8,128)(2,1)S(1)}, bf16[112,128]{1,0:T(8,128)(2,1)S(1)}, u32[]{:S(2)}, u32[]{:S(2)}) collective-permute-start(bf16[112,128]{1,0:T(8,128)(2,1)S(1)} %get-tuple-element.49), channel_id=1, source_target_pairs={{0,6},{2,4},{4,2},{6,0},{1,7},{3,5},{5,3},{7,1},{8,14},{10,12},{12... | collective-permute-start | bytes 86024 | tf_op jit(solution)/shard_map/ppermute | solution.py:35
  35.1 4.7 %collective-permute-start.8 = (bf16[112,128]{1,0:T(8,128)(2,1)S(1)}, bf16[112,128]{1,0:T(8,128)(2,1)S(1)}, u32[]{:S(2)}, u32[]{:S(2)}) collective-permute-start(bf16[112,128]{1,0:T(8,128)(2,1)S(1)} %get-tuple-element.48), channel_id=1, source_target_pairs={{0,2},{2,0},{4,6},{6,4},{1,3},{3,1},{5,7},{7,5},{8,10},{10,8},{12,... | collective-permute-start | bytes 86024 | tf_op jit(solution)/shard_map/ppermute | solution.py:35
  35.1 4.6 %collective-permute-start.10 = (bf16[64,128]{1,0:T(8,128)(2,1)S(1)}, bf16[64,128]{1,0:T(8,128)(2,1)S(1)}, u32[]{:S(2)}, u32[]{:S(2)}) collective-permute-start(bf16[64,128]{1,0:T(8,128)(2,1)S(1)} %slice.3), channel_id=1, source_target_pairs={{0,4},{2,6},{4,0},{6,2},{1,5},{3,7},{5,1},{7,3},{8,12},{10,14},{12... | collective-permute-start | bytes 49160 | tf_op jit(solution)/shard_map/ppermute | solution.py:35
  39.9 3.8 %collective-permute-start.11 = (bf16[96,128]{1,0:T(8,128)(2,1)S(1)}, bf16[96,128]{1,0:T(8,128)(2,1)S(1)}, u32[]{:S(2)}, u32[]{:S(2)}) collective-permute-start(bf16[96,128]{1,0:T(8,128)(2,1)S(1)} %get-tuple-element.52), channel_id=1, source_target_pairs={{0,1},{1,0},{2,3},{3,2},{4,5},{5,4},{6,7},{7,6},{8,9},{9,8},{10,11... | collective-permute-start | bytes 73736 | tf_op jit(solution)/shard_map/ppermute | solution.py:35

commit v6 on v5

--- a/solution.py
+++ b/solution.py
@@ -21,6 +21,10 @@
 
 def iota(shape, dim):
     return lax.broadcasted_iota(jnp.int32, shape, dim)
+
+
+def aligned(start, tile):
+    return start if isinstance(start, int) else pl.multiple_of(start, tile)
 
 
 def swapped(array, axis, pairing):
@@ -135,7 +139,7 @@
 def main_kernel(
     cells, got_0, got_1, rows_in, left_in, right_in, spread, wbig, wback,
     sums, field, sent_0, sent_1, wpart, wframe, rows_out, cols,
-    stage, patches, left, right, carry, gram, deltas,
+    stage, patches, left, right, carry, gram, delta_a, delta_b,
 ):
     chan, count_x, count_y, _ = cells.shape
     pool_x, pool_y = count_x // 2, count_y // 2
@@ -188,36 +192,34 @@
     size = 3 * wide
     inside, outside = lane != lanes - 1, lane != 0
 
-    def finish(y, whole):
+    def finish(y, whole, edge):
         first, last = whole[0:wide], whole[2 * wide : 3 * wide]
         inner = (
             whole[wide : 2 * wide]
             + jnp.where(inside, pltpu.roll(first, lanes - 1, 1), 0.0)
             + jnp.where(outside, pltpu.roll(last, 1, 1), 0.0)
         )
-        field[pl.ds(pl.multiple_of(y * wide, 8), wide), :] = inner
+        field[pl.ds(aligned(y * wide, 8), wide), :] = inner
         here = lane == y
-        cols[0:wide, :] = jnp.where(here, pltpu.roll(first, y, 1), cols[0:wide, :])
-        cols[wide : 2 * wide, :] = jnp.where(
-            here, pltpu.roll(last, y + 1, 1), cols[wide : 2 * wide, :]
-        )
+        edge[0] = jnp.where(here, pltpu.roll(first, y, 1), edge[0])
+        edge[1] = jnp.where(here, pltpu.roll(last, y + 1, 1), edge[1])
 
     def block_of(j):
         return jnp.concatenate(
             [
-                patches[pl.ds(pl.multiple_of((2 * j + h) * depth, 16), 3 * depth), :]
+                patches[pl.ds(aligned((2 * j + h) * depth, 16), 3 * depth), :]
                 for h in range(2)
             ],
             axis=1,
         )
 
-    def forward(i, k):
+    def forward(i, k, ref):
         j = i * pairs + k
         preact = dot(wbig[...], block_of(j))
         slope = jnp.tanh(5.0 * preact)
         linear = jnp.maximum(preact, 0.3 * preact)
         factor = 1.0 + jnp.abs(slope)
-        here = spread[pl.ds(pl.multiple_of(j * pool_x * chan_out, 8), pool_x * chan_out), :]
+        here = spread[pl.ds(aligned(j * pool_x * chan_out, 8), pool_x * chan_out), :]
         slope = 0.65 + 0.35 * slope
         delta = []
         for x in range(pool_x):
@@ -233,38 +235,61 @@
             prod = prod[:, :lanes] * prod[:, lanes:]
             total = total - log_scale * jnp.log(prod)
             sums[pl.ds(x * pool_y + j, chan_out, stride=pool_x * pool_y), :] = total
-        slot = lax.rem(i, 2)
-        deltas[slot, :, 2 * k * lanes : 2 * (k + 1) * lanes] = jnp.concatenate(delta, axis=0)
-
-    def backward(i, k):
+        ref[:, 2 * k * lanes : 2 * (k + 1) * lanes] = jnp.concatenate(delta, axis=0)
+
+    def backward(i, k, ref, held, edge):
         j = i * pairs + k
-        parts = dot(wback[...], deltas[lax.rem(i, 2), :, 2 * k * lanes : 2 * (k + 1) * lanes])
+        parts = dot(wback[...], ref[:, 2 * k * lanes : 2 * (k + 1) * lanes])
         part = lambda b, h: parts[b * size : (b + 1) * size, h * lanes : (h + 1) * lanes]
-        finish(2 * j, carry[0:size, :] + part(0, 0))
-        finish(2 * j + 1, carry[size : 2 * size, :] + part(1, 0) + part(0, 1))
-        carry[0:size, :] = part(2, 0) + part(1, 1)
-        carry[size : 2 * size, :] = part(2, 1)
-
-    def weigh(i):
+        finish(2 * j, held[0] + part(0, 0), edge)
+        finish(2 * j + 1, held[1] + part(1, 0) + part(0, 1), edge)
+        held[0] = part(2, 0) + part(1, 1)
+        held[1] = part(2, 1)
+
+    def weigh(i, ref):
         blocks = jnp.concatenate([block_of(i * pairs + k) for k in range(pairs)], axis=1)
-        gram[...] += dot(deltas[lax.rem(i, 2)], blocks, ((1,), (1,)))
-
-    def step(i, _):
-        weigh(i - 1)
+        return dot(ref[...], blocks, ((1,), (1,)))
+
+    def opened():
+        return (
+            [carry[0:size, :], carry[size : 2 * size, :]],
+            [cols[0:wide, :], cols[wide : 2 * wide, :]],
+        )
+
+    def closed(held, edge):
+        carry[0:size, :] = held[0]
+        carry[size : 2 * size, :] = held[1]
+        cols[0:wide, :] = edge[0]
+        cols[wide : 2 * wide, :] = edge[1]
+
+    def step(t, _):
+        held, edge = opened()
+        total = gram[...] + weigh(2 * t, delta_a)
         for k in range(pairs):
-            forward(i, k)
-            backward(i - 1, k)
+            forward(2 * t + 1, k, delta_b)
+            backward(2 * t, k, delta_a, held, edge)
+        total = total + weigh(2 * t + 1, delta_b)
+        for k in range(pairs):
+            forward(2 * t + 2, k, delta_a)
+            backward(2 * t + 1, k, delta_b, held, edge)
+        gram[...] = total
+        closed(held, edge)
         return 0
 
     for k in range(pairs):
-        forward(jnp.int32(0), k)
-    lax.fori_loop(1, steps, step, 0)
-    last_step = jnp.int32(steps - 1)
-    weigh(last_step)
+        forward(0, k, delta_a)
+    lax.fori_loop(0, steps // 2 - 1, step, 0)
+    held, edge = opened()
+    total = gram[...] + weigh(steps - 2, delta_a)
     for k in range(pairs):
-        backward(last_step, k)
-    finish(count_y, carry[0:size, :])
-    finish(count_y + 1, carry[size : 2 * size, :])
+        forward(steps - 1, k, delta_b)
+        backward(steps - 2, k, delta_a, held, edge)
+    gram[...] = total + weigh(steps - 1, delta_b)
+    for k in range(pairs):
+        backward(steps - 1, k, delta_b, held, edge)
+    finish(count_y, held[0], edge)
+    finish(count_y + 1, held[1], edge)
+    closed(held, edge)
 
     span = gram.shape[1]
     straight, turned = 0.0, 0.0
@@ -490,7 +515,8 @@
             pltpu.VMEM((wide, lanes), f32),
             pltpu.VMEM((6 * wide, lanes), f32),
             pltpu.VMEM((count_x * chan_out, 3 * depth), f32),
-            pltpu.VMEM((2, count_x * chan_out, 8 * lanes), bf16),
+            pltpu.VMEM((count_x * chan_out, 8 * lanes), bf16),
+            pltpu.VMEM((count_x * chan_out, 8 * lanes), bf16),
         ],
     )(cells, face_0, face_1, rows, left, right, spread, wbig, wback)
 

time: 45.2 us -> 41.4 us (0.916)
  Pallas kernels: 12.9 us -> 9.07 us
    pallas_call x1, Pallas kernels: 8.86 us -> 5.06 us  [on_device(): call(main_kernel, [pooled_rows, shape(((count_y + 2) * wide, lanes), f32)...]
where the time goes in v6:
time: 41.4 us; the launch traced here: 41.2 us
  starting transfers between devices  17 us (41%)
  waiting for transfers between devices  12.6 us (30%)
  Pallas kernels  9.07 us (22%)
  local copies, waits for them, and re-layouts  1.63 us (4%)
  between operations  0.77 us (2%)
    ppermute x12, starting transfers between devices, swapped(): return lax.ppermute(array, axis, pairs)  17 us
    ppermute x12, waiting for transfers between devices, swapped(): return lax.ppermute(array, axis, pairs)  12.6 us
    pallas_call x1, Pallas kernels, on_device(): call(main_kernel, [pooled_rows, shape(((count_y + 2) * wide, lanes), f32)...  5.06 us
    pallas_call x1, Pallas kernels, on_device(): call(final_kernel, [shape(cells.shape, f32), shape((27, chan, chan_out),...  1.31 us
    pallas_call x1, Pallas kernels, on_device(): pooled = call(pool_kernel, shape(cotangent.shape, bf16))(sums)  1.24 us
    unnamed x10, local copies, waits for them, and re-layouts  0.97 us
    pallas_call x1, Pallas kernels, on_device(): spread = call(spread_kernel, pooled_rows)(cotangent)  0.88 us
  transfers between devices with their start and end apart: 12, of which 7 were waited for; matrix products, arithmetic and copies ran while one was open for 2% of the time, Pallas kernels for 5%

profile of v6, /device:TPU:0, one launch (start us, length us, event | category | flops | bytes accessed | tf_op | source)
XLA Modules:
  0.0 41.2 jit_solution(10512358853351667045)
XLA Ops:
  0.6 0.9 %copy-done = bf16[4,4,64,128]{3,2,1,0:T(8,128)(2,1)S(1)} copy-done((bf16[4,4,64,128]{3,2,1,0:T(8,128)(2,1)S(1)}, bf16[4,4,64,128]{3,2,1,0:T(8,128)(2,1)}, u32[]{:S(2)}) %copy-start) | copy-done | bytes 262168
  1.6 0.3 shard_map.75
  1.9 3.0 %collective-permute-start = (bf16[32,128]{1,0:T(8,128)(2,1)S(1)}, bf16[32,128]{1,0:T(8,128)(2,1)S(1)}, u32[]{:S(2)}, u32[]{:S(2)}) collective-permute-start(bf16[32,128]{1,0:T(8,128)(2,1)S(1)} %get-tuple-element.30), channel_id=1, source_target_pairs={{0,1},{1,0},{2,3},{3,2},{4,5},{5,4},{6,7},{7,6},{8,9},{9,8},{10,11... | collective-permute-start | bytes 24584 | tf_op jit(solution)/shard_map/ppermute | solution.py:39
  4.9 0.2 pad_maximum_fusion
  5.2 1.3 %collective-permute-done.edges = bf16[32,128]{1,0:T(8,128)(2,1)S(1)} collective-permute-done((bf16[32,128]{1,0:T(8,128)(2,1)S(1)}, bf16[32,128]{1,0:T(8,128)(2,1)S(1)}, u32[]{:S(2)}, u32[]{:S(2)}) %collective-permute-start) | collective-permute-done | bytes 8224 | tf_op jit(solution)/shard_map/ppermute | solution.py:39
  6.5 4.1 %collective-permute-start.2 = (bf16[48,128]{1,0:T(8,128)(2,1)S(1)}, bf16[48,128]{1,0:T(8,128)(2,1)S(1)}, u32[]{:S(2)}, u32[]{:S(2)}) collective-permute-start(bf16[48,128]{1,0:T(8,128)(2,1)S(1)} %get-tuple-element.60), channel_id=1, source_target_pairs={{0,6},{2,4},{4,2},{6,0},{1,7},{3,5},{5,3},{7,1},{8,14},{10,12},{12... | collective-permute-start | bytes 36872 | tf_op jit(solution)/shard_map/ppermute | solution.py:39
  10.7 0.2 reshape_reshape.3
  11.1 1.1 %collective-permute-done.2.got_1 = bf16[48,128]{1,0:T(8,128)(2,1)S(1)} collective-permute-done((bf16[48,128]{1,0:T(8,128)(2,1)S(1)}, bf16[48,128]{1,0:T(8,128)(2,1)S(1)}, u32[]{:S(2)}, u32[]{:S(2)}) %collective-permute-start.2) | collective-permute-done | bytes 12320 | tf_op jit(solution)/shard_map/ppermute | solution.py:39
  12.3 2.0 %collective-permute-done.1.got_0 = bf16[48,128]{1,0:T(8,128)(2,1)S(1)} collective-permute-done((bf16[48,128]{1,0:T(8,128)(2,1)S(1)}, bf16[48,128]{1,0:T(8,128)(2,1)S(1)}, u32[]{:S(2)}, u32[]{:S(2)}) %collective-permute-start.1) | collective-permute-done | bytes 12320 | tf_op jit(solution)/shard_map/ppermute | solution.py:39
  14.4 1.6 %collective-permute-start.4 = (bf16[288,128]{1,0:T(8,128)(2,1)S(1)}, bf16[288,128]{1,0:T(8,128)(2,1)S(1)}, u32[]{:S(2)}, u32[]{:S(2)}) collective-permute-start(bf16[288,128]{1,0:T(8,128)(2,1)S(1)} %get-tuple-element.34), channel_id=1, source_target_pairs={{0,24},{8,16},{16,8},{24,0},{1,25},{9,17},{17,9},{25,1},{2,26},{10... | collective-permute-start | bytes 221192 | tf_op jit(solution)/shard_map/ppermute | solution.py:39
  16.1 0.9 %shard_map.77.spread = f32[2048,128]{1,0:T(8,128)S(1)} custom-call(bf16[32,2,32,64]{3,2,1,0:T(8,128)(2,1)S(1)} %copy-done.2), custom_call_target="tpu_custom_call" | custom-call | tf_op jit(solution)/shard_map/pallas_call | solution.py:485
  17.0 1.4 %collective-permute-done.4.got_1 = bf16[288,128]{1,0:T(8,128)(2,1)S(1)} collective-permute-done((bf16[288,128]{1,0:T(8,128)(2,1)S(1)}, bf16[288,128]{1,0:T(8,128)(2,1)S(1)}, u32[]{:S(2)}, u32[]{:S(2)}) %collective-permute-start.4) | collective-permute-done | bytes 73760 | tf_op jit(solution)/shard_map/ppermute | solution.py:39
  18.5 5.1 %shard_map.78 = (f32[2048,128]{1,0:T(8,128)S(1)}, f32[1584,128]{1,0:T(8,128)S(1)}, bf16[384,128]{1,0:T(8,128)(2,1)S(1)}, bf16[384,128]{1,0:T(8,128)(2,1)S(1)}, f...) custom-call(bf16[4,4,64,128]{3,2,1,0:T(8,128)(2,1)S(1)} %copy-done.1, ...), custom_call_target="tpu_custom_call" | custom-call | tf_op jit(solution)/shard_map/pallas_call | solution.py:499
  23.5 0.5 %collective-permute-start.5 = (bf16[384,128]{1,0:T(8,128)(2,1)S(1)}, bf16[384,128]{1,0:T(8,128)(2,1)S(1)}, u32[]{:S(2)}, u32[]{:S(2)}) collective-permute-start(bf16[384,128]{1,0:T(8,128)(2,1)S(1)} %get-tuple-element.40), channel_id=1, source_target_pairs={{0,8},{8,0},{16,24},{24,16},{1,9},{9,1},{17,25},{25,17},{2,10},{10... | collective-permute-start | bytes 294920 | tf_op jit(solution)/shard_map/ppermute | solution.py:39
  24.0 1.2 %collective-permute-start.6 = (bf16[384,128]{1,0:T(8,128)(2,1)S(1)}, bf16[384,128]{1,0:T(8,128)(2,1)S(1)}, u32[]{:S(2)}, u32[]{:S(2)}) collective-permute-start(bf16[384,128]{1,0:T(8,128)(2,1)S(1)} %get-tuple-element.41), channel_id=1, source_target_pairs={{0,24},{8,16},{16,8},{24,0},{1,25},{9,17},{17,9},{25,1},{2,26},{10... | collective-permute-start | bytes 294920 | tf_op jit(solution)/shard_map/ppermute | solution.py:39
  25.2 0.6 %collective-permute-start.7 = (bf16[64,128]{1,0:T(8,128)(2,1)S(1)}, bf16[64,128]{1,0:T(8,128)(2,1)S(1)}, u32[]{:S(2)}, u32[]{:S(2)}) collective-permute-start(bf16[64,128]{1,0:T(8,128)(2,1)S(1)} %get-tuple-element.43.wframe), channel_id=1, source_target_pairs={{0,16},{8,24},{16,0},{24,8},{1,17},{9,25},{17,1},{25,9},{2,18},{10... | collective-permute-start | bytes 49160 | tf_op jit(solution)/shard_map/ppermute | solution.py:39
  25.8 3.7 %collective-permute-done.7.far = bf16[64,128]{1,0:T(8,128)(2,1)S(1)} collective-permute-done((bf16[64,128]{1,0:T(8,128)(2,1)S(1)}, bf16[64,128]{1,0:T(8,128)(2,1)S(1)}, u32[]{:S(2)}, u32[]{:S(2)}) %collective-permute-start.7) | collective-permute-done | bytes 16416 | tf_op jit(solution)/shard_map/ppermute | solution.py:39
  29.5 1.9 %collective-permute-start.9 = (bf16[112,128]{1,0:T(8,128)(2,1)S(1)}, bf16[112,128]{1,0:T(8,128)(2,1)S(1)}, u32[]{:S(2)}, u32[]{:S(2)}) collective-permute-start(bf16[112,128]{1,0:T(8,128)(2,1)S(1)} %get-tuple-element.49), channel_id=1, source_target_pairs={{0,6},{2,4},{4,2},{6,0},{1,7},{3,5},{5,3},{7,1},{8,14},{10,12},{12... | collective-permute-start | bytes 86024 | tf_op jit(solution)/shard_map/ppermute | solution.py:39
  31.4 2.6 %collective-permute-start.10 = (bf16[64,128]{1,0:T(8,128)(2,1)S(1)}, bf16[64,128]{1,0:T(8,128)(2,1)S(1)}, u32[]{:S(2)}, u32[]{:S(2)}) collective-permute-start(bf16[64,128]{1,0:T(8,128)(2,1)S(1)} %slice.3), channel_id=1, source_target_pairs={{0,4},{2,6},{4,0},{6,2},{1,5},{3,7},{5,1},{7,3},{8,12},{10,14},{12... | collective-permute-start | bytes 49160 | tf_op jit(solution)/shard_map/ppermute | solution.py:39
  33.9 2.1 %collective-permute-done.10.far = bf16[64,128]{1,0:T(8,128)(2,1)S(1)} collective-permute-done((bf16[64,128]{1,0:T(8,128)(2,1)S(1)}, bf16[64,128]{1,0:T(8,128)(2,1)S(1)}, u32[]{:S(2)}, u32[]{:S(2)}) %collective-permute-start.10) | collective-permute-done | bytes 16416 | tf_op jit(solution)/shard_map/ppermute | solution.py:39
  36.1 1.5 %collective-permute-start.11 = (bf16[96,128]{1,0:T(8,128)(2,1)S(1)}, bf16[96,128]{1,0:T(8,128)(2,1)S(1)}, u32[]{:S(2)}, u32[]{:S(2)}) collective-permute-start(bf16[96,128]{1,0:T(8,128)(2,1)S(1)} %get-tuple-element.52), channel_id=1, source_target_pairs={{0,1},{1,0},{2,3},{3,2},{4,5},{5,4},{6,7},{7,6},{8,9},{9,8},{10,11... | collective-permute-start | bytes 73736 | tf_op jit(solution)/shard_map/ppermute | solution.py:39
  37.6 1.2 %shard_map.79 = bf16[32,2,32,64]{3,2,1,0:T(8,128)(2,1)} custom-call(f32[2048,128]{1,0:T(8,128)S(1)} %get-tuple-element.38.sums), custom_call_target="tpu_custom_call" | custom-call | tf_op jit(solution)/shard_map/pallas_call | solution.py:530
  39.0 1.0 %collective-permute-done.11.frame = bf16[96,128]{1,0:T(8,128)(2,1)S(1)} collective-permute-done((bf16[96,128]{1,0:T(8,128)(2,1)S(1)}, bf16[96,128]{1,0:T(8,128)(2,1)S(1)}, u32[]{:S(2)}, u32[]{:S(2)}) %collective-permute-start.11) | collective-permute-done | bytes 24608 | tf_op jit(solution)/shard_map/ppermute | solution.py:39
  39.9 1.3 %shard_map.83 = (f32[4,4,64,128]{3,2,1,0:T(8,128)}, f32[27,4,32]{2,1,0:T(4,128)}, f32[1,32]{1,0:T(1,128)}) custom-call(f32[4,4,64,128]{3,2,1,0:T(8,128)S(1)} %shard_map.80.grad, f32[32,128]{1,0:T(8,128)S(1)} %get-tuple-element.50.wsum, f32[32,128]{1,0:T(8,128)S(1)} %get-tuple-element.51.rows, bf16[96,128]{1,0:T(8,128)(2,1)S(1)} %collective-permute-done.11.frame), custom_call_target="tpu_custom_call" | custom-call | tf_op jit(solution)/shard_map/pallas_call | solution.py:551
  (32 shorter events, 0.9 us)
Async XLA Ops:
  0.6 1.0 %copy-start = (bf16[4,4,64,128]{3,2,1,0:T(8,128)(2,1)S(1)}, bf16[4,4,64,128]{3,2,1,0:T(8,128)(2,1)}, u32[]{:S(2)}) copy-start(bf16[4,4,64,128]{3,2,1,0:T(8,128)(2,1)} %cells.5) | copy-start | bytes 786436
  1.6 3.3 %copy-start.3 = (bf16[32,4,3,3,3]{0,1,4,3,2:T(4,128)(2,1)S(1)}, bf16[32,4,3,3,3]{0,1,4,3,2:T(4,128)(2,1)}, u32[]{:S(2)}) copy-start(bf16[32,4,3,3,3]{0,1,4,3,2:T(4,128)(2,1)} %param.5) | copy-start | bytes 20740
  1.9 3.0 %copy-start.4 = (f32[32]{0:T(128)S(1)}, f32[32]{0:T(128)}, u32[]{:S(2)}) copy-start(f32[32]{0:T(128)} %param.6) | copy-start | bytes 388
  1.9 4.6 %collective-permute-start = (bf16[32,128]{1,0:T(8,128)(2,1)S(1)}, bf16[32,128]{1,0:T(8,128)(2,1)S(1)}, u32[]{:S(2)}, u32[]{:S(2)}) collective-permute-start(bf16[32,128]{1,0:T(8,128)(2,1)S(1)} %get-tuple-element.30), channel_id=1, source_target_pairs={{0,1},{1,0},{2,3},{3,2},{4,5},{5,4},{6,7},{7,6},{8,9},{9,8},{10,11... | collective-permute-start | bytes 24584 | tf_op jit(solution)/shard_map/ppermute | solution.py:39
  6.5 5.8 %collective-permute-start.2 = (bf16[48,128]{1,0:T(8,128)(2,1)S(1)}, bf16[48,128]{1,0:T(8,128)(2,1)S(1)}, u32[]{:S(2)}, u32[]{:S(2)}) collective-permute-start(bf16[48,128]{1,0:T(8,128)(2,1)S(1)} %get-tuple-element.60), channel_id=1, source_target_pairs={{0,6},{2,4},{4,2},{6,0},{1,7},{3,5},{5,3},{7,1},{8,14},{10,12},{12... | collective-permute-start | bytes 36872 | tf_op jit(solution)/shard_map/ppermute | solution.py:39
  10.6 3.7 %collective-permute-start.1 = (bf16[48,128]{1,0:T(8,128)(2,1)S(1)}, bf16[48,128]{1,0:T(8,128)(2,1)S(1)}, u32[]{:S(2)}, u32[]{:S(2)}) collective-permute-start(bf16[48,128]{1,0:T(8,128)(2,1)S(1)} %get-tuple-element.61), channel_id=1, source_target_pairs={{0,2},{2,0},{4,6},{6,4},{1,3},{3,1},{5,7},{7,5},{8,10},{10,8},{12,... | collective-permute-start | bytes 36872 | tf_op jit(solution)/shard_map/ppermute | solution.py:39
  10.7 3.6 %copy-start.1 = (bf16[4,4,64,128]{3,2,1,0:T(8,128)(2,1)S(1)}, bf16[4,4,64,128]{3,2,1,0:T(8,128)(2,1)}, u32[]{:S(2)}) copy-start(bf16[4,4,64,128]{3,2,1,0:T(8,128)(2,1)} %cells.5) | copy-start | bytes 786436
  10.7 5.4 %copy-start.2 = (bf16[32,2,32,64]{3,2,1,0:T(8,128)(2,1)S(1)}, bf16[32,2,32,64]{3,2,1,0:T(8,128)(2,1)}, u32[]{:S(2)}) copy-start(bf16[32,2,32,64]{3,2,1,0:T(8,128)(2,1)} %cot.1) | copy-start | bytes 786436
  14.4 2.7 %collective-permute-start.3 = (bf16[288,128]{1,0:T(8,128)(2,1)S(1)}, bf16[288,128]{1,0:T(8,128)(2,1)S(1)}, u32[]{:S(2)}, u32[]{:S(2)}) collective-permute-start(bf16[288,128]{1,0:T(8,128)(2,1)S(1)} %get-tuple-element.33), channel_id=1, source_target_pairs={{0,8},{8,0},{16,24},{24,16},{1,9},{9,1},{17,25},{25,17},{2,10},{10... | collective-permute-start | bytes 221192 | tf_op jit(solution)/shard_map/ppermute | solution.py:39
  14.4 4.1 %collective-permute-start.4 = (bf16[288,128]{1,0:T(8,128)(2,1)S(1)}, bf16[288,128]{1,0:T(8,128)(2,1)S(1)}, u32[]{:S(2)}, u32[]{:S(2)}) collective-permute-start(bf16[288,128]{1,0:T(8,128)(2,1)S(1)} %get-tuple-element.34), channel_id=1, source_target_pairs={{0,24},{8,16},{16,8},{24,0},{1,25},{9,17},{17,9},{25,1},{2,26},{10... | collective-permute-start | bytes 221192 | tf_op jit(solution)/shard_map/ppermute | solution.py:39
  23.5 5.9 %collective-permute-start.5 = (bf16[384,128]{1,0:T(8,128)(2,1)S(1)}, bf16[384,128]{1,0:T(8,128)(2,1)S(1)}, u32[]{:S(2)}, u32[]{:S(2)}) collective-permute-start(bf16[384,128]{1,0:T(8,128)(2,1)S(1)} %get-tuple-element.40), channel_id=1, source_target_pairs={{0,8},{8,0},{16,24},{24,16},{1,9},{9,1},{17,25},{25,17},{2,10},{10... | collective-permute-start | bytes 294920 | tf_op jit(solution)/shard_map/ppermute | solution.py:39
  24.0 5.5 %collective-permute-start.6 = (bf16[384,128]{1,0:T(8,128)(2,1)S(1)}, bf16[384,128]{1,0:T(8,128)(2,1)S(1)}, u32[]{:S(2)}, u32[]{:S(2)}) collective-permute-start(bf16[384,128]{1,0:T(8,128)(2,1)S(1)} %get-tuple-element.41), channel_id=1, source_target_pairs={{0,24},{8,16},{16,8},{24,0},{1,25},{9,17},{17,9},{25,1},{2,26},{10... | collective-permute-start | bytes 294920 | tf_op jit(solution)/shard_map/ppermute | solution.py:39
  25.2 4.2 %collective-permute-start.7 = (bf16[64,128]{1,0:T(8,128)(2,1)S(1)}, bf16[64,128]{1,0:T(8,128)(2,1)S(1)}, u32[]{:S(2)}, u32[]{:S(2)}) collective-permute-start(bf16[64,128]{1,0:T(8,128)(2,1)S(1)} %get-tuple-element.43.wframe), channel_id=1, source_target_pairs={{0,16},{8,24},{16,0},{24,8},{1,17},{9,25},{17,1},{25,9},{2,18},{10... | collective-permute-start | bytes 49160 | tf_op jit(solution)/shard_map/ppermute | solution.py:39
  29.5 6.5 %collective-permute-start.9 = (bf16[112,128]{1,0:T(8,128)(2,1)S(1)}, bf16[112,128]{1,0:T(8,128)(2,1)S(1)}, u32[]{:S(2)}, u32[]{:S(2)}) collective-permute-start(bf16[112,128]{1,0:T(8,128)(2,1)S(1)} %get-tuple-element.49), channel_id=1, source_target_pairs={{0,6},{2,4},{4,2},{6,0},{1,7},{3,5},{5,3},{7,1},{8,14},{10,12},{12... | collective-permute-start | bytes 86024 | tf_op jit(solution)/shard_map/ppermute | solution.py:39
  31.4 4.7 %collective-permute-start.8 = (bf16[112,128]{1,0:T(8,128)(2,1)S(1)}, bf16[112,128]{1,0:T(8,128)(2,1)S(1)}, u32[]{:S(2)}, u32[]{:S(2)}) collective-permute-start(bf16[112,128]{1,0:T(8,128)(2,1)S(1)} %get-tuple-element.48), channel_id=1, source_target_pairs={{0,2},{2,0},{4,6},{6,4},{1,3},{3,1},{5,7},{7,5},{8,10},{10,8},{12,... | collective-permute-start | bytes 86024 | tf_op jit(solution)/shard_map/ppermute | solution.py:39
  31.4 4.6 %collective-permute-start.10 = (bf16[64,128]{1,0:T(8,128)(2,1)S(1)}, bf16[64,128]{1,0:T(8,128)(2,1)S(1)}, u32[]{:S(2)}, u32[]{:S(2)}) collective-permute-start(bf16[64,128]{1,0:T(8,128)(2,1)S(1)} %slice.3), channel_id=1, source_target_pairs={{0,4},{2,6},{4,0},{6,2},{1,5},{3,7},{5,1},{7,3},{8,12},{10,14},{12... | collective-permute-start | bytes 49160 | tf_op jit(solution)/shard_map/ppermute | solution.py:39
  36.1 3.8 %collective-permute-start.11 = (bf16[96,128]{1,0:T(8,128)(2,1)S(1)}, bf16[96,128]{1,0:T(8,128)(2,1)S(1)}, u32[]{:S(2)}, u32[]{:S(2)}) collective-permute-start(bf16[96,128]{1,0:T(8,128)(2,1)S(1)} %get-tuple-element.52), channel_id=1, source_target_pairs={{0,1},{1,0},{2,3},{3,2},{4,5},{5,4},{6,7},{7,6},{8,9},{9,8},{10,11... | collective-permute-start | bytes 73736 | tf_op jit(solution)/shard_map/ppermute | solution.py:39

commit v7 on v6

--- a/solution.py
+++ b/solution.py
@@ -138,7 +138,7 @@
 
 def main_kernel(
     cells, got_0, got_1, rows_in, left_in, right_in, spread, wbig, wback,
-    sums, field, sent_0, sent_1, wpart, wframe, rows_out, cols,
+    sums, field, face_0, face_1, sent_0, sent_1, wpart, wframe, rows_out, cols,
     stage, patches, left, right, carry, gram, delta_a, delta_b,
 ):
     chan, count_x, count_y, _ = cells.shape
@@ -318,7 +318,7 @@
     tall = cols.shape[0]
     found = cols[...].astype(bf16)
     zero = jnp.zeros((8, lanes), f32)
-    for ref, odd in ((sent_0, 0), (sent_1, 1)):
+    for face, ref, odd in ((face_0, sent_0, 0), (face_1, sent_1, 1)):
         high = even != (odd == 1)
         for c in range(chan):
             low_plane, high_plane = [
@@ -326,33 +326,28 @@
                 for x in (0, count_x + 1)
             ]
             plane = jnp.where(high, high_plane, low_plane)
-            ref[c * count_y : (c + 1) * count_y, :] = plane.astype(bf16)
+            face[c * count_y : (c + 1) * count_y, :] = plane.astype(bf16)
         low_frame, high_frame = [
             jnp.concatenate([end[x * chan : (x + 1) * chan] for end in ends] + [zero], axis=0)
             for x in (0, count_x + 1)
         ]
-        ref[body : body + 16, :] = jnp.where(high, high_frame, low_frame).astype(bf16)
-        ref[body + 16 : body + 16 + tall, :] = found
-        ref[body + 16 + tall :, :] = sides
-
-
-def x_kernel(alone, wpart, wframe, rows, cols, got_0, got_1, far, wsum, sent_0, sent_1, cols_out):
+        ref[0:16, :] = jnp.where(high, high_frame, low_frame).astype(bf16)
+        ref[16 : 16 + tall, :] = found
+        ref[16 + tall :, :] = sides
+
+
+def x_kernel(alone, wpart, wframe, rows, cols, got_0, got_1, far, frame, rows_out):
     tall = cols.shape[0]
-    chan_out = wpart.shape[0]
     own = rows.shape[0] // 2
-    body = got_0.shape[0] - 16 - tall - 2 * chan_out
-    chan = 4
-    wide = own + 2 * chan
+    wide = tall // 2
+    chan = (wide - own) // 2
     if alone:
-        total = joined(jnp.concatenate(split(wpart[...]), axis=0))
+        total = wpart[...]
     else:
         total = joined(wframe[...]) + joined(far[...])
-        sides = [ref[body + 16 + tall :, :] for ref in (got_0, got_1)]
-        total = total + (joined(sides[0]) + joined(sides[1]))
-    wsum[...] = total
-    sides = jnp.concatenate(split(total), axis=0)
-    one = got_0[body : body + 16 + tall, :].astype(f32)
-    two = got_1[body : body + 16 + tall, :].astype(f32)
+        total = total + (joined(got_0[16 + tall :, :]) + joined(got_1[16 + tall :, :]))
+    frame[2 * own :, :] = jnp.concatenate(split(total), axis=0)
+    one, two = got_0[0 : 16 + tall, :].astype(f32), got_1[0 : 16 + tall, :].astype(f32)
     from_low, from_high = pick("gx", two, one), pick("gx", one, two)
     mid = jnp.zeros((own - 2 * chan, lanes), f32)
     found = []
@@ -360,91 +355,97 @@
         more = [from_low[16 + top + chan + own : 16 + top + wide], mid]
         more.append(from_high[16 + top : 16 + top + chan])
         found.append(cols[top + chan : top + chan + own, :] + jnp.concatenate(more, axis=0))
-    found = jnp.concatenate(found, axis=0)
-    cols_out[...] = found
-    both = []
+    frame[0 : 2 * own, :] = jnp.concatenate(found, axis=0).astype(bf16)
     for at in (0, 1):
         more = [from_low[at * chan : (at + 1) * chan], mid, from_high[at * chan : (at + 1) * chan]]
-        total = rows[at * own : (at + 1) * own, :] + jnp.concatenate(more, axis=0)
-        both.append(total)
+        place = slice(at * own, (at + 1) * own)
+        rows_out[place, :] = rows[place, :] + jnp.concatenate(more, axis=0)
+
+
+def z_kernel(count_y, mine, got, rows, sent_0, sent_1, wframe):
+    own = rows.shape[0] // 2
+    total = joined(mine[2 * own :, :]) + joined(got[2 * own :, :])
+    sides = jnp.concatenate(split(total), axis=0)
+    wframe[...] = sides
+    last = got[0:own, :].astype(f32)
+    first = got[own : 2 * own, :].astype(f32)
+    spot = iota((own, lanes), 1)
+    both = []
+    for at, line in ((0, 0), (1, count_y + 1)):
+        more = jnp.where(spot == lanes - 1, pltpu.roll(last, lanes - 1 - line, 1), 0.0)
+        turned = pltpu.roll(first, lanes - line, 1) if line else first
+        more = jnp.where(spot == 0, turned, more)
+        both.append(rows[at * own : (at + 1) * own, :] + more)
     sent_0[0:own, :] = pick("gy", both[1], both[0]).astype(bf16)
     sent_1[0:own, :] = pick("gy", both[0], both[1]).astype(bf16)
     for ref in (sent_0, sent_1):
-        ref[own : 3 * own, :] = found.astype(bf16)
-        ref[3 * own :, :] = sides
-
-
-def y_kernel(alone, count_y, wsum, cols, got_0, got_1, far, wout, frame, rows):
-    tall = cols.shape[0]
-    chan_out = wsum.shape[0]
-    top = got_0.shape[0] - 2 * chan_out
-    one, two = got_0[0:top, :].astype(f32), got_1[0:top, :].astype(f32)
-    above, below = pick("gy", two, one), pick("gy", one, two)
-    rows[...] = jnp.concatenate([above[: top - tall], below[: top - tall]], axis=0)
-    if alone:
-        total = joined(jnp.concatenate(split(wsum[...]), axis=0))
-    else:
-        total = joined(jnp.concatenate(split(wsum[...]), axis=0)) + joined(far[...])
-        total = total + (joined(got_0[top:, :]) + joined(got_1[top:, :]))
-    wout[...] = total
-    frame[tall:, :] = jnp.concatenate(split(total), axis=0)
-    spot = iota((tall, lanes), 1)
-    above = pltpu.roll(above[top - tall :], lanes - count_y, 1)
-    below = pltpu.roll(below[top - tall :], count_y, 1)
-    found = cols[...]
-    found = found + jnp.where(spot == 1, above, jnp.where(spot == count_y, below, 0.0))
-    frame[0:tall, :] = found.astype(bf16)
-
-
-def grad_kernel(field, got_0, got_1, grad):
+        ref[own:, :] = sides
+
+
+def grad_kernel(field, face_0, face_1, got, grad, ends):
     chan, count_x, count_y, _ = grad.shape
-    wide = chan * (count_x + 2)
+    own = chan * count_x
+    wide = own + 2 * chan
+    spot = iota((count_y, lanes), 1)
+    columns = pltpu.roll(got[0 : 2 * own, :].astype(f32), lanes - 1, 1)
+    columns = jnp.concatenate([columns, jnp.zeros((lanes - 2 * own, lanes), f32)], axis=0)
+    columns = columns.T[0:count_y]
     for x in range(count_x):
         for c in range(chan):
-            plane = field[pl.ds(wide + (x + 1) * chan + c, count_y, stride=wide), :]
+            at = x * chan + c
+            plane = field[pl.ds(wide + chan + at, count_y, stride=wide), :]
             place = slice(c * count_y, (c + 1) * count_y)
             if x == 0:
-                plane = plane + pick("gx", got_1[place, :].astype(f32), got_0[place, :].astype(f32))
+                plane = plane + pick("gx", face_1[place, :].astype(f32), face_0[place, :].astype(f32))
             if x == count_x - 1:
-                plane = plane + pick("gx", got_0[place, :].astype(f32), got_1[place, :].astype(f32))
+                plane = plane + pick("gx", face_0[place, :].astype(f32), face_1[place, :].astype(f32))
+            more = jnp.where(spot == lanes - 1, columns[:, at : at + 1], 0.0)
+            plane = plane + jnp.where(spot == 0, columns[:, own + at : own + at + 1], more)
             grad[c, x] = plane
-
-
-def final_kernel(grad, wsum, rows, frame, out, wout, bout):
-    chan, count_x, count_y, _ = grad.shape
-    chan_out = wsum.shape[0]
+            ends[0, c, x] = plane[0:8]
+            ends[1, c, x] = plane[count_y - 8 : count_y]
+
+
+def final_kernel(whole, ends, mine, got_0, got_1, far, out, wout, bout, tiles, sems):
+    chan, count_x, count_y, _ = whole.shape
     own = chan * count_x
-    wide = own + 2 * chan
-    tall = frame.shape[0] - 2 * chan_out
-    total = joined(jnp.concatenate(split(wsum[...]), axis=0)) + joined(frame[tall:, :])
-    columns = pltpu.roll(frame[0:tall, :].astype(f32), lanes - 1, 1)
-    rest = jnp.zeros((lanes - chan_out - tall, lanes), f32)
-    total = jnp.concatenate([total, columns, rest], axis=0)
+    chan_out = mine.shape[0] // 2
+    row = iota((8, lanes), 0)
+    one, two = got_0[0:own, :].astype(f32), got_1[0:own, :].astype(f32)
+    above, below = pick("gy", two, one), pick("gy", one, two)
+    copies = []
+    for side, more, line in ((0, above, 0), (1, below, 7)):
+        for x in range(count_x):
+            for c in range(chan):
+                at = x * chan + c
+                extra = jnp.where(row == line, more[at : at + 1], 0.0)
+                tiles[side, c, x] = ends[side, c, x] + extra
+        copies.append(
+            pltpu.make_async_copy(
+                tiles.at[side],
+                out.at[:, :, pl.ds(side * (count_y - 8), 8), :],
+                sems.at[side],
+            )
+        )
+        copies[-1].start()
+    total = joined(mine[...]) + joined(far[...])
+    total = total + (joined(got_0[own:, :]) + joined(got_1[own:, :]))
+    total = jnp.concatenate([total, jnp.zeros((lanes - chan_out, lanes), f32)], axis=0)
     total = total.T
     for a in range(3):
         for be in range(9):
             at = (be * 3 + a) * chan
             wout[a * 9 + be] = total[at : at + chan, :chan_out]
     bout[...] = total[27 * chan : 27 * chan + 1, :chan_out]
-    spot = iota((count_y, lanes), 1)
-    row = iota((count_y, lanes), 0)
-    columns = total[0:count_y]
-    first, final = rows[0:own, :], rows[own : 2 * own, :]
-    for x in range(count_x):
-        for c in range(chan):
-            at = x * chan + c
-            r = chan_out + at
-            more = jnp.where(spot == lanes - 1, columns[:, r : r + 1], 0.0)
-            more = jnp.where(spot == 0, columns[:, own + r : own + r + 1], more)
-            more = more + jnp.where(row == 0, first[at : at + 1], 0.0)
-            more = more + jnp.where(row == count_y - 1, final[at : at + 1], 0.0)
-            out[c, x] = grad[c, x] + more
-
-
-def call(kernel, outs, scratch=(), cost=None):
+    for copy in copies:
+        copy.wait()
+
+
+def call(kernel, outs, scratch=(), cost=None, **rest):
     return pl.pallas_call(
         kernel,
         out_shape=outs,
+        **rest,
         scratch_shapes=list(scratch),
         cost_estimate=cost,
         compiler_params=pltpu.CompilerParams(vmem_limit_bytes=limit),
@@ -495,12 +496,15 @@
     face_1, face_0 = swapped(face_1, "gx", 1), swapped(face_0, "gx", 0)
 
     tall = 2 * wide
-    bundle = shape((body + 16 + tall + 2 * chan_out, lanes), bf16)
-    sums, field, face_0, face_1, wpart, wframe, rows, cols = call(
+    bundle = shape((16 + tall + 2 * chan_out, lanes), bf16)
+    face = shape((body, lanes), bf16)
+    sums, field, face_0, face_1, row_0, row_1, wpart, wframe, rows, cols = call(
         main_kernel,
         [
             pooled_rows,
             shape(((count_y + 2) * wide, lanes), f32),
+            face,
+            face,
             bundle,
             bundle,
             shape((chan_out, lanes), f32),
@@ -520,34 +524,31 @@
         ],
     )(cells, face_0, face_1, rows, left, right, spread, wbig, wback)
 
-    alone_x = lax.axis_size("gx") != 4
-    alone_y = lax.axis_size("gy") != 4
-    if alone_x:
+    alone = lax.axis_size("gx") != 4
+    if alone:
         wpart, far = lax.psum(wpart, "gx"), wframe
     else:
         far = swapped(wframe, "gx", 2)
+    row_1, row_0 = swapped(row_1, "gx", 1), swapped(row_0, "gx", 0)
     face_1, face_0 = swapped(face_1, "gx", 1), swapped(face_0, "gx", 0)
     pooled = call(pool_kernel, shape(cotangent.shape, bf16))(sums)
-    rows_out = shape((3 * own + 2 * chan_out, lanes), bf16)
-    wsum, row_0, row_1, cols = call(
-        functools.partial(x_kernel, alone_x),
-        [shape((chan_out, lanes), f32), rows_out, rows_out, shape((2 * own, lanes), f32)],
-    )(wpart, wframe, rows, cols, face_0, face_1, far)
-    grad = call(grad_kernel, shape(cells.shape, f32))(field, face_0, face_1)
-    if alone_y:
-        far, wsum = wframe, lax.psum(wsum, "gy")
-    else:
-        far = swapped(row_0[3 * own :], "gy", 2)
+    mine, rows = call(
+        functools.partial(x_kernel, alone),
+        [shape((2 * own + 2 * chan_out, lanes), bf16), shape((2 * own, lanes), f32)],
+    )(wpart, wframe, rows, cols, row_0, row_1, far)
+    frame = swapped(mine, "gz", 0)
+    bundle = shape((own + 2 * chan_out, lanes), bf16)
+    row_0, row_1, mine = call(
+        functools.partial(z_kernel, count_y),
+        [bundle, bundle, shape((2 * chan_out, lanes), bf16)],
+    )(mine, frame, rows)
     row_1, row_0 = swapped(row_1, "gy", 1), swapped(row_0, "gy", 0)
-    wsum, frame, rows = call(
-        functools.partial(y_kernel, alone_y, count_y),
-        [
-            shape((chan_out, lanes), f32),
-            shape((2 * own + 2 * chan_out, lanes), bf16),
-            shape((2 * own, lanes), f32),
-        ],
-    )(wsum, cols, row_0, row_1, far)
-    frame = swapped(frame, "gz", 0)
+    far = swapped(mine, "gy", 2)
+    tiles = (2, chan, count_x, 8, lanes)
+    grad, ends = call(grad_kernel, [shape(cells.shape, f32), shape(tiles, f32)])(
+        field, face_0, face_1, frame
+    )
+    vmem, anywhere = pl.BlockSpec(memory_space=pltpu.VMEM), pl.BlockSpec(memory_space=pl.ANY)
     input_grad, wsum, bias_grad = call(
         final_kernel,
         [
@@ -555,7 +556,11 @@
             shape((27, chan, chan_out), f32),
             shape((1, chan_out), f32),
         ],
-    )(grad, wsum, rows, frame)
+        [pltpu.VMEM(tiles, f32), pltpu.SemaphoreType.DMA((2,))],
+        in_specs=[anywhere] + [vmem] * 5,
+        out_specs=[anywhere, vmem, vmem],
+        input_output_aliases={0: 0},
+    )(grad, ends, mine, row_0, row_1, far)
     weight_grad = wsum.reshape(3, 3, 3, chan, chan_out).transpose(4, 3, 0, 1, 2)
     return (pooled, weight_grad, bias_grad.reshape(chan_out), input_grad)
 

time: 41.4 us -> 42.4 us (1.024)
  Pallas kernels: 9.07 us -> 10.1 us
  waiting for transfers between devices: 12.6 us -> 11.8 us
  starting transfers between devices: 17 us -> 17.7 us
    pallas_call x3, Pallas kernels: 0.23 us -> 1.29 us  [the longest x1 1.19 us: on_device(): call(grad_kernel, [shape(cells.shape, f32), shape(tiles, f32)])]
    ppermute x12 -> x14, waiting for transfers between devices: 12.6 us -> 11.8 us  [swapped(): return lax.ppermute(array, axis, pairs)]
    ppermute x12 -> x14, starting transfers between devices: 17 us -> 17.7 us  [swapped(): return lax.ppermute(array, axis, pairs)]
  transfers between devices with their start and end apart: 12 -> 14, of which waited for: 7 -> 7; matrix products, arithmetic and copies ran while one was open for 2% -> 2% of each run, Pallas kernels for 5% -> 8%
where the time goes in v7:
time: 42.4 us; the launch traced here: 42.2 us
  starting transfers between devices  17.7 us (42%)
  waiting for transfers between devices  11.8 us (28%)
  Pallas kernels  10.1 us (24%)
  local copies, waits for them, and re-layouts  1.63 us (4%)
  between operations  0.77 us (2%)
    ppermute x14, starting transfers between devices, swapped(): return lax.ppermute(array, axis, pairs)  17.7 us
    ppermute x14, waiting for transfers between devices, swapped(): return lax.ppermute(array, axis, pairs)  11.8 us
    pallas_call x1, Pallas kernels, on_device(): call(main_kernel, [pooled_rows, shape(((count_y + 2) * wide, lanes), f32)...  5.07 us
    pallas_call x1, Pallas kernels, on_device(): call(final_kernel, [shape(cells.shape, f32), shape((27, chan, chan_out),...  1.32 us
    pallas_call x1, Pallas kernels, on_device(): pooled = call(pool_kernel, shape(cotangent.shape, bf16))(sums)  1.23 us
    pallas_call x1, Pallas kernels, on_device(): call(grad_kernel, [shape(cells.shape, f32), shape(tiles, f32)])  1.19 us
    unnamed x10, local copies, waits for them, and re-layouts  0.97 us
    pallas_call x1, Pallas kernels, on_device(): spread = call(spread_kernel, pooled_rows)(cotangent)  0.88 us
  transfers between devices with their start and end apart: 14, of which 7 were waited for; matrix products, arithmetic and copies ran while one was open for 2% of the time, Pallas kernels for 8%

profile of v7, /device:TPU:0, one launch (start us, length us, event | category | flops | bytes accessed | tf_op | source)
XLA Modules:
  0.0 42.2 jit_solution(5564745663931688440)
XLA Ops:
  0.6 0.9 %copy-done = bf16[4,4,64,128]{3,2,1,0:T(8,128)(2,1)S(1)} copy-done((bf16[4,4,64,128]{3,2,1,0:T(8,128)(2,1)S(1)}, bf16[4,4,64,128]{3,2,1,0:T(8,128)(2,1)}, u32[]{:S(2)}) %copy-start) | copy-done | bytes 262168
  1.6 0.3 shard_map.75
  1.9 3.0 %collective-permute-start = (bf16[32,128]{1,0:T(8,128)(2,1)S(1)}, bf16[32,128]{1,0:T(8,128)(2,1)S(1)}, u32[]{:S(2)}, u32[]{:S(2)}) collective-permute-start(bf16[32,128]{1,0:T(8,128)(2,1)S(1)} %get-tuple-element.32), channel_id=1, source_target_pairs={{0,1},{1,0},{2,3},{3,2},{4,5},{5,4},{6,7},{7,6},{8,9},{9,8},{10,11... | collective-permute-start | bytes 24584 | tf_op jit(solution)/shard_map/ppermute | solution.py:39
  5.2 1.3 %collective-permute-done.edges = bf16[32,128]{1,0:T(8,128)(2,1)S(1)} collective-permute-done((bf16[32,128]{1,0:T(8,128)(2,1)S(1)}, bf16[32,128]{1,0:T(8,128)(2,1)S(1)}, u32[]{:S(2)}, u32[]{:S(2)}) %collective-permute-start) | collective-permute-done | bytes 8224 | tf_op jit(solution)/shard_map/ppermute | solution.py:39
  6.5 4.1 %collective-permute-start.2 = (bf16[48,128]{1,0:T(8,128)(2,1)S(1)}, bf16[48,128]{1,0:T(8,128)(2,1)S(1)}, u32[]{:S(2)}, u32[]{:S(2)}) collective-permute-start(bf16[48,128]{1,0:T(8,128)(2,1)S(1)} %get-tuple-element.64), channel_id=1, source_target_pairs={{0,6},{2,4},{4,2},{6,0},{1,7},{3,5},{5,3},{7,1},{8,14},{10,12},{12... | collective-permute-start | bytes 36872 | tf_op jit(solution)/shard_map/ppermute | solution.py:39
  11.1 1.1 %collective-permute-done.2.got_1 = bf16[48,128]{1,0:T(8,128)(2,1)S(1)} collective-permute-done((bf16[48,128]{1,0:T(8,128)(2,1)S(1)}, bf16[48,128]{1,0:T(8,128)(2,1)S(1)}, u32[]{:S(2)}, u32[]{:S(2)}) %collective-permute-start.2) | collective-permute-done | bytes 12320 | tf_op jit(solution)/shard_map/ppermute | solution.py:39
  12.3 2.0 %collective-permute-done.1.got_0 = bf16[48,128]{1,0:T(8,128)(2,1)S(1)} collective-permute-done((bf16[48,128]{1,0:T(8,128)(2,1)S(1)}, bf16[48,128]{1,0:T(8,128)(2,1)S(1)}, u32[]{:S(2)}, u32[]{:S(2)}) %collective-permute-start.1) | collective-permute-done | bytes 12320 | tf_op jit(solution)/shard_map/ppermute | solution.py:39
  14.4 1.6 %collective-permute-start.4 = (bf16[288,128]{1,0:T(8,128)(2,1)S(1)}, bf16[288,128]{1,0:T(8,128)(2,1)S(1)}, u32[]{:S(2)}, u32[]{:S(2)}) collective-permute-start(bf16[288,128]{1,0:T(8,128)(2,1)S(1)} %get-tuple-element.36), channel_id=1, source_target_pairs={{0,24},{8,16},{16,8},{24,0},{1,25},{9,17},{17,9},{25,1},{2,26},{10... | collective-permute-start | bytes 221192 | tf_op jit(solution)/shard_map/ppermute | solution.py:39
  16.1 0.9 %shard_map.77.spread = f32[2048,128]{1,0:T(8,128)S(1)} custom-call(bf16[32,2,32,64]{3,2,1,0:T(8,128)(2,1)S(1)} %copy-done.2), custom_call_target="tpu_custom_call" | custom-call | tf_op jit(solution)/shard_map/pallas_call | solution.py:486
  17.0 1.4 %collective-permute-done.4.got_1 = bf16[288,128]{1,0:T(8,128)(2,1)S(1)} collective-permute-done((bf16[288,128]{1,0:T(8,128)(2,1)S(1)}, bf16[288,128]{1,0:T(8,128)(2,1)S(1)}, u32[]{:S(2)}, u32[]{:S(2)}) %collective-permute-start.4) | collective-permute-done | bytes 73760 | tf_op jit(solution)/shard_map/ppermute | solution.py:39
  18.5 5.1 %shard_map.78 = (f32[2048,128]{1,0:T(8,128)S(1)}, f32[1584,128]{1,0:T(8,128)S(1)}, bf16[256,128]{1,0:T(8,128)(2,1)S(1)}, bf16[256,128]{1,0:T(8,128)(2,1)S(1)}, b...) custom-call(bf16[4,4,64,128]{3,2,1,0:T(8,128)(2,1)S(1)} %copy-done.1, ...), custom_call_target="tpu_custom_call" | custom-call | tf_op jit(solution)/shard_map/pallas_call | solution.py:501
  23.5 0.5 %collective-permute-start.7 = (bf16[128,128]{1,0:T(8,128)(2,1)S(1)}, bf16[128,128]{1,0:T(8,128)(2,1)S(1)}, u32[]{:S(2)}, u32[]{:S(2)}) collective-permute-start(bf16[128,128]{1,0:T(8,128)(2,1)S(1)} %get-tuple-element.48), channel_id=1, source_target_pairs={{0,8},{8,0},{16,24},{24,16},{1,9},{9,1},{17,25},{25,17},{2,10},{10... | collective-permute-start | bytes 98312 | tf_op jit(solution)/shard_map/ppermute | solution.py:39
  24.0 1.2 %collective-permute-start.8 = (bf16[128,128]{1,0:T(8,128)(2,1)S(1)}, bf16[128,128]{1,0:T(8,128)(2,1)S(1)}, u32[]{:S(2)}, u32[]{:S(2)}) collective-permute-start(bf16[128,128]{1,0:T(8,128)(2,1)S(1)} %get-tuple-element.49), channel_id=1, source_target_pairs={{0,24},{8,16},{16,8},{24,0},{1,25},{9,17},{17,9},{25,1},{2,26},{10... | collective-permute-start | bytes 98312 | tf_op jit(solution)/shard_map/ppermute | solution.py:39
  25.2 0.4 collective-permute-start.5
  25.9 1.5 %collective-permute-start.9 = (bf16[64,128]{1,0:T(8,128)(2,1)S(1)}, bf16[64,128]{1,0:T(8,128)(2,1)S(1)}, u32[]{:S(2)}, u32[]{:S(2)}) collective-permute-start(bf16[64,128]{1,0:T(8,128)(2,1)S(1)} %get-tuple-element.45.wframe), channel_id=1, source_target_pairs={{0,16},{8,24},{16,0},{24,8},{1,17},{9,25},{17,1},{25,9},{2,18},{10... | collective-permute-start | bytes 49160 | tf_op jit(solution)/shard_map/ppermute | solution.py:39
  27.4 3.0 %collective-permute-done.9.far = bf16[64,128]{1,0:T(8,128)(2,1)S(1)} collective-permute-done((bf16[64,128]{1,0:T(8,128)(2,1)S(1)}, bf16[64,128]{1,0:T(8,128)(2,1)S(1)}, u32[]{:S(2)}, u32[]{:S(2)}) %collective-permute-start.9) | collective-permute-done | bytes 16416 | tf_op jit(solution)/shard_map/ppermute | solution.py:39
  30.4 1.6 %collective-permute-start.10 = (bf16[96,128]{1,0:T(8,128)(2,1)S(1)}, bf16[96,128]{1,0:T(8,128)(2,1)S(1)}, u32[]{:S(2)}, u32[]{:S(2)}) collective-permute-start(bf16[96,128]{1,0:T(8,128)(2,1)S(1)} %get-tuple-element.50.mine), channel_id=1, source_target_pairs={{0,1},{1,0},{2,3},{3,2},{4,5},{5,4},{6,7},{7,6},{8,9},{9,8},{10,11... | collective-permute-start | bytes 73736 | tf_op jit(solution)/shard_map/ppermute | solution.py:39
  32.0 2.3 %collective-permute-done.10.got = bf16[96,128]{1,0:T(8,128)(2,1)S(1)} collective-permute-done((bf16[96,128]{1,0:T(8,128)(2,1)S(1)}, bf16[96,128]{1,0:T(8,128)(2,1)S(1)}, u32[]{:S(2)}, u32[]{:S(2)}) %collective-permute-start.10) | collective-permute-done | bytes 24608 | tf_op jit(solution)/shard_map/ppermute | solution.py:39
  34.5 1.8 %collective-permute-start.12 = (bf16[80,128]{1,0:T(8,128)(2,1)S(1)}, bf16[80,128]{1,0:T(8,128)(2,1)S(1)}, u32[]{:S(2)}, u32[]{:S(2)}) collective-permute-start(bf16[80,128]{1,0:T(8,128)(2,1)S(1)} %get-tuple-element.56), channel_id=1, source_target_pairs={{0,6},{2,4},{4,2},{6,0},{1,7},{3,5},{5,3},{7,1},{8,14},{10,12},{12... | collective-permute-start | bytes 61448 | tf_op jit(solution)/shard_map/ppermute | solution.py:39
  36.3 1.6 %collective-permute-start.13 = (bf16[64,128]{1,0:T(8,128)(2,1)S(1)}, bf16[64,128]{1,0:T(8,128)(2,1)S(1)}, u32[]{:S(2)}, u32[]{:S(2)}) collective-permute-start(bf16[64,128]{1,0:T(8,128)(2,1)S(1)} %get-tuple-element.54.mine), channel_id=1, source_target_pairs={{0,4},{2,6},{4,0},{6,2},{1,5},{3,7},{5,1},{7,3},{8,12},{10,14},{12... | collective-permute-start | bytes 49160 | tf_op jit(solution)/shard_map/ppermute | solution.py:39
  37.9 1.2 %shard_map.79 = bf16[32,2,32,64]{3,2,1,0:T(8,128)(2,1)} custom-call(f32[2048,128]{1,0:T(8,128)S(1)} %get-tuple-element.40.sums), custom_call_target="tpu_custom_call" | custom-call | tf_op jit(solution)/shard_map/pallas_call | solution.py:534
  39.1 1.2 %shard_map.81 = (f32[4,4,64,128]{3,2,1,0:T(8,128)}, f32[2,4,4,8,128]{4,3,2,1,0:T(8,128)S(1)}) custom-call(f32[1584,128]{1,0:T(8,128)S(1)} %get-tuple-element.41.field, bf16[256,128]{1,0:T(8,128)(2,1)S(1)} %collective-permute-done.5.face_0, bf16[256,128]{1,0:T(8,128)(2,1)S(1)} %collective-permute-done.6.face_1, bf16[96,128]{1,0:T(8,128)(2,1)S(1)} %collective-permute-done.10.got), custom_call_target="tpu_custom_call" | custom-call | tf_op jit(solution)/shard_map/pallas_call | solution.py:548
  40.3 0.6 %collective-permute-done.13.far = bf16[64,128]{1,0:T(8,128)(2,1)S(1)} collective-permute-done((bf16[64,128]{1,0:T(8,128)(2,1)S(1)}, bf16[64,128]{1,0:T(8,128)(2,1)S(1)}, u32[]{:S(2)}, u32[]{:S(2)}) %collective-permute-start.13) | collective-permute-done | bytes 16416 | tf_op jit(solution)/shard_map/ppermute | solution.py:39
  40.9 1.3 %shard_map.83 = (f32[4,4,64,128]{3,2,1,0:T(8,128)}, f32[27,4,32]{2,1,0:T(4,128)}, f32[1,32]{1,0:T(1,128)}) custom-call(f32[4,4,64,128]{3,2,1,0:T(8,128)} %get-tuple-element.51.whole, f32[2,4,4,8,128]{4,3,2,1,0:T(8,128)S(1)} %get-tuple-element.52.ends, bf16[64,128]{1,0:T(8,128)(2,1)S(1)} %get-tuple-element.54.mine, ...), custom_call_target="tpu_custom_call", output_to_operand_aliasing={{0}: (0, {})} | custom-call | tf_op jit(solution)/shard_map/pallas_call | solution.py:552
  (35 shorter events, 1.6 us)
Async XLA Ops:
  0.6 1.0 %copy-start = (bf16[4,4,64,128]{3,2,1,0:T(8,128)(2,1)S(1)}, bf16[4,4,64,128]{3,2,1,0:T(8,128)(2,1)}, u32[]{:S(2)}) copy-start(bf16[4,4,64,128]{3,2,1,0:T(8,128)(2,1)} %cells.5) | copy-start | bytes 786436
  1.6 3.3 %copy-start.3 = (bf16[32,4,3,3,3]{0,1,4,3,2:T(4,128)(2,1)S(1)}, bf16[32,4,3,3,3]{0,1,4,3,2:T(4,128)(2,1)}, u32[]{:S(2)}) copy-start(bf16[32,4,3,3,3]{0,1,4,3,2:T(4,128)(2,1)} %param.5) | copy-start | bytes 20740
  1.9 3.0 %copy-start.4 = (f32[32]{0:T(128)S(1)}, f32[32]{0:T(128)}, u32[]{:S(2)}) copy-start(f32[32]{0:T(128)} %param.6) | copy-start | bytes 388
  1.9 4.6 %collective-permute-start = (bf16[32,128]{1,0:T(8,128)(2,1)S(1)}, bf16[32,128]{1,0:T(8,128)(2,1)S(1)}, u32[]{:S(2)}, u32[]{:S(2)}) collective-permute-start(bf16[32,128]{1,0:T(8,128)(2,1)S(1)} %get-tuple-element.32), channel_id=1, source_target_pairs={{0,1},{1,0},{2,3},{3,2},{4,5},{5,4},{6,7},{7,6},{8,9},{9,8},{10,11... | collective-permute-start | bytes 24584 | tf_op jit(solution)/shard_map/ppermute | solution.py:39
  6.5 5.8 %collective-permute-start.2 = (bf16[48,128]{1,0:T(8,128)(2,1)S(1)}, bf16[48,128]{1,0:T(8,128)(2,1)S(1)}, u32[]{:S(2)}, u32[]{:S(2)}) collective-permute-start(bf16[48,128]{1,0:T(8,128)(2,1)S(1)} %get-tuple-element.64), channel_id=1, source_target_pairs={{0,6},{2,4},{4,2},{6,0},{1,7},{3,5},{5,3},{7,1},{8,14},{10,12},{12... | collective-permute-start | bytes 36872 | tf_op jit(solution)/shard_map/ppermute | solution.py:39
  10.6 3.7 %collective-permute-start.1 = (bf16[48,128]{1,0:T(8,128)(2,1)S(1)}, bf16[48,128]{1,0:T(8,128)(2,1)S(1)}, u32[]{:S(2)}, u32[]{:S(2)}) collective-permute-start(bf16[48,128]{1,0:T(8,128)(2,1)S(1)} %get-tuple-element.65), channel_id=1, source_target_pairs={{0,2},{2,0},{4,6},{6,4},{1,3},{3,1},{5,7},{7,5},{8,10},{10,8},{12,... | collective-permute-start | bytes 36872 | tf_op jit(solution)/shard_map/ppermute | solution.py:39
  10.7 3.6 %copy-start.1 = (bf16[4,4,64,128]{3,2,1,0:T(8,128)(2,1)S(1)}, bf16[4,4,64,128]{3,2,1,0:T(8,128)(2,1)}, u32[]{:S(2)}) copy-start(bf16[4,4,64,128]{3,2,1,0:T(8,128)(2,1)} %cells.5) | copy-start | bytes 786436
  10.7 5.4 %copy-start.2 = (bf16[32,2,32,64]{3,2,1,0:T(8,128)(2,1)S(1)}, bf16[32,2,32,64]{3,2,1,0:T(8,128)(2,1)}, u32[]{:S(2)}) copy-start(bf16[32,2,32,64]{3,2,1,0:T(8,128)(2,1)} %cot.1) | copy-start | bytes 786436
  14.4 2.7 %collective-permute-start.3 = (bf16[288,128]{1,0:T(8,128)(2,1)S(1)}, bf16[288,128]{1,0:T(8,128)(2,1)S(1)}, u32[]{:S(2)}, u32[]{:S(2)}) collective-permute-start(bf16[288,128]{1,0:T(8,128)(2,1)S(1)} %get-tuple-element.35), channel_id=1, source_target_pairs={{0,8},{8,0},{16,24},{24,16},{1,9},{9,1},{17,25},{25,17},{2,10},{10... | collective-permute-start | bytes 221192 | tf_op jit(solution)/shard_map/ppermute | solution.py:39
  14.4 4.1 %collective-permute-start.4 = (bf16[288,128]{1,0:T(8,128)(2,1)S(1)}, bf16[288,128]{1,0:T(8,128)(2,1)S(1)}, u32[]{:S(2)}, u32[]{:S(2)}) collective-permute-start(bf16[288,128]{1,0:T(8,128)(2,1)S(1)} %get-tuple-element.36), channel_id=1, source_target_pairs={{0,24},{8,16},{16,8},{24,0},{1,25},{9,17},{17,9},{25,1},{2,26},{10... | collective-permute-start | bytes 221192 | tf_op jit(solution)/shard_map/ppermute | solution.py:39
  23.5 6.8 %collective-permute-start.7 = (bf16[128,128]{1,0:T(8,128)(2,1)S(1)}, bf16[128,128]{1,0:T(8,128)(2,1)S(1)}, u32[]{:S(2)}, u32[]{:S(2)}) collective-permute-start(bf16[128,128]{1,0:T(8,128)(2,1)S(1)} %get-tuple-element.48), channel_id=1, source_target_pairs={{0,8},{8,0},{16,24},{24,16},{1,9},{9,1},{17,25},{25,17},{2,10},{10... | collective-permute-start | bytes 98312 | tf_op jit(solution)/shard_map/ppermute | solution.py:39
  24.0 6.4 %collective-permute-start.8 = (bf16[128,128]{1,0:T(8,128)(2,1)S(1)}, bf16[128,128]{1,0:T(8,128)(2,1)S(1)}, u32[]{:S(2)}, u32[]{:S(2)}) collective-permute-start(bf16[128,128]{1,0:T(8,128)(2,1)S(1)} %get-tuple-element.49), channel_id=1, source_target_pairs={{0,24},{8,16},{16,8},{24,0},{1,25},{9,17},{17,9},{25,1},{2,26},{10... | collective-permute-start | bytes 98312 | tf_op jit(solution)/shard_map/ppermute | solution.py:39
  25.2 13.9 %collective-permute-start.5 = (bf16[256,128]{1,0:T(8,128)(2,1)S(1)}, bf16[256,128]{1,0:T(8,128)(2,1)S(1)}, u32[]{:S(2)}, u32[]{:S(2)}) collective-permute-start(bf16[256,128]{1,0:T(8,128)(2,1)S(1)} %get-tuple-element.42), channel_id=1, source_target_pairs={{0,8},{8,0},{16,24},{24,16},{1,9},{9,1},{17,25},{25,17},{2,10},{10... | collective-permute-start | bytes 196616 | tf_op jit(solution)/shard_map/ppermute | solution.py:39
  25.6 13.5 %collective-permute-start.6 = (bf16[256,128]{1,0:T(8,128)(2,1)S(1)}, bf16[256,128]{1,0:T(8,128)(2,1)S(1)}, u32[]{:S(2)}, u32[]{:S(2)}) collective-permute-start(bf16[256,128]{1,0:T(8,128)(2,1)S(1)} %get-tuple-element.43), channel_id=1, source_target_pairs={{0,24},{8,16},{16,8},{24,0},{1,25},{9,17},{17,9},{25,1},{2,26},{10... | collective-permute-start | bytes 196616 | tf_op jit(solution)/shard_map/ppermute | solution.py:39
  25.9 4.5 %collective-permute-start.9 = (bf16[64,128]{1,0:T(8,128)(2,1)S(1)}, bf16[64,128]{1,0:T(8,128)(2,1)S(1)}, u32[]{:S(2)}, u32[]{:S(2)}) collective-permute-start(bf16[64,128]{1,0:T(8,128)(2,1)S(1)} %get-tuple-element.45.wframe), channel_id=1, source_target_pairs={{0,16},{8,24},{16,0},{24,8},{1,17},{9,25},{17,1},{25,9},{2,18},{10... | collective-permute-start | bytes 49160 | tf_op jit(solution)/shard_map/ppermute | solution.py:39
  30.4 3.9 %collective-permute-start.10 = (bf16[96,128]{1,0:T(8,128)(2,1)S(1)}, bf16[96,128]{1,0:T(8,128)(2,1)S(1)}, u32[]{:S(2)}, u32[]{:S(2)}) collective-permute-start(bf16[96,128]{1,0:T(8,128)(2,1)S(1)} %get-tuple-element.50.mine), channel_id=1, source_target_pairs={{0,1},{1,0},{2,3},{3,2},{4,5},{5,4},{6,7},{7,6},{8,9},{9,8},{10,11... | collective-permute-start | bytes 73736 | tf_op jit(solution)/shard_map/ppermute | solution.py:39
  34.4 6.5 %collective-permute-start.11 = (bf16[80,128]{1,0:T(8,128)(2,1)S(1)}, bf16[80,128]{1,0:T(8,128)(2,1)S(1)}, u32[]{:S(2)}, u32[]{:S(2)}) collective-permute-start(bf16[80,128]{1,0:T(8,128)(2,1)S(1)} %get-tuple-element.55), channel_id=1, source_target_pairs={{0,2},{2,0},{4,6},{6,4},{1,3},{3,1},{5,7},{7,5},{8,10},{10,8},{12,... | collective-permute-start | bytes 61448 | tf_op jit(solution)/shard_map/ppermute | solution.py:39
  34.5 6.4 %collective-permute-start.12 = (bf16[80,128]{1,0:T(8,128)(2,1)S(1)}, bf16[80,128]{1,0:T(8,128)(2,1)S(1)}, u32[]{:S(2)}, u32[]{:S(2)}) collective-permute-start(bf16[80,128]{1,0:T(8,128)(2,1)S(1)} %get-tuple-element.56), channel_id=1, source_target_pairs={{0,6},{2,4},{4,2},{6,0},{1,7},{3,5},{5,3},{7,1},{8,14},{10,12},{12... | collective-permute-start | bytes 61448 | tf_op jit(solution)/shard_map/ppermute | solution.py:39
  36.3 4.6 %collective-permute-start.13 = (bf16[64,128]{1,0:T(8,128)(2,1)S(1)}, bf16[64,128]{1,0:T(8,128)(2,1)S(1)}, u32[]{:S(2)}, u32[]{:S(2)}) collective-permute-start(bf16[64,128]{1,0:T(8,128)(2,1)S(1)} %get-tuple-element.54.mine), channel_id=1, source_target_pairs={{0,4},{2,6},{4,0},{6,2},{1,5},{3,7},{5,1},{7,3},{8,12},{10,14},{12... | collective-permute-start | bytes 49160 | tf_op jit(solution)/shard_map/ppermute | solution.py:39

commit v8 on v7

--- a/solution.py
+++ b/solution.py
@@ -60,12 +60,12 @@
 def pack_kernel(cells, edges, sent_0, sent_1, rows):
     chan, count_x, count_y, _ = cells.shape
     count = chan * count_x
-    planes = [cells[c, x] for x in range(count_x) for c in range(chan)]
-    wide = jnp.concatenate(planes, axis=1)
     row = iota((2 * count, count * lanes), 0)
     lane = iota((2 * count, count * lanes), 1)
     want = jnp.where(row < count, row * lanes, (row - count) * lanes + lanes - 1)
     chosen = (lane == want).astype(f32).astype(bf16)
+    planes = [cells[c, x] for x in range(count_x) for c in range(chan)]
+    wide = jnp.concatenate(planes, axis=1)
     found = dot(chosen, wide, ((1,), (1,)))
     found = jnp.concatenate([found, jnp.zeros((2 * count, lanes - count_y), f32)], axis=1)
     edges[...] = pltpu.roll(found, 1, 1).astype(bf16)
@@ -138,7 +138,7 @@
 
 def main_kernel(
     cells, got_0, got_1, rows_in, left_in, right_in, spread, wbig, wback,
-    sums, field, face_0, face_1, sent_0, sent_1, wpart, wframe, rows_out, cols,
+    sums, field, sent_0, sent_1, wpart, wframe, rows_out, cols,
     stage, patches, left, right, carry, gram, delta_a, delta_b,
 ):
     chan, count_x, count_y, _ = cells.shape
@@ -318,15 +318,8 @@
     tall = cols.shape[0]
     found = cols[...].astype(bf16)
     zero = jnp.zeros((8, lanes), f32)
-    for face, ref, odd in ((face_0, sent_0, 0), (face_1, sent_1, 1)):
+    for ref, odd in ((sent_0, 0), (sent_1, 1)):
         high = even != (odd == 1)
-        for c in range(chan):
-            low_plane, high_plane = [
-                field[pl.ds(wide + x * chan + c, count_y, stride=wide), :]
-                for x in (0, count_x + 1)
-            ]
-            plane = jnp.where(high, high_plane, low_plane)
-            face[c * count_y : (c + 1) * count_y, :] = plane.astype(bf16)
         low_frame, high_frame = [
             jnp.concatenate([end[x * chan : (x + 1) * chan] for end in ends] + [zero], axis=0)
             for x in (0, count_x + 1)
@@ -334,6 +327,19 @@
         ref[0:16, :] = jnp.where(high, high_frame, low_frame).astype(bf16)
         ref[16 : 16 + tall, :] = found
         ref[16 + tall :, :] = sides
+
+
+def face_kernel(chan, field, face_0, face_1):
+    count_y = face_0.shape[0] // chan
+    wide = field.shape[0] // (count_y + 2)
+    even = is_even("gx")
+    for c in range(chan):
+        low, high = [
+            field[pl.ds(wide + at + c, count_y, stride=wide), :] for at in (0, wide - chan)
+        ]
+        place = slice(c * count_y, (c + 1) * count_y)
+        face_0[place, :] = jnp.where(even, high, low).astype(bf16)
+        face_1[place, :] = jnp.where(even, low, high).astype(bf16)
 
 
 def x_kernel(alone, wpart, wframe, rows, cols, got_0, got_1, far, frame, rows_out):
@@ -344,7 +350,7 @@
     if alone:
         total = wpart[...]
     else:
-        total = joined(wframe[...]) + joined(far[...])
+        total = joined(wframe[...]) + joined(far[16 + tall :, :])
         total = total + (joined(got_0[16 + tall :, :]) + joined(got_1[16 + tall :, :]))
     frame[2 * own :, :] = jnp.concatenate(split(total), axis=0)
     one, two = got_0[0 : 16 + tall, :].astype(f32), got_1[0 : 16 + tall, :].astype(f32)
@@ -406,7 +412,7 @@
             ends[1, c, x] = plane[count_y - 8 : count_y]
 
 
-def final_kernel(whole, ends, mine, got_0, got_1, far, out, wout, bout, tiles, sems):
+def final_kernel(whole, ends, mine, got_0, got_1, far, out, wout, bout, tiles, wtile, btile, sems):
     chan, count_x, count_y, _ = whole.shape
     own = chan * count_x
     chan_out = mine.shape[0] // 2
@@ -435,10 +441,18 @@
     for a in range(3):
         for be in range(9):
             at = (be * 3 + a) * chan
-            wout[a * 9 + be] = total[at : at + chan, :chan_out]
-    bout[...] = total[27 * chan : 27 * chan + 1, :chan_out]
+            wtile[a * 9 + be] = total[at : at + chan, :chan_out]
+    btile[...] = total[27 * chan : 27 * chan + 1, :chan_out]
+    copies.append(pltpu.make_async_copy(wtile, wout, sems.at[2]))
+    copies.append(pltpu.make_async_copy(btile, bout, sems.at[3]))
+    copies[2].start()
+    copies[3].start()
     for copy in copies:
         copy.wait()
+
+
+def traffic(mib):
+    return pl.CostEstimate(flops=0, bytes_accessed=mib << 20, transcendentals=0)
 
 
 def call(kernel, outs, scratch=(), cost=None, **rest):
@@ -479,7 +493,9 @@
     edges, row_0, row_1 = call(
         pack_kernel,
         [shape((2 * own, lanes), bf16), own_block, own_block],
-        [pltpu.VMEM((2 * own, lanes), f32)],
+        [
+            pltpu.VMEM((2 * own, lanes), f32),
+        ],
     )(cells)
     pool_x, pool_y, pool_z = cotangent.shape[1:]
     pooled_rows = shape((pool_y * pool_x * chan_out, lanes), f32)
@@ -498,13 +514,11 @@
     tall = 2 * wide
     bundle = shape((16 + tall + 2 * chan_out, lanes), bf16)
     face = shape((body, lanes), bf16)
-    sums, field, face_0, face_1, row_0, row_1, wpart, wframe, rows, cols = call(
+    sums, field, row_0, row_1, wpart, wframe, rows, cols = call(
         main_kernel,
         [
             pooled_rows,
             shape(((count_y + 2) * wide, lanes), f32),
-            face,
-            face,
             bundle,
             bundle,
             shape((chan_out, lanes), f32),
@@ -526,12 +540,13 @@
 
     alone = lax.axis_size("gx") != 4
     if alone:
-        wpart, far = lax.psum(wpart, "gx"), wframe
+        wpart, far = lax.psum(wpart, "gx"), row_0
     else:
-        far = swapped(wframe, "gx", 2)
+        far = swapped(row_0, "gx", 2)
     row_1, row_0 = swapped(row_1, "gx", 1), swapped(row_0, "gx", 0)
+    face_0, face_1 = call(functools.partial(face_kernel, chan), [face, face], cost=traffic(2))(field)
     face_1, face_0 = swapped(face_1, "gx", 1), swapped(face_0, "gx", 0)
-    pooled = call(pool_kernel, shape(cotangent.shape, bf16))(sums)
+    pooled = call(pool_kernel, shape(cotangent.shape, bf16), cost=traffic(8))(sums)
     mine, rows = call(
         functools.partial(x_kernel, alone),
         [shape((2 * own + 2 * chan_out, lanes), bf16), shape((2 * own, lanes), f32)],
@@ -545,7 +560,7 @@
     row_1, row_0 = swapped(row_1, "gy", 1), swapped(row_0, "gy", 0)
     far = swapped(mine, "gy", 2)
     tiles = (2, chan, count_x, 8, lanes)
-    grad, ends = call(grad_kernel, [shape(cells.shape, f32), shape(tiles, f32)])(
+    grad, ends = call(grad_kernel, [shape(cells.shape, f32), shape(tiles, f32)], cost=traffic(8))(
         field, face_0, face_1, frame
     )
     vmem, anywhere = pl.BlockSpec(memory_space=pltpu.VMEM), pl.BlockSpec(memory_space=pl.ANY)
@@ -556,9 +571,14 @@
             shape((27, chan, chan_out), f32),
             shape((1, chan_out), f32),
         ],
-        [pltpu.VMEM(tiles, f32), pltpu.SemaphoreType.DMA((2,))],
+        [
+            pltpu.VMEM(tiles, f32),
+            pltpu.VMEM((27, chan, chan_out), f32),
+            pltpu.VMEM((1, chan_out), f32),
+            pltpu.SemaphoreType.DMA((4,)),
+        ],
         in_specs=[anywhere] + [vmem] * 5,
-        out_specs=[anywhere, vmem, vmem],
+        out_specs=[anywhere] * 3,
         input_output_aliases={0: 0},
     )(grad, ends, mine, row_0, row_1, far)
     weight_grad = wsum.reshape(3, 3, 3, chan, chan_out).transpose(4, 3, 0, 1, 2)

time: 42.4 us -> 40.5 us (0.955)
  waiting for transfers between devices: 11.8 us -> 10.4 us
  Pallas kernels: 10.1 us -> 9.64 us
    ppermute x14, waiting for transfers between devices: 11.8 us -> 10.4 us  [swapped(): return lax.ppermute(array, axis, pairs)]
    pallas_call x1, Pallas kernels: 1.32 us -> 0.76 us  [on_device(): call(final_kernel, [shape(cells.shape, f32), shape((27, chan, chan_out),...]
    pallas_call x2 -> x3, Pallas kernels: 2.43 us -> 2.47 us  [the longest x1 1.24 us: on_device(): call(pool_kernel, shape(cotangent.shape, bf16), cost=traffic(8))(sums)]
  transfers between devices with their start and end apart: 14 -> 14, of which waited for: 7 -> 7; matrix products, arithmetic and copies ran while one was open for 2% -> 2% of each run, Pallas kernels for 8% -> 9%
where the time goes in v8:
time: 40.5 us; the launch traced here: 40.3 us
  starting transfers between devices  17.7 us (44%)
  waiting for transfers between devices  10.4 us (26%)
  Pallas kernels  9.64 us (24%)
  local copies, waits for them, and re-layouts  1.63 us (4%)
  between operations  0.77 us (2%)
    ppermute x14, starting transfers between devices, swapped(): return lax.ppermute(array, axis, pairs)  17.7 us
    ppermute x14, waiting for transfers between devices, swapped(): return lax.ppermute(array, axis, pairs)  10.4 us
    pallas_call x1, Pallas kernels, on_device(): call(main_kernel, [pooled_rows, shape(((count_y + 2) * wide, lanes), f32)...  5.08 us
    pallas_call x1, Pallas kernels, on_device(): call(pool_kernel, shape(cotangent.shape, bf16), cost=traffic(8))(sums)  1.24 us
    pallas_call x1, Pallas kernels, on_device(): call(grad_kernel, [shape(cells.shape, f32), shape(tiles, f32)], cost=traf...  1.19 us
    unnamed x10, local copies, waits for them, and re-layouts  0.97 us
    pallas_call x1, Pallas kernels, on_device(): spread = call(spread_kernel, pooled_rows)(cotangent)  0.88 us
  transfers between devices with their start and end apart: 14, of which 7 were waited for; matrix products, arithmetic and copies ran while one was open for 2% of the time, Pallas kernels for 9%

profile of v8, /device:TPU:0, one launch (start us, length us, event | category | flops | bytes accessed | tf_op | source)
XLA Modules:
  0.0 40.3 jit_solution(14580059674522249990)
XLA Ops:
  0.6 0.9 %copy-done = bf16[4,4,64,128]{3,2,1,0:T(8,128)(2,1)S(1)} copy-done((bf16[4,4,64,128]{3,2,1,0:T(8,128)(2,1)S(1)}, bf16[4,4,64,128]{3,2,1,0:T(8,128)(2,1)}, u32[]{:S(2)}) %copy-start) | copy-done | bytes 262168
  1.6 0.3 shard_map.75
  1.9 3.0 %collective-permute-start = (bf16[32,128]{1,0:T(8,128)(2,1)S(1)}, bf16[32,128]{1,0:T(8,128)(2,1)S(1)}, u32[]{:S(2)}, u32[]{:S(2)}) collective-permute-start(bf16[32,128]{1,0:T(8,128)(2,1)S(1)} %get-tuple-element.32), channel_id=1, source_target_pairs={{0,1},{1,0},{2,3},{3,2},{4,5},{5,4},{6,7},{7,6},{8,9},{9,8},{10,11... | collective-permute-start | bytes 24584 | tf_op jit(solution)/shard_map/ppermute | solution.py:39
  5.2 1.3 %collective-permute-done.edges = bf16[32,128]{1,0:T(8,128)(2,1)S(1)} collective-permute-done((bf16[32,128]{1,0:T(8,128)(2,1)S(1)}, bf16[32,128]{1,0:T(8,128)(2,1)S(1)}, u32[]{:S(2)}, u32[]{:S(2)}) %collective-permute-start) | collective-permute-done | bytes 8224 | tf_op jit(solution)/shard_map/ppermute | solution.py:39
  6.5 4.1 %collective-permute-start.2 = (bf16[48,128]{1,0:T(8,128)(2,1)S(1)}, bf16[48,128]{1,0:T(8,128)(2,1)S(1)}, u32[]{:S(2)}, u32[]{:S(2)}) collective-permute-start(bf16[48,128]{1,0:T(8,128)(2,1)S(1)} %get-tuple-element.64), channel_id=1, source_target_pairs={{0,6},{2,4},{4,2},{6,0},{1,7},{3,5},{5,3},{7,1},{8,14},{10,12},{12... | collective-permute-start | bytes 36872 | tf_op jit(solution)/shard_map/ppermute | solution.py:39
  11.1 1.1 %collective-permute-done.2.got_1 = bf16[48,128]{1,0:T(8,128)(2,1)S(1)} collective-permute-done((bf16[48,128]{1,0:T(8,128)(2,1)S(1)}, bf16[48,128]{1,0:T(8,128)(2,1)S(1)}, u32[]{:S(2)}, u32[]{:S(2)}) %collective-permute-start.2) | collective-permute-done | bytes 12320 | tf_op jit(solution)/shard_map/ppermute | solution.py:39
  12.3 2.0 %collective-permute-done.1.got_0 = bf16[48,128]{1,0:T(8,128)(2,1)S(1)} collective-permute-done((bf16[48,128]{1,0:T(8,128)(2,1)S(1)}, bf16[48,128]{1,0:T(8,128)(2,1)S(1)}, u32[]{:S(2)}, u32[]{:S(2)}) %collective-permute-start.1) | collective-permute-done | bytes 12320 | tf_op jit(solution)/shard_map/ppermute | solution.py:39
  14.4 1.6 %collective-permute-start.4 = (bf16[288,128]{1,0:T(8,128)(2,1)S(1)}, bf16[288,128]{1,0:T(8,128)(2,1)S(1)}, u32[]{:S(2)}, u32[]{:S(2)}) collective-permute-start(bf16[288,128]{1,0:T(8,128)(2,1)S(1)} %get-tuple-element.36), channel_id=1, source_target_pairs={{0,24},{8,16},{16,8},{24,0},{1,25},{9,17},{17,9},{25,1},{2,26},{10... | collective-permute-start | bytes 221192 | tf_op jit(solution)/shard_map/ppermute | solution.py:39
  16.1 0.9 %shard_map.77.spread = f32[2048,128]{1,0:T(8,128)S(1)} custom-call(bf16[32,2,32,64]{3,2,1,0:T(8,128)(2,1)S(1)} %copy-done.2), custom_call_target="tpu_custom_call" | custom-call | tf_op jit(solution)/shard_map/pallas_call | solution.py:502
  17.0 1.4 %collective-permute-done.4.got_1 = bf16[288,128]{1,0:T(8,128)(2,1)S(1)} collective-permute-done((bf16[288,128]{1,0:T(8,128)(2,1)S(1)}, bf16[288,128]{1,0:T(8,128)(2,1)S(1)}, u32[]{:S(2)}, u32[]{:S(2)}) %collective-permute-start.4) | collective-permute-done | bytes 73760 | tf_op jit(solution)/shard_map/ppermute | solution.py:39
  18.5 5.1 %shard_map.78 = (f32[2048,128]{1,0:T(8,128)S(1)}, f32[1584,128]{1,0:T(8,128)S(1)}, bf16[128,128]{1,0:T(8,128)(2,1)S(1)}, bf16[128,128]{1,0:T(8,128)(2,1)S(1)}, f...) custom-call(bf16[4,4,64,128]{3,2,1,0:T(8,128)(2,1)S(1)} %copy-done.1, ...), custom_call_target="tpu_custom_call" | custom-call | tf_op jit(solution)/shard_map/pallas_call | solution.py:517
  23.6 1.6 %collective-permute-start.8 = (bf16[128,128]{1,0:T(8,128)(2,1)S(1)}, bf16[128,128]{1,0:T(8,128)(2,1)S(1)}, u32[]{:S(2)}, u32[]{:S(2)}) collective-permute-start(bf16[128,128]{1,0:T(8,128)(2,1)S(1)} %get-tuple-element.49), channel_id=1, source_target_pairs={{0,24},{8,16},{16,8},{24,0},{1,25},{9,17},{17,9},{25,1},{2,26},{10... | collective-permute-start | bytes 98312 | tf_op jit(solution)/shard_map/ppermute | solution.py:39
  25.1 0.5 %collective-permute-start.9 = (bf16[128,128]{1,0:T(8,128)(2,1)S(1)}, bf16[128,128]{1,0:T(8,128)(2,1)S(1)}, u32[]{:S(2)}, u32[]{:S(2)}) collective-permute-start(bf16[128,128]{1,0:T(8,128)(2,1)S(1)} %get-tuple-element.48), channel_id=1, source_target_pairs={{0,16},{8,24},{16,0},{24,8},{1,17},{9,25},{17,1},{25,9},{2,18},{10... | collective-permute-start | bytes 98312 | tf_op jit(solution)/shard_map/ppermute | solution.py:39
  25.7 0.6 %collective-permute-start.5 = (bf16[256,128]{1,0:T(8,128)(2,1)S(1)}, bf16[256,128]{1,0:T(8,128)(2,1)S(1)}, u32[]{:S(2)}, u32[]{:S(2)}) collective-permute-start(bf16[256,128]{1,0:T(8,128)(2,1)S(1)} %get-tuple-element.42), channel_id=1, source_target_pairs={{0,8},{8,0},{16,24},{24,16},{1,9},{9,1},{17,25},{25,17},{2,10},{10... | collective-permute-start | bytes 196616 | tf_op jit(solution)/shard_map/ppermute | solution.py:39
  26.3 1.2 %collective-permute-start.6 = (bf16[256,128]{1,0:T(8,128)(2,1)S(1)}, bf16[256,128]{1,0:T(8,128)(2,1)S(1)}, u32[]{:S(2)}, u32[]{:S(2)}) collective-permute-start(bf16[256,128]{1,0:T(8,128)(2,1)S(1)} %get-tuple-element.43), channel_id=1, source_target_pairs={{0,24},{8,16},{16,8},{24,0},{1,25},{9,17},{17,9},{25,1},{2,26},{10... | collective-permute-start | bytes 196616 | tf_op jit(solution)/shard_map/ppermute | solution.py:39
  27.5 1.6 %collective-permute-done.9.far = bf16[128,128]{1,0:T(8,128)(2,1)S(1)} collective-permute-done((bf16[128,128]{1,0:T(8,128)(2,1)S(1)}, bf16[128,128]{1,0:T(8,128)(2,1)S(1)}, u32[]{:S(2)}, u32[]{:S(2)}) %collective-permute-start.9) | collective-permute-done | bytes 32800 | tf_op jit(solution)/shard_map/ppermute | solution.py:39
  29.1 1.5 %collective-permute-start.10 = (bf16[96,128]{1,0:T(8,128)(2,1)S(1)}, bf16[96,128]{1,0:T(8,128)(2,1)S(1)}, u32[]{:S(2)}, u32[]{:S(2)}) collective-permute-start(bf16[96,128]{1,0:T(8,128)(2,1)S(1)} %get-tuple-element.50.mine), channel_id=1, source_target_pairs={{0,1},{1,0},{2,3},{3,2},{4,5},{5,4},{6,7},{7,6},{8,9},{9,8},{10,11... | collective-permute-start | bytes 73736 | tf_op jit(solution)/shard_map/ppermute | solution.py:39
  30.6 2.3 %collective-permute-done.10.got = bf16[96,128]{1,0:T(8,128)(2,1)S(1)} collective-permute-done((bf16[96,128]{1,0:T(8,128)(2,1)S(1)}, bf16[96,128]{1,0:T(8,128)(2,1)S(1)}, u32[]{:S(2)}, u32[]{:S(2)}) %collective-permute-start.10) | collective-permute-done | bytes 24608 | tf_op jit(solution)/shard_map/ppermute | solution.py:39
  33.2 1.7 %collective-permute-start.12 = (bf16[80,128]{1,0:T(8,128)(2,1)S(1)}, bf16[80,128]{1,0:T(8,128)(2,1)S(1)}, u32[]{:S(2)}, u32[]{:S(2)}) collective-permute-start(bf16[80,128]{1,0:T(8,128)(2,1)S(1)} %get-tuple-element.56), channel_id=1, source_target_pairs={{0,6},{2,4},{4,2},{6,0},{1,7},{3,5},{5,3},{7,1},{8,14},{10,12},{12... | collective-permute-start | bytes 61448 | tf_op jit(solution)/shard_map/ppermute | solution.py:39
  34.9 1.6 %collective-permute-start.13 = (bf16[64,128]{1,0:T(8,128)(2,1)S(1)}, bf16[64,128]{1,0:T(8,128)(2,1)S(1)}, u32[]{:S(2)}, u32[]{:S(2)}) collective-permute-start(bf16[64,128]{1,0:T(8,128)(2,1)S(1)} %get-tuple-element.54.mine), channel_id=1, source_target_pairs={{0,4},{2,6},{4,0},{6,2},{1,5},{3,7},{5,1},{7,3},{8,12},{10,14},{12... | collective-permute-start | bytes 49160 | tf_op jit(solution)/shard_map/ppermute | solution.py:39
  36.6 1.2 %shard_map.79 = bf16[32,2,32,64]{3,2,1,0:T(8,128)(2,1)} custom-call(f32[2048,128]{1,0:T(8,128)S(1)} %get-tuple-element.40.sums), custom_call_target="tpu_custom_call" | custom-call | bytes 8388608 | tf_op jit(solution)/shard_map/pallas_call | solution.py:549
  37.8 1.2 %shard_map.82 = (f32[4,4,64,128]{3,2,1,0:T(8,128)}, f32[2,4,4,8,128]{4,3,2,1,0:T(8,128)S(1)}) custom-call(f32[1584,128]{1,0:T(8,128)S(1)} %get-tuple-element.41.field, bf16[256,128]{1,0:T(8,128)(2,1)S(1)} %collective-permute-done.5.face_0, bf16[256,128]{1,0:T(8,128)(2,1)S(1)} %collective-permute-done.6.face_1, bf16[96,128]{1,0:T(8,128)(2,1)S(1)} %collective-permute-done.10.got), custom_call_target="tpu_custom_call" | custom-call | bytes 8388608 | tf_op jit(solution)/shard_map/pallas_call | solution.py:563
  39.0 0.6 %collective-permute-done.13.far = bf16[64,128]{1,0:T(8,128)(2,1)S(1)} collective-permute-done((bf16[64,128]{1,0:T(8,128)(2,1)S(1)}, bf16[64,128]{1,0:T(8,128)(2,1)S(1)}, u32[]{:S(2)}, u32[]{:S(2)}) %collective-permute-start.13) | collective-permute-done | bytes 16416 | tf_op jit(solution)/shard_map/ppermute | solution.py:39
  39.6 0.8 %shard_map.84 = (f32[4,4,64,128]{3,2,1,0:T(8,128)}, f32[27,4,32]{2,1,0:T(4,128)}, f32[1,32]{1,0:T(1,128)}) custom-call(f32[4,4,64,128]{3,2,1,0:T(8,128)} %get-tuple-element.51.whole, f32[2,4,4,8,128]{4,3,2,1,0:T(8,128)S(1)} %get-tuple-element.52.ends, bf16[64,128]{1,0:T(8,128)(2,1)S(1)} %get-tuple-element.54.mine, ...), custom_call_target="tpu_custom_call", output_to_operand_aliasing={{0}: (0, {})} | custom-call | tf_op jit(solution)/shard_map/pallas_call | solution.py:567
  (36 shorter events, 1.3 us)
Async XLA Ops:
  0.6 1.0 %copy-start = (bf16[4,4,64,128]{3,2,1,0:T(8,128)(2,1)S(1)}, bf16[4,4,64,128]{3,2,1,0:T(8,128)(2,1)}, u32[]{:S(2)}) copy-start(bf16[4,4,64,128]{3,2,1,0:T(8,128)(2,1)} %cells.5) | copy-start | bytes 786436
  1.6 3.3 %copy-start.3 = (bf16[32,4,3,3,3]{0,1,4,3,2:T(4,128)(2,1)S(1)}, bf16[32,4,3,3,3]{0,1,4,3,2:T(4,128)(2,1)}, u32[]{:S(2)}) copy-start(bf16[32,4,3,3,3]{0,1,4,3,2:T(4,128)(2,1)} %param.5) | copy-start | bytes 20740
  1.9 3.0 %copy-start.4 = (f32[32]{0:T(128)S(1)}, f32[32]{0:T(128)}, u32[]{:S(2)}) copy-start(f32[32]{0:T(128)} %param.6) | copy-start | bytes 388
  1.9 4.6 %collective-permute-start = (bf16[32,128]{1,0:T(8,128)(2,1)S(1)}, bf16[32,128]{1,0:T(8,128)(2,1)S(1)}, u32[]{:S(2)}, u32[]{:S(2)}) collective-permute-start(bf16[32,128]{1,0:T(8,128)(2,1)S(1)} %get-tuple-element.32), channel_id=1, source_target_pairs={{0,1},{1,0},{2,3},{3,2},{4,5},{5,4},{6,7},{7,6},{8,9},{9,8},{10,11... | collective-permute-start | bytes 24584 | tf_op jit(solution)/shard_map/ppermute | solution.py:39
  6.5 5.8 %collective-permute-start.2 = (bf16[48,128]{1,0:T(8,128)(2,1)S(1)}, bf16[48,128]{1,0:T(8,128)(2,1)S(1)}, u32[]{:S(2)}, u32[]{:S(2)}) collective-permute-start(bf16[48,128]{1,0:T(8,128)(2,1)S(1)} %get-tuple-element.64), channel_id=1, source_target_pairs={{0,6},{2,4},{4,2},{6,0},{1,7},{3,5},{5,3},{7,1},{8,14},{10,12},{12... | collective-permute-start | bytes 36872 | tf_op jit(solution)/shard_map/ppermute | solution.py:39
  10.6 3.7 %collective-permute-start.1 = (bf16[48,128]{1,0:T(8,128)(2,1)S(1)}, bf16[48,128]{1,0:T(8,128)(2,1)S(1)}, u32[]{:S(2)}, u32[]{:S(2)}) collective-permute-start(bf16[48,128]{1,0:T(8,128)(2,1)S(1)} %get-tuple-element.65), channel_id=1, source_target_pairs={{0,2},{2,0},{4,6},{6,4},{1,3},{3,1},{5,7},{7,5},{8,10},{10,8},{12,... | collective-permute-start | bytes 36872 | tf_op jit(solution)/shard_map/ppermute | solution.py:39
  10.7 3.6 %copy-start.1 = (bf16[4,4,64,128]{3,2,1,0:T(8,128)(2,1)S(1)}, bf16[4,4,64,128]{3,2,1,0:T(8,128)(2,1)}, u32[]{:S(2)}) copy-start(bf16[4,4,64,128]{3,2,1,0:T(8,128)(2,1)} %cells.5) | copy-start | bytes 786436
  10.7 5.4 %copy-start.2 = (bf16[32,2,32,64]{3,2,1,0:T(8,128)(2,1)S(1)}, bf16[32,2,32,64]{3,2,1,0:T(8,128)(2,1)}, u32[]{:S(2)}) copy-start(bf16[32,2,32,64]{3,2,1,0:T(8,128)(2,1)} %cot.1) | copy-start | bytes 786436
  14.4 2.7 %collective-permute-start.3 = (bf16[288,128]{1,0:T(8,128)(2,1)S(1)}, bf16[288,128]{1,0:T(8,128)(2,1)S(1)}, u32[]{:S(2)}, u32[]{:S(2)}) collective-permute-start(bf16[288,128]{1,0:T(8,128)(2,1)S(1)} %get-tuple-element.35), channel_id=1, source_target_pairs={{0,8},{8,0},{16,24},{24,16},{1,9},{9,1},{17,25},{25,17},{2,10},{10... | collective-permute-start | bytes 221192 | tf_op jit(solution)/shard_map/ppermute | solution.py:39
  14.4 4.1 %collective-permute-start.4 = (bf16[288,128]{1,0:T(8,128)(2,1)S(1)}, bf16[288,128]{1,0:T(8,128)(2,1)S(1)}, u32[]{:S(2)}, u32[]{:S(2)}) collective-permute-start(bf16[288,128]{1,0:T(8,128)(2,1)S(1)} %get-tuple-element.36), channel_id=1, source_target_pairs={{0,24},{8,16},{16,8},{24,0},{1,25},{9,17},{17,9},{25,1},{2,26},{10... | collective-permute-start | bytes 221192 | tf_op jit(solution)/shard_map/ppermute | solution.py:39
  23.6 3.9 %collective-permute-start.8 = (bf16[128,128]{1,0:T(8,128)(2,1)S(1)}, bf16[128,128]{1,0:T(8,128)(2,1)S(1)}, u32[]{:S(2)}, u32[]{:S(2)}) collective-permute-start(bf16[128,128]{1,0:T(8,128)(2,1)S(1)} %get-tuple-element.49), channel_id=1, source_target_pairs={{0,24},{8,16},{16,8},{24,0},{1,25},{9,17},{17,9},{25,1},{2,26},{10... | collective-permute-start | bytes 98312 | tf_op jit(solution)/shard_map/ppermute | solution.py:39
  25.1 3.9 %collective-permute-start.9 = (bf16[128,128]{1,0:T(8,128)(2,1)S(1)}, bf16[128,128]{1,0:T(8,128)(2,1)S(1)}, u32[]{:S(2)}, u32[]{:S(2)}) collective-permute-start(bf16[128,128]{1,0:T(8,128)(2,1)S(1)} %get-tuple-element.48), channel_id=1, source_target_pairs={{0,16},{8,24},{16,0},{24,8},{1,17},{9,25},{17,1},{25,9},{2,18},{10... | collective-permute-start | bytes 98312 | tf_op jit(solution)/shard_map/ppermute | solution.py:39
  25.6 3.4 %collective-permute-start.7 = (bf16[128,128]{1,0:T(8,128)(2,1)S(1)}, bf16[128,128]{1,0:T(8,128)(2,1)S(1)}, u32[]{:S(2)}, u32[]{:S(2)}) collective-permute-start(bf16[128,128]{1,0:T(8,128)(2,1)S(1)} %get-tuple-element.48), channel_id=1, source_target_pairs={{0,8},{8,0},{16,24},{24,16},{1,9},{9,1},{17,25},{25,17},{2,10},{10... | collective-permute-start | bytes 98312 | tf_op jit(solution)/shard_map/ppermute | solution.py:39
  25.7 12.1 %collective-permute-start.5 = (bf16[256,128]{1,0:T(8,128)(2,1)S(1)}, bf16[256,128]{1,0:T(8,128)(2,1)S(1)}, u32[]{:S(2)}, u32[]{:S(2)}) collective-permute-start(bf16[256,128]{1,0:T(8,128)(2,1)S(1)} %get-tuple-element.42), channel_id=1, source_target_pairs={{0,8},{8,0},{16,24},{24,16},{1,9},{9,1},{17,25},{25,17},{2,10},{10... | collective-permute-start | bytes 196616 | tf_op jit(solution)/shard_map/ppermute | solution.py:39
  26.3 11.5 %collective-permute-start.6 = (bf16[256,128]{1,0:T(8,128)(2,1)S(1)}, bf16[256,128]{1,0:T(8,128)(2,1)S(1)}, u32[]{:S(2)}, u32[]{:S(2)}) collective-permute-start(bf16[256,128]{1,0:T(8,128)(2,1)S(1)} %get-tuple-element.43), channel_id=1, source_target_pairs={{0,24},{8,16},{16,8},{24,0},{1,25},{9,17},{17,9},{25,1},{2,26},{10... | collective-permute-start | bytes 196616 | tf_op jit(solution)/shard_map/ppermute | solution.py:39
  29.1 3.9 %collective-permute-start.10 = (bf16[96,128]{1,0:T(8,128)(2,1)S(1)}, bf16[96,128]{1,0:T(8,128)(2,1)S(1)}, u32[]{:S(2)}, u32[]{:S(2)}) collective-permute-start(bf16[96,128]{1,0:T(8,128)(2,1)S(1)} %get-tuple-element.50.mine), channel_id=1, source_target_pairs={{0,1},{1,0},{2,3},{3,2},{4,5},{5,4},{6,7},{7,6},{8,9},{9,8},{10,11... | collective-permute-start | bytes 73736 | tf_op jit(solution)/shard_map/ppermute | solution.py:39
  33.1 6.5 %collective-permute-start.11 = (bf16[80,128]{1,0:T(8,128)(2,1)S(1)}, bf16[80,128]{1,0:T(8,128)(2,1)S(1)}, u32[]{:S(2)}, u32[]{:S(2)}) collective-permute-start(bf16[80,128]{1,0:T(8,128)(2,1)S(1)} %get-tuple-element.55), channel_id=1, source_target_pairs={{0,2},{2,0},{4,6},{6,4},{1,3},{3,1},{5,7},{7,5},{8,10},{10,8},{12,... | collective-permute-start | bytes 61448 | tf_op jit(solution)/shard_map/ppermute | solution.py:39
  33.2 6.4 %collective-permute-start.12 = (bf16[80,128]{1,0:T(8,128)(2,1)S(1)}, bf16[80,128]{1,0:T(8,128)(2,1)S(1)}, u32[]{:S(2)}, u32[]{:S(2)}) collective-permute-start(bf16[80,128]{1,0:T(8,128)(2,1)S(1)} %get-tuple-element.56), channel_id=1, source_target_pairs={{0,6},{2,4},{4,2},{6,0},{1,7},{3,5},{5,3},{7,1},{8,14},{10,12},{12... | collective-permute-start | bytes 61448 | tf_op jit(solution)/shard_map/ppermute | solution.py:39
  34.9 4.6 %collective-permute-start.13 = (bf16[64,128]{1,0:T(8,128)(2,1)S(1)}, bf16[64,128]{1,0:T(8,128)(2,1)S(1)}, u32[]{:S(2)}, u32[]{:S(2)}) collective-permute-start(bf16[64,128]{1,0:T(8,128)(2,1)S(1)} %get-tuple-element.54.mine), channel_id=1, source_target_pairs={{0,4},{2,6},{4,0},{6,2},{1,5},{3,7},{5,1},{7,3},{8,12},{10,14},{12... | collective-permute-start | bytes 49160 | tf_op jit(solution)/shard_map/ppermute | solution.py:39

commit v9 on v8

--- a/solution.py
+++ b/solution.py
@@ -136,17 +136,45 @@
         pooled[o : o + 4] = mean.astype(bf16).reshape(4, pool_x, pool_y, pool_z)
 
 
+def shifted(mid, left, right, y):
+    lane = iota(mid.shape, 1)
+    low = pltpu.roll(left, (lanes - y) % lanes, 1)
+    high = pltpu.roll(right, (lanes - 1 - y) % lanes, 1)
+    before = jnp.where(lane == 0, low, pltpu.roll(mid, 1, 1))
+    after = jnp.where(lane == lanes - 1, high, pltpu.roll(mid, lanes - 1, 1))
+    return [before, mid, after]
+
+
+def own_kernel(cells, rows, left, right, inner, stage):
+    chan, count_x, count_y, _ = cells.shape
+    own = chan * count_x
+    for x in range(count_x):
+        for c in range(chan):
+            plane = cells[c, x].astype(f32)
+            stage[pl.ds(own + x * chan + c, count_y, stride=own), :] = plane
+    stage[0:own, :] = rows[0:own, :]
+    stage[(count_y + 1) * own : (count_y + 2) * own, :] = rows[own : 2 * own, :]
+    left_cols, right_cols = left[...], right[...]
+    for y in range(count_y + 2):
+        whole = shifted(stage[y * own : (y + 1) * own, :], left_cols, right_cols, y)
+        whole = jnp.concatenate(whole, axis=0)
+        inner[y * 3 * own : (y + 1) * 3 * own, :] = whole.astype(bf16)
+
+
 def main_kernel(
-    cells, got_0, got_1, rows_in, left_in, right_in, spread, wbig, wback,
+    count_x, got_0, got_1, inner, spread, wbig, wback,
     sums, field, sent_0, sent_1, wpart, wframe, rows_out, cols,
-    stage, patches, left, right, carry, gram, delta_a, delta_b,
+    stage, patches, carry, gram, delta_a, delta_b,
 ):
-    chan, count_x, count_y, _ = cells.shape
-    pool_x, pool_y = count_x // 2, count_y // 2
+    pool_x = count_x // 2
     chan_out = wbig.shape[0] // count_x
-    own = chan * count_x
+    pool_y = spread.shape[0] // (pool_x * chan_out)
+    count_y = 2 * pool_y
+    own = inner.shape[0] // (3 * (count_y + 2))
+    chan = own // count_x
     wide = own + 2 * chan
-    depth = 3 * wide + 8
+    outside_rows = 2 * chan
+    depth = 3 * outside_rows + 8
     body = chan * count_y
     lane = iota((wide, lanes), 1)
     even = is_even("gx")
@@ -156,33 +184,23 @@
         two = got_1[start : start + size, :].astype(f32)
         return jnp.where(even, one, two) if up else jnp.where(even, two, one)
 
-    for x in range(count_x + 2):
+    for side in range(2):
         for c in range(chan):
-            if x == 0:
-                plane = got(False, c * count_y, count_y)
-            elif x == count_x + 1:
-                plane = got(True, c * count_y, count_y)
-            else:
-                plane = cells[c, x - 1]
-            stage[pl.ds(wide + x * chan + c, count_y, stride=wide), :] = plane.astype(f32)
+            plane = got(side == 1, c * count_y, count_y)
+            at = outside_rows + side * chan + c
+            stage[pl.ds(at, count_y, stride=outside_rows), :] = plane
     rest_low, rest_high = got(False, body, 32), got(True, body, 32)
-    for base, top, at in ((0, 0, 0), ((count_y + 1) * wide, own, chan)):
-        stage[base : base + chan, :] = rest_low[at : at + chan]
-        stage[base + chan : base + chan + own, :] = rows_in[top : top + own, :]
-        stage[base + chan + own : base + wide, :] = rest_high[at : at + chan]
-    for ref, mine, at in ((left, left_in, 16), (right, right_in, 16 + chan)):
-        ref[0:chan, :] = rest_low[at : at + chan]
-        ref[chan : chan + own, :] = mine[...]
-        ref[chan + own : wide, :] = rest_high[at : at + chan]
-    left_cols, right_cols = left[...], right[...]
+    both = lambda at: jnp.concatenate(
+        [rest_low[at : at + chan], rest_high[at : at + chan]], axis=0
+    )
+    stage[0:outside_rows, :] = both(0)
+    end = (count_y + 1) * outside_rows
+    stage[end : end + outside_rows, :] = both(chan)
+    left_cols, right_cols = both(16), both(16 + chan)
     for y in range(count_y + 2):
-        mid = stage[y * wide : (y + 1) * wide, :]
-        low_col = pltpu.roll(left_cols, (lanes - y) % lanes, 1)
-        high_col = pltpu.roll(right_cols, (lanes - 1 - y) % lanes, 1)
-        before = jnp.where(lane == 0, low_col, pltpu.roll(mid, 1, 1))
-        after = jnp.where(lane == lanes - 1, high_col, pltpu.roll(mid, lanes - 1, 1))
-        whole = jnp.concatenate([before, mid, after, jnp.ones((8, lanes), f32)], axis=0)
-        patches[y * depth : (y + 1) * depth, :] = whole.astype(bf16)
+        mid = stage[y * outside_rows : (y + 1) * outside_rows, :]
+        whole = shifted(mid, left_cols, right_cols, y) + [jnp.ones((8, lanes), f32)]
+        patches[y * depth : (y + 1) * depth, :] = jnp.concatenate(whole, axis=0).astype(bf16)
 
     carry[...] = jnp.zeros_like(carry)
     gram[...] = jnp.zeros_like(gram)
@@ -205,13 +223,13 @@
         edge[1] = jnp.where(here, pltpu.roll(last, y + 1, 1), edge[1])
 
     def block_of(j):
-        return jnp.concatenate(
-            [
-                patches[pl.ds(aligned((2 * j + h) * depth, 16), 3 * depth), :]
-                for h in range(2)
-            ],
-            axis=1,
-        )
+        columns = []
+        for h in range(2):
+            y = 2 * j + h
+            near = inner[pl.ds(aligned(y * 3 * own, 16), 9 * own), :]
+            rest = patches[pl.ds(aligned(y * depth, 16), 3 * depth), :]
+            columns.append(jnp.concatenate([near, rest], axis=0))
+        return jnp.concatenate(columns, axis=1)
 
     def forward(i, k, ref):
         j = i * pairs + k
@@ -292,23 +310,36 @@
     closed(held, edge)
 
     span = gram.shape[1]
-    straight, turned = 0.0, 0.0
+    spot = iota((chan_out, 2 * lanes), 1)
+    first = 9 * own
+    turn = lambda part, shift: pltpu.roll(part, (2 * lanes - shift) % (2 * lanes), 1)
+    straight, turned, extra = 0.0, 0.0, 0.0
     for x in range(count_x):
         part = gram[x * chan_out : (x + 1) * chan_out, :]
         part = jnp.concatenate([part, jnp.zeros((chan_out, 2 * lanes - span), f32)], axis=1)
         straight = straight + part
-        turned = turned + (pltpu.roll(part, 2 * lanes - chan * x, 1) if x else part)
-    spot = iota((chan_out, lanes), 1)
-    tight = 0.0
+        moved = turn(part, chan * (x - 1)) if x != 1 else part
+        a = spot % own // chan
+        turned = turned + jnp.where((a + x >= 1) & (a + x <= count_x), moved, 0.0)
+        if x == 0:
+            extra = extra + jnp.where((spot - first) % outside_rows < chan, part, 0.0)
+        if x == count_x - 1:
+            extra = extra + jnp.where((spot - first) % outside_rows >= chan, part, 0.0)
     group = 3 * chan
+    tight = jnp.zeros((chan_out, 2 * lanes), f32)
     for b in range(3):
         for e in range(3):
-            shift = (b * depth + e * wide) - (b * 3 + e) * group
-            part = pltpu.roll(turned, 2 * lanes - shift, 1)[:, :lanes] if shift else turned[:, :lanes]
-            tight = jnp.where(spot // group == b * 3 + e, part, tight)
-    part = pltpu.roll(straight, 2 * lanes + 9 * group - 3 * wide, 1)[:, :lanes]
-    tight = jnp.where(spot == 9 * group, part, tight)
-    coarse = tight.astype(bf16)
+            at = (b * 3 + e) * group
+            here = spot // group == b * 3 + e
+            value = turn(turned, b * 3 * own + e * own - at)
+            source = first + b * depth + e * outside_rows
+            low, high = turn(extra, source - at), turn(extra, source - at - chan)
+            a = (spot - at) // chan
+            value = value + jnp.where(a == 0, low, 0.0) + jnp.where(a == 2, high, 0.0)
+            tight = jnp.where(here, value, tight)
+    bias_at = first + 3 * outside_rows
+    tight = jnp.where(spot == 9 * group, turn(straight, bias_at - 9 * group), tight)
+    tight = tight[:, :lanes]
     wpart[...] = tight
     sides = jnp.concatenate(split(tight), axis=0)
     wframe[...] = sides
@@ -471,7 +502,7 @@
     chan_out = weight.shape[0]
     own = chan * count_x
     wide = own + 2 * chan
-    depth = 3 * wide + 8
+    depth = 6 * chan + 8
     shape = jax.ShapeDtypeStruct
 
     kernel = weight.transpose(0, 3, 4, 2, 1)
@@ -480,13 +511,16 @@
             jnp.pad(kernel, ((0, 0), (0, 0), (0, 0), (x, count_x - 1 - x), (0, 0)))
             for x in range(count_x)
         ]
-    ).reshape(count_x * chan_out, 3, 3 * wide)
+    ).reshape(count_x * chan_out, 3, 3, count_x + 2, chan)
     coarse = lax.reduce_precision(bias, 8, 7)
     middle = lax.reduce_precision(bias - coarse, 8, 7)
     fine = bias - coarse - middle
     pieces = jnp.stack([coarse, middle, fine], axis=1).astype(bf16)
     pieces = jnp.pad(jnp.tile(pieces, (count_x, 1))[:, None], ((0, 0), (0, 2), (0, 5)))
-    wbig = jnp.concatenate([placed, pieces], axis=2).reshape(count_x * chan_out, 3 * depth)
+    near = placed[:, :, :, 1 : count_x + 1].reshape(count_x * chan_out, 9 * own)
+    rest = jnp.concatenate([placed[:, :, :, :1], placed[:, :, :, count_x + 1 :]], axis=3)
+    rest = jnp.concatenate([rest.reshape(count_x * chan_out, 3, 6 * chan), pieces], axis=2)
+    wbig = jnp.concatenate([near, rest.reshape(count_x * chan_out, 3 * depth)], axis=1)
     wback = placed.reshape(count_x * chan_out, 9 * wide).T
 
     own_block = shape((own, lanes), bf16)
@@ -510,12 +544,18 @@
         bundle_kernel, [bundle, bundle, side, side, shape((2 * own, lanes), f32)]
     )(cells, edges, row_0, row_1)
     face_1, face_0 = swapped(face_1, "gx", 1), swapped(face_0, "gx", 0)
+    inner = call(
+        own_kernel,
+        shape(((count_y + 2) * 3 * own, lanes), bf16),
+        [pltpu.VMEM(((count_y + 2) * own, lanes), f32)],
+        traffic(4),
+    )(cells, rows, left, right)
 
     tall = 2 * wide
     bundle = shape((16 + tall + 2 * chan_out, lanes), bf16)
     face = shape((body, lanes), bf16)
     sums, field, row_0, row_1, wpart, wframe, rows, cols = call(
-        main_kernel,
+        functools.partial(main_kernel, count_x),
         [
             pooled_rows,
             shape(((count_y + 2) * wide, lanes), f32),
@@ -527,16 +567,14 @@
             shape((tall, lanes), f32),
         ],
         [
-            pltpu.VMEM(((count_y + 2) * wide, lanes), f32),
+            pltpu.VMEM(((count_y + 2) * 2 * chan, lanes), f32),
             pltpu.VMEM(((count_y + 2) * depth, lanes), bf16),
-            pltpu.VMEM((wide, lanes), f32),
-            pltpu.VMEM((wide, lanes), f32),
             pltpu.VMEM((6 * wide, lanes), f32),
-            pltpu.VMEM((count_x * chan_out, 3 * depth), f32),
+            pltpu.VMEM((count_x * chan_out, 9 * own + 3 * depth), f32),
             pltpu.VMEM((count_x * chan_out, 8 * lanes), bf16),
             pltpu.VMEM((count_x * chan_out, 8 * lanes), bf16),
         ],
-    )(cells, face_0, face_1, rows, left, right, spread, wbig, wback)
+    )(face_0, face_1, inner, spread, wbig, wback)
 
     alone = lax.axis_size("gx") != 4
     if alone:

time: 40.5 us -> 40.4 us (level)
  waiting for transfers between devices: 10.4 us -> 9 us
  local copies, waits for them, and re-layouts: 1.63 us -> 2.4 us
    ppermute x14, waiting for transfers between devices: 10.4 us -> 9 us  [swapped(): return lax.ppermute(array, axis, pairs)]
    slice x0 -> x3, local copies, waits for them, and re-layouts: none -> 0.66 us  [the longest x2 0.65 us: on_device(): near = placed[:, :, :, 1:count_x + 1].reshape(count_x * chan_out, 9 * own)]
    pallas_call x1 -> x2, Pallas kernels: 5.08 us -> 5.37 us  [the longest x1 4.94 us: on_device(): call(functools.partial(main_kernel, count_x), [pooled_rows, shape(((count...]
    unnamed x10 -> x12, local copies, waits for them, and re-layouts: 0.97 us -> 0.97 us
  transfers between devices with their start and end apart: 14 -> 14, of which waited for: 7 -> 6; matrix products, arithmetic and copies ran while one was open for 2% -> 3% of each run, Pallas kernels for 9% -> 10%
where the time goes in v9:
time: 40.4 us; the launch traced here: 40.2 us
  starting transfers between devices  17.7 us (44%)
  Pallas kernels  9.94 us (25%)
  waiting for transfers between devices  9 us (22%)
  local copies, waits for them, and re-layouts  2.4 us (6%)
  between operations  0.83 us (2%)
    ppermute x14, starting transfers between devices, swapped(): return lax.ppermute(array, axis, pairs)  17.7 us
    ppermute x14, waiting for transfers between devices, swapped(): return lax.ppermute(array, axis, pairs)  9 us
    pallas_call x1, Pallas kernels, on_device(): call(functools.partial(main_kernel, count_x), [pooled_rows, shape(((count...  4.94 us
    pallas_call x1, Pallas kernels, on_device(): call(pool_kernel, shape(cotangent.shape, bf16), cost=traffic(8))(sums)  1.24 us
    pallas_call x1, Pallas kernels, on_device(): call(grad_kernel, [shape(cells.shape, f32), shape(tiles, f32)], cost=traf...  1.19 us
    unnamed x12, local copies, waits for them, and re-layouts  0.97 us
    pallas_call x1, Pallas kernels, on_device(): spread = call(spread_kernel, pooled_rows)(cotangent)  0.88 us
  transfers between devices with their start and end apart: 14, of which 6 were waited for; matrix products, arithmetic and copies ran while one was open for 3% of the time, Pallas kernels for 10%

profile of v9, /device:TPU:0, one launch (start us, length us, event | category | flops | bytes accessed | tf_op | source)
XLA Modules:
  0.0 40.2 jit_solution(8385331902744050726)
XLA Ops:
  0.6 0.9 %copy-done = bf16[4,4,64,128]{3,2,1,0:T(8,128)(2,1)S(1)} copy-done((bf16[4,4,64,128]{3,2,1,0:T(8,128)(2,1)S(1)}, bf16[4,4,64,128]{3,2,1,0:T(8,128)(2,1)}, u32[]{:S(2)}) %copy-start) | copy-done | bytes 262168
  1.9 3.0 %collective-permute-start = (bf16[32,128]{1,0:T(8,128)(2,1)S(1)}, bf16[32,128]{1,0:T(8,128)(2,1)S(1)}, u32[]{:S(2)}, u32[]{:S(2)}) collective-permute-start(bf16[32,128]{1,0:T(8,128)(2,1)S(1)} %get-tuple-element.32), channel_id=1, source_target_pairs={{0,1},{1,0},{2,3},{3,2},{4,5},{5,4},{6,7},{7,6},{8,9},{9,8},{10,11... | collective-permute-start | bytes 24584 | tf_op jit(solution)/shard_map/ppermute | solution.py:39
  5.6 0.9 %collective-permute-done.edges = bf16[32,128]{1,0:T(8,128)(2,1)S(1)} collective-permute-done((bf16[32,128]{1,0:T(8,128)(2,1)S(1)}, bf16[32,128]{1,0:T(8,128)(2,1)S(1)}, u32[]{:S(2)}, u32[]{:S(2)}) %collective-permute-start) | collective-permute-done | bytes 8224 | tf_op jit(solution)/shard_map/ppermute | solution.py:39
  6.5 4.1 %collective-permute-start.2 = (bf16[48,128]{1,0:T(8,128)(2,1)S(1)}, bf16[48,128]{1,0:T(8,128)(2,1)S(1)}, u32[]{:S(2)}, u32[]{:S(2)}) collective-permute-start(bf16[48,128]{1,0:T(8,128)(2,1)S(1)} %get-tuple-element.66), channel_id=1, source_target_pairs={{0,6},{2,4},{4,2},{6,0},{1,7},{3,5},{5,3},{7,1},{8,14},{10,12},{12... | collective-permute-start | bytes 36872 | tf_op jit(solution)/shard_map/ppermute | solution.py:39
  10.9 0.6 %slice-done = bf16[128,3,3,4,4]{0,4,3,2,1:T(4,128)(2,1)S(1)} async-done(((bf16[128,3,3,6,4]{0,4,3,2,1:T(4,128)(2,1)}), bf16[128,3,3,4,4]{0,4,3,2,1:T(4,128)(2,1)S(1)}, s32[]{:S(2)}) %slice-start) | async-done | bytes 36888 | tf_op jit(solution)/shard_map/slice | solution.py:520
  11.7 0.9 %shard_map.78.spread = f32[2048,128]{1,0:T(8,128)S(1)} custom-call(bf16[32,2,32,64]{3,2,1,0:T(8,128)(2,1)S(1)} %copy-done.2), custom_call_target="tpu_custom_call" | custom-call | tf_op jit(solution)/shard_map/pallas_call | solution.py:536
  12.6 1.7 %collective-permute-done.1.got_0 = bf16[48,128]{1,0:T(8,128)(2,1)S(1)} collective-permute-done((bf16[48,128]{1,0:T(8,128)(2,1)S(1)}, bf16[48,128]{1,0:T(8,128)(2,1)S(1)}, u32[]{:S(2)}, u32[]{:S(2)}) %collective-permute-start.1) | collective-permute-done | bytes 12320 | tf_op jit(solution)/shard_map/ppermute | solution.py:39
  14.4 1.6 %collective-permute-start.4 = (bf16[288,128]{1,0:T(8,128)(2,1)S(1)}, bf16[288,128]{1,0:T(8,128)(2,1)S(1)}, u32[]{:S(2)}, u32[]{:S(2)}) collective-permute-start(bf16[288,128]{1,0:T(8,128)(2,1)S(1)} %get-tuple-element.36), channel_id=1, source_target_pairs={{0,24},{8,16},{16,8},{24,0},{1,25},{9,17},{17,9},{25,1},{2,26},{10... | collective-permute-start | bytes 221192 | tf_op jit(solution)/shard_map/ppermute | solution.py:39
  16.1 0.4 %shard_map.77.inner = bf16[3168,128]{1,0:T(8,128)(2,1)S(1)} custom-call(bf16[4,4,64,128]{3,2,1,0:T(8,128)(2,1)S(1)} %copy-done.1, f32[32,128]{1,0:T(8,128)S(1)} %get-tuple-element.37.rows, f32[16,128]{1,0:T(8,128)S(1)} %get-tuple-element.38.left, f32[16,128]{1,0:T(8,128)S(1)} %get-tuple-element.39.right), custom_call_target="tpu_custom_call" | custom-call | bytes 4194304 | tf_op jit(solution)/shard_map/pallas_call | solution.py:547
  16.5 1.9 %collective-permute-done.4.got_1 = bf16[288,128]{1,0:T(8,128)(2,1)S(1)} collective-permute-done((bf16[288,128]{1,0:T(8,128)(2,1)S(1)}, bf16[288,128]{1,0:T(8,128)(2,1)S(1)}, u32[]{:S(2)}, u32[]{:S(2)}) %collective-permute-start.4) | collective-permute-done | bytes 73760 | tf_op jit(solution)/shard_map/ppermute | solution.py:39
  18.5 4.9 %shard_map.79 = (f32[2048,128]{1,0:T(8,128)S(1)}, f32[1584,128]{1,0:T(8,128)S(1)}, bf16[128,128]{1,0:T(8,128)(2,1)S(1)}, bf16[128,128]{1,0:T(8,128)(2,1)S(1)}, f...) custom-call(bf16[288,128]{1,0:T(8,128)(2,1)S(1)} %collective-permute-done.3.g, ...), custom_call_target="tpu_custom_call" | custom-call | tf_op jit(solution)/shard_map/pallas_call | solution.py:557
  23.4 1.6 %collective-permute-start.8 = (bf16[128,128]{1,0:T(8,128)(2,1)S(1)}, bf16[128,128]{1,0:T(8,128)(2,1)S(1)}, u32[]{:S(2)}, u32[]{:S(2)}) collective-permute-start(bf16[128,128]{1,0:T(8,128)(2,1)S(1)} %get-tuple-element.49), channel_id=1, source_target_pairs={{0,24},{8,16},{16,8},{24,0},{1,25},{9,17},{17,9},{25,1},{2,26},{10... | collective-permute-start | bytes 98312 | tf_op jit(solution)/shard_map/ppermute | solution.py:39
  25.0 0.5 %collective-permute-start.9 = (bf16[128,128]{1,0:T(8,128)(2,1)S(1)}, bf16[128,128]{1,0:T(8,128)(2,1)S(1)}, u32[]{:S(2)}, u32[]{:S(2)}) collective-permute-start(bf16[128,128]{1,0:T(8,128)(2,1)S(1)} %get-tuple-element.48), channel_id=1, source_target_pairs={{0,16},{8,24},{16,0},{24,8},{1,17},{9,25},{17,1},{25,9},{2,18},{10... | collective-permute-start | bytes 98312 | tf_op jit(solution)/shard_map/ppermute | solution.py:39
  25.6 0.6 %collective-permute-start.5 = (bf16[256,128]{1,0:T(8,128)(2,1)S(1)}, bf16[256,128]{1,0:T(8,128)(2,1)S(1)}, u32[]{:S(2)}, u32[]{:S(2)}) collective-permute-start(bf16[256,128]{1,0:T(8,128)(2,1)S(1)} %get-tuple-element.42), channel_id=1, source_target_pairs={{0,8},{8,0},{16,24},{24,16},{1,9},{9,1},{17,25},{25,17},{2,10},{10... | collective-permute-start | bytes 196616 | tf_op jit(solution)/shard_map/ppermute | solution.py:39
  26.1 1.2 %collective-permute-start.6 = (bf16[256,128]{1,0:T(8,128)(2,1)S(1)}, bf16[256,128]{1,0:T(8,128)(2,1)S(1)}, u32[]{:S(2)}, u32[]{:S(2)}) collective-permute-start(bf16[256,128]{1,0:T(8,128)(2,1)S(1)} %get-tuple-element.43), channel_id=1, source_target_pairs={{0,24},{8,16},{16,8},{24,0},{1,25},{9,17},{17,9},{25,1},{2,26},{10... | collective-permute-start | bytes 196616 | tf_op jit(solution)/shard_map/ppermute | solution.py:39
  27.3 1.6 %collective-permute-done.9.far = bf16[128,128]{1,0:T(8,128)(2,1)S(1)} collective-permute-done((bf16[128,128]{1,0:T(8,128)(2,1)S(1)}, bf16[128,128]{1,0:T(8,128)(2,1)S(1)}, u32[]{:S(2)}, u32[]{:S(2)}) %collective-permute-start.9) | collective-permute-done | bytes 32800 | tf_op jit(solution)/shard_map/ppermute | solution.py:39
  28.9 1.6 %collective-permute-start.10 = (bf16[96,128]{1,0:T(8,128)(2,1)S(1)}, bf16[96,128]{1,0:T(8,128)(2,1)S(1)}, u32[]{:S(2)}, u32[]{:S(2)}) collective-permute-start(bf16[96,128]{1,0:T(8,128)(2,1)S(1)} %get-tuple-element.50.mine), channel_id=1, source_target_pairs={{0,1},{1,0},{2,3},{3,2},{4,5},{5,4},{6,7},{7,6},{8,9},{9,8},{10,11... | collective-permute-start | bytes 73736 | tf_op jit(solution)/shard_map/ppermute | solution.py:39
  30.5 2.3 %collective-permute-done.10.got = bf16[96,128]{1,0:T(8,128)(2,1)S(1)} collective-permute-done((bf16[96,128]{1,0:T(8,128)(2,1)S(1)}, bf16[96,128]{1,0:T(8,128)(2,1)S(1)}, u32[]{:S(2)}, u32[]{:S(2)}) %collective-permute-start.10) | collective-permute-done | bytes 24608 | tf_op jit(solution)/shard_map/ppermute | solution.py:39
  33.3 1.5 %collective-permute-start.12 = (bf16[80,128]{1,0:T(8,128)(2,1)S(1)}, bf16[80,128]{1,0:T(8,128)(2,1)S(1)}, u32[]{:S(2)}, u32[]{:S(2)}) collective-permute-start(bf16[80,128]{1,0:T(8,128)(2,1)S(1)} %get-tuple-element.56), channel_id=1, source_target_pairs={{0,6},{2,4},{4,2},{6,0},{1,7},{3,5},{5,3},{7,1},{8,14},{10,12},{12... | collective-permute-start | bytes 61448 | tf_op jit(solution)/shard_map/ppermute | solution.py:39
  34.8 1.6 %collective-permute-start.13 = (bf16[64,128]{1,0:T(8,128)(2,1)S(1)}, bf16[64,128]{1,0:T(8,128)(2,1)S(1)}, u32[]{:S(2)}, u32[]{:S(2)}) collective-permute-start(bf16[64,128]{1,0:T(8,128)(2,1)S(1)} %get-tuple-element.54.mine), channel_id=1, source_target_pairs={{0,4},{2,6},{4,0},{6,2},{1,5},{3,7},{5,1},{7,3},{8,12},{10,14},{12... | collective-permute-start | bytes 49160 | tf_op jit(solution)/shard_map/ppermute | solution.py:39
  36.4 1.2 %shard_map.80 = bf16[32,2,32,64]{3,2,1,0:T(8,128)(2,1)} custom-call(f32[2048,128]{1,0:T(8,128)S(1)} %get-tuple-element.40.sums), custom_call_target="tpu_custom_call" | custom-call | bytes 8388608 | tf_op jit(solution)/shard_map/pallas_call | solution.py:587
  37.6 1.2 %shard_map.83 = (f32[4,4,64,128]{3,2,1,0:T(8,128)}, f32[2,4,4,8,128]{4,3,2,1,0:T(8,128)S(1)}) custom-call(f32[1584,128]{1,0:T(8,128)S(1)} %get-tuple-element.41.field, bf16[256,128]{1,0:T(8,128)(2,1)S(1)} %collective-permute-done.5.face_0, bf16[256,128]{1,0:T(8,128)(2,1)S(1)} %collective-permute-done.6.face_1, bf16[96,128]{1,0:T(8,128)(2,1)S(1)} %collective-permute-done.10.got), custom_call_target="tpu_custom_call" | custom-call | bytes 8388608 | tf_op jit(solution)/shard_map/pallas_call | solution.py:601
  38.8 0.6 %collective-permute-done.13.far = bf16[64,128]{1,0:T(8,128)(2,1)S(1)} collective-permute-done((bf16[64,128]{1,0:T(8,128)(2,1)S(1)}, bf16[64,128]{1,0:T(8,128)(2,1)S(1)}, u32[]{:S(2)}, u32[]{:S(2)}) %collective-permute-start.13) | collective-permute-done | bytes 16416 | tf_op jit(solution)/shard_map/ppermute | solution.py:39
  39.4 0.8 %shard_map.85 = (f32[4,4,64,128]{3,2,1,0:T(8,128)}, f32[27,4,32]{2,1,0:T(4,128)}, f32[1,32]{1,0:T(1,128)}) custom-call(f32[4,4,64,128]{3,2,1,0:T(8,128)} %get-tuple-element.51.whole, f32[2,4,4,8,128]{4,3,2,1,0:T(8,128)S(1)} %get-tuple-element.52.ends, bf16[64,128]{1,0:T(8,128)(2,1)S(1)} %get-tuple-element.54.mine, ...), custom_call_target="tpu_custom_call", output_to_operand_aliasing={{0}: (0, {})} | custom-call | tf_op jit(solution)/shard_map/pallas_call | solution.py:605
  (45 shorter events, 2.1 us)
Async XLA Ops:
  0.6 1.0 %copy-start = (bf16[4,4,64,128]{3,2,1,0:T(8,128)(2,1)S(1)}, bf16[4,4,64,128]{3,2,1,0:T(8,128)(2,1)}, u32[]{:S(2)}) copy-start(bf16[4,4,64,128]{3,2,1,0:T(8,128)(2,1)} %cells.5) | copy-start | bytes 786436
  1.6 3.3 %copy-start.4 = (bf16[32,4,3,3,3]{0,1,4,3,2:T(4,128)(2,1)S(1)}, bf16[32,4,3,3,3]{0,1,4,3,2:T(4,128)(2,1)}, u32[]{:S(2)}) copy-start(bf16[32,4,3,3,3]{0,1,4,3,2:T(4,128)(2,1)} %param.5) | copy-start | bytes 20740
  1.9 3.0 %copy-start.5 = (f32[32]{0:T(128)S(1)}, f32[32]{0:T(128)}, u32[]{:S(2)}) copy-start(f32[32]{0:T(128)} %param.6) | copy-start | bytes 388
  1.9 4.6 %collective-permute-start = (bf16[32,128]{1,0:T(8,128)(2,1)S(1)}, bf16[32,128]{1,0:T(8,128)(2,1)S(1)}, u32[]{:S(2)}, u32[]{:S(2)}) collective-permute-start(bf16[32,128]{1,0:T(8,128)(2,1)S(1)} %get-tuple-element.32), channel_id=1, source_target_pairs={{0,1},{1,0},{2,3},{3,2},{4,5},{5,4},{6,7},{7,6},{8,9},{9,8},{10,11... | collective-permute-start | bytes 24584 | tf_op jit(solution)/shard_map/ppermute | solution.py:39
  5.3 6.4 %copy-start.2 = (bf16[32,2,32,64]{3,2,1,0:T(8,128)(2,1)S(1)}, bf16[32,2,32,64]{3,2,1,0:T(8,128)(2,1)}, u32[]{:S(2)}) copy-start(bf16[32,2,32,64]{3,2,1,0:T(8,128)(2,1)} %cot.1) | copy-start | bytes 786436
  5.4 5.3 %copy-start.3 = (bf16[128,3,3,6,4]{0,4,3,2,1:T(4,128)(2,1)}, bf16[128,3,3,6,4]{0,4,3,2,1:T(4,128)(2,1)S(1)}, u32[]{:S(2)}) copy-start(bf16[128,3,3,6,4]{0,4,3,2,1:T(4,128)(2,1)S(1)} %reshape.59) | copy-start | bytes 165892
  6.5 6.1 %collective-permute-start.2 = (bf16[48,128]{1,0:T(8,128)(2,1)S(1)}, bf16[48,128]{1,0:T(8,128)(2,1)S(1)}, u32[]{:S(2)}, u32[]{:S(2)}) collective-permute-start(bf16[48,128]{1,0:T(8,128)(2,1)S(1)} %get-tuple-element.66), channel_id=1, source_target_pairs={{0,6},{2,4},{4,2},{6,0},{1,7},{3,5},{5,3},{7,1},{8,14},{10,12},{12... | collective-permute-start | bytes 36872 | tf_op jit(solution)/shard_map/ppermute | solution.py:39
  10.6 3.7 %collective-permute-start.1 = (bf16[48,128]{1,0:T(8,128)(2,1)S(1)}, bf16[48,128]{1,0:T(8,128)(2,1)S(1)}, u32[]{:S(2)}, u32[]{:S(2)}) collective-permute-start(bf16[48,128]{1,0:T(8,128)(2,1)S(1)} %get-tuple-element.67), channel_id=1, source_target_pairs={{0,2},{2,0},{4,6},{6,4},{1,3},{3,1},{5,7},{7,5},{8,10},{10,8},{12,... | collective-permute-start | bytes 36872 | tf_op jit(solution)/shard_map/ppermute | solution.py:39
  10.8 0.8 %slice-start = ((bf16[128,3,3,6,4]{0,4,3,2,1:T(4,128)(2,1)}), bf16[128,3,3,4,4]{0,4,3,2,1:T(4,128)(2,1)S(1)}, s32[]{:S(2)}) async-start(bf16[128,3,3,6,4]{0,4,3,2,1:T(4,128)(2,1)} %copy-done.3), calls=%async_computation | async-start | bytes 73728 | tf_op jit(solution)/shard_map/slice | solution.py:520
  11.7 2.6 %copy-start.1 = (bf16[4,4,64,128]{3,2,1,0:T(8,128)(2,1)S(1)}, bf16[4,4,64,128]{3,2,1,0:T(8,128)(2,1)}, u32[]{:S(2)}) copy-start(bf16[4,4,64,128]{3,2,1,0:T(8,128)(2,1)} %cells.5) | copy-start | bytes 786436
  14.4 2.2 %collective-permute-start.3 = (bf16[288,128]{1,0:T(8,128)(2,1)S(1)}, bf16[288,128]{1,0:T(8,128)(2,1)S(1)}, u32[]{:S(2)}, u32[]{:S(2)}) collective-permute-start(bf16[288,128]{1,0:T(8,128)(2,1)S(1)} %get-tuple-element.35), channel_id=1, source_target_pairs={{0,8},{8,0},{16,24},{24,16},{1,9},{9,1},{17,25},{25,17},{2,10},{10... | collective-permute-start | bytes 221192 | tf_op jit(solution)/shard_map/ppermute | solution.py:39
  14.4 4.1 %collective-permute-start.4 = (bf16[288,128]{1,0:T(8,128)(2,1)S(1)}, bf16[288,128]{1,0:T(8,128)(2,1)S(1)}, u32[]{:S(2)}, u32[]{:S(2)}) collective-permute-start(bf16[288,128]{1,0:T(8,128)(2,1)S(1)} %get-tuple-element.36), channel_id=1, source_target_pairs={{0,24},{8,16},{16,8},{24,0},{1,25},{9,17},{17,9},{25,1},{2,26},{10... | collective-permute-start | bytes 221192 | tf_op jit(solution)/shard_map/ppermute | solution.py:39
  23.4 3.9 %collective-permute-start.8 = (bf16[128,128]{1,0:T(8,128)(2,1)S(1)}, bf16[128,128]{1,0:T(8,128)(2,1)S(1)}, u32[]{:S(2)}, u32[]{:S(2)}) collective-permute-start(bf16[128,128]{1,0:T(8,128)(2,1)S(1)} %get-tuple-element.49), channel_id=1, source_target_pairs={{0,24},{8,16},{16,8},{24,0},{1,25},{9,17},{17,9},{25,1},{2,26},{10... | collective-permute-start | bytes 98312 | tf_op jit(solution)/shard_map/ppermute | solution.py:39
  25.0 3.9 %collective-permute-start.9 = (bf16[128,128]{1,0:T(8,128)(2,1)S(1)}, bf16[128,128]{1,0:T(8,128)(2,1)S(1)}, u32[]{:S(2)}, u32[]{:S(2)}) collective-permute-start(bf16[128,128]{1,0:T(8,128)(2,1)S(1)} %get-tuple-element.48), channel_id=1, source_target_pairs={{0,16},{8,24},{16,0},{24,8},{1,17},{9,25},{17,1},{25,9},{2,18},{10... | collective-permute-start | bytes 98312 | tf_op jit(solution)/shard_map/ppermute | solution.py:39
  25.5 3.4 %collective-permute-start.7 = (bf16[128,128]{1,0:T(8,128)(2,1)S(1)}, bf16[128,128]{1,0:T(8,128)(2,1)S(1)}, u32[]{:S(2)}, u32[]{:S(2)}) collective-permute-start(bf16[128,128]{1,0:T(8,128)(2,1)S(1)} %get-tuple-element.48), channel_id=1, source_target_pairs={{0,8},{8,0},{16,24},{24,16},{1,9},{9,1},{17,25},{25,17},{2,10},{10... | collective-permute-start | bytes 98312 | tf_op jit(solution)/shard_map/ppermute | solution.py:39
  25.6 12.1 %collective-permute-start.5 = (bf16[256,128]{1,0:T(8,128)(2,1)S(1)}, bf16[256,128]{1,0:T(8,128)(2,1)S(1)}, u32[]{:S(2)}, u32[]{:S(2)}) collective-permute-start(bf16[256,128]{1,0:T(8,128)(2,1)S(1)} %get-tuple-element.42), channel_id=1, source_target_pairs={{0,8},{8,0},{16,24},{24,16},{1,9},{9,1},{17,25},{25,17},{2,10},{10... | collective-permute-start | bytes 196616 | tf_op jit(solution)/shard_map/ppermute | solution.py:39
  26.1 11.5 %collective-permute-start.6 = (bf16[256,128]{1,0:T(8,128)(2,1)S(1)}, bf16[256,128]{1,0:T(8,128)(2,1)S(1)}, u32[]{:S(2)}, u32[]{:S(2)}) collective-permute-start(bf16[256,128]{1,0:T(8,128)(2,1)S(1)} %get-tuple-element.43), channel_id=1, source_target_pairs={{0,24},{8,16},{16,8},{24,0},{1,25},{9,17},{17,9},{25,1},{2,26},{10... | collective-permute-start | bytes 196616 | tf_op jit(solution)/shard_map/ppermute | solution.py:39
  28.9 3.9 %collective-permute-start.10 = (bf16[96,128]{1,0:T(8,128)(2,1)S(1)}, bf16[96,128]{1,0:T(8,128)(2,1)S(1)}, u32[]{:S(2)}, u32[]{:S(2)}) collective-permute-start(bf16[96,128]{1,0:T(8,128)(2,1)S(1)} %get-tuple-element.50.mine), channel_id=1, source_target_pairs={{0,1},{1,0},{2,3},{3,2},{4,5},{5,4},{6,7},{7,6},{8,9},{9,8},{10,11... | collective-permute-start | bytes 73736 | tf_op jit(solution)/shard_map/ppermute | solution.py:39
  32.9 6.5 %collective-permute-start.11 = (bf16[80,128]{1,0:T(8,128)(2,1)S(1)}, bf16[80,128]{1,0:T(8,128)(2,1)S(1)}, u32[]{:S(2)}, u32[]{:S(2)}) collective-permute-start(bf16[80,128]{1,0:T(8,128)(2,1)S(1)} %get-tuple-element.55), channel_id=1, source_target_pairs={{0,2},{2,0},{4,6},{6,4},{1,3},{3,1},{5,7},{7,5},{8,10},{10,8},{12,... | collective-permute-start | bytes 61448 | tf_op jit(solution)/shard_map/ppermute | solution.py:39
  33.3 6.2 %collective-permute-start.12 = (bf16[80,128]{1,0:T(8,128)(2,1)S(1)}, bf16[80,128]{1,0:T(8,128)(2,1)S(1)}, u32[]{:S(2)}, u32[]{:S(2)}) collective-permute-start(bf16[80,128]{1,0:T(8,128)(2,1)S(1)} %get-tuple-element.56), channel_id=1, source_target_pairs={{0,6},{2,4},{4,2},{6,0},{1,7},{3,5},{5,3},{7,1},{8,14},{10,12},{12... | collective-permute-start | bytes 61448 | tf_op jit(solution)/shard_map/ppermute | solution.py:39
  34.8 4.6 %collective-permute-start.13 = (bf16[64,128]{1,0:T(8,128)(2,1)S(1)}, bf16[64,128]{1,0:T(8,128)(2,1)S(1)}, u32[]{:S(2)}, u32[]{:S(2)}) collective-permute-start(bf16[64,128]{1,0:T(8,128)(2,1)S(1)} %get-tuple-element.54.mine), channel_id=1, source_target_pairs={{0,4},{2,6},{4,0},{6,2},{1,5},{3,7},{5,1},{7,3},{8,12},{10,14},{12... | collective-permute-start | bytes 49160 | tf_op jit(solution)/shard_map/ppermute | solution.py:39

commit v10 on v9

--- a/solution.py
+++ b/solution.py
@@ -57,7 +57,7 @@
     return pair[:half].astype(f32) + pair[half:].astype(f32)
 
 
-def pack_kernel(cells, edges, sent_0, sent_1, rows):
+def pack_kernel(cells, edges, rows):
     chan, count_x, count_y, _ = cells.shape
     count = chan * count_x
     row = iota((2 * count, count * lanes), 0)
@@ -73,42 +73,55 @@
         wide_plane = plane.astype(f32)
         rows[at : at + 1, :] = wide_plane[0:1]
         rows[count + at : count + at + 1, :] = wide_plane[count_y - 1 : count_y]
-    first, last = rows[0:count, :], rows[count : 2 * count, :]
-    sent_0[...] = pick("gy", last, first).astype(bf16)
-    sent_1[...] = pick("gy", first, last).astype(bf16)
-
-
-def bundle_kernel(cells, edges, got_0, got_1, sent_0, sent_1, left, right, rows):
+
+
+def bundle_kernel(cells, edges, sent_0, sent_1, left, right):
     chan, count_x, count_y, _ = cells.shape
     own = chan * count_x
-    above = pick("gy", got_1[...].astype(f32), got_0[...].astype(f32))
-    below = pick("gy", got_0[...].astype(f32), got_1[...].astype(f32))
-    spot = iota((2 * own, lanes), 1)
-    before = pltpu.roll(above[own:], count_y, 1)
-    after = pltpu.roll(below[own:], lanes - count_y, 1)
-    whole = jnp.where(
-        spot == 0, before, jnp.where(spot == count_y + 1, after, edges[...].astype(f32))
-    )
+    whole = edges[...].astype(f32)
     right[...] = whole[0:own]
     left[...] = whole[own : 2 * own]
-    rows_above, rows_below = above[0:own], below[0:own]
-    rows[0:own, :] = rows_above
-    rows[own : 2 * own, :] = rows_below
     zero = jnp.zeros((8, lanes), f32)
     body = chan * count_y
     frames = []
     for x in (0, count_x - 1):
         at = slice(x * chan, x * chan + chan)
-        frame = [rows_above[at], rows_below[at], zero]
-        frame += [whole[own + x * chan : own + (x + 1) * chan], whole[at], zero]
-        frames.append(jnp.concatenate(frame, axis=0))
+        frames.append(jnp.concatenate([whole[own + x * chan :][:chan], whole[at], zero], axis=0))
     even = is_even("gx")
     for ref, odd in ((sent_0, 0), (sent_1, 1)):
         high = even != (odd == 1)
         x = jnp.where(high, count_x - 1, 0)
         for c in range(chan):
             ref[c * count_y : (c + 1) * count_y, :] = cells[c, x]
-        ref[body : body + 32, :] = jnp.where(high, frames[1], frames[0]).astype(bf16)
+        ref[body : body + 16, :] = jnp.where(high, frames[1], frames[0]).astype(bf16)
+
+
+def from_sides(got_0, got_1, start, size):
+    one = got_0[start : start + size, :].astype(f32)
+    two = got_1[start : start + size, :].astype(f32)
+    return pick("gx", two, one), pick("gx", one, two)
+
+
+def rows_kernel(chan, rows, left, right, got_0, got_1, sent_0, sent_1):
+    own = rows.shape[0] // 2
+    body = got_0.shape[0] - 16
+    count_y = body // chan
+    low, high = from_sides(got_0, got_1, body, 16)
+    edges = []
+    for ref, at in ((left, 0), (right, chan)):
+        edges += [ref[...], low[at : at + chan], high[at : at + chan]]
+    edges.append(jnp.zeros((8, lanes), f32))
+    low, high = from_sides(got_0, got_1, 0, body)
+    both = []
+    for at, line in ((0, 0), (own, count_y - 1)):
+        outer = [
+            plane[c * count_y + line : c * count_y + line + 1]
+            for plane in (low, high)
+            for c in range(chan)
+        ]
+        both.append(jnp.concatenate([rows[at : at + own, :]] + outer + edges, axis=0))
+    sent_0[...] = pick("gy", both[1], both[0]).astype(bf16)
+    sent_1[...] = pick("gy", both[0], both[1]).astype(bf16)
 
 
 def spread_kernel(cot, spread):
@@ -124,7 +137,7 @@
             ]
 
 
-def pool_kernel(sums, pooled):
+def pool_kernel(edge, sums, outer_sums, pooled):
     chan_out, pool_x, pool_y, pool_z = pooled.shape
     halves = jnp.where(
         iota((2 * lanes, pool_z), 0) % lanes // 2 == iota((2 * lanes, pool_z), 1), 0.125, 0.0
@@ -132,6 +145,9 @@
     for o in range(0, chan_out, 4):
         rows = 4 * pool_x * pool_y
         part = sums[o * pool_x * pool_y : o * pool_x * pool_y + rows, :]
+        at = iota((rows, lanes), 0) % pool_y
+        near = (at >= edge) & (at < pool_y - edge)
+        part = jnp.where(near, part, outer_sums[o * pool_x * pool_y : o * pool_x * pool_y + rows, :])
         mean = dot(jnp.concatenate(split(part), axis=1), halves) + log_scale * float(np.log(2.0))
         pooled[o : o + 4] = mean.astype(bf16).reshape(4, pool_x, pool_y, pool_z)
 
@@ -145,69 +161,36 @@
     return [before, mid, after]
 
 
-def own_kernel(cells, rows, left, right, inner, stage):
+def own_kernel(cells, left, right, inner, stage):
     chan, count_x, count_y, _ = cells.shape
     own = chan * count_x
     for x in range(count_x):
         for c in range(chan):
             plane = cells[c, x].astype(f32)
             stage[pl.ds(own + x * chan + c, count_y, stride=own), :] = plane
-    stage[0:own, :] = rows[0:own, :]
-    stage[(count_y + 1) * own : (count_y + 2) * own, :] = rows[own : 2 * own, :]
     left_cols, right_cols = left[...], right[...]
-    for y in range(count_y + 2):
+    for y in range(1, count_y + 1):
         whole = shifted(stage[y * own : (y + 1) * own, :], left_cols, right_cols, y)
         whole = jnp.concatenate(whole, axis=0)
         inner[y * 3 * own : (y + 1) * 3 * own, :] = whole.astype(bf16)
 
 
-def main_kernel(
-    count_x, got_0, got_1, inner, spread, wbig, wback,
-    sums, field, sent_0, sent_1, wpart, wframe, rows_out, cols,
-    stage, patches, carry, gram, delta_a, delta_b,
-):
+pairs = 4
+
+
+def sizes_of(count_x, inner, spread, wbig):
     pool_x = count_x // 2
     chan_out = wbig.shape[0] // count_x
     pool_y = spread.shape[0] // (pool_x * chan_out)
-    count_y = 2 * pool_y
-    own = inner.shape[0] // (3 * (count_y + 2))
-    chan = own // count_x
+    own = inner.shape[0] // (3 * (2 * pool_y + 2))
+    return pool_x, chan_out, pool_y, own, own // count_x
+
+
+def worker(count_x, pool_x, chan_out, pool_y, own, chan, near_of, rest_of, refs):
+    spread, wbig, wback, sums, field = refs
     wide = own + 2 * chan
-    outside_rows = 2 * chan
-    depth = 3 * outside_rows + 8
-    body = chan * count_y
+    size = 3 * wide
     lane = iota((wide, lanes), 1)
-    even = is_even("gx")
-
-    def got(up, start, size):
-        one = got_0[start : start + size, :].astype(f32)
-        two = got_1[start : start + size, :].astype(f32)
-        return jnp.where(even, one, two) if up else jnp.where(even, two, one)
-
-    for side in range(2):
-        for c in range(chan):
-            plane = got(side == 1, c * count_y, count_y)
-            at = outside_rows + side * chan + c
-            stage[pl.ds(at, count_y, stride=outside_rows), :] = plane
-    rest_low, rest_high = got(False, body, 32), got(True, body, 32)
-    both = lambda at: jnp.concatenate(
-        [rest_low[at : at + chan], rest_high[at : at + chan]], axis=0
-    )
-    stage[0:outside_rows, :] = both(0)
-    end = (count_y + 1) * outside_rows
-    stage[end : end + outside_rows, :] = both(chan)
-    left_cols, right_cols = both(16), both(16 + chan)
-    for y in range(count_y + 2):
-        mid = stage[y * outside_rows : (y + 1) * outside_rows, :]
-        whole = shifted(mid, left_cols, right_cols, y) + [jnp.ones((8, lanes), f32)]
-        patches[y * depth : (y + 1) * depth, :] = jnp.concatenate(whole, axis=0).astype(bf16)
-
-    carry[...] = jnp.zeros_like(carry)
-    gram[...] = jnp.zeros_like(gram)
-    cols[...] = jnp.zeros_like(cols)
-    pairs = 4
-    steps = count_y // (2 * pairs)
-    size = 3 * wide
     inside, outside = lane != lanes - 1, lane != 0
 
     def finish(y, whole, edge):
@@ -223,12 +206,9 @@
         edge[1] = jnp.where(here, pltpu.roll(last, y + 1, 1), edge[1])
 
     def block_of(j):
-        columns = []
-        for h in range(2):
-            y = 2 * j + h
-            near = inner[pl.ds(aligned(y * 3 * own, 16), 9 * own), :]
-            rest = patches[pl.ds(aligned(y * depth, 16), 3 * depth), :]
-            columns.append(jnp.concatenate([near, rest], axis=0))
+        columns = [
+            jnp.concatenate([near_of(2 * j + h), rest_of(2 * j + h)], axis=0) for h in range(2)
+        ]
         return jnp.concatenate(columns, axis=1)
 
     def forward(i, k, ref):
@@ -268,6 +248,48 @@
         blocks = jnp.concatenate([block_of(i * pairs + k) for k in range(pairs)], axis=1)
         return dot(ref[...], blocks, ((1,), (1,)))
 
+    return finish, forward, backward, weigh
+
+
+def inner_kernel(
+    count_x, got_0, got_1, inner, spread, wbig, wback,
+    sums, field, patches, cols, gram, stage, carry, delta_a, delta_b,
+):
+    shape = sizes_of(count_x, inner, spread, wbig)
+    pool_x, chan_out, pool_y, own, chan = shape
+    count_y = 2 * pool_y
+    wide = own + 2 * chan
+    size = 3 * wide
+    outside_rows = 2 * chan
+    depth = 3 * outside_rows + 8
+    body = chan * count_y
+    for side, planes in enumerate(from_sides(got_0, got_1, 0, body)):
+        for c in range(chan):
+            at = outside_rows + side * chan + c
+            plane = planes[c * count_y : (c + 1) * count_y]
+            stage[pl.ds(at, count_y, stride=outside_rows), :] = plane
+    low, high = from_sides(got_0, got_1, body, 16)
+    left_cols, right_cols = [
+        jnp.concatenate([low[at : at + chan], high[at : at + chan]], axis=0) for at in (0, chan)
+    ]
+    for y in range(1, count_y + 1):
+        mid = stage[y * outside_rows : (y + 1) * outside_rows, :]
+        whole = shifted(mid, left_cols, right_cols, y) + [jnp.ones((8, lanes), f32)]
+        patches[y * depth : (y + 1) * depth, :] = jnp.concatenate(whole, axis=0).astype(bf16)
+
+    def near_of(y):
+        return inner[pl.ds(aligned(y * 3 * own, 16), 9 * own), :]
+
+    def rest_of(y):
+        return patches[pl.ds(aligned(y * depth, 16), 3 * depth), :]
+
+    finish, forward, backward, weigh = worker(
+        count_x, *shape, near_of, rest_of, (spread, wbig, wback, sums, field)
+    )
+    carry[...] = jnp.zeros_like(carry)
+    gram[...] = jnp.zeros_like(gram)
+    cols[...] = jnp.zeros_like(cols)
+
     def opened():
         return (
             [carry[0:size, :], carry[size : 2 * size, :]],
@@ -280,34 +302,100 @@
         cols[0:wide, :] = edge[0]
         cols[wide : 2 * wide, :] = edge[1]
 
+    def both(at):
+        held, edge = opened()
+        total = gram[...] + weigh(at, delta_a)
+        for k in range(pairs):
+            forward(at + 1, k, delta_b)
+            backward(at, k, delta_a, held, edge)
+        return held, edge, total + weigh(at + 1, delta_b)
+
     def step(t, _):
-        held, edge = opened()
-        total = gram[...] + weigh(2 * t, delta_a)
+        at = 2 * t + 1
+        held, edge, total = both(at)
         for k in range(pairs):
-            forward(2 * t + 1, k, delta_b)
-            backward(2 * t, k, delta_a, held, edge)
-        total = total + weigh(2 * t + 1, delta_b)
-        for k in range(pairs):
-            forward(2 * t + 2, k, delta_a)
-            backward(2 * t + 1, k, delta_b, held, edge)
+            forward(at + 2, k, delta_a)
+            backward(at + 1, k, delta_b, held, edge)
         gram[...] = total
         closed(held, edge)
         return 0
 
+    steps = count_y // (2 * pairs)
+    for k in range(pairs):
+        forward(1, k, delta_a)
+    lax.fori_loop(0, steps // 2 - 2, step, 0)
+    held, edge, total = both(steps - 3)
+    gram[...] = total
+    for k in range(pairs):
+        backward(steps - 2, k, delta_b, held, edge)
+    end = (steps - 1) * 2 * pairs
+    finish(end, held[0], edge)
+    finish(end + 1, held[1], edge)
+    closed(held, edge)
+
+
+def main_kernel(
+    count_x, row_0, row_1, inner, patches, inner_cols, inner_gram, spread, wbig, wback,
+    sums, field, sent_0, sent_1, wpart, wframe, rows_out, cols,
+    near, rest, gram, delta_a, delta_b,
+):
+    shape = sizes_of(count_x, inner, spread, wbig)
+    pool_x, chan_out, pool_y, own, chan = shape
+    count_y = 2 * pool_y
+    wide = own + 2 * chan
+    size = 3 * wide
+    outside_rows = 2 * chan
+    depth = 3 * outside_rows + 8
+    even = is_even("gx")
+    span_y = 2 * pairs
+    top = span_y + 2
+    start = count_y - span_y
+    for ref, source, height in ((near, inner, 3 * own), (rest, patches, depth)):
+        ref[height : top * height, :] = source[height : top * height, :]
+        last = (2 * top - 1) * height
+        ref[top * height : last, :] = source[start * height : (count_y + 1) * height, :]
+    one, two = row_0[...].astype(f32), row_1[...].astype(f32)
+    above, below = pick("gy", two, one), pick("gy", one, two)
+    for at, got, line in ((0, above, count_y), (2 * top - 1, below, 1)):
+        left, right = got[wide : 2 * wide], got[2 * wide : 3 * wide]
+        whole = jnp.concatenate(shifted(got[:own], left[:own], right[:own], line), axis=0)
+        near[at * 3 * own : (at + 1) * 3 * own, :] = whole.astype(bf16)
+        whole = shifted(got[own:wide], left[own:], right[own:], line)
+        whole = jnp.concatenate(whole + [jnp.ones((8, lanes), f32)], axis=0)
+        rest[at * depth : (at + 1) * depth, :] = whole.astype(bf16)
+
+    def place(y):
+        return y if y < top else y - start + top
+
+    def near_of(y):
+        return near[place(y) * 3 * own : (place(y) + 3) * 3 * own, :]
+
+    def rest_of(y):
+        return rest[place(y) * depth : (place(y) + 3) * depth, :]
+
+    finish, forward, backward, weigh = worker(
+        count_x, *shape, near_of, rest_of, (spread, wbig, wback, sums, field)
+    )
+    final = count_y // span_y - 1
+    zero = jnp.zeros((size, lanes), f32)
+    held, edge = [zero, zero], [inner_cols[0:wide, :], inner_cols[wide : 2 * wide, :]]
+    extra = [jnp.zeros((wide, lanes), f32)] * 2
     for k in range(pairs):
         forward(0, k, delta_a)
-    lax.fori_loop(0, steps // 2 - 1, step, 0)
-    held, edge = opened()
-    total = gram[...] + weigh(steps - 2, delta_a)
     for k in range(pairs):
-        forward(steps - 1, k, delta_b)
-        backward(steps - 2, k, delta_a, held, edge)
-    gram[...] = total + weigh(steps - 1, delta_b)
+        forward(final, k, delta_b)
+        backward(0, k, delta_a, held, extra)
+    total = inner_gram[...] + weigh(0, delta_a)
+    finish(span_y, held[0], extra)
+    finish(span_y + 1, held[1], extra)
+    held = [zero, zero]
     for k in range(pairs):
-        backward(steps - 1, k, delta_b, held, edge)
-    finish(count_y, held[0], edge)
-    finish(count_y + 1, held[1], edge)
-    closed(held, edge)
+        backward(final, k, delta_b, held, extra)
+    gram[...] = total + weigh(final, delta_b)
+    finish(count_y, held[0], extra)
+    finish(count_y + 1, held[1], extra)
+    cols[0:wide, :] = edge[0] + extra[0]
+    cols[wide : 2 * wide, :] = edge[1] + extra[1]
 
     span = gram.shape[1]
     spot = iota((chan_out, 2 * lanes), 1)
@@ -360,13 +448,22 @@
         ref[16 + tall :, :] = sides
 
 
-def face_kernel(chan, field, face_0, face_1):
+def plane_of(field, outer_field, at, wide, count_y):
+    row = iota((count_y, lanes), 0) + 1
+    span_y = 2 * pairs
+    place = pl.ds(wide + at, count_y, stride=wide)
+    near = (row >= span_y) & (row < count_y - span_y + 2)
+    far = (row < span_y + 2) | (row >= count_y - span_y)
+    return jnp.where(near, field[place, :], 0.0) + jnp.where(far, outer_field[place, :], 0.0)
+
+
+def face_kernel(chan, field, outer_field, face_0, face_1):
     count_y = face_0.shape[0] // chan
     wide = field.shape[0] // (count_y + 2)
     even = is_even("gx")
     for c in range(chan):
         low, high = [
-            field[pl.ds(wide + at + c, count_y, stride=wide), :] for at in (0, wide - chan)
+            plane_of(field, outer_field, at + c, wide, count_y) for at in (0, wide - chan)
         ]
         place = slice(c * count_y, (c + 1) * count_y)
         face_0[place, :] = jnp.where(even, high, low).astype(bf16)
@@ -419,7 +516,7 @@
         ref[own:, :] = sides
 
 
-def grad_kernel(field, face_0, face_1, got, grad, ends):
+def grad_kernel(field, outer_field, face_0, face_1, got, grad, ends):
     chan, count_x, count_y, _ = grad.shape
     own = chan * count_x
     wide = own + 2 * chan
@@ -430,7 +527,7 @@
     for x in range(count_x):
         for c in range(chan):
             at = x * chan + c
-            plane = field[pl.ds(wide + chan + at, count_y, stride=wide), :]
+            plane = plane_of(field, outer_field, chan + at, wide, count_y)
             place = slice(c * count_y, (c + 1) * count_y)
             if x == 0:
                 plane = plane + pick("gx", face_1[place, :].astype(f32), face_0[place, :].astype(f32))
@@ -523,42 +620,58 @@
     wbig = jnp.concatenate([near, rest.reshape(count_x * chan_out, 3 * depth)], axis=1)
     wback = placed.reshape(count_x * chan_out, 9 * wide).T
 
-    own_block = shape((own, lanes), bf16)
-    edges, row_0, row_1 = call(
-        pack_kernel,
-        [shape((2 * own, lanes), bf16), own_block, own_block],
-        [
-            pltpu.VMEM((2 * own, lanes), f32),
-        ],
+    edges, rows = call(
+        pack_kernel, [shape((2 * own, lanes), bf16), shape((2 * own, lanes), f32)]
     )(cells)
     pool_x, pool_y, pool_z = cotangent.shape[1:]
     pooled_rows = shape((pool_y * pool_x * chan_out, lanes), f32)
     spread = call(spread_kernel, pooled_rows)(cotangent)
     edges = swapped(edges, "gz", 0)
-    row_1 = swapped(jnp.concatenate([row_1, edges]), "gy", 1)
-    row_0 = swapped(jnp.concatenate([row_0, edges]), "gy", 0)
     body = chan * count_y
-    bundle = shape((body + 32, lanes), bf16)
+    bundle = shape((body + 16, lanes), bf16)
     side = shape((own, lanes), f32)
-    face_0, face_1, left, right, rows = call(
-        bundle_kernel, [bundle, bundle, side, side, shape((2 * own, lanes), f32)]
-    )(cells, edges, row_0, row_1)
+    face_0, face_1, left, right = call(bundle_kernel, [bundle, bundle, side, side])(cells, edges)
     face_1, face_0 = swapped(face_1, "gx", 1), swapped(face_0, "gx", 0)
     inner = call(
         own_kernel,
         shape(((count_y + 2) * 3 * own, lanes), bf16),
         [pltpu.VMEM(((count_y + 2) * own, lanes), f32)],
         traffic(4),
-    )(cells, rows, left, right)
+    )(cells, left, right)
+    bundle = shape((3 * wide + 8, lanes), bf16)
+    row_0, row_1 = call(functools.partial(rows_kernel, chan), [bundle, bundle])(
+        rows, left, right, face_0, face_1
+    )
+    row_1, row_0 = swapped(row_1, "gy", 1), swapped(row_0, "gy", 0)
 
     tall = 2 * wide
+    all_field = shape(((count_y + 2) * wide, lanes), f32)
+    all_gram = shape((count_x * chan_out, 9 * own + 3 * depth), f32)
+    deltas = [pltpu.VMEM((count_x * chan_out, 8 * lanes), bf16)] * 2
+    sums, field, patches, cols, gram = call(
+        functools.partial(inner_kernel, count_x),
+        [
+            pooled_rows,
+            all_field,
+            shape(((count_y + 2) * depth, lanes), bf16),
+            shape((tall, lanes), f32),
+            all_gram,
+        ],
+        [
+            pltpu.VMEM(((count_y + 2) * 2 * chan, lanes), f32),
+            pltpu.VMEM((6 * wide, lanes), f32),
+        ]
+        + deltas,
+        traffic(16),
+    )(face_0, face_1, inner, spread, wbig, wback)
+
     bundle = shape((16 + tall + 2 * chan_out, lanes), bf16)
     face = shape((body, lanes), bf16)
-    sums, field, row_0, row_1, wpart, wframe, rows, cols = call(
+    outer_sums, outer_field, row_0, row_1, wpart, wframe, rows, cols = call(
         functools.partial(main_kernel, count_x),
         [
             pooled_rows,
-            shape(((count_y + 2) * wide, lanes), f32),
+            all_field,
             bundle,
             bundle,
             shape((chan_out, lanes), f32),
@@ -567,14 +680,12 @@
             shape((tall, lanes), f32),
         ],
         [
-            pltpu.VMEM(((count_y + 2) * 2 * chan, lanes), f32),
-            pltpu.VMEM(((count_y + 2) * depth, lanes), bf16),
-            pltpu.VMEM((6 * wide, lanes), f32),
+            pltpu.VMEM((4 * (pairs + 1) * 3 * own, lanes), bf16),
+            pltpu.VMEM((4 * (pairs + 1) * depth, lanes), bf16),
             pltpu.VMEM((count_x * chan_out, 9 * own + 3 * depth), f32),
-            pltpu.VMEM((count_x * chan_out, 8 * lanes), bf16),
-            pltpu.VMEM((count_x * chan_out, 8 * lanes), bf16),
-        ],
-    )(face_0, face_1, inner, spread, wbig, wback)
+        ]
+        + deltas,
+    )(row_0, row_1, inner, patches, cols, gram, spread, wbig, wback)
 
     alone = lax.axis_size("gx") != 4
     if alone:
@@ -582,9 +693,13 @@
     else:
         far = swapped(row_0, "gx", 2)
     row_1, row_0 = swapped(row_1, "gx", 1), swapped(row_0, "gx", 0)
-    face_0, face_1 = call(functools.partial(face_kernel, chan), [face, face], cost=traffic(2))(field)
+    face_0, face_1 = call(functools.partial(face_kernel, chan), [face, face], cost=traffic(2))(
+        field, outer_field
+    )
     face_1, face_0 = swapped(face_1, "gx", 1), swapped(face_0, "gx", 0)
-    pooled = call(pool_kernel, shape(cotangent.shape, bf16), cost=traffic(8))(sums)
+    pooled = call(
+        functools.partial(pool_kernel, pairs), shape(cotangent.shape, bf16), cost=traffic(8)
+    )(sums, outer_sums)
     mine, rows = call(
         functools.partial(x_kernel, alone),
         [shape((2 * own + 2 * chan_out, lanes), bf16), shape((2 * own, lanes), f32)],
@@ -599,7 +714,7 @@
     far = swapped(mine, "gy", 2)
     tiles = (2, chan, count_x, 8, lanes)
     grad, ends = call(grad_kernel, [shape(cells.shape, f32), shape(tiles, f32)], cost=traffic(8))(
-        field, face_0, face_1, frame
+        field, outer_field, face_0, face_1, frame
     )
     vmem, anywhere = pl.BlockSpec(memory_space=pltpu.VMEM), pl.BlockSpec(memory_space=pl.ANY)
     input_grad, wsum, bias_grad = call(

time: 40.4 us -> 38.5 us (0.953)
  waiting for transfers between devices: 9 us -> 6.73 us
    ppermute x14, waiting for transfers between devices: 9 us -> 6.73 us  [swapped(): return lax.ppermute(array, axis, pairs)]
    slice x2, local copies, waits for them, and re-layouts: 0.65 us -> 0.01 us  [on_device(): near = placed[:, :, :, 1:count_x + 1].reshape(count_x * chan_out, 9 * own)]
    unnamed x12, local copies, waits for them, and re-layouts: 0.97 us -> 1.52 us
    pallas_call x4 -> x6, Pallas kernels: 6.53 us -> 6.68 us  [the longest x1 3.67 us: on_device(): call(functools.partial(inner_kernel, count_x), [pooled_rows, all_field, s...]
  transfers between devices with their start and end apart: 14 -> 14, of which waited for: 6 -> 5; matrix products, arithmetic and copies ran while one was open for 3% -> 3% of each run, Pallas kernels for 10% -> 20%
where the time goes in v10:
time: 38.5 us; the launch traced here: 38.4 us
  starting transfers between devices  18 us (47%)
  Pallas kernels  10.1 us (26%)
  waiting for transfers between devices  6.73 us (17%)
  local copies, waits for them, and re-layouts  2.31 us (6%)
  between operations  0.84 us (2%)
    ppermute x14, starting transfers between devices, swapped(): return lax.ppermute(array, axis, pairs)  18 us
    ppermute x14, waiting for transfers between devices, swapped(): return lax.ppermute(array, axis, pairs)  6.73 us
    pallas_call x1, Pallas kernels, on_device(): call(functools.partial(inner_kernel, count_x), [pooled_rows, all_field, s...  3.67 us
    unnamed x12, local copies, waits for them, and re-layouts  1.52 us
    pallas_call x1, Pallas kernels, on_device(): call(functools.partial(main_kernel, count_x), [pooled_rows, all_field, bu...  1.49 us
    pallas_call x1, Pallas kernels, on_device(): call(functools.partial(pool_kernel, pairs), shape(cotangent.shape, bf16),...  1.23 us
    pallas_call x1, Pallas kernels, on_device(): call(grad_kernel, [shape(cells.shape, f32), shape(tiles, f32)], cost=traf...  1.19 us
    pallas_call x1, Pallas kernels, on_device(): spread = call(spread_kernel, pooled_rows)(cotangent)  0.88 us
  transfers between devices with their start and end apart: 14, of which 5 were waited for; matrix products, arithmetic and copies ran while one was open for 3% of the time, Pallas kernels for 20%

profile of v10, /device:TPU:0, one launch (start us, length us, event | category | flops | bytes accessed | tf_op | source)
XLA Modules:
  0.0 38.4 jit_solution(16802193732382762146)
XLA Ops:
  0.6 0.9 %copy-done = bf16[4,4,64,128]{3,2,1,0:T(8,128)(2,1)S(1)} copy-done((bf16[4,4,64,128]{3,2,1,0:T(8,128)(2,1)S(1)}, bf16[4,4,64,128]{3,2,1,0:T(8,128)(2,1)}, u32[]{:S(2)}) %copy-start) | copy-done | bytes 262168
  1.8 3.0 %collective-permute-start = (bf16[32,128]{1,0:T(8,128)(2,1)S(1)}, bf16[32,128]{1,0:T(8,128)(2,1)S(1)}, u32[]{:S(2)}, u32[]{:S(2)}) collective-permute-start(bf16[32,128]{1,0:T(8,128)(2,1)S(1)} %get-tuple-element.37), channel_id=1, source_target_pairs={{0,1},{1,0},{2,3},{3,2},{4,5},{5,4},{6,7},{7,6},{8,9},{9,8},{10,11... | collective-permute-start | bytes 24584 | tf_op jit(solution)/shard_map/ppermute | solution.py:39
  5.5 0.6 %copy-done.3 = bf16[128,3,3,6,4]{0,4,3,2,1:T(4,128)(2,1)} copy-done((bf16[128,3,3,6,4]{0,4,3,2,1:T(4,128)(2,1)}, bf16[128,3,3,6,4]{0,4,3,2,1:T(4,128)(2,1)S(1)}, u32[]{:S(2)}) %copy-start.3) | copy-done | bytes 55320
  6.6 2.1 %collective-permute-start.2 = (bf16[272,128]{1,0:T(8,128)(2,1)S(1)}, bf16[272,128]{1,0:T(8,128)(2,1)S(1)}, u32[]{:S(2)}, u32[]{:S(2)}) collective-permute-start(bf16[272,128]{1,0:T(8,128)(2,1)S(1)} %get-tuple-element.39), channel_id=1, source_target_pairs={{0,24},{8,16},{16,8},{24,0},{1,25},{9,17},{17,9},{25,1},{2,26},{10... | collective-permute-start | bytes 208904 | tf_op jit(solution)/shard_map/ppermute | solution.py:39
  8.9 2.1 %collective-permute-done.2.got_1 = bf16[272,128]{1,0:T(8,128)(2,1)S(1)} collective-permute-done((bf16[272,128]{1,0:T(8,128)(2,1)S(1)}, bf16[272,128]{1,0:T(8,128)(2,1)S(1)}, u32[]{:S(2)}, u32[]{:S(2)}) %collective-permute-start.2) | collective-permute-done | bytes 69664 | tf_op jit(solution)/shard_map/ppermute | solution.py:39
  11.1 1.7 %collective-permute-start.3 = (bf16[80,128]{1,0:T(8,128)(2,1)S(1)}, bf16[80,128]{1,0:T(8,128)(2,1)S(1)}, u32[]{:S(2)}, u32[]{:S(2)}) collective-permute-start(bf16[80,128]{1,0:T(8,128)(2,1)S(1)} %get-tuple-element.44), channel_id=1, source_target_pairs={{0,2},{2,0},{4,6},{6,4},{1,3},{3,1},{5,7},{7,5},{8,10},{10,8},{12,... | collective-permute-start | bytes 61448 | tf_op jit(solution)/shard_map/ppermute | solution.py:39
  12.8 2.5 %collective-permute-start.4 = (bf16[80,128]{1,0:T(8,128)(2,1)S(1)}, bf16[80,128]{1,0:T(8,128)(2,1)S(1)}, u32[]{:S(2)}, u32[]{:S(2)}) collective-permute-start(bf16[80,128]{1,0:T(8,128)(2,1)S(1)} %get-tuple-element.45), channel_id=1, source_target_pairs={{0,6},{2,4},{4,2},{6,0},{1,7},{3,5},{5,3},{7,1},{8,14},{10,12},{12... | collective-permute-start | bytes 61448 | tf_op jit(solution)/shard_map/ppermute | solution.py:39
  15.5 0.9 %shard_map.78.spread = f32[2048,128]{1,0:T(8,128)S(1)} custom-call(bf16[32,2,32,64]{3,2,1,0:T(8,128)(2,1)S(1)} %copy-done.2), custom_call_target="tpu_custom_call" | custom-call | tf_op jit(solution)/shard_map/pallas_call | solution.py:628
  16.4 0.4 %shard_map.77.inner = bf16[3168,128]{1,0:T(8,128)(2,1)S(1)} custom-call(bf16[4,4,64,128]{3,2,1,0:T(8,128)(2,1)S(1)} %copy-done.1, f32[16,128]{1,0:T(8,128)S(1)} %get-tuple-element.40.left, f32[16,128]{1,0:T(8,128)S(1)} %get-tuple-element.41.right), custom_call_target="tpu_custom_call" | custom-call | bytes 4194304 | tf_op jit(solution)/shard_map/pallas_call | solution.py:635
  16.8 3.7 %shard_map.79 = (f32[2048,128]{1,0:T(8,128)S(1)}, f32[1584,128]{1,0:T(8,128)S(1)}, bf16[2112,128]{1,0:T(8,128)(2,1)S(1)}, f32[48,128]{1,0:T(8,128)S(1)}, f32[128,240]{1,0:T(8,128)S(1)}) custom-call(bf16[272,128]{1,0:T(8,128)(2,1)S(1)} %collective-permute-done.1.got_0, bf16[272,128]{1,0:T(8,128)(2,1)S(1)} %collective-permute-done.2.got_1, ...), custom_call_target="tpu_custom_call" | custom-call | bytes 16777216 | tf_op jit(solution)/shard_map/pallas_call | solution.py:651
  20.5 1.5 %shard_map.81 = (f32[2048,128]{1,0:T(8,128)S(1)}, f32[1584,128]{1,0:T(8,128)S(1)}, bf16[128,128]{1,0:T(8,128)(2,1)S(1)}, bf16[128,128]{1,0:T(8,128)(2,1)S(1)}, f...) custom-call(bf16[80,128]{1,0:T(8,128)(2,1)S(1)} %collective-permute-done.3.ro, ...), custom_call_target="tpu_custom_call" | custom-call | tf_op jit(solution)/shard_map/pallas_call | solution.py:670
  22.0 1.0 %collective-permute-start.8 = (bf16[128,128]{1,0:T(8,128)(2,1)S(1)}, bf16[128,128]{1,0:T(8,128)(2,1)S(1)}, u32[]{:S(2)}, u32[]{:S(2)}) collective-permute-start(bf16[128,128]{1,0:T(8,128)(2,1)S(1)} %get-tuple-element.59), channel_id=1, source_target_pairs={{0,24},{8,16},{16,8},{24,0},{1,25},{9,17},{17,9},{25,1},{2,26},{10... | collective-permute-start | bytes 98312 | tf_op jit(solution)/shard_map/ppermute | solution.py:39
  22.9 0.7 %collective-permute-start.9 = (bf16[128,128]{1,0:T(8,128)(2,1)S(1)}, bf16[128,128]{1,0:T(8,128)(2,1)S(1)}, u32[]{:S(2)}, u32[]{:S(2)}) collective-permute-start(bf16[128,128]{1,0:T(8,128)(2,1)S(1)} %get-tuple-element.58), channel_id=1, source_target_pairs={{0,16},{8,24},{16,0},{24,8},{1,17},{9,25},{17,1},{25,9},{2,18},{10... | collective-permute-start | bytes 98312 | tf_op jit(solution)/shard_map/ppermute | solution.py:39
  24.3 1.4 %collective-permute-start.6 = (bf16[256,128]{1,0:T(8,128)(2,1)S(1)}, bf16[256,128]{1,0:T(8,128)(2,1)S(1)}, u32[]{:S(2)}, u32[]{:S(2)}) collective-permute-start(bf16[256,128]{1,0:T(8,128)(2,1)S(1)} %get-tuple-element.53), channel_id=1, source_target_pairs={{0,24},{8,16},{16,8},{24,0},{1,25},{9,17},{17,9},{25,1},{2,26},{10... | collective-permute-start | bytes 196616 | tf_op jit(solution)/shard_map/ppermute | solution.py:39
  25.7 1.3 %collective-permute-done.9.far = bf16[128,128]{1,0:T(8,128)(2,1)S(1)} collective-permute-done((bf16[128,128]{1,0:T(8,128)(2,1)S(1)}, bf16[128,128]{1,0:T(8,128)(2,1)S(1)}, u32[]{:S(2)}, u32[]{:S(2)}) %collective-permute-start.9) | collective-permute-done | bytes 32800 | tf_op jit(solution)/shard_map/ppermute | solution.py:39
  27.0 1.6 %collective-permute-start.10 = (bf16[96,128]{1,0:T(8,128)(2,1)S(1)}, bf16[96,128]{1,0:T(8,128)(2,1)S(1)}, u32[]{:S(2)}, u32[]{:S(2)}) collective-permute-start(bf16[96,128]{1,0:T(8,128)(2,1)S(1)} %get-tuple-element.60.mine), channel_id=1, source_target_pairs={{0,1},{1,0},{2,3},{3,2},{4,5},{5,4},{6,7},{7,6},{8,9},{9,8},{10,11... | collective-permute-start | bytes 73736 | tf_op jit(solution)/shard_map/ppermute | solution.py:39
  28.6 2.3 %collective-permute-done.10.got = bf16[96,128]{1,0:T(8,128)(2,1)S(1)} collective-permute-done((bf16[96,128]{1,0:T(8,128)(2,1)S(1)}, bf16[96,128]{1,0:T(8,128)(2,1)S(1)}, u32[]{:S(2)}, u32[]{:S(2)}) %collective-permute-start.10) | collective-permute-done | bytes 24608 | tf_op jit(solution)/shard_map/ppermute | solution.py:39
  31.0 0.7 %collective-permute-start.11 = (bf16[80,128]{1,0:T(8,128)(2,1)S(1)}, bf16[80,128]{1,0:T(8,128)(2,1)S(1)}, u32[]{:S(2)}, u32[]{:S(2)}) collective-permute-start(bf16[80,128]{1,0:T(8,128)(2,1)S(1)} %get-tuple-element.65), channel_id=1, source_target_pairs={{0,2},{2,0},{4,6},{6,4},{1,3},{3,1},{5,7},{7,5},{8,10},{10,8},{12,... | collective-permute-start | bytes 61448 | tf_op jit(solution)/shard_map/ppermute | solution.py:39
  31.7 1.1 %collective-permute-start.12 = (bf16[80,128]{1,0:T(8,128)(2,1)S(1)}, bf16[80,128]{1,0:T(8,128)(2,1)S(1)}, u32[]{:S(2)}, u32[]{:S(2)}) collective-permute-start(bf16[80,128]{1,0:T(8,128)(2,1)S(1)} %get-tuple-element.66), channel_id=1, source_target_pairs={{0,6},{2,4},{4,2},{6,0},{1,7},{3,5},{5,3},{7,1},{8,14},{10,12},{12... | collective-permute-start | bytes 61448 | tf_op jit(solution)/shard_map/ppermute | solution.py:39
  32.7 1.7 %collective-permute-start.13 = (bf16[64,128]{1,0:T(8,128)(2,1)S(1)}, bf16[64,128]{1,0:T(8,128)(2,1)S(1)}, u32[]{:S(2)}, u32[]{:S(2)}) collective-permute-start(bf16[64,128]{1,0:T(8,128)(2,1)S(1)} %get-tuple-element.64.mine), channel_id=1, source_target_pairs={{0,4},{2,6},{4,0},{6,2},{1,5},{3,7},{5,1},{7,3},{8,12},{10,14},{12... | collective-permute-start | bytes 49160 | tf_op jit(solution)/shard_map/ppermute | solution.py:39
  34.5 1.2 %shard_map.82 = bf16[32,2,32,64]{3,2,1,0:T(8,128)(2,1)} custom-call(f32[2048,128]{1,0:T(8,128)S(1)} %get-tuple-element.42.sums, f32[2048,128]{1,0:T(8,128)S(1)} %get-tuple-element.49.outer_sums), custom_call_target="tpu_custom_call" | custom-call | bytes 8388608 | tf_op jit(solution)/shard_map/pallas_call | solution.py:700
  35.7 1.2 %shard_map.85 = (f32[4,4,64,128]{3,2,1,0:T(8,128)}, f32[2,4,4,8,128]{4,3,2,1,0:T(8,128)S(1)}) custom-call(f32[1584,128]{1,0:T(8,128)S(1)} %get-tuple-element.50.field, f32[1584,128]{1,0:T(8,128)S(1)} %get-tuple-element.51.outer_field, bf16[256,128]{1,0:T(8,128)(2,1)S(1)} %collective-permute-done.5.face_0, ...), custom_call_target="tpu_custom_call" | custom-call | bytes 8388608 | tf_op jit(solution)/shard_map/pallas_call | solution.py:716
  36.9 0.7 %collective-permute-done.13.far = bf16[64,128]{1,0:T(8,128)(2,1)S(1)} collective-permute-done((bf16[64,128]{1,0:T(8,128)(2,1)S(1)}, bf16[64,128]{1,0:T(8,128)(2,1)S(1)}, u32[]{:S(2)}, u32[]{:S(2)}) %collective-permute-start.13) | collective-permute-done | bytes 16416 | tf_op jit(solution)/shard_map/ppermute | solution.py:39
  37.6 0.8 %shard_map.87 = (f32[4,4,64,128]{3,2,1,0:T(8,128)}, f32[27,4,32]{2,1,0:T(4,128)}, f32[1,32]{1,0:T(1,128)}) custom-call(f32[4,4,64,128]{3,2,1,0:T(8,128)} %get-tuple-element.61.whole, f32[2,4,4,8,128]{4,3,2,1,0:T(8,128)S(1)} %get-tuple-element.62.ends, bf16[64,128]{1,0:T(8,128)(2,1)S(1)} %get-tuple-element.64.mine, ...), custom_call_target="tpu_custom_call", output_to_operand_aliasing={{0}: (0, {})} | custom-call | tf_op jit(solution)/shard_map/pallas_call | solution.py:720
  (46 shorter events, 2.6 us)
Async XLA Ops:
  0.6 1.0 %copy-start = (bf16[4,4,64,128]{3,2,1,0:T(8,128)(2,1)S(1)}, bf16[4,4,64,128]{3,2,1,0:T(8,128)(2,1)}, u32[]{:S(2)}) copy-start(bf16[4,4,64,128]{3,2,1,0:T(8,128)(2,1)} %cells.5) | copy-start | bytes 786436
  1.6 3.3 %copy-start.4 = (bf16[32,4,3,3,3]{0,1,4,3,2:T(4,128)(2,1)S(1)}, bf16[32,4,3,3,3]{0,1,4,3,2:T(4,128)(2,1)}, u32[]{:S(2)}) copy-start(bf16[32,4,3,3,3]{0,1,4,3,2:T(4,128)(2,1)} %param.5) | copy-start | bytes 20740
  1.8 3.0 %copy-start.5 = (f32[32]{0:T(128)S(1)}, f32[32]{0:T(128)}, u32[]{:S(2)}) copy-start(f32[32]{0:T(128)} %param.6) | copy-start | bytes 388
  1.8 4.6 %collective-permute-start = (bf16[32,128]{1,0:T(8,128)(2,1)S(1)}, bf16[32,128]{1,0:T(8,128)(2,1)S(1)}, u32[]{:S(2)}, u32[]{:S(2)}) collective-permute-start(bf16[32,128]{1,0:T(8,128)(2,1)S(1)} %get-tuple-element.37), channel_id=1, source_target_pairs={{0,1},{1,0},{2,3},{3,2},{4,5},{5,4},{6,7},{7,6},{8,9},{9,8},{10,11... | collective-permute-start | bytes 24584 | tf_op jit(solution)/shard_map/ppermute | solution.py:39
  5.2 1.2 %copy-start.1 = (bf16[4,4,64,128]{3,2,1,0:T(8,128)(2,1)S(1)}, bf16[4,4,64,128]{3,2,1,0:T(8,128)(2,1)}, u32[]{:S(2)}) copy-start(bf16[4,4,64,128]{3,2,1,0:T(8,128)(2,1)} %cells.5) | copy-start | bytes 786436
  5.4 0.6 %copy-start.3 = (bf16[128,3,3,6,4]{0,4,3,2,1:T(4,128)(2,1)}, bf16[128,3,3,6,4]{0,4,3,2,1:T(4,128)(2,1)S(1)}, u32[]{:S(2)}) copy-start(bf16[128,3,3,6,4]{0,4,3,2,1:T(4,128)(2,1)S(1)} %reshape.59) | copy-start | bytes 165892
  6.1 2.8 %slice-start = ((bf16[128,3,3,6,4]{0,4,3,2,1:T(4,128)(2,1)}), bf16[128,3,3,4,4]{0,4,3,2,1:T(4,128)(2,1)S(1)}, s32[]{:S(2)}) async-start(bf16[128,3,3,6,4]{0,4,3,2,1:T(4,128)(2,1)} %copy-done.3), calls=%async_computation | async-start | bytes 73728 | tf_op jit(solution)/shard_map/slice | solution.py:617
  6.1 9.3 %copy-start.2 = (bf16[32,2,32,64]{3,2,1,0:T(8,128)(2,1)S(1)}, bf16[32,2,32,64]{3,2,1,0:T(8,128)(2,1)}, u32[]{:S(2)}) copy-start(bf16[32,2,32,64]{3,2,1,0:T(8,128)(2,1)} %cot.1) | copy-start | bytes 786436
  6.5 2.4 %collective-permute-start.1 = (bf16[272,128]{1,0:T(8,128)(2,1)S(1)}, bf16[272,128]{1,0:T(8,128)(2,1)S(1)}, u32[]{:S(2)}, u32[]{:S(2)}) collective-permute-start(bf16[272,128]{1,0:T(8,128)(2,1)S(1)} %get-tuple-element.38), channel_id=1, source_target_pairs={{0,8},{8,0},{16,24},{24,16},{1,9},{9,1},{17,25},{25,17},{2,10},{10... | collective-permute-start | bytes 208904 | tf_op jit(solution)/shard_map/ppermute | solution.py:39
  6.6 4.5 %collective-permute-start.2 = (bf16[272,128]{1,0:T(8,128)(2,1)S(1)}, bf16[272,128]{1,0:T(8,128)(2,1)S(1)}, u32[]{:S(2)}, u32[]{:S(2)}) collective-permute-start(bf16[272,128]{1,0:T(8,128)(2,1)S(1)} %get-tuple-element.39), channel_id=1, source_target_pairs={{0,24},{8,16},{16,8},{24,0},{1,25},{9,17},{17,9},{25,1},{2,26},{10... | collective-permute-start | bytes 208904 | tf_op jit(solution)/shard_map/ppermute | solution.py:39
  11.1 9.4 %collective-permute-start.3 = (bf16[80,128]{1,0:T(8,128)(2,1)S(1)}, bf16[80,128]{1,0:T(8,128)(2,1)S(1)}, u32[]{:S(2)}, u32[]{:S(2)}) collective-permute-start(bf16[80,128]{1,0:T(8,128)(2,1)S(1)} %get-tuple-element.44), channel_id=1, source_target_pairs={{0,2},{2,0},{4,6},{6,4},{1,3},{3,1},{5,7},{7,5},{8,10},{10,8},{12,... | collective-permute-start | bytes 61448 | tf_op jit(solution)/shard_map/ppermute | solution.py:39
  12.8 7.7 %collective-permute-start.4 = (bf16[80,128]{1,0:T(8,128)(2,1)S(1)}, bf16[80,128]{1,0:T(8,128)(2,1)S(1)}, u32[]{:S(2)}, u32[]{:S(2)}) collective-permute-start(bf16[80,128]{1,0:T(8,128)(2,1)S(1)} %get-tuple-element.45), channel_id=1, source_target_pairs={{0,6},{2,4},{4,2},{6,0},{1,7},{3,5},{5,3},{7,1},{8,14},{10,12},{12... | collective-permute-start | bytes 61448 | tf_op jit(solution)/shard_map/ppermute | solution.py:39
  22.0 3.7 %collective-permute-start.8 = (bf16[128,128]{1,0:T(8,128)(2,1)S(1)}, bf16[128,128]{1,0:T(8,128)(2,1)S(1)}, u32[]{:S(2)}, u32[]{:S(2)}) collective-permute-start(bf16[128,128]{1,0:T(8,128)(2,1)S(1)} %get-tuple-element.59), channel_id=1, source_target_pairs={{0,24},{8,16},{16,8},{24,0},{1,25},{9,17},{17,9},{25,1},{2,26},{10... | collective-permute-start | bytes 98312 | tf_op jit(solution)/shard_map/ppermute | solution.py:39
  22.9 4.0 %collective-permute-start.9 = (bf16[128,128]{1,0:T(8,128)(2,1)S(1)}, bf16[128,128]{1,0:T(8,128)(2,1)S(1)}, u32[]{:S(2)}, u32[]{:S(2)}) collective-permute-start(bf16[128,128]{1,0:T(8,128)(2,1)S(1)} %get-tuple-element.58), channel_id=1, source_target_pairs={{0,16},{8,24},{16,0},{24,8},{1,17},{9,25},{17,1},{25,9},{2,18},{10... | collective-permute-start | bytes 98312 | tf_op jit(solution)/shard_map/ppermute | solution.py:39
  23.6 3.3 %collective-permute-start.7 = (bf16[128,128]{1,0:T(8,128)(2,1)S(1)}, bf16[128,128]{1,0:T(8,128)(2,1)S(1)}, u32[]{:S(2)}, u32[]{:S(2)}) collective-permute-start(bf16[128,128]{1,0:T(8,128)(2,1)S(1)} %get-tuple-element.58), channel_id=1, source_target_pairs={{0,8},{8,0},{16,24},{24,16},{1,9},{9,1},{17,25},{25,17},{2,10},{10... | collective-permute-start | bytes 98312 | tf_op jit(solution)/shard_map/ppermute | solution.py:39
  24.0 11.7 %collective-permute-start.5 = (bf16[256,128]{1,0:T(8,128)(2,1)S(1)}, bf16[256,128]{1,0:T(8,128)(2,1)S(1)}, u32[]{:S(2)}, u32[]{:S(2)}) collective-permute-start(bf16[256,128]{1,0:T(8,128)(2,1)S(1)} %get-tuple-element.52), channel_id=1, source_target_pairs={{0,8},{8,0},{16,24},{24,16},{1,9},{9,1},{17,25},{25,17},{2,10},{10... | collective-permute-start | bytes 196616 | tf_op jit(solution)/shard_map/ppermute | solution.py:39
  24.3 11.4 %collective-permute-start.6 = (bf16[256,128]{1,0:T(8,128)(2,1)S(1)}, bf16[256,128]{1,0:T(8,128)(2,1)S(1)}, u32[]{:S(2)}, u32[]{:S(2)}) collective-permute-start(bf16[256,128]{1,0:T(8,128)(2,1)S(1)} %get-tuple-element.53), channel_id=1, source_target_pairs={{0,24},{8,16},{16,8},{24,0},{1,25},{9,17},{17,9},{25,1},{2,26},{10... | collective-permute-start | bytes 196616 | tf_op jit(solution)/shard_map/ppermute | solution.py:39
  27.0 3.9 %collective-permute-start.10 = (bf16[96,128]{1,0:T(8,128)(2,1)S(1)}, bf16[96,128]{1,0:T(8,128)(2,1)S(1)}, u32[]{:S(2)}, u32[]{:S(2)}) collective-permute-start(bf16[96,128]{1,0:T(8,128)(2,1)S(1)} %get-tuple-element.60.mine), channel_id=1, source_target_pairs={{0,1},{1,0},{2,3},{3,2},{4,5},{5,4},{6,7},{7,6},{8,9},{9,8},{10,11... | collective-permute-start | bytes 73736 | tf_op jit(solution)/shard_map/ppermute | solution.py:39
  31.0 6.6 %collective-permute-start.11 = (bf16[80,128]{1,0:T(8,128)(2,1)S(1)}, bf16[80,128]{1,0:T(8,128)(2,1)S(1)}, u32[]{:S(2)}, u32[]{:S(2)}) collective-permute-start(bf16[80,128]{1,0:T(8,128)(2,1)S(1)} %get-tuple-element.65), channel_id=1, source_target_pairs={{0,2},{2,0},{4,6},{6,4},{1,3},{3,1},{5,7},{7,5},{8,10},{10,8},{12,... | collective-permute-start | bytes 61448 | tf_op jit(solution)/shard_map/ppermute | solution.py:39
  31.7 5.9 %collective-permute-start.12 = (bf16[80,128]{1,0:T(8,128)(2,1)S(1)}, bf16[80,128]{1,0:T(8,128)(2,1)S(1)}, u32[]{:S(2)}, u32[]{:S(2)}) collective-permute-start(bf16[80,128]{1,0:T(8,128)(2,1)S(1)} %get-tuple-element.66), channel_id=1, source_target_pairs={{0,6},{2,4},{4,2},{6,0},{1,7},{3,5},{5,3},{7,1},{8,14},{10,12},{12... | collective-permute-start | bytes 61448 | tf_op jit(solution)/shard_map/ppermute | solution.py:39
  32.7 4.8 %collective-permute-start.13 = (bf16[64,128]{1,0:T(8,128)(2,1)S(1)}, bf16[64,128]{1,0:T(8,128)(2,1)S(1)}, u32[]{:S(2)}, u32[]{:S(2)}) collective-permute-start(bf16[64,128]{1,0:T(8,128)(2,1)S(1)} %get-tuple-element.64.mine), channel_id=1, source_target_pairs={{0,4},{2,6},{4,0},{6,2},{1,5},{3,7},{5,1},{7,3},{8,12},{10,14},{12... | collective-permute-start | bytes 49160 | tf_op jit(solution)/shard_map/ppermute | solution.py:39

commit v11 on v10

--- a/solution.py
+++ b/solution.py
@@ -102,7 +102,7 @@
     return pick("gx", two, one), pick("gx", one, two)
 
 
-def rows_kernel(chan, rows, left, right, got_0, got_1, sent_0, sent_1):
+def rows_kernel(chan, rows, left, right, got_0, got_1, inner, spread, sent_0, sent_1):
     own = rows.shape[0] // 2
     body = got_0.shape[0] - 16
     count_y = body // chan
@@ -434,18 +434,19 @@
 
     ends = [field[0:wide, :], field[(count_y + 1) * wide : (count_y + 2) * wide, :]]
     rows_out[...] = jnp.concatenate([end[chan : chan + own] for end in ends], axis=0)
-    tall = cols.shape[0]
-    found = cols[...].astype(bf16)
     zero = jnp.zeros((8, lanes), f32)
     for ref, odd in ((sent_0, 0), (sent_1, 1)):
         high = even != (odd == 1)
         low_frame, high_frame = [
-            jnp.concatenate([end[x * chan : (x + 1) * chan] for end in ends] + [zero], axis=0)
+            jnp.concatenate(
+                [end[x * chan : (x + 1) * chan] for end in ends]
+                + [cols[top + x * chan : top + (x + 1) * chan, :] for top in (0, wide)],
+                axis=0,
+            )
             for x in (0, count_x + 1)
         ]
         ref[0:16, :] = jnp.where(high, high_frame, low_frame).astype(bf16)
-        ref[16 : 16 + tall, :] = found
-        ref[16 + tall :, :] = sides
+        ref[16:, :] = sides
 
 
 def plane_of(field, outer_field, at, wide, count_y):
@@ -471,23 +472,21 @@
 
 
 def x_kernel(alone, wpart, wframe, rows, cols, got_0, got_1, far, frame, rows_out):
-    tall = cols.shape[0]
     own = rows.shape[0] // 2
-    wide = tall // 2
+    wide = cols.shape[0] // 2
     chan = (wide - own) // 2
     if alone:
         total = wpart[...]
     else:
-        total = joined(wframe[...]) + joined(far[16 + tall :, :])
-        total = total + (joined(got_0[16 + tall :, :]) + joined(got_1[16 + tall :, :]))
+        total = joined(wframe[...]) + joined(far[16:, :])
+        total = total + (joined(got_0[16:, :]) + joined(got_1[16:, :]))
     frame[2 * own :, :] = jnp.concatenate(split(total), axis=0)
-    one, two = got_0[0 : 16 + tall, :].astype(f32), got_1[0 : 16 + tall, :].astype(f32)
+    one, two = got_0[0:16, :].astype(f32), got_1[0:16, :].astype(f32)
     from_low, from_high = pick("gx", two, one), pick("gx", one, two)
     mid = jnp.zeros((own - 2 * chan, lanes), f32)
     found = []
-    for top in (0, wide):
-        more = [from_low[16 + top + chan + own : 16 + top + wide], mid]
-        more.append(from_high[16 + top : 16 + top + chan])
+    for top, at in ((0, 2 * chan), (wide, 3 * chan)):
+        more = [from_low[at : at + chan], mid, from_high[at : at + chan]]
         found.append(cols[top + chan : top + chan + own, :] + jnp.concatenate(more, axis=0))
     frame[0 : 2 * own, :] = jnp.concatenate(found, axis=0).astype(bf16)
     for at in (0, 1):
@@ -639,9 +638,12 @@
         traffic(4),
     )(cells, left, right)
     bundle = shape((3 * wide + 8, lanes), bf16)
-    row_0, row_1 = call(functools.partial(rows_kernel, chan), [bundle, bundle])(
-        rows, left, right, face_0, face_1
-    )
+    vmem, anywhere = pl.BlockSpec(memory_space=pltpu.VMEM), pl.BlockSpec(memory_space=pl.ANY)
+    row_0, row_1 = call(
+        functools.partial(rows_kernel, chan),
+        [bundle, bundle],
+        in_specs=[vmem] * 5 + [anywhere] * 2,
+    )(rows, left, right, face_0, face_1, inner, spread)
     row_1, row_0 = swapped(row_1, "gy", 1), swapped(row_0, "gy", 0)
 
     tall = 2 * wide
@@ -665,7 +667,7 @@
         traffic(16),
     )(face_0, face_1, inner, spread, wbig, wback)
 
-    bundle = shape((16 + tall + 2 * chan_out, lanes), bf16)
+    bundle = shape((16 + 2 * chan_out, lanes), bf16)
     face = shape((body, lanes), bf16)
     outer_sums, outer_field, row_0, row_1, wpart, wframe, rows, cols = call(
         functools.partial(main_kernel, count_x),
@@ -716,7 +718,6 @@
     grad, ends = call(grad_kernel, [shape(cells.shape, f32), shape(tiles, f32)], cost=traffic(8))(
         field, outer_field, face_0, face_1, frame
     )
-    vmem, anywhere = pl.BlockSpec(memory_space=pltpu.VMEM), pl.BlockSpec(memory_space=pl.ANY)
     input_grad, wsum, bias_grad = call(
         final_kernel,
         [

time: 38.5 us -> 37 us (0.961)
  waiting for transfers between devices: 6.73 us -> 4.43 us
  local copies, waits for them, and re-layouts: 2.31 us -> 2.95 us
    ppermute x14, waiting for transfers between devices: 6.73 us -> 4.43 us  [swapped(): return lax.ppermute(array, axis, pairs)]
    slice x2, local copies, waits for them, and re-layouts: 0.01 us -> 0.65 us  [on_device(): near = placed[:, :, :, 1:count_x + 1].reshape(count_x * chan_out, 9 * own)]
  transfers between devices with their start and end apart: 14 -> 14, of which waited for: 5 -> 5; matrix products, arithmetic and copies ran while one was open for 3% -> 3% of each run, Pallas kernels for 20% -> 21%
where the time goes in v11:
time: 37 us; the launch traced here: 36.7 us
  starting transfers between devices  18 us (49%)
  Pallas kernels  10.2 us (28%)
  waiting for transfers between devices  4.43 us (12%)
  local copies, waits for them, and re-layouts  2.95 us (8%)
  between operations  0.84 us (2%)
    ppermute x14, starting transfers between devices, swapped(): return lax.ppermute(array, axis, pairs)  18 us
    ppermute x14, waiting for transfers between devices, swapped(): return lax.ppermute(array, axis, pairs)  4.43 us
    pallas_call x1, Pallas kernels, on_device(): call(functools.partial(inner_kernel, count_x), [pooled_rows, all_field, s...  3.7 us
    unnamed x12, local copies, waits for them, and re-layouts  1.52 us
    pallas_call x1, Pallas kernels, on_device(): call(functools.partial(main_kernel, count_x), [pooled_rows, all_field, bu...  1.5 us
    pallas_call x1, Pallas kernels, on_device(): call(functools.partial(pool_kernel, pairs), shape(cotangent.shape, bf16),...  1.24 us
    pallas_call x1, Pallas kernels, on_device(): call(grad_kernel, [shape(cells.shape, f32), shape(tiles, f32)], cost=traf...  1.19 us
    pallas_call x1, Pallas kernels, on_device(): spread = call(spread_kernel, pooled_rows)(cotangent)  0.88 us
  transfers between devices with their start and end apart: 14, of which 5 were waited for; matrix products, arithmetic and copies ran while one was open for 3% of the time, Pallas kernels for 21%

profile of v11, /device:TPU:0, one launch (start us, length us, event | category | flops | bytes accessed | tf_op | source)
XLA Modules:
  0.0 36.7 jit_solution(8639058446136825813)
XLA Ops:
  0.6 0.9 %copy-done = bf16[4,4,64,128]{3,2,1,0:T(8,128)(2,1)S(1)} copy-done((bf16[4,4,64,128]{3,2,1,0:T(8,128)(2,1)S(1)}, bf16[4,4,64,128]{3,2,1,0:T(8,128)(2,1)}, u32[]{:S(2)}) %copy-start) | copy-done | bytes 262168
  1.8 3.0 %collective-permute-start = (bf16[32,128]{1,0:T(8,128)(2,1)S(1)}, bf16[32,128]{1,0:T(8,128)(2,1)S(1)}, u32[]{:S(2)}, u32[]{:S(2)}) collective-permute-start(bf16[32,128]{1,0:T(8,128)(2,1)S(1)} %get-tuple-element.37), channel_id=1, source_target_pairs={{0,1},{1,0},{2,3},{3,2},{4,5},{5,4},{6,7},{7,6},{8,9},{9,8},{10,11... | collective-permute-start | bytes 24584 | tf_op jit(solution)/shard_map/ppermute | solution.py:39
  5.5 0.6 %copy-done.3 = bf16[128,3,3,6,4]{0,4,3,2,1:T(4,128)(2,1)} copy-done((bf16[128,3,3,6,4]{0,4,3,2,1:T(4,128)(2,1)}, bf16[128,3,3,6,4]{0,4,3,2,1:T(4,128)(2,1)S(1)}, u32[]{:S(2)}) %copy-start.3) | copy-done | bytes 55320
  6.6 2.1 %collective-permute-start.2 = (bf16[272,128]{1,0:T(8,128)(2,1)S(1)}, bf16[272,128]{1,0:T(8,128)(2,1)S(1)}, u32[]{:S(2)}, u32[]{:S(2)}) collective-permute-start(bf16[272,128]{1,0:T(8,128)(2,1)S(1)} %get-tuple-element.39), channel_id=1, source_target_pairs={{0,24},{8,16},{16,8},{24,0},{1,25},{9,17},{17,9},{25,1},{2,26},{10... | collective-permute-start | bytes 208904 | tf_op jit(solution)/shard_map/ppermute | solution.py:39
  8.8 0.6 %slice-done = bf16[128,3,3,4,4]{0,4,3,2,1:T(4,128)(2,1)S(1)} async-done(((bf16[128,3,3,6,4]{0,4,3,2,1:T(4,128)(2,1)}), bf16[128,3,3,4,4]{0,4,3,2,1:T(4,128)(2,1)S(1)}, s32[]{:S(2)}) %slice-start) | async-done | bytes 36888 | tf_op jit(solution)/shard_map/slice | solution.py:616
  9.6 0.9 %shard_map.78.spread = f32[2048,128]{1,0:T(8,128)S(1)} custom-call(bf16[32,2,32,64]{3,2,1,0:T(8,128)(2,1)S(1)} %copy-done.2), custom_call_target="tpu_custom_call" | custom-call | tf_op jit(solution)/shard_map/pallas_call | solution.py:627
  10.5 0.4 %shard_map.77.inner = bf16[3168,128]{1,0:T(8,128)(2,1)S(1)} custom-call(bf16[4,4,64,128]{3,2,1,0:T(8,128)(2,1)S(1)} %copy-done.1, f32[16,128]{1,0:T(8,128)S(1)} %get-tuple-element.40.left, f32[16,128]{1,0:T(8,128)S(1)} %get-tuple-element.41.right), custom_call_target="tpu_custom_call" | custom-call | bytes 4194304 | tf_op jit(solution)/shard_map/pallas_call | solution.py:634
  11.1 1.7 %collective-permute-start.3 = (bf16[80,128]{1,0:T(8,128)(2,1)S(1)}, bf16[80,128]{1,0:T(8,128)(2,1)S(1)}, u32[]{:S(2)}, u32[]{:S(2)}) collective-permute-start(bf16[80,128]{1,0:T(8,128)(2,1)S(1)} %get-tuple-element.44), channel_id=1, source_target_pairs={{0,2},{2,0},{4,6},{6,4},{1,3},{3,1},{5,7},{7,5},{8,10},{10,8},{12,... | collective-permute-start | bytes 61448 | tf_op jit(solution)/shard_map/ppermute | solution.py:39
  12.8 2.5 %collective-permute-start.4 = (bf16[80,128]{1,0:T(8,128)(2,1)S(1)}, bf16[80,128]{1,0:T(8,128)(2,1)S(1)}, u32[]{:S(2)}, u32[]{:S(2)}) collective-permute-start(bf16[80,128]{1,0:T(8,128)(2,1)S(1)} %get-tuple-element.45), channel_id=1, source_target_pairs={{0,6},{2,4},{4,2},{6,0},{1,7},{3,5},{5,3},{7,1},{8,14},{10,12},{12... | collective-permute-start | bytes 61448 | tf_op jit(solution)/shard_map/ppermute | solution.py:39
  15.5 3.7 %shard_map.79 = (f32[2048,128]{1,0:T(8,128)S(1)}, f32[1584,128]{1,0:T(8,128)S(1)}, bf16[2112,128]{1,0:T(8,128)(2,1)S(1)}, f32[48,128]{1,0:T(8,128)S(1)}, f32[128,240]{1,0:T(8,128)S(1)}) custom-call(bf16[272,128]{1,0:T(8,128)(2,1)S(1)} %collective-permute-done.1.got_0, bf16[272,128]{1,0:T(8,128)(2,1)S(1)} %collective-permute-done.2.got_1, ...), custom_call_target="tpu_custom_call" | custom-call | bytes 16777216 | tf_op jit(solution)/shard_map/pallas_call | solution.py:653
  19.2 1.5 %shard_map.81 = (f32[2048,128]{1,0:T(8,128)S(1)}, f32[1584,128]{1,0:T(8,128)S(1)}, bf16[80,128]{1,0:T(8,128)(2,1)S(1)}, bf16[80,128]{1,0:T(8,128)(2,1)S(1)}, f32...) custom-call(bf16[80,128]{1,0:T(8,128)(2,1)S(1)} %collective-permute-done.3.row_, ...), custom_call_target="tpu_custom_call" | custom-call | tf_op jit(solution)/shard_map/pallas_call | solution.py:672
  20.7 1.0 %collective-permute-start.8 = (bf16[80,128]{1,0:T(8,128)(2,1)S(1)}, bf16[80,128]{1,0:T(8,128)(2,1)S(1)}, u32[]{:S(2)}, u32[]{:S(2)}) collective-permute-start(bf16[80,128]{1,0:T(8,128)(2,1)S(1)} %get-tuple-element.59), channel_id=1, source_target_pairs={{0,24},{8,16},{16,8},{24,0},{1,25},{9,17},{17,9},{25,1},{2,26},{10... | collective-permute-start | bytes 61448 | tf_op jit(solution)/shard_map/ppermute | solution.py:39
  21.7 0.7 %collective-permute-start.9 = (bf16[80,128]{1,0:T(8,128)(2,1)S(1)}, bf16[80,128]{1,0:T(8,128)(2,1)S(1)}, u32[]{:S(2)}, u32[]{:S(2)}) collective-permute-start(bf16[80,128]{1,0:T(8,128)(2,1)S(1)} %get-tuple-element.58), channel_id=1, source_target_pairs={{0,16},{8,24},{16,0},{24,8},{1,17},{9,25},{17,1},{25,9},{2,18},{10... | collective-permute-start | bytes 61448 | tf_op jit(solution)/shard_map/ppermute | solution.py:39
  23.0 1.4 %collective-permute-start.6 = (bf16[256,128]{1,0:T(8,128)(2,1)S(1)}, bf16[256,128]{1,0:T(8,128)(2,1)S(1)}, u32[]{:S(2)}, u32[]{:S(2)}) collective-permute-start(bf16[256,128]{1,0:T(8,128)(2,1)S(1)} %get-tuple-element.53), channel_id=1, source_target_pairs={{0,24},{8,16},{16,8},{24,0},{1,25},{9,17},{17,9},{25,1},{2,26},{10... | collective-permute-start | bytes 196616 | tf_op jit(solution)/shard_map/ppermute | solution.py:39
  24.4 1.1 %collective-permute-done.9.far = bf16[80,128]{1,0:T(8,128)(2,1)S(1)} collective-permute-done((bf16[80,128]{1,0:T(8,128)(2,1)S(1)}, bf16[80,128]{1,0:T(8,128)(2,1)S(1)}, u32[]{:S(2)}, u32[]{:S(2)}) %collective-permute-start.9) | collective-permute-done | bytes 20512 | tf_op jit(solution)/shard_map/ppermute | solution.py:39
  25.5 1.6 %collective-permute-start.10 = (bf16[96,128]{1,0:T(8,128)(2,1)S(1)}, bf16[96,128]{1,0:T(8,128)(2,1)S(1)}, u32[]{:S(2)}, u32[]{:S(2)}) collective-permute-start(bf16[96,128]{1,0:T(8,128)(2,1)S(1)} %get-tuple-element.60.mine), channel_id=1, source_target_pairs={{0,1},{1,0},{2,3},{3,2},{4,5},{5,4},{6,7},{7,6},{8,9},{9,8},{10,11... | collective-permute-start | bytes 73736 | tf_op jit(solution)/shard_map/ppermute | solution.py:39
  27.1 2.3 %collective-permute-done.10.got = bf16[96,128]{1,0:T(8,128)(2,1)S(1)} collective-permute-done((bf16[96,128]{1,0:T(8,128)(2,1)S(1)}, bf16[96,128]{1,0:T(8,128)(2,1)S(1)}, u32[]{:S(2)}, u32[]{:S(2)}) %collective-permute-start.10) | collective-permute-done | bytes 24608 | tf_op jit(solution)/shard_map/ppermute | solution.py:39
  29.5 0.7 %collective-permute-start.11 = (bf16[80,128]{1,0:T(8,128)(2,1)S(1)}, bf16[80,128]{1,0:T(8,128)(2,1)S(1)}, u32[]{:S(2)}, u32[]{:S(2)}) collective-permute-start(bf16[80,128]{1,0:T(8,128)(2,1)S(1)} %get-tuple-element.65), channel_id=1, source_target_pairs={{0,2},{2,0},{4,6},{6,4},{1,3},{3,1},{5,7},{7,5},{8,10},{10,8},{12,... | collective-permute-start | bytes 61448 | tf_op jit(solution)/shard_map/ppermute | solution.py:39
  30.2 1.2 %collective-permute-start.12 = (bf16[80,128]{1,0:T(8,128)(2,1)S(1)}, bf16[80,128]{1,0:T(8,128)(2,1)S(1)}, u32[]{:S(2)}, u32[]{:S(2)}) collective-permute-start(bf16[80,128]{1,0:T(8,128)(2,1)S(1)} %get-tuple-element.66), channel_id=1, source_target_pairs={{0,6},{2,4},{4,2},{6,0},{1,7},{3,5},{5,3},{7,1},{8,14},{10,12},{12... | collective-permute-start | bytes 61448 | tf_op jit(solution)/shard_map/ppermute | solution.py:39
  31.3 1.6 %collective-permute-start.13 = (bf16[64,128]{1,0:T(8,128)(2,1)S(1)}, bf16[64,128]{1,0:T(8,128)(2,1)S(1)}, u32[]{:S(2)}, u32[]{:S(2)}) collective-permute-start(bf16[64,128]{1,0:T(8,128)(2,1)S(1)} %get-tuple-element.64.mine), channel_id=1, source_target_pairs={{0,4},{2,6},{4,0},{6,2},{1,5},{3,7},{5,1},{7,3},{8,12},{10,14},{12... | collective-permute-start | bytes 49160 | tf_op jit(solution)/shard_map/ppermute | solution.py:39
  33.0 1.2 %shard_map.82 = bf16[32,2,32,64]{3,2,1,0:T(8,128)(2,1)} custom-call(f32[2048,128]{1,0:T(8,128)S(1)} %get-tuple-element.42.sums, f32[2048,128]{1,0:T(8,128)S(1)} %get-tuple-element.49.outer_sums), custom_call_target="tpu_custom_call" | custom-call | bytes 8388608 | tf_op jit(solution)/shard_map/pallas_call | solution.py:702
  34.2 1.2 %shard_map.85 = (f32[4,4,64,128]{3,2,1,0:T(8,128)}, f32[2,4,4,8,128]{4,3,2,1,0:T(8,128)S(1)}) custom-call(f32[1584,128]{1,0:T(8,128)S(1)} %get-tuple-element.50.field, f32[1584,128]{1,0:T(8,128)S(1)} %get-tuple-element.51.outer_field, bf16[256,128]{1,0:T(8,128)(2,1)S(1)} %collective-permute-done.5.face_0, ...), custom_call_target="tpu_custom_call" | custom-call | bytes 8388608 | tf_op jit(solution)/shard_map/pallas_call | solution.py:718
  35.4 0.6 %collective-permute-done.13.far = bf16[64,128]{1,0:T(8,128)(2,1)S(1)} collective-permute-done((bf16[64,128]{1,0:T(8,128)(2,1)S(1)}, bf16[64,128]{1,0:T(8,128)(2,1)S(1)}, u32[]{:S(2)}, u32[]{:S(2)}) %collective-permute-start.13) | collective-permute-done | bytes 16416 | tf_op jit(solution)/shard_map/ppermute | solution.py:39
  36.0 0.8 %shard_map.87 = (f32[4,4,64,128]{3,2,1,0:T(8,128)}, f32[27,4,32]{2,1,0:T(4,128)}, f32[1,32]{1,0:T(1,128)}) custom-call(f32[4,4,64,128]{3,2,1,0:T(8,128)} %get-tuple-element.61.whole, f32[2,4,4,8,128]{4,3,2,1,0:T(8,128)S(1)} %get-tuple-element.62.ends, bf16[64,128]{1,0:T(8,128)(2,1)S(1)} %get-tuple-element.64.mine, ...), custom_call_target="tpu_custom_call", output_to_operand_aliasing={{0}: (0, {})} | custom-call | tf_op jit(solution)/shard_map/pallas_call | solution.py:721
  (46 shorter events, 2.8 us)
Async XLA Ops:
  0.6 1.0 %copy-start = (bf16[4,4,64,128]{3,2,1,0:T(8,128)(2,1)S(1)}, bf16[4,4,64,128]{3,2,1,0:T(8,128)(2,1)}, u32[]{:S(2)}) copy-start(bf16[4,4,64,128]{3,2,1,0:T(8,128)(2,1)} %cells.5) | copy-start | bytes 786436
  1.6 3.3 %copy-start.4 = (bf16[32,4,3,3,3]{0,1,4,3,2:T(4,128)(2,1)S(1)}, bf16[32,4,3,3,3]{0,1,4,3,2:T(4,128)(2,1)}, u32[]{:S(2)}) copy-start(bf16[32,4,3,3,3]{0,1,4,3,2:T(4,128)(2,1)} %param.5) | copy-start | bytes 20740
  1.8 3.0 %copy-start.5 = (f32[32]{0:T(128)S(1)}, f32[32]{0:T(128)}, u32[]{:S(2)}) copy-start(f32[32]{0:T(128)} %param.6) | copy-start | bytes 388
  1.8 4.6 %collective-permute-start = (bf16[32,128]{1,0:T(8,128)(2,1)S(1)}, bf16[32,128]{1,0:T(8,128)(2,1)S(1)}, u32[]{:S(2)}, u32[]{:S(2)}) collective-permute-start(bf16[32,128]{1,0:T(8,128)(2,1)S(1)} %get-tuple-element.37), channel_id=1, source_target_pairs={{0,1},{1,0},{2,3},{3,2},{4,5},{5,4},{6,7},{7,6},{8,9},{9,8},{10,11... | collective-permute-start | bytes 24584 | tf_op jit(solution)/shard_map/ppermute | solution.py:39
  5.2 1.2 %copy-start.1 = (bf16[4,4,64,128]{3,2,1,0:T(8,128)(2,1)S(1)}, bf16[4,4,64,128]{3,2,1,0:T(8,128)(2,1)}, u32[]{:S(2)}) copy-start(bf16[4,4,64,128]{3,2,1,0:T(8,128)(2,1)} %cells.5) | copy-start | bytes 786436
  5.3 4.3 %copy-start.2 = (bf16[32,2,32,64]{3,2,1,0:T(8,128)(2,1)S(1)}, bf16[32,2,32,64]{3,2,1,0:T(8,128)(2,1)}, u32[]{:S(2)}) copy-start(bf16[32,2,32,64]{3,2,1,0:T(8,128)(2,1)} %cot.1) | copy-start | bytes 786436
  5.4 0.6 %copy-start.3 = (bf16[128,3,3,6,4]{0,4,3,2,1:T(4,128)(2,1)}, bf16[128,3,3,6,4]{0,4,3,2,1:T(4,128)(2,1)S(1)}, u32[]{:S(2)}) copy-start(bf16[128,3,3,6,4]{0,4,3,2,1:T(4,128)(2,1)S(1)} %reshape.59) | copy-start | bytes 165892
  6.5 4.4 %collective-permute-start.1 = (bf16[272,128]{1,0:T(8,128)(2,1)S(1)}, bf16[272,128]{1,0:T(8,128)(2,1)S(1)}, u32[]{:S(2)}, u32[]{:S(2)}) collective-permute-start(bf16[272,128]{1,0:T(8,128)(2,1)S(1)} %get-tuple-element.38), channel_id=1, source_target_pairs={{0,8},{8,0},{16,24},{24,16},{1,9},{9,1},{17,25},{25,17},{2,10},{10... | collective-permute-start | bytes 208904 | tf_op jit(solution)/shard_map/ppermute | solution.py:39
  6.6 4.5 %collective-permute-start.2 = (bf16[272,128]{1,0:T(8,128)(2,1)S(1)}, bf16[272,128]{1,0:T(8,128)(2,1)S(1)}, u32[]{:S(2)}, u32[]{:S(2)}) collective-permute-start(bf16[272,128]{1,0:T(8,128)(2,1)S(1)} %get-tuple-element.39), channel_id=1, source_target_pairs={{0,24},{8,16},{16,8},{24,0},{1,25},{9,17},{17,9},{25,1},{2,26},{10... | collective-permute-start | bytes 208904 | tf_op jit(solution)/shard_map/ppermute | solution.py:39
  8.7 0.8 %slice-start = ((bf16[128,3,3,6,4]{0,4,3,2,1:T(4,128)(2,1)}), bf16[128,3,3,4,4]{0,4,3,2,1:T(4,128)(2,1)S(1)}, s32[]{:S(2)}) async-start(bf16[128,3,3,6,4]{0,4,3,2,1:T(4,128)(2,1)} %copy-done.3), calls=%async_computation | async-start | bytes 73728 | tf_op jit(solution)/shard_map/slice | solution.py:616
  11.1 8.1 %collective-permute-start.3 = (bf16[80,128]{1,0:T(8,128)(2,1)S(1)}, bf16[80,128]{1,0:T(8,128)(2,1)S(1)}, u32[]{:S(2)}, u32[]{:S(2)}) collective-permute-start(bf16[80,128]{1,0:T(8,128)(2,1)S(1)} %get-tuple-element.44), channel_id=1, source_target_pairs={{0,2},{2,0},{4,6},{6,4},{1,3},{3,1},{5,7},{7,5},{8,10},{10,8},{12,... | collective-permute-start | bytes 61448 | tf_op jit(solution)/shard_map/ppermute | solution.py:39
  12.8 6.4 %collective-permute-start.4 = (bf16[80,128]{1,0:T(8,128)(2,1)S(1)}, bf16[80,128]{1,0:T(8,128)(2,1)S(1)}, u32[]{:S(2)}, u32[]{:S(2)}) collective-permute-start(bf16[80,128]{1,0:T(8,128)(2,1)S(1)} %get-tuple-element.45), channel_id=1, source_target_pairs={{0,6},{2,4},{4,2},{6,0},{1,7},{3,5},{5,3},{7,1},{8,14},{10,12},{12... | collective-permute-start | bytes 61448 | tf_op jit(solution)/shard_map/ppermute | solution.py:39
  20.7 3.7 %collective-permute-start.8 = (bf16[80,128]{1,0:T(8,128)(2,1)S(1)}, bf16[80,128]{1,0:T(8,128)(2,1)S(1)}, u32[]{:S(2)}, u32[]{:S(2)}) collective-permute-start(bf16[80,128]{1,0:T(8,128)(2,1)S(1)} %get-tuple-element.59), channel_id=1, source_target_pairs={{0,24},{8,16},{16,8},{24,0},{1,25},{9,17},{17,9},{25,1},{2,26},{10... | collective-permute-start | bytes 61448 | tf_op jit(solution)/shard_map/ppermute | solution.py:39
  21.7 3.8 %collective-permute-start.9 = (bf16[80,128]{1,0:T(8,128)(2,1)S(1)}, bf16[80,128]{1,0:T(8,128)(2,1)S(1)}, u32[]{:S(2)}, u32[]{:S(2)}) collective-permute-start(bf16[80,128]{1,0:T(8,128)(2,1)S(1)} %get-tuple-element.58), channel_id=1, source_target_pairs={{0,16},{8,24},{16,0},{24,8},{1,17},{9,25},{17,1},{25,9},{2,18},{10... | collective-permute-start | bytes 61448 | tf_op jit(solution)/shard_map/ppermute | solution.py:39
  22.3 3.1 %collective-permute-start.7 = (bf16[80,128]{1,0:T(8,128)(2,1)S(1)}, bf16[80,128]{1,0:T(8,128)(2,1)S(1)}, u32[]{:S(2)}, u32[]{:S(2)}) collective-permute-start(bf16[80,128]{1,0:T(8,128)(2,1)S(1)} %get-tuple-element.58), channel_id=1, source_target_pairs={{0,8},{8,0},{16,24},{24,16},{1,9},{9,1},{17,25},{25,17},{2,10},{10... | collective-permute-start | bytes 61448 | tf_op jit(solution)/shard_map/ppermute | solution.py:39
  22.7 11.5 %collective-permute-start.5 = (bf16[256,128]{1,0:T(8,128)(2,1)S(1)}, bf16[256,128]{1,0:T(8,128)(2,1)S(1)}, u32[]{:S(2)}, u32[]{:S(2)}) collective-permute-start(bf16[256,128]{1,0:T(8,128)(2,1)S(1)} %get-tuple-element.52), channel_id=1, source_target_pairs={{0,8},{8,0},{16,24},{24,16},{1,9},{9,1},{17,25},{25,17},{2,10},{10... | collective-permute-start | bytes 196616 | tf_op jit(solution)/shard_map/ppermute | solution.py:39
  23.0 11.2 %collective-permute-start.6 = (bf16[256,128]{1,0:T(8,128)(2,1)S(1)}, bf16[256,128]{1,0:T(8,128)(2,1)S(1)}, u32[]{:S(2)}, u32[]{:S(2)}) collective-permute-start(bf16[256,128]{1,0:T(8,128)(2,1)S(1)} %get-tuple-element.53), channel_id=1, source_target_pairs={{0,24},{8,16},{16,8},{24,0},{1,25},{9,17},{17,9},{25,1},{2,26},{10... | collective-permute-start | bytes 196616 | tf_op jit(solution)/shard_map/ppermute | solution.py:39
  25.5 3.9 %collective-permute-start.10 = (bf16[96,128]{1,0:T(8,128)(2,1)S(1)}, bf16[96,128]{1,0:T(8,128)(2,1)S(1)}, u32[]{:S(2)}, u32[]{:S(2)}) collective-permute-start(bf16[96,128]{1,0:T(8,128)(2,1)S(1)} %get-tuple-element.60.mine), channel_id=1, source_target_pairs={{0,1},{1,0},{2,3},{3,2},{4,5},{5,4},{6,7},{7,6},{8,9},{9,8},{10,11... | collective-permute-start | bytes 73736 | tf_op jit(solution)/shard_map/ppermute | solution.py:39
  29.5 6.5 %collective-permute-start.11 = (bf16[80,128]{1,0:T(8,128)(2,1)S(1)}, bf16[80,128]{1,0:T(8,128)(2,1)S(1)}, u32[]{:S(2)}, u32[]{:S(2)}) collective-permute-start(bf16[80,128]{1,0:T(8,128)(2,1)S(1)} %get-tuple-element.65), channel_id=1, source_target_pairs={{0,2},{2,0},{4,6},{6,4},{1,3},{3,1},{5,7},{7,5},{8,10},{10,8},{12,... | collective-permute-start | bytes 61448 | tf_op jit(solution)/shard_map/ppermute | solution.py:39
  30.2 5.8 %collective-permute-start.12 = (bf16[80,128]{1,0:T(8,128)(2,1)S(1)}, bf16[80,128]{1,0:T(8,128)(2,1)S(1)}, u32[]{:S(2)}, u32[]{:S(2)}) collective-permute-start(bf16[80,128]{1,0:T(8,128)(2,1)S(1)} %get-tuple-element.66), channel_id=1, source_target_pairs={{0,6},{2,4},{4,2},{6,0},{1,7},{3,5},{5,3},{7,1},{8,14},{10,12},{12... | collective-permute-start | bytes 61448 | tf_op jit(solution)/shard_map/ppermute | solution.py:39
  31.3 4.6 %collective-permute-start.13 = (bf16[64,128]{1,0:T(8,128)(2,1)S(1)}, bf16[64,128]{1,0:T(8,128)(2,1)S(1)}, u32[]{:S(2)}, u32[]{:S(2)}) collective-permute-start(bf16[64,128]{1,0:T(8,128)(2,1)S(1)} %get-tuple-element.64.mine), channel_id=1, source_target_pairs={{0,4},{2,6},{4,0},{6,2},{1,5},{3,7},{5,1},{7,3},{8,12},{10,14},{12... | collective-permute-start | bytes 49160 | tf_op jit(solution)/shard_map/ppermute | solution.py:39

commit v12 on v11

--- a/solution.py
+++ b/solution.py
@@ -335,7 +335,7 @@
 
 
 def main_kernel(
-    count_x, row_0, row_1, inner, patches, inner_cols, inner_gram, spread, wbig, wback,
+    count_x, row_1, row_0, inner, patches, inner_cols, inner_gram, spread, wbig, wback,
     sums, field, sent_0, sent_1, wpart, wframe, rows_out, cols,
     near, rest, gram, delta_a, delta_b,
 ):
@@ -539,7 +539,7 @@
             ends[1, c, x] = plane[count_y - 8 : count_y]
 
 
-def final_kernel(whole, ends, mine, got_0, got_1, far, out, wout, bout, tiles, wtile, btile, sems):
+def final_kernel(whole, ends, mine, got_1, far, got_0, out, wout, bout, tiles, wtile, btile, sems):
     chan, count_x, count_y, _ = whole.shape
     own = chan * count_x
     chan_out = mine.shape[0] // 2
@@ -561,7 +561,7 @@
             )
         )
         copies[-1].start()
-    total = joined(mine[...]) + joined(far[...])
+    total = joined(mine[...]) + joined(far[own:, :])
     total = total + (joined(got_0[own:, :]) + joined(got_1[own:, :]))
     total = jnp.concatenate([total, jnp.zeros((lanes - chan_out, lanes), f32)], axis=0)
     total = total.T
@@ -687,7 +687,7 @@
             pltpu.VMEM((count_x * chan_out, 9 * own + 3 * depth), f32),
         ]
         + deltas,
-    )(row_0, row_1, inner, patches, cols, gram, spread, wbig, wback)
+    )(row_1, row_0, inner, patches, cols, gram, spread, wbig, wback)
 
     alone = lax.axis_size("gx") != 4
     if alone:
@@ -712,8 +712,8 @@
         functools.partial(z_kernel, count_y),
         [bundle, bundle, shape((2 * chan_out, lanes), bf16)],
     )(mine, frame, rows)
+    far = swapped(row_1, "gy", 2)
     row_1, row_0 = swapped(row_1, "gy", 1), swapped(row_0, "gy", 0)
-    far = swapped(mine, "gy", 2)
     tiles = (2, chan, count_x, 8, lanes)
     grad, ends = call(grad_kernel, [shape(cells.shape, f32), shape(tiles, f32)], cost=traffic(8))(
         field, outer_field, face_0, face_1, frame
@@ -734,7 +734,7 @@
         in_specs=[anywhere] + [vmem] * 5,
         out_specs=[anywhere] * 3,
         input_output_aliases={0: 0},
-    )(grad, ends, mine, row_0, row_1, far)
+    )(grad, ends, mine, row_1, far, row_0)
     weight_grad = wsum.reshape(3, 3, 3, chan, chan_out).transpose(4, 3, 0, 1, 2)
     return (pooled, weight_grad, bias_grad.reshape(chan_out), input_grad)
 

time: 37 us -> 37.6 us (1.016)
  starting transfers between devices: 18 us -> 18.5 us
    ppermute x14, starting transfers between devices: 18 us -> 18.5 us  [swapped(): return lax.ppermute(array, axis, pairs)]
  transfers between devices with their start and end apart: 14 -> 14, of which waited for: 5 -> 5; matrix products, arithmetic and copies ran while one was open for 3% -> 3% of each run, Pallas kernels for 21% -> 20%
where the time goes in v12:
time: 37.6 us; the launch traced here: 37.4 us
  starting transfers between devices  18.5 us (49%)
  Pallas kernels  10.2 us (27%)
  waiting for transfers between devices  4.65 us (12%)
  local copies, waits for them, and re-layouts  2.95 us (8%)
  between operations  0.84 us (2%)
    ppermute x14, starting transfers between devices, swapped(): return lax.ppermute(array, axis, pairs)  18.5 us
    ppermute x14, waiting for transfers between devices, swapped(): return lax.ppermute(array, axis, pairs)  4.65 us
    pallas_call x1, Pallas kernels, on_device(): call(functools.partial(inner_kernel, count_x), [pooled_rows, all_field, s...  3.7 us
    unnamed x12, local copies, waits for them, and re-layouts  1.52 us
    pallas_call x1, Pallas kernels, on_device(): call(functools.partial(main_kernel, count_x), [pooled_rows, all_field, bu...  1.5 us
    pallas_call x1, Pallas kernels, on_device(): call(functools.partial(pool_kernel, pairs), shape(cotangent.shape, bf16),...  1.24 us
    pallas_call x1, Pallas kernels, on_device(): call(grad_kernel, [shape(cells.shape, f32), shape(tiles, f32)], cost=traf...  1.19 us
    pallas_call x1, Pallas kernels, on_device(): spread = call(spread_kernel, pooled_rows)(cotangent)  0.88 us
  transfers between devices with their start and end apart: 14, of which 5 were waited for; matrix products, arithmetic and copies ran while one was open for 3% of the time, Pallas kernels for 20%

profile of v12, /device:TPU:0, one launch (start us, length us, event | category | flops | bytes accessed | tf_op | source)
XLA Modules:
  0.0 37.4 jit_solution(5838003974669899786)
XLA Ops:
  0.6 0.9 %copy-done = bf16[4,4,64,128]{3,2,1,0:T(8,128)(2,1)S(1)} copy-done((bf16[4,4,64,128]{3,2,1,0:T(8,128)(2,1)S(1)}, bf16[4,4,64,128]{3,2,1,0:T(8,128)(2,1)}, u32[]{:S(2)}) %copy-start) | copy-done | bytes 262168
  1.8 3.0 %collective-permute-start = (bf16[32,128]{1,0:T(8,128)(2,1)S(1)}, bf16[32,128]{1,0:T(8,128)(2,1)S(1)}, u32[]{:S(2)}, u32[]{:S(2)}) collective-permute-start(bf16[32,128]{1,0:T(8,128)(2,1)S(1)} %get-tuple-element.37), channel_id=1, source_target_pairs={{0,1},{1,0},{2,3},{3,2},{4,5},{5,4},{6,7},{7,6},{8,9},{9,8},{10,11... | collective-permute-start | bytes 24584 | tf_op jit(solution)/shard_map/ppermute | solution.py:39
  5.5 0.6 %copy-done.3 = bf16[128,3,3,6,4]{0,4,3,2,1:T(4,128)(2,1)} copy-done((bf16[128,3,3,6,4]{0,4,3,2,1:T(4,128)(2,1)}, bf16[128,3,3,6,4]{0,4,3,2,1:T(4,128)(2,1)S(1)}, u32[]{:S(2)}) %copy-start.3) | copy-done | bytes 55320
  6.2 0.3 collective-permute-done.edges
  6.6 2.1 %collective-permute-start.2 = (bf16[272,128]{1,0:T(8,128)(2,1)S(1)}, bf16[272,128]{1,0:T(8,128)(2,1)S(1)}, u32[]{:S(2)}, u32[]{:S(2)}) collective-permute-start(bf16[272,128]{1,0:T(8,128)(2,1)S(1)} %get-tuple-element.39), channel_id=1, source_target_pairs={{0,24},{8,16},{16,8},{24,0},{1,25},{9,17},{17,9},{25,1},{2,26},{10... | collective-permute-start | bytes 208904 | tf_op jit(solution)/shard_map/ppermute | solution.py:39
  8.8 0.6 %slice-done = bf16[128,3,3,4,4]{0,4,3,2,1:T(4,128)(2,1)S(1)} async-done(((bf16[128,3,3,6,4]{0,4,3,2,1:T(4,128)(2,1)}), bf16[128,3,3,4,4]{0,4,3,2,1:T(4,128)(2,1)S(1)}, s32[]{:S(2)}) %slice-start) | async-done | bytes 36888 | tf_op jit(solution)/shard_map/slice | solution.py:616
  9.6 0.9 %shard_map.78.spread = f32[2048,128]{1,0:T(8,128)S(1)} custom-call(bf16[32,2,32,64]{3,2,1,0:T(8,128)(2,1)S(1)} %copy-done.2), custom_call_target="tpu_custom_call" | custom-call | tf_op jit(solution)/shard_map/pallas_call | solution.py:627
  10.5 0.4 %shard_map.77.inner = bf16[3168,128]{1,0:T(8,128)(2,1)S(1)} custom-call(bf16[4,4,64,128]{3,2,1,0:T(8,128)(2,1)S(1)} %copy-done.1, f32[16,128]{1,0:T(8,128)S(1)} %get-tuple-element.40.left, f32[16,128]{1,0:T(8,128)S(1)} %get-tuple-element.41.right), custom_call_target="tpu_custom_call" | custom-call | bytes 4194304 | tf_op jit(solution)/shard_map/pallas_call | solution.py:634
  11.1 3.7 %collective-permute-start.3 = (bf16[80,128]{1,0:T(8,128)(2,1)S(1)}, bf16[80,128]{1,0:T(8,128)(2,1)S(1)}, u32[]{:S(2)}, u32[]{:S(2)}) collective-permute-start(bf16[80,128]{1,0:T(8,128)(2,1)S(1)} %get-tuple-element.44), channel_id=1, source_target_pairs={{0,6},{2,4},{4,2},{6,0},{1,7},{3,5},{5,3},{7,1},{8,14},{10,12},{12... | collective-permute-start | bytes 61448 | tf_op jit(solution)/shard_map/ppermute | solution.py:39
  15.0 3.7 %shard_map.79 = (f32[2048,128]{1,0:T(8,128)S(1)}, f32[1584,128]{1,0:T(8,128)S(1)}, bf16[2112,128]{1,0:T(8,128)(2,1)S(1)}, f32[48,128]{1,0:T(8,128)S(1)}, f32[128,240]{1,0:T(8,128)S(1)}) custom-call(bf16[272,128]{1,0:T(8,128)(2,1)S(1)} %collective-permute-done.1.got_0, bf16[272,128]{1,0:T(8,128)(2,1)S(1)} %collective-permute-done.2.got_1, ...), custom_call_target="tpu_custom_call" | custom-call | bytes 16777216 | tf_op jit(solution)/shard_map/pallas_call | solution.py:653
  18.8 1.5 %shard_map.81 = (f32[2048,128]{1,0:T(8,128)S(1)}, f32[1584,128]{1,0:T(8,128)S(1)}, bf16[80,128]{1,0:T(8,128)(2,1)S(1)}, bf16[80,128]{1,0:T(8,128)(2,1)S(1)}, f32...) custom-call(bf16[80,128]{1,0:T(8,128)(2,1)S(1)} %collective-permute-done.3.row_, ...), custom_call_target="tpu_custom_call" | custom-call | tf_op jit(solution)/shard_map/pallas_call | solution.py:672
  20.3 1.2 %collective-permute-start.8 = (bf16[80,128]{1,0:T(8,128)(2,1)S(1)}, bf16[80,128]{1,0:T(8,128)(2,1)S(1)}, u32[]{:S(2)}, u32[]{:S(2)}) collective-permute-start(bf16[80,128]{1,0:T(8,128)(2,1)S(1)} %get-tuple-element.59), channel_id=1, source_target_pairs={{0,24},{8,16},{16,8},{24,0},{1,25},{9,17},{17,9},{25,1},{2,26},{10... | collective-permute-start | bytes 61448 | tf_op jit(solution)/shard_map/ppermute | solution.py:39
  21.5 0.5 %collective-permute-start.9 = (bf16[80,128]{1,0:T(8,128)(2,1)S(1)}, bf16[80,128]{1,0:T(8,128)(2,1)S(1)}, u32[]{:S(2)}, u32[]{:S(2)}) collective-permute-start(bf16[80,128]{1,0:T(8,128)(2,1)S(1)} %get-tuple-element.58), channel_id=1, source_target_pairs={{0,16},{8,24},{16,0},{24,8},{1,17},{9,25},{17,1},{25,9},{2,18},{10... | collective-permute-start | bytes 61448 | tf_op jit(solution)/shard_map/ppermute | solution.py:39
  22.3 0.4 %collective-permute-start.5 = (bf16[256,128]{1,0:T(8,128)(2,1)S(1)}, bf16[256,128]{1,0:T(8,128)(2,1)S(1)}, u32[]{:S(2)}, u32[]{:S(2)}) collective-permute-start(bf16[256,128]{1,0:T(8,128)(2,1)S(1)} %get-tuple-element.52), channel_id=1, source_target_pairs={{0,8},{8,0},{16,24},{24,16},{1,9},{9,1},{17,25},{25,17},{2,10},{10... | collective-permute-start | bytes 196616 | tf_op jit(solution)/shard_map/ppermute | solution.py:39
  22.7 1.3 %collective-permute-start.6 = (bf16[256,128]{1,0:T(8,128)(2,1)S(1)}, bf16[256,128]{1,0:T(8,128)(2,1)S(1)}, u32[]{:S(2)}, u32[]{:S(2)}) collective-permute-start(bf16[256,128]{1,0:T(8,128)(2,1)S(1)} %get-tuple-element.53), channel_id=1, source_target_pairs={{0,24},{8,16},{16,8},{24,0},{1,25},{9,17},{17,9},{25,1},{2,26},{10... | collective-permute-start | bytes 196616 | tf_op jit(solution)/shard_map/ppermute | solution.py:39
  24.0 1.3 %collective-permute-done.9.far = bf16[80,128]{1,0:T(8,128)(2,1)S(1)} collective-permute-done((bf16[80,128]{1,0:T(8,128)(2,1)S(1)}, bf16[80,128]{1,0:T(8,128)(2,1)S(1)}, u32[]{:S(2)}, u32[]{:S(2)}) %collective-permute-start.9) | collective-permute-done | bytes 20512 | tf_op jit(solution)/shard_map/ppermute | solution.py:39
  25.3 1.6 %collective-permute-start.10 = (bf16[96,128]{1,0:T(8,128)(2,1)S(1)}, bf16[96,128]{1,0:T(8,128)(2,1)S(1)}, u32[]{:S(2)}, u32[]{:S(2)}) collective-permute-start(bf16[96,128]{1,0:T(8,128)(2,1)S(1)} %get-tuple-element.60.mine), channel_id=1, source_target_pairs={{0,1},{1,0},{2,3},{3,2},{4,5},{5,4},{6,7},{7,6},{8,9},{9,8},{10,11... | collective-permute-start | bytes 73736 | tf_op jit(solution)/shard_map/ppermute | solution.py:39
  26.9 2.3 %collective-permute-done.10.got = bf16[96,128]{1,0:T(8,128)(2,1)S(1)} collective-permute-done((bf16[96,128]{1,0:T(8,128)(2,1)S(1)}, bf16[96,128]{1,0:T(8,128)(2,1)S(1)}, u32[]{:S(2)}, u32[]{:S(2)}) %collective-permute-start.10) | collective-permute-done | bytes 24608 | tf_op jit(solution)/shard_map/ppermute | solution.py:39
  29.3 1.8 %collective-permute-start.13 = (bf16[80,128]{1,0:T(8,128)(2,1)S(1)}, bf16[80,128]{1,0:T(8,128)(2,1)S(1)}, u32[]{:S(2)}, u32[]{:S(2)}) collective-permute-start(bf16[80,128]{1,0:T(8,128)(2,1)S(1)} %get-tuple-element.66), channel_id=1, source_target_pairs={{0,2},{2,0},{4,6},{6,4},{1,3},{3,1},{5,7},{7,5},{8,10},{10,8},{12,... | collective-permute-start | bytes 61448 | tf_op jit(solution)/shard_map/ppermute | solution.py:39
  31.1 2.6 %collective-permute-start.11 = (bf16[80,128]{1,0:T(8,128)(2,1)S(1)}, bf16[80,128]{1,0:T(8,128)(2,1)S(1)}, u32[]{:S(2)}, u32[]{:S(2)}) collective-permute-start(bf16[80,128]{1,0:T(8,128)(2,1)S(1)} %get-tuple-element.65), channel_id=1, source_target_pairs={{0,6},{2,4},{4,2},{6,0},{1,7},{3,5},{5,3},{7,1},{8,14},{10,12},{12... | collective-permute-start | bytes 61448 | tf_op jit(solution)/shard_map/ppermute | solution.py:39
  33.7 1.2 %shard_map.82 = bf16[32,2,32,64]{3,2,1,0:T(8,128)(2,1)} custom-call(f32[2048,128]{1,0:T(8,128)S(1)} %get-tuple-element.42.sums, f32[2048,128]{1,0:T(8,128)S(1)} %get-tuple-element.49.outer_sums), custom_call_target="tpu_custom_call" | custom-call | bytes 8388608 | tf_op jit(solution)/shard_map/pallas_call | solution.py:702
  34.9 1.2 %shard_map.85 = (f32[4,4,64,128]{3,2,1,0:T(8,128)}, f32[2,4,4,8,128]{4,3,2,1,0:T(8,128)S(1)}) custom-call(f32[1584,128]{1,0:T(8,128)S(1)} %get-tuple-element.50.field, f32[1584,128]{1,0:T(8,128)S(1)} %get-tuple-element.51.outer_field, bf16[256,128]{1,0:T(8,128)(2,1)S(1)} %collective-permute-done.5.face_0, ...), custom_call_target="tpu_custom_call" | custom-call | bytes 8388608 | tf_op jit(solution)/shard_map/pallas_call | solution.py:718
  36.1 0.5 %collective-permute-done.11.got_1 = bf16[80,128]{1,0:T(8,128)(2,1)S(1)} collective-permute-done((bf16[80,128]{1,0:T(8,128)(2,1)S(1)}, bf16[80,128]{1,0:T(8,128)(2,1)S(1)}, u32[]{:S(2)}, u32[]{:S(2)}) %collective-permute-start.11) | collective-permute-done | bytes 20512 | tf_op jit(solution)/shard_map/ppermute | solution.py:39
  36.6 0.8 %shard_map.87 = (f32[4,4,64,128]{3,2,1,0:T(8,128)}, f32[27,4,32]{2,1,0:T(4,128)}, f32[1,32]{1,0:T(1,128)}) custom-call(f32[4,4,64,128]{3,2,1,0:T(8,128)} %get-tuple-element.61.whole, f32[2,4,4,8,128]{4,3,2,1,0:T(8,128)S(1)} %get-tuple-element.62.ends, bf16[64,128]{1,0:T(8,128)(2,1)S(1)} %get-tuple-element.64.mine, ...), custom_call_target="tpu_custom_call", output_to_operand_aliasing={{0}: (0, {})} | custom-call | tf_op jit(solution)/shard_map/pallas_call | solution.py:721
  (46 shorter events, 2.1 us)
Async XLA Ops:
  0.6 1.0 %copy-start = (bf16[4,4,64,128]{3,2,1,0:T(8,128)(2,1)S(1)}, bf16[4,4,64,128]{3,2,1,0:T(8,128)(2,1)}, u32[]{:S(2)}) copy-start(bf16[4,4,64,128]{3,2,1,0:T(8,128)(2,1)} %cells.5) | copy-start | bytes 786436
  1.6 3.3 %copy-start.4 = (bf16[32,4,3,3,3]{0,1,4,3,2:T(4,128)(2,1)S(1)}, bf16[32,4,3,3,3]{0,1,4,3,2:T(4,128)(2,1)}, u32[]{:S(2)}) copy-start(bf16[32,4,3,3,3]{0,1,4,3,2:T(4,128)(2,1)} %param.5) | copy-start | bytes 20740
  1.8 3.0 %copy-start.5 = (f32[32]{0:T(128)S(1)}, f32[32]{0:T(128)}, u32[]{:S(2)}) copy-start(f32[32]{0:T(128)} %param.6) | copy-start | bytes 388
  1.8 4.6 %collective-permute-start = (bf16[32,128]{1,0:T(8,128)(2,1)S(1)}, bf16[32,128]{1,0:T(8,128)(2,1)S(1)}, u32[]{:S(2)}, u32[]{:S(2)}) collective-permute-start(bf16[32,128]{1,0:T(8,128)(2,1)S(1)} %get-tuple-element.37), channel_id=1, source_target_pairs={{0,1},{1,0},{2,3},{3,2},{4,5},{5,4},{6,7},{7,6},{8,9},{9,8},{10,11... | collective-permute-start | bytes 24584 | tf_op jit(solution)/shard_map/ppermute | solution.py:39
  5.2 1.2 %copy-start.1 = (bf16[4,4,64,128]{3,2,1,0:T(8,128)(2,1)S(1)}, bf16[4,4,64,128]{3,2,1,0:T(8,128)(2,1)}, u32[]{:S(2)}) copy-start(bf16[4,4,64,128]{3,2,1,0:T(8,128)(2,1)} %cells.5) | copy-start | bytes 786436
  5.3 4.3 %copy-start.2 = (bf16[32,2,32,64]{3,2,1,0:T(8,128)(2,1)S(1)}, bf16[32,2,32,64]{3,2,1,0:T(8,128)(2,1)}, u32[]{:S(2)}) copy-start(bf16[32,2,32,64]{3,2,1,0:T(8,128)(2,1)} %cot.1) | copy-start | bytes 786436
  5.4 0.6 %copy-start.3 = (bf16[128,3,3,6,4]{0,4,3,2,1:T(4,128)(2,1)}, bf16[128,3,3,6,4]{0,4,3,2,1:T(4,128)(2,1)S(1)}, u32[]{:S(2)}) copy-start(bf16[128,3,3,6,4]{0,4,3,2,1:T(4,128)(2,1)S(1)} %reshape.59) | copy-start | bytes 165892
  6.5 4.4 %collective-permute-start.1 = (bf16[272,128]{1,0:T(8,128)(2,1)S(1)}, bf16[272,128]{1,0:T(8,128)(2,1)S(1)}, u32[]{:S(2)}, u32[]{:S(2)}) collective-permute-start(bf16[272,128]{1,0:T(8,128)(2,1)S(1)} %get-tuple-element.38), channel_id=1, source_target_pairs={{0,8},{8,0},{16,24},{24,16},{1,9},{9,1},{17,25},{25,17},{2,10},{10... | collective-permute-start | bytes 208904 | tf_op jit(solution)/shard_map/ppermute | solution.py:39
  6.6 4.5 %collective-permute-start.2 = (bf16[272,128]{1,0:T(8,128)(2,1)S(1)}, bf16[272,128]{1,0:T(8,128)(2,1)S(1)}, u32[]{:S(2)}, u32[]{:S(2)}) collective-permute-start(bf16[272,128]{1,0:T(8,128)(2,1)S(1)} %get-tuple-element.39), channel_id=1, source_target_pairs={{0,24},{8,16},{16,8},{24,0},{1,25},{9,17},{17,9},{25,1},{2,26},{10... | collective-permute-start | bytes 208904 | tf_op jit(solution)/shard_map/ppermute | solution.py:39
  8.7 0.8 %slice-start = ((bf16[128,3,3,6,4]{0,4,3,2,1:T(4,128)(2,1)}), bf16[128,3,3,4,4]{0,4,3,2,1:T(4,128)(2,1)S(1)}, s32[]{:S(2)}) async-start(bf16[128,3,3,6,4]{0,4,3,2,1:T(4,128)(2,1)} %copy-done.3), calls=%async_computation | async-start | bytes 73728 | tf_op jit(solution)/shard_map/slice | solution.py:616
  11.1 7.7 %collective-permute-start.3 = (bf16[80,128]{1,0:T(8,128)(2,1)S(1)}, bf16[80,128]{1,0:T(8,128)(2,1)S(1)}, u32[]{:S(2)}, u32[]{:S(2)}) collective-permute-start(bf16[80,128]{1,0:T(8,128)(2,1)S(1)} %get-tuple-element.44), channel_id=1, source_target_pairs={{0,6},{2,4},{4,2},{6,0},{1,7},{3,5},{5,3},{7,1},{8,14},{10,12},{12... | collective-permute-start | bytes 61448 | tf_op jit(solution)/shard_map/ppermute | solution.py:39
  14.8 4.0 %collective-permute-start.4 = (bf16[80,128]{1,0:T(8,128)(2,1)S(1)}, bf16[80,128]{1,0:T(8,128)(2,1)S(1)}, u32[]{:S(2)}, u32[]{:S(2)}) collective-permute-start(bf16[80,128]{1,0:T(8,128)(2,1)S(1)} %get-tuple-element.45), channel_id=1, source_target_pairs={{0,2},{2,0},{4,6},{6,4},{1,3},{3,1},{5,7},{7,5},{8,10},{10,8},{12,... | collective-permute-start | bytes 61448 | tf_op jit(solution)/shard_map/ppermute | solution.py:39
  20.3 3.7 %collective-permute-start.8 = (bf16[80,128]{1,0:T(8,128)(2,1)S(1)}, bf16[80,128]{1,0:T(8,128)(2,1)S(1)}, u32[]{:S(2)}, u32[]{:S(2)}) collective-permute-start(bf16[80,128]{1,0:T(8,128)(2,1)S(1)} %get-tuple-element.59), channel_id=1, source_target_pairs={{0,24},{8,16},{16,8},{24,0},{1,25},{9,17},{17,9},{25,1},{2,26},{10... | collective-permute-start | bytes 61448 | tf_op jit(solution)/shard_map/ppermute | solution.py:39
  21.5 3.8 %collective-permute-start.9 = (bf16[80,128]{1,0:T(8,128)(2,1)S(1)}, bf16[80,128]{1,0:T(8,128)(2,1)S(1)}, u32[]{:S(2)}, u32[]{:S(2)}) collective-permute-start(bf16[80,128]{1,0:T(8,128)(2,1)S(1)} %get-tuple-element.58), channel_id=1, source_target_pairs={{0,16},{8,24},{16,0},{24,8},{1,17},{9,25},{17,1},{25,9},{2,18},{10... | collective-permute-start | bytes 61448 | tf_op jit(solution)/shard_map/ppermute | solution.py:39
  22.0 3.2 %collective-permute-start.7 = (bf16[80,128]{1,0:T(8,128)(2,1)S(1)}, bf16[80,128]{1,0:T(8,128)(2,1)S(1)}, u32[]{:S(2)}, u32[]{:S(2)}) collective-permute-start(bf16[80,128]{1,0:T(8,128)(2,1)S(1)} %get-tuple-element.58), channel_id=1, source_target_pairs={{0,8},{8,0},{16,24},{24,16},{1,9},{9,1},{17,25},{25,17},{2,10},{10... | collective-permute-start | bytes 61448 | tf_op jit(solution)/shard_map/ppermute | solution.py:39
  22.3 12.7 %collective-permute-start.5 = (bf16[256,128]{1,0:T(8,128)(2,1)S(1)}, bf16[256,128]{1,0:T(8,128)(2,1)S(1)}, u32[]{:S(2)}, u32[]{:S(2)}) collective-permute-start(bf16[256,128]{1,0:T(8,128)(2,1)S(1)} %get-tuple-element.52), channel_id=1, source_target_pairs={{0,8},{8,0},{16,24},{24,16},{1,9},{9,1},{17,25},{25,17},{2,10},{10... | collective-permute-start | bytes 196616 | tf_op jit(solution)/shard_map/ppermute | solution.py:39
  22.7 12.2 %collective-permute-start.6 = (bf16[256,128]{1,0:T(8,128)(2,1)S(1)}, bf16[256,128]{1,0:T(8,128)(2,1)S(1)}, u32[]{:S(2)}, u32[]{:S(2)}) collective-permute-start(bf16[256,128]{1,0:T(8,128)(2,1)S(1)} %get-tuple-element.53), channel_id=1, source_target_pairs={{0,24},{8,16},{16,8},{24,0},{1,25},{9,17},{17,9},{25,1},{2,26},{10... | collective-permute-start | bytes 196616 | tf_op jit(solution)/shard_map/ppermute | solution.py:39
  25.3 3.9 %collective-permute-start.10 = (bf16[96,128]{1,0:T(8,128)(2,1)S(1)}, bf16[96,128]{1,0:T(8,128)(2,1)S(1)}, u32[]{:S(2)}, u32[]{:S(2)}) collective-permute-start(bf16[96,128]{1,0:T(8,128)(2,1)S(1)} %get-tuple-element.60.mine), channel_id=1, source_target_pairs={{0,1},{1,0},{2,3},{3,2},{4,5},{5,4},{6,7},{7,6},{8,9},{9,8},{10,11... | collective-permute-start | bytes 73736 | tf_op jit(solution)/shard_map/ppermute | solution.py:39
  29.3 6.8 %collective-permute-start.13 = (bf16[80,128]{1,0:T(8,128)(2,1)S(1)}, bf16[80,128]{1,0:T(8,128)(2,1)S(1)}, u32[]{:S(2)}, u32[]{:S(2)}) collective-permute-start(bf16[80,128]{1,0:T(8,128)(2,1)S(1)} %get-tuple-element.66), channel_id=1, source_target_pairs={{0,2},{2,0},{4,6},{6,4},{1,3},{3,1},{5,7},{7,5},{8,10},{10,8},{12,... | collective-permute-start | bytes 61448 | tf_op jit(solution)/shard_map/ppermute | solution.py:39
  31.1 5.1 %collective-permute-start.12 = (bf16[80,128]{1,0:T(8,128)(2,1)S(1)}, bf16[80,128]{1,0:T(8,128)(2,1)S(1)}, u32[]{:S(2)}, u32[]{:S(2)}) collective-permute-start(bf16[80,128]{1,0:T(8,128)(2,1)S(1)} %get-tuple-element.65), channel_id=1, source_target_pairs={{0,4},{2,6},{4,0},{6,2},{1,5},{3,7},{5,1},{7,3},{8,12},{10,14},{12... | collective-permute-start | bytes 61448 | tf_op jit(solution)/shard_map/ppermute | solution.py:39
  31.1 5.6 %collective-permute-start.11 = (bf16[80,128]{1,0:T(8,128)(2,1)S(1)}, bf16[80,128]{1,0:T(8,128)(2,1)S(1)}, u32[]{:S(2)}, u32[]{:S(2)}) collective-permute-start(bf16[80,128]{1,0:T(8,128)(2,1)S(1)} %get-tuple-element.65), channel_id=1, source_target_pairs={{0,6},{2,4},{4,2},{6,0},{1,7},{3,5},{5,3},{7,1},{8,14},{10,12},{12... | collective-permute-start | bytes 61448 | tf_op jit(solution)/shard_map/ppermute | solution.py:39

commit v13 on v12

--- a/solution.py
+++ b/solution.py
@@ -561,7 +561,7 @@
             )
         )
         copies[-1].start()
-    total = joined(mine[...]) + joined(far[own:, :])
+    total = joined(mine[...]) + joined(far[...])
     total = total + (joined(got_0[own:, :]) + joined(got_1[own:, :]))
     total = jnp.concatenate([total, jnp.zeros((lanes - chan_out, lanes), f32)], axis=0)
     total = total.T
@@ -712,8 +712,8 @@
         functools.partial(z_kernel, count_y),
         [bundle, bundle, shape((2 * chan_out, lanes), bf16)],
     )(mine, frame, rows)
-    far = swapped(row_1, "gy", 2)
     row_1, row_0 = swapped(row_1, "gy", 1), swapped(row_0, "gy", 0)
+    far = swapped(mine, "gy", 2)
     tiles = (2, chan, count_x, 8, lanes)
     grad, ends = call(grad_kernel, [shape(cells.shape, f32), shape(tiles, f32)], cost=traffic(8))(
         field, outer_field, face_0, face_1, frame

time: 37.6 us -> 37.1 us (0.987)
  waiting for transfers between devices: 4.65 us -> 4.15 us
    ppermute x14, waiting for transfers between devices: 4.65 us -> 4.15 us  [swapped(): return lax.ppermute(array, axis, pairs)]
  transfers between devices with their start and end apart: 14 -> 14, of which waited for: 5 -> 4; matrix products, arithmetic and copies ran while one was open for 3% -> 3% of each run, Pallas kernels for 20% -> 21%
where the time goes in v13:
time: 37.1 us; the launch traced here: 36.9 us
  starting transfers between devices  18.5 us (50%)
  Pallas kernels  10.2 us (27%)
  waiting for transfers between devices  4.15 us (11%)
  local copies, waits for them, and re-layouts  2.95 us (8%)
  between operations  0.84 us (2%)
    ppermute x14, starting transfers between devices, swapped(): return lax.ppermute(array, axis, pairs)  18.5 us
    ppermute x14, waiting for transfers between devices, swapped(): return lax.ppermute(array, axis, pairs)  4.15 us
    pallas_call x1, Pallas kernels, on_device(): call(functools.partial(inner_kernel, count_x), [pooled_rows, all_field, s...  3.7 us
    unnamed x12, local copies, waits for them, and re-layouts  1.52 us
    pallas_call x1, Pallas kernels, on_device(): call(functools.partial(main_kernel, count_x), [pooled_rows, all_field, bu...  1.5 us
    pallas_call x1, Pallas kernels, on_device(): call(functools.partial(pool_kernel, pairs), shape(cotangent.shape, bf16),...  1.24 us
    pallas_call x1, Pallas kernels, on_device(): call(grad_kernel, [shape(cells.shape, f32), shape(tiles, f32)], cost=traf...  1.19 us
    pallas_call x1, Pallas kernels, on_device(): spread = call(spread_kernel, pooled_rows)(cotangent)  0.88 us
  transfers between devices with their start and end apart: 14, of which 4 were waited for; matrix products, arithmetic and copies ran while one was open for 3% of the time, Pallas kernels for 21%

profile of v13, /device:TPU:0, one launch (start us, length us, event | category | flops | bytes accessed | tf_op | source)
XLA Modules:
  0.0 36.9 jit_solution(18434949411946438766)
XLA Ops:
  0.6 0.9 %copy-done = bf16[4,4,64,128]{3,2,1,0:T(8,128)(2,1)S(1)} copy-done((bf16[4,4,64,128]{3,2,1,0:T(8,128)(2,1)S(1)}, bf16[4,4,64,128]{3,2,1,0:T(8,128)(2,1)}, u32[]{:S(2)}) %copy-start) | copy-done | bytes 262168
  1.8 3.0 %collective-permute-start = (bf16[32,128]{1,0:T(8,128)(2,1)S(1)}, bf16[32,128]{1,0:T(8,128)(2,1)S(1)}, u32[]{:S(2)}, u32[]{:S(2)}) collective-permute-start(bf16[32,128]{1,0:T(8,128)(2,1)S(1)} %get-tuple-element.37), channel_id=1, source_target_pairs={{0,1},{1,0},{2,3},{3,2},{4,5},{5,4},{6,7},{7,6},{8,9},{9,8},{10,11... | collective-permute-start | bytes 24584 | tf_op jit(solution)/shard_map/ppermute | solution.py:39
  5.5 0.6 %copy-done.3 = bf16[128,3,3,6,4]{0,4,3,2,1:T(4,128)(2,1)} copy-done((bf16[128,3,3,6,4]{0,4,3,2,1:T(4,128)(2,1)}, bf16[128,3,3,6,4]{0,4,3,2,1:T(4,128)(2,1)S(1)}, u32[]{:S(2)}) %copy-start.3) | copy-done | bytes 55320
  6.2 0.3 collective-permute-done.edges
  6.6 2.1 %collective-permute-start.2 = (bf16[272,128]{1,0:T(8,128)(2,1)S(1)}, bf16[272,128]{1,0:T(8,128)(2,1)S(1)}, u32[]{:S(2)}, u32[]{:S(2)}) collective-permute-start(bf16[272,128]{1,0:T(8,128)(2,1)S(1)} %get-tuple-element.39), channel_id=1, source_target_pairs={{0,24},{8,16},{16,8},{24,0},{1,25},{9,17},{17,9},{25,1},{2,26},{10... | collective-permute-start | bytes 208904 | tf_op jit(solution)/shard_map/ppermute | solution.py:39
  8.8 0.6 %slice-done = bf16[128,3,3,4,4]{0,4,3,2,1:T(4,128)(2,1)S(1)} async-done(((bf16[128,3,3,6,4]{0,4,3,2,1:T(4,128)(2,1)}), bf16[128,3,3,4,4]{0,4,3,2,1:T(4,128)(2,1)S(1)}, s32[]{:S(2)}) %slice-start) | async-done | bytes 36888 | tf_op jit(solution)/shard_map/slice | solution.py:616
  9.6 0.9 %shard_map.78.spread = f32[2048,128]{1,0:T(8,128)S(1)} custom-call(bf16[32,2,32,64]{3,2,1,0:T(8,128)(2,1)S(1)} %copy-done.2), custom_call_target="tpu_custom_call" | custom-call | tf_op jit(solution)/shard_map/pallas_call | solution.py:627
  10.5 0.4 %shard_map.77.inner = bf16[3168,128]{1,0:T(8,128)(2,1)S(1)} custom-call(bf16[4,4,64,128]{3,2,1,0:T(8,128)(2,1)S(1)} %copy-done.1, f32[16,128]{1,0:T(8,128)S(1)} %get-tuple-element.40.left, f32[16,128]{1,0:T(8,128)S(1)} %get-tuple-element.41.right), custom_call_target="tpu_custom_call" | custom-call | bytes 4194304 | tf_op jit(solution)/shard_map/pallas_call | solution.py:634
  11.1 3.7 %collective-permute-start.3 = (bf16[80,128]{1,0:T(8,128)(2,1)S(1)}, bf16[80,128]{1,0:T(8,128)(2,1)S(1)}, u32[]{:S(2)}, u32[]{:S(2)}) collective-permute-start(bf16[80,128]{1,0:T(8,128)(2,1)S(1)} %get-tuple-element.44), channel_id=1, source_target_pairs={{0,6},{2,4},{4,2},{6,0},{1,7},{3,5},{5,3},{7,1},{8,14},{10,12},{12... | collective-permute-start | bytes 61448 | tf_op jit(solution)/shard_map/ppermute | solution.py:39
  15.0 3.7 %shard_map.79 = (f32[2048,128]{1,0:T(8,128)S(1)}, f32[1584,128]{1,0:T(8,128)S(1)}, bf16[2112,128]{1,0:T(8,128)(2,1)S(1)}, f32[48,128]{1,0:T(8,128)S(1)}, f32[128,240]{1,0:T(8,128)S(1)}) custom-call(bf16[272,128]{1,0:T(8,128)(2,1)S(1)} %collective-permute-done.1.got_0, bf16[272,128]{1,0:T(8,128)(2,1)S(1)} %collective-permute-done.2.got_1, ...), custom_call_target="tpu_custom_call" | custom-call | bytes 16777216 | tf_op jit(solution)/shard_map/pallas_call | solution.py:653
  18.8 1.5 %shard_map.81 = (f32[2048,128]{1,0:T(8,128)S(1)}, f32[1584,128]{1,0:T(8,128)S(1)}, bf16[80,128]{1,0:T(8,128)(2,1)S(1)}, bf16[80,128]{1,0:T(8,128)(2,1)S(1)}, f32...) custom-call(bf16[80,128]{1,0:T(8,128)(2,1)S(1)} %collective-permute-done.3.row_, ...), custom_call_target="tpu_custom_call" | custom-call | tf_op jit(solution)/shard_map/pallas_call | solution.py:672
  20.3 1.2 %collective-permute-start.8 = (bf16[80,128]{1,0:T(8,128)(2,1)S(1)}, bf16[80,128]{1,0:T(8,128)(2,1)S(1)}, u32[]{:S(2)}, u32[]{:S(2)}) collective-permute-start(bf16[80,128]{1,0:T(8,128)(2,1)S(1)} %get-tuple-element.59), channel_id=1, source_target_pairs={{0,24},{8,16},{16,8},{24,0},{1,25},{9,17},{17,9},{25,1},{2,26},{10... | collective-permute-start | bytes 61448 | tf_op jit(solution)/shard_map/ppermute | solution.py:39
  21.5 0.5 %collective-permute-start.9 = (bf16[80,128]{1,0:T(8,128)(2,1)S(1)}, bf16[80,128]{1,0:T(8,128)(2,1)S(1)}, u32[]{:S(2)}, u32[]{:S(2)}) collective-permute-start(bf16[80,128]{1,0:T(8,128)(2,1)S(1)} %get-tuple-element.58), channel_id=1, source_target_pairs={{0,16},{8,24},{16,0},{24,8},{1,17},{9,25},{17,1},{25,9},{2,18},{10... | collective-permute-start | bytes 61448 | tf_op jit(solution)/shard_map/ppermute | solution.py:39
  22.3 0.4 %collective-permute-start.5 = (bf16[256,128]{1,0:T(8,128)(2,1)S(1)}, bf16[256,128]{1,0:T(8,128)(2,1)S(1)}, u32[]{:S(2)}, u32[]{:S(2)}) collective-permute-start(bf16[256,128]{1,0:T(8,128)(2,1)S(1)} %get-tuple-element.52), channel_id=1, source_target_pairs={{0,8},{8,0},{16,24},{24,16},{1,9},{9,1},{17,25},{25,17},{2,10},{10... | collective-permute-start | bytes 196616 | tf_op jit(solution)/shard_map/ppermute | solution.py:39
  22.7 1.3 %collective-permute-start.6 = (bf16[256,128]{1,0:T(8,128)(2,1)S(1)}, bf16[256,128]{1,0:T(8,128)(2,1)S(1)}, u32[]{:S(2)}, u32[]{:S(2)}) collective-permute-start(bf16[256,128]{1,0:T(8,128)(2,1)S(1)} %get-tuple-element.53), channel_id=1, source_target_pairs={{0,24},{8,16},{16,8},{24,0},{1,25},{9,17},{17,9},{25,1},{2,26},{10... | collective-permute-start | bytes 196616 | tf_op jit(solution)/shard_map/ppermute | solution.py:39
  24.0 1.3 %collective-permute-done.9.far = bf16[80,128]{1,0:T(8,128)(2,1)S(1)} collective-permute-done((bf16[80,128]{1,0:T(8,128)(2,1)S(1)}, bf16[80,128]{1,0:T(8,128)(2,1)S(1)}, u32[]{:S(2)}, u32[]{:S(2)}) %collective-permute-start.9) | collective-permute-done | bytes 20512 | tf_op jit(solution)/shard_map/ppermute | solution.py:39
  25.3 1.6 %collective-permute-start.10 = (bf16[96,128]{1,0:T(8,128)(2,1)S(1)}, bf16[96,128]{1,0:T(8,128)(2,1)S(1)}, u32[]{:S(2)}, u32[]{:S(2)}) collective-permute-start(bf16[96,128]{1,0:T(8,128)(2,1)S(1)} %get-tuple-element.60.mine), channel_id=1, source_target_pairs={{0,1},{1,0},{2,3},{3,2},{4,5},{5,4},{6,7},{7,6},{8,9},{9,8},{10,11... | collective-permute-start | bytes 73736 | tf_op jit(solution)/shard_map/ppermute | solution.py:39
  26.9 2.3 %collective-permute-done.10.got = bf16[96,128]{1,0:T(8,128)(2,1)S(1)} collective-permute-done((bf16[96,128]{1,0:T(8,128)(2,1)S(1)}, bf16[96,128]{1,0:T(8,128)(2,1)S(1)}, u32[]{:S(2)}, u32[]{:S(2)}) %collective-permute-start.10) | collective-permute-done | bytes 24608 | tf_op jit(solution)/shard_map/ppermute | solution.py:39
  29.3 0.7 %collective-permute-start.11 = (bf16[80,128]{1,0:T(8,128)(2,1)S(1)}, bf16[80,128]{1,0:T(8,128)(2,1)S(1)}, u32[]{:S(2)}, u32[]{:S(2)}) collective-permute-start(bf16[80,128]{1,0:T(8,128)(2,1)S(1)} %get-tuple-element.65), channel_id=1, source_target_pairs={{0,6},{2,4},{4,2},{6,0},{1,7},{3,5},{5,3},{7,1},{8,14},{10,12},{12... | collective-permute-start | bytes 61448 | tf_op jit(solution)/shard_map/ppermute | solution.py:39
  30.0 1.1 %collective-permute-start.13 = (bf16[80,128]{1,0:T(8,128)(2,1)S(1)}, bf16[80,128]{1,0:T(8,128)(2,1)S(1)}, u32[]{:S(2)}, u32[]{:S(2)}) collective-permute-start(bf16[80,128]{1,0:T(8,128)(2,1)S(1)} %get-tuple-element.66), channel_id=1, source_target_pairs={{0,2},{2,0},{4,6},{6,4},{1,3},{3,1},{5,7},{7,5},{8,10},{10,8},{12,... | collective-permute-start | bytes 61448 | tf_op jit(solution)/shard_map/ppermute | solution.py:39
  31.1 2.6 %collective-permute-start.12 = (bf16[64,128]{1,0:T(8,128)(2,1)S(1)}, bf16[64,128]{1,0:T(8,128)(2,1)S(1)}, u32[]{:S(2)}, u32[]{:S(2)}) collective-permute-start(bf16[64,128]{1,0:T(8,128)(2,1)S(1)} %get-tuple-element.64.mine), channel_id=1, source_target_pairs={{0,4},{2,6},{4,0},{6,2},{1,5},{3,7},{5,1},{7,3},{8,12},{10,14},{12... | collective-permute-start | bytes 49160 | tf_op jit(solution)/shard_map/ppermute | solution.py:39
  33.7 1.2 %shard_map.82 = bf16[32,2,32,64]{3,2,1,0:T(8,128)(2,1)} custom-call(f32[2048,128]{1,0:T(8,128)S(1)} %get-tuple-element.42.sums, f32[2048,128]{1,0:T(8,128)S(1)} %get-tuple-element.49.outer_sums), custom_call_target="tpu_custom_call" | custom-call | bytes 8388608 | tf_op jit(solution)/shard_map/pallas_call | solution.py:702
  34.9 1.2 %shard_map.85 = (f32[4,4,64,128]{3,2,1,0:T(8,128)}, f32[2,4,4,8,128]{4,3,2,1,0:T(8,128)S(1)}) custom-call(f32[1584,128]{1,0:T(8,128)S(1)} %get-tuple-element.50.field, f32[1584,128]{1,0:T(8,128)S(1)} %get-tuple-element.51.outer_field, bf16[256,128]{1,0:T(8,128)(2,1)S(1)} %collective-permute-done.5.face_0, ...), custom_call_target="tpu_custom_call" | custom-call | bytes 8388608 | tf_op jit(solution)/shard_map/pallas_call | solution.py:718
  36.1 0.8 %shard_map.87 = (f32[4,4,64,128]{3,2,1,0:T(8,128)}, f32[27,4,32]{2,1,0:T(4,128)}, f32[1,32]{1,0:T(1,128)}) custom-call(f32[4,4,64,128]{3,2,1,0:T(8,128)} %get-tuple-element.61.whole, f32[2,4,4,8,128]{4,3,2,1,0:T(8,128)S(1)} %get-tuple-element.62.ends, bf16[64,128]{1,0:T(8,128)(2,1)S(1)} %get-tuple-element.64.mine, ...), custom_call_target="tpu_custom_call", output_to_operand_aliasing={{0}: (0, {})} | custom-call | tf_op jit(solution)/shard_map/pallas_call | solution.py:721
  (46 shorter events, 2.1 us)
Async XLA Ops:
  0.6 1.0 %copy-start = (bf16[4,4,64,128]{3,2,1,0:T(8,128)(2,1)S(1)}, bf16[4,4,64,128]{3,2,1,0:T(8,128)(2,1)}, u32[]{:S(2)}) copy-start(bf16[4,4,64,128]{3,2,1,0:T(8,128)(2,1)} %cells.5) | copy-start | bytes 786436
  1.6 3.3 %copy-start.4 = (bf16[32,4,3,3,3]{0,1,4,3,2:T(4,128)(2,1)S(1)}, bf16[32,4,3,3,3]{0,1,4,3,2:T(4,128)(2,1)}, u32[]{:S(2)}) copy-start(bf16[32,4,3,3,3]{0,1,4,3,2:T(4,128)(2,1)} %param.5) | copy-start | bytes 20740
  1.8 3.0 %copy-start.5 = (f32[32]{0:T(128)S(1)}, f32[32]{0:T(128)}, u32[]{:S(2)}) copy-start(f32[32]{0:T(128)} %param.6) | copy-start | bytes 388
  1.8 4.6 %collective-permute-start = (bf16[32,128]{1,0:T(8,128)(2,1)S(1)}, bf16[32,128]{1,0:T(8,128)(2,1)S(1)}, u32[]{:S(2)}, u32[]{:S(2)}) collective-permute-start(bf16[32,128]{1,0:T(8,128)(2,1)S(1)} %get-tuple-element.37), channel_id=1, source_target_pairs={{0,1},{1,0},{2,3},{3,2},{4,5},{5,4},{6,7},{7,6},{8,9},{9,8},{10,11... | collective-permute-start | bytes 24584 | tf_op jit(solution)/shard_map/ppermute | solution.py:39
  5.2 1.2 %copy-start.1 = (bf16[4,4,64,128]{3,2,1,0:T(8,128)(2,1)S(1)}, bf16[4,4,64,128]{3,2,1,0:T(8,128)(2,1)}, u32[]{:S(2)}) copy-start(bf16[4,4,64,128]{3,2,1,0:T(8,128)(2,1)} %cells.5) | copy-start | bytes 786436
  5.3 4.3 %copy-start.2 = (bf16[32,2,32,64]{3,2,1,0:T(8,128)(2,1)S(1)}, bf16[32,2,32,64]{3,2,1,0:T(8,128)(2,1)}, u32[]{:S(2)}) copy-start(bf16[32,2,32,64]{3,2,1,0:T(8,128)(2,1)} %cot.1) | copy-start | bytes 786436
  5.4 0.6 %copy-start.3 = (bf16[128,3,3,6,4]{0,4,3,2,1:T(4,128)(2,1)}, bf16[128,3,3,6,4]{0,4,3,2,1:T(4,128)(2,1)S(1)}, u32[]{:S(2)}) copy-start(bf16[128,3,3,6,4]{0,4,3,2,1:T(4,128)(2,1)S(1)} %reshape.59) | copy-start | bytes 165892
  6.5 4.4 %collective-permute-start.1 = (bf16[272,128]{1,0:T(8,128)(2,1)S(1)}, bf16[272,128]{1,0:T(8,128)(2,1)S(1)}, u32[]{:S(2)}, u32[]{:S(2)}) collective-permute-start(bf16[272,128]{1,0:T(8,128)(2,1)S(1)} %get-tuple-element.38), channel_id=1, source_target_pairs={{0,8},{8,0},{16,24},{24,16},{1,9},{9,1},{17,25},{25,17},{2,10},{10... | collective-permute-start | bytes 208904 | tf_op jit(solution)/shard_map/ppermute | solution.py:39
  6.6 4.5 %collective-permute-start.2 = (bf16[272,128]{1,0:T(8,128)(2,1)S(1)}, bf16[272,128]{1,0:T(8,128)(2,1)S(1)}, u32[]{:S(2)}, u32[]{:S(2)}) collective-permute-start(bf16[272,128]{1,0:T(8,128)(2,1)S(1)} %get-tuple-element.39), channel_id=1, source_target_pairs={{0,24},{8,16},{16,8},{24,0},{1,25},{9,17},{17,9},{25,1},{2,26},{10... | collective-permute-start | bytes 208904 | tf_op jit(solution)/shard_map/ppermute | solution.py:39
  8.7 0.8 %slice-start = ((bf16[128,3,3,6,4]{0,4,3,2,1:T(4,128)(2,1)}), bf16[128,3,3,4,4]{0,4,3,2,1:T(4,128)(2,1)S(1)}, s32[]{:S(2)}) async-start(bf16[128,3,3,6,4]{0,4,3,2,1:T(4,128)(2,1)} %copy-done.3), calls=%async_computation | async-start | bytes 73728 | tf_op jit(solution)/shard_map/slice | solution.py:616
  11.1 7.7 %collective-permute-start.3 = (bf16[80,128]{1,0:T(8,128)(2,1)S(1)}, bf16[80,128]{1,0:T(8,128)(2,1)S(1)}, u32[]{:S(2)}, u32[]{:S(2)}) collective-permute-start(bf16[80,128]{1,0:T(8,128)(2,1)S(1)} %get-tuple-element.44), channel_id=1, source_target_pairs={{0,6},{2,4},{4,2},{6,0},{1,7},{3,5},{5,3},{7,1},{8,14},{10,12},{12... | collective-permute-start | bytes 61448 | tf_op jit(solution)/shard_map/ppermute | solution.py:39
  14.8 4.0 %collective-permute-start.4 = (bf16[80,128]{1,0:T(8,128)(2,1)S(1)}, bf16[80,128]{1,0:T(8,128)(2,1)S(1)}, u32[]{:S(2)}, u32[]{:S(2)}) collective-permute-start(bf16[80,128]{1,0:T(8,128)(2,1)S(1)} %get-tuple-element.45), channel_id=1, source_target_pairs={{0,2},{2,0},{4,6},{6,4},{1,3},{3,1},{5,7},{7,5},{8,10},{10,8},{12,... | collective-permute-start | bytes 61448 | tf_op jit(solution)/shard_map/ppermute | solution.py:39
  20.3 3.7 %collective-permute-start.8 = (bf16[80,128]{1,0:T(8,128)(2,1)S(1)}, bf16[80,128]{1,0:T(8,128)(2,1)S(1)}, u32[]{:S(2)}, u32[]{:S(2)}) collective-permute-start(bf16[80,128]{1,0:T(8,128)(2,1)S(1)} %get-tuple-element.59), channel_id=1, source_target_pairs={{0,24},{8,16},{16,8},{24,0},{1,25},{9,17},{17,9},{25,1},{2,26},{10... | collective-permute-start | bytes 61448 | tf_op jit(solution)/shard_map/ppermute | solution.py:39
  21.5 3.8 %collective-permute-start.9 = (bf16[80,128]{1,0:T(8,128)(2,1)S(1)}, bf16[80,128]{1,0:T(8,128)(2,1)S(1)}, u32[]{:S(2)}, u32[]{:S(2)}) collective-permute-start(bf16[80,128]{1,0:T(8,128)(2,1)S(1)} %get-tuple-element.58), channel_id=1, source_target_pairs={{0,16},{8,24},{16,0},{24,8},{1,17},{9,25},{17,1},{25,9},{2,18},{10... | collective-permute-start | bytes 61448 | tf_op jit(solution)/shard_map/ppermute | solution.py:39
  22.0 3.2 %collective-permute-start.7 = (bf16[80,128]{1,0:T(8,128)(2,1)S(1)}, bf16[80,128]{1,0:T(8,128)(2,1)S(1)}, u32[]{:S(2)}, u32[]{:S(2)}) collective-permute-start(bf16[80,128]{1,0:T(8,128)(2,1)S(1)} %get-tuple-element.58), channel_id=1, source_target_pairs={{0,8},{8,0},{16,24},{24,16},{1,9},{9,1},{17,25},{25,17},{2,10},{10... | collective-permute-start | bytes 61448 | tf_op jit(solution)/shard_map/ppermute | solution.py:39
  22.3 12.7 %collective-permute-start.5 = (bf16[256,128]{1,0:T(8,128)(2,1)S(1)}, bf16[256,128]{1,0:T(8,128)(2,1)S(1)}, u32[]{:S(2)}, u32[]{:S(2)}) collective-permute-start(bf16[256,128]{1,0:T(8,128)(2,1)S(1)} %get-tuple-element.52), channel_id=1, source_target_pairs={{0,8},{8,0},{16,24},{24,16},{1,9},{9,1},{17,25},{25,17},{2,10},{10... | collective-permute-start | bytes 196616 | tf_op jit(solution)/shard_map/ppermute | solution.py:39
  22.7 12.2 %collective-permute-start.6 = (bf16[256,128]{1,0:T(8,128)(2,1)S(1)}, bf16[256,128]{1,0:T(8,128)(2,1)S(1)}, u32[]{:S(2)}, u32[]{:S(2)}) collective-permute-start(bf16[256,128]{1,0:T(8,128)(2,1)S(1)} %get-tuple-element.53), channel_id=1, source_target_pairs={{0,24},{8,16},{16,8},{24,0},{1,25},{9,17},{17,9},{25,1},{2,26},{10... | collective-permute-start | bytes 196616 | tf_op jit(solution)/shard_map/ppermute | solution.py:39
  25.3 3.9 %collective-permute-start.10 = (bf16[96,128]{1,0:T(8,128)(2,1)S(1)}, bf16[96,128]{1,0:T(8,128)(2,1)S(1)}, u32[]{:S(2)}, u32[]{:S(2)}) collective-permute-start(bf16[96,128]{1,0:T(8,128)(2,1)S(1)} %get-tuple-element.60.mine), channel_id=1, source_target_pairs={{0,1},{1,0},{2,3},{3,2},{4,5},{5,4},{6,7},{7,6},{8,9},{9,8},{10,11... | collective-permute-start | bytes 73736 | tf_op jit(solution)/shard_map/ppermute | solution.py:39
  29.3 6.8 %collective-permute-start.11 = (bf16[80,128]{1,0:T(8,128)(2,1)S(1)}, bf16[80,128]{1,0:T(8,128)(2,1)S(1)}, u32[]{:S(2)}, u32[]{:S(2)}) collective-permute-start(bf16[80,128]{1,0:T(8,128)(2,1)S(1)} %get-tuple-element.65), channel_id=1, source_target_pairs={{0,6},{2,4},{4,2},{6,0},{1,7},{3,5},{5,3},{7,1},{8,14},{10,12},{12... | collective-permute-start | bytes 61448 | tf_op jit(solution)/shard_map/ppermute | solution.py:39
  30.0 6.1 %collective-permute-start.13 = (bf16[80,128]{1,0:T(8,128)(2,1)S(1)}, bf16[80,128]{1,0:T(8,128)(2,1)S(1)}, u32[]{:S(2)}, u32[]{:S(2)}) collective-permute-start(bf16[80,128]{1,0:T(8,128)(2,1)S(1)} %get-tuple-element.66), channel_id=1, source_target_pairs={{0,2},{2,0},{4,6},{6,4},{1,3},{3,1},{5,7},{7,5},{8,10},{10,8},{12,... | collective-permute-start | bytes 61448 | tf_op jit(solution)/shard_map/ppermute | solution.py:39
  31.1 5.0 %collective-permute-start.12 = (bf16[64,128]{1,0:T(8,128)(2,1)S(1)}, bf16[64,128]{1,0:T(8,128)(2,1)S(1)}, u32[]{:S(2)}, u32[]{:S(2)}) collective-permute-start(bf16[64,128]{1,0:T(8,128)(2,1)S(1)} %get-tuple-element.64.mine), channel_id=1, source_target_pairs={{0,4},{2,6},{4,0},{6,2},{1,5},{3,7},{5,1},{7,3},{8,12},{10,14},{12... | collective-permute-start | bytes 49160 | tf_op jit(solution)/shard_map/ppermute | solution.py:39

commit v14 on v13

--- a/solution.py
+++ b/solution.py
@@ -137,7 +137,8 @@
             ]
 
 
-def pool_kernel(edge, sums, outer_sums, pooled):
+def pool_kernel(edge, sums, outer_sums, pooled, token):
+    token[...] = jnp.zeros_like(token)
     chan_out, pool_x, pool_y, pool_z = pooled.shape
     halves = jnp.where(
         iota((2 * lanes, pool_z), 0) % lanes // 2 == iota((2 * lanes, pool_z), 1), 0.125, 0.0
@@ -495,7 +496,7 @@
         rows_out[place, :] = rows[place, :] + jnp.concatenate(more, axis=0)
 
 
-def z_kernel(count_y, mine, got, rows, sent_0, sent_1, wframe):
+def z_kernel(count_y, mine, got, rows, token, sent_0, sent_1, wframe):
     own = rows.shape[0] // 2
     total = joined(mine[2 * own :, :]) + joined(got[2 * own :, :])
     sides = jnp.concatenate(split(total), axis=0)
@@ -539,7 +540,7 @@
             ends[1, c, x] = plane[count_y - 8 : count_y]
 
 
-def final_kernel(whole, ends, mine, got_1, far, got_0, out, wout, bout, tiles, wtile, btile, sems):
+def final_kernel(whole, ends, mine, got_0, got_1, far, out, wout, bout, tiles, wtile, btile, sems):
     chan, count_x, count_y, _ = whole.shape
     own = chan * count_x
     chan_out = mine.shape[0] // 2
@@ -699,8 +700,10 @@
         field, outer_field
     )
     face_1, face_0 = swapped(face_1, "gx", 1), swapped(face_0, "gx", 0)
-    pooled = call(
-        functools.partial(pool_kernel, pairs), shape(cotangent.shape, bf16), cost=traffic(8)
+    pooled, token = call(
+        functools.partial(pool_kernel, pairs),
+        [shape(cotangent.shape, bf16), shape((8, lanes), f32)],
+        cost=traffic(8),
     )(sums, outer_sums)
     mine, rows = call(
         functools.partial(x_kernel, alone),
@@ -711,7 +714,8 @@
     row_0, row_1, mine = call(
         functools.partial(z_kernel, count_y),
         [bundle, bundle, shape((2 * chan_out, lanes), bf16)],
-    )(mine, frame, rows)
+        in_specs=[vmem] * 3 + [anywhere],
+    )(mine, frame, rows, token)
     row_1, row_0 = swapped(row_1, "gy", 1), swapped(row_0, "gy", 0)
     far = swapped(mine, "gy", 2)
     tiles = (2, chan, count_x, 8, lanes)
@@ -734,7 +738,7 @@
         in_specs=[anywhere] + [vmem] * 5,
         out_specs=[anywhere] * 3,
         input_output_aliases={0: 0},
-    )(grad, ends, mine, row_1, far, row_0)
+    )(grad, ends, mine, row_0, row_1, far)
     weight_grad = wsum.reshape(3, 3, 3, chan, chan_out).transpose(4, 3, 0, 1, 2)
     return (pooled, weight_grad, bias_grad.reshape(chan_out), input_grad)
 

time: 37.1 us -> 37.6 us (1.013)
  waiting for transfers between devices: 4.15 us -> 5.54 us
  starting transfers between devices: 18.5 us -> 17.6 us
    ppermute x14, waiting for transfers between devices: 4.15 us -> 5.54 us  [swapped(): return lax.ppermute(array, axis, pairs)]
    ppermute x14, starting transfers between devices: 18.5 us -> 17.6 us  [swapped(): return lax.ppermute(array, axis, pairs)]
  transfers between devices with their start and end apart: 14 -> 14, of which waited for: 4 -> 6; matrix products, arithmetic and copies ran while one was open for 3% -> 3% of each run, Pallas kernels for 21% -> 20%
where the time goes in v14:
time: 37.6 us; the launch traced here: 37.4 us
  starting transfers between devices  17.6 us (47%)
  Pallas kernels  10.1 us (27%)
  waiting for transfers between devices  5.54 us (15%)
  local copies, waits for them, and re-layouts  2.95 us (8%)
  between operations  0.84 us (2%)
    ppermute x14, starting transfers between devices, swapped(): return lax.ppermute(array, axis, pairs)  17.6 us
    ppermute x14, waiting for transfers between devices, swapped(): return lax.ppermute(array, axis, pairs)  5.54 us
    pallas_call x1, Pallas kernels, on_device(): call(functools.partial(inner_kernel, count_x), [pooled_rows, all_field, s...  3.7 us
    unnamed x12, local copies, waits for them, and re-layouts  1.52 us
    pallas_call x1, Pallas kernels, on_device(): call(functools.partial(main_kernel, count_x), [pooled_rows, all_field, bu...  1.5 us
    pallas_call x1, Pallas kernels, on_device(): call(functools.partial(pool_kernel, pairs), [shape(cotangent.shape, bf16)...  1.24 us
    pallas_call x1, Pallas kernels, on_device(): call(grad_kernel, [shape(cells.shape, f32), shape(tiles, f32)], cost=traf...  1.19 us
    pallas_call x1, Pallas kernels, on_device(): spread = call(spread_kernel, pooled_rows)(cotangent)  0.88 us
  transfers between devices with their start and end apart: 14, of which 6 were waited for; matrix products, arithmetic and copies ran while one was open for 3% of the time, Pallas kernels for 20%

profile of v14, /device:TPU:0, one launch (start us, length us, event | category | flops | bytes accessed | tf_op | source)
XLA Modules:
  0.0 37.4 jit_solution(12902799981297775889)
XLA Ops:
  0.6 0.9 %copy-done = bf16[4,4,64,128]{3,2,1,0:T(8,128)(2,1)S(1)} copy-done((bf16[4,4,64,128]{3,2,1,0:T(8,128)(2,1)S(1)}, bf16[4,4,64,128]{3,2,1,0:T(8,128)(2,1)}, u32[]{:S(2)}) %copy-start) | copy-done | bytes 262168
  1.8 3.0 %collective-permute-start = (bf16[32,128]{1,0:T(8,128)(2,1)S(1)}, bf16[32,128]{1,0:T(8,128)(2,1)S(1)}, u32[]{:S(2)}, u32[]{:S(2)}) collective-permute-start(bf16[32,128]{1,0:T(8,128)(2,1)S(1)} %get-tuple-element.39), channel_id=1, source_target_pairs={{0,1},{1,0},{2,3},{3,2},{4,5},{5,4},{6,7},{7,6},{8,9},{9,8},{10,11... | collective-permute-start | bytes 24584 | tf_op jit(solution)/shard_map/ppermute | solution.py:39
  5.5 0.6 %copy-done.3 = bf16[128,3,3,6,4]{0,4,3,2,1:T(4,128)(2,1)} copy-done((bf16[128,3,3,6,4]{0,4,3,2,1:T(4,128)(2,1)}, bf16[128,3,3,6,4]{0,4,3,2,1:T(4,128)(2,1)S(1)}, u32[]{:S(2)}) %copy-start.3) | copy-done | bytes 55320
  6.6 2.1 %collective-permute-start.2 = (bf16[272,128]{1,0:T(8,128)(2,1)S(1)}, bf16[272,128]{1,0:T(8,128)(2,1)S(1)}, u32[]{:S(2)}, u32[]{:S(2)}) collective-permute-start(bf16[272,128]{1,0:T(8,128)(2,1)S(1)} %get-tuple-element.41), channel_id=1, source_target_pairs={{0,24},{8,16},{16,8},{24,0},{1,25},{9,17},{17,9},{25,1},{2,26},{10... | collective-permute-start | bytes 208904 | tf_op jit(solution)/shard_map/ppermute | solution.py:39
  8.8 0.6 %slice-done = bf16[128,3,3,4,4]{0,4,3,2,1:T(4,128)(2,1)S(1)} async-done(((bf16[128,3,3,6,4]{0,4,3,2,1:T(4,128)(2,1)}), bf16[128,3,3,4,4]{0,4,3,2,1:T(4,128)(2,1)S(1)}, s32[]{:S(2)}) %slice-start) | async-done | bytes 36888 | tf_op jit(solution)/shard_map/slice | solution.py:617
  9.6 0.9 %shard_map.78.spread = f32[2048,128]{1,0:T(8,128)S(1)} custom-call(bf16[32,2,32,64]{3,2,1,0:T(8,128)(2,1)S(1)} %copy-done.2), custom_call_target="tpu_custom_call" | custom-call | tf_op jit(solution)/shard_map/pallas_call | solution.py:628
  10.5 0.4 %shard_map.77.inner = bf16[3168,128]{1,0:T(8,128)(2,1)S(1)} custom-call(bf16[4,4,64,128]{3,2,1,0:T(8,128)(2,1)S(1)} %copy-done.1, f32[16,128]{1,0:T(8,128)S(1)} %get-tuple-element.42.left, f32[16,128]{1,0:T(8,128)S(1)} %get-tuple-element.43.right), custom_call_target="tpu_custom_call" | custom-call | bytes 4194304 | tf_op jit(solution)/shard_map/pallas_call | solution.py:635
  11.1 3.7 %collective-permute-start.3 = (bf16[80,128]{1,0:T(8,128)(2,1)S(1)}, bf16[80,128]{1,0:T(8,128)(2,1)S(1)}, u32[]{:S(2)}, u32[]{:S(2)}) collective-permute-start(bf16[80,128]{1,0:T(8,128)(2,1)S(1)} %get-tuple-element.46), channel_id=1, source_target_pairs={{0,6},{2,4},{4,2},{6,0},{1,7},{3,5},{5,3},{7,1},{8,14},{10,12},{12... | collective-permute-start | bytes 61448 | tf_op jit(solution)/shard_map/ppermute | solution.py:39
  15.0 3.7 %shard_map.79 = (f32[2048,128]{1,0:T(8,128)S(1)}, f32[1584,128]{1,0:T(8,128)S(1)}, bf16[2112,128]{1,0:T(8,128)(2,1)S(1)}, f32[48,128]{1,0:T(8,128)S(1)}, f32[128,240]{1,0:T(8,128)S(1)}) custom-call(bf16[272,128]{1,0:T(8,128)(2,1)S(1)} %collective-permute-done.1.got_0, bf16[272,128]{1,0:T(8,128)(2,1)S(1)} %collective-permute-done.2.got_1, ...), custom_call_target="tpu_custom_call" | custom-call | bytes 16777216 | tf_op jit(solution)/shard_map/pallas_call | solution.py:654
  18.8 1.5 %shard_map.81 = (f32[2048,128]{1,0:T(8,128)S(1)}, f32[1584,128]{1,0:T(8,128)S(1)}, bf16[80,128]{1,0:T(8,128)(2,1)S(1)}, bf16[80,128]{1,0:T(8,128)(2,1)S(1)}, f32...) custom-call(bf16[80,128]{1,0:T(8,128)(2,1)S(1)} %collective-permute-done.3.row_, ...), custom_call_target="tpu_custom_call" | custom-call | tf_op jit(solution)/shard_map/pallas_call | solution.py:673
  20.3 1.2 %collective-permute-start.8 = (bf16[80,128]{1,0:T(8,128)(2,1)S(1)}, bf16[80,128]{1,0:T(8,128)(2,1)S(1)}, u32[]{:S(2)}, u32[]{:S(2)}) collective-permute-start(bf16[80,128]{1,0:T(8,128)(2,1)S(1)} %get-tuple-element.62), channel_id=1, source_target_pairs={{0,24},{8,16},{16,8},{24,0},{1,25},{9,17},{17,9},{25,1},{2,26},{10... | collective-permute-start | bytes 61448 | tf_op jit(solution)/shard_map/ppermute | solution.py:39
  21.5 0.5 %collective-permute-start.9 = (bf16[80,128]{1,0:T(8,128)(2,1)S(1)}, bf16[80,128]{1,0:T(8,128)(2,1)S(1)}, u32[]{:S(2)}, u32[]{:S(2)}) collective-permute-start(bf16[80,128]{1,0:T(8,128)(2,1)S(1)} %get-tuple-element.61), channel_id=1, source_target_pairs={{0,16},{8,24},{16,0},{24,8},{1,17},{9,25},{17,1},{25,9},{2,18},{10... | collective-permute-start | bytes 61448 | tf_op jit(solution)/shard_map/ppermute | solution.py:39
  22.3 0.4 %collective-permute-start.5 = (bf16[256,128]{1,0:T(8,128)(2,1)S(1)}, bf16[256,128]{1,0:T(8,128)(2,1)S(1)}, u32[]{:S(2)}, u32[]{:S(2)}) collective-permute-start(bf16[256,128]{1,0:T(8,128)(2,1)S(1)} %get-tuple-element.55), channel_id=1, source_target_pairs={{0,8},{8,0},{16,24},{24,16},{1,9},{9,1},{17,25},{25,17},{2,10},{10... | collective-permute-start | bytes 196616 | tf_op jit(solution)/shard_map/ppermute | solution.py:39
  22.7 1.3 %collective-permute-start.6 = (bf16[256,128]{1,0:T(8,128)(2,1)S(1)}, bf16[256,128]{1,0:T(8,128)(2,1)S(1)}, u32[]{:S(2)}, u32[]{:S(2)}) collective-permute-start(bf16[256,128]{1,0:T(8,128)(2,1)S(1)} %get-tuple-element.56), channel_id=1, source_target_pairs={{0,24},{8,16},{16,8},{24,0},{1,25},{9,17},{17,9},{25,1},{2,26},{10... | collective-permute-start | bytes 196616 | tf_op jit(solution)/shard_map/ppermute | solution.py:39
  24.0 1.3 %collective-permute-done.9.far = bf16[80,128]{1,0:T(8,128)(2,1)S(1)} collective-permute-done((bf16[80,128]{1,0:T(8,128)(2,1)S(1)}, bf16[80,128]{1,0:T(8,128)(2,1)S(1)}, u32[]{:S(2)}, u32[]{:S(2)}) %collective-permute-start.9) | collective-permute-done | bytes 20512 | tf_op jit(solution)/shard_map/ppermute | solution.py:39
  25.3 1.6 %collective-permute-start.10 = (bf16[96,128]{1,0:T(8,128)(2,1)S(1)}, bf16[96,128]{1,0:T(8,128)(2,1)S(1)}, u32[]{:S(2)}, u32[]{:S(2)}) collective-permute-start(bf16[96,128]{1,0:T(8,128)(2,1)S(1)} %get-tuple-element.63.mine), channel_id=1, source_target_pairs={{0,1},{1,0},{2,3},{3,2},{4,5},{5,4},{6,7},{7,6},{8,9},{9,8},{10,11... | collective-permute-start | bytes 73736 | tf_op jit(solution)/shard_map/ppermute | solution.py:39
  26.9 1.2 %shard_map.82 = (bf16[32,2,32,64]{3,2,1,0:T(8,128)(2,1)}, f32[8,128]{1,0:T(8,128)S(1)}) custom-call(f32[2048,128]{1,0:T(8,128)S(1)} %get-tuple-element.44.sums, f32[2048,128]{1,0:T(8,128)S(1)} %get-tuple-element.51.outer_sums), custom_call_target="tpu_custom_call" | custom-call | bytes 8388608 | tf_op jit(solution)/shard_map/pallas_call | solution.py:703
  28.1 1.1 %collective-permute-done.10.got = bf16[96,128]{1,0:T(8,128)(2,1)S(1)} collective-permute-done((bf16[96,128]{1,0:T(8,128)(2,1)S(1)}, bf16[96,128]{1,0:T(8,128)(2,1)S(1)}, u32[]{:S(2)}, u32[]{:S(2)}) %collective-permute-start.10) | collective-permute-done | bytes 24608 | tf_op jit(solution)/shard_map/ppermute | solution.py:39
  29.3 1.8 %collective-permute-start.11 = (bf16[80,128]{1,0:T(8,128)(2,1)S(1)}, bf16[80,128]{1,0:T(8,128)(2,1)S(1)}, u32[]{:S(2)}, u32[]{:S(2)}) collective-permute-start(bf16[80,128]{1,0:T(8,128)(2,1)S(1)} %get-tuple-element.69), channel_id=1, source_target_pairs={{0,2},{2,0},{4,6},{6,4},{1,3},{3,1},{5,7},{7,5},{8,10},{10,8},{12,... | collective-permute-start | bytes 61448 | tf_op jit(solution)/shard_map/ppermute | solution.py:39
  31.4 1.4 %collective-permute-start.13 = (bf16[64,128]{1,0:T(8,128)(2,1)S(1)}, bf16[64,128]{1,0:T(8,128)(2,1)S(1)}, u32[]{:S(2)}, u32[]{:S(2)}) collective-permute-start(bf16[64,128]{1,0:T(8,128)(2,1)S(1)} %get-tuple-element.68.mine), channel_id=1, source_target_pairs={{0,4},{2,6},{4,0},{6,2},{1,5},{3,7},{5,1},{7,3},{8,12},{10,14},{12... | collective-permute-start | bytes 49160 | tf_op jit(solution)/shard_map/ppermute | solution.py:39
  32.8 1.2 %shard_map.85 = (f32[4,4,64,128]{3,2,1,0:T(8,128)}, f32[2,4,4,8,128]{4,3,2,1,0:T(8,128)S(1)}) custom-call(f32[1584,128]{1,0:T(8,128)S(1)} %get-tuple-element.53.field, f32[1584,128]{1,0:T(8,128)S(1)} %get-tuple-element.54.outer_field, bf16[256,128]{1,0:T(8,128)(2,1)S(1)} %collective-permute-done.5.face_0, ...), custom_call_target="tpu_custom_call" | custom-call | bytes 8388608 | tf_op jit(solution)/shard_map/pallas_call | solution.py:722
  34.0 2.0 %collective-permute-done.13.far = bf16[64,128]{1,0:T(8,128)(2,1)S(1)} collective-permute-done((bf16[64,128]{1,0:T(8,128)(2,1)S(1)}, bf16[64,128]{1,0:T(8,128)(2,1)S(1)}, u32[]{:S(2)}, u32[]{:S(2)}) %collective-permute-start.13) | collective-permute-done | bytes 16416 | tf_op jit(solution)/shard_map/ppermute | solution.py:39
  36.1 0.6 %collective-permute-done.12.got_1 = bf16[80,128]{1,0:T(8,128)(2,1)S(1)} collective-permute-done((bf16[80,128]{1,0:T(8,128)(2,1)S(1)}, bf16[80,128]{1,0:T(8,128)(2,1)S(1)}, u32[]{:S(2)}, u32[]{:S(2)}) %collective-permute-start.12) | collective-permute-done | bytes 20512 | tf_op jit(solution)/shard_map/ppermute | solution.py:39
  36.6 0.8 %shard_map.87 = (f32[4,4,64,128]{3,2,1,0:T(8,128)}, f32[27,4,32]{2,1,0:T(4,128)}, f32[1,32]{1,0:T(1,128)}) custom-call(f32[4,4,64,128]{3,2,1,0:T(8,128)} %get-tuple-element.64.whole, f32[2,4,4,8,128]{4,3,2,1,0:T(8,128)S(1)} %get-tuple-element.65.ends, bf16[64,128]{1,0:T(8,128)(2,1)S(1)} %get-tuple-element.68.mine, ...), custom_call_target="tpu_custom_call", output_to_operand_aliasing={{0}: (0, {})} | custom-call | tf_op jit(solution)/shard_map/pallas_call | solution.py:725
  (46 shorter events, 2.7 us)
Async XLA Ops:
  0.6 1.0 %copy-start = (bf16[4,4,64,128]{3,2,1,0:T(8,128)(2,1)S(1)}, bf16[4,4,64,128]{3,2,1,0:T(8,128)(2,1)}, u32[]{:S(2)}) copy-start(bf16[4,4,64,128]{3,2,1,0:T(8,128)(2,1)} %cells.5) | copy-start | bytes 786436
  1.6 3.3 %copy-start.4 = (bf16[32,4,3,3,3]{0,1,4,3,2:T(4,128)(2,1)S(1)}, bf16[32,4,3,3,3]{0,1,4,3,2:T(4,128)(2,1)}, u32[]{:S(2)}) copy-start(bf16[32,4,3,3,3]{0,1,4,3,2:T(4,128)(2,1)} %param.5) | copy-start | bytes 20740
  1.8 3.0 %copy-start.5 = (f32[32]{0:T(128)S(1)}, f32[32]{0:T(128)}, u32[]{:S(2)}) copy-start(f32[32]{0:T(128)} %param.6) | copy-start | bytes 388
  1.8 4.6 %collective-permute-start = (bf16[32,128]{1,0:T(8,128)(2,1)S(1)}, bf16[32,128]{1,0:T(8,128)(2,1)S(1)}, u32[]{:S(2)}, u32[]{:S(2)}) collective-permute-start(bf16[32,128]{1,0:T(8,128)(2,1)S(1)} %get-tuple-element.39), channel_id=1, source_target_pairs={{0,1},{1,0},{2,3},{3,2},{4,5},{5,4},{6,7},{7,6},{8,9},{9,8},{10,11... | collective-permute-start | bytes 24584 | tf_op jit(solution)/shard_map/ppermute | solution.py:39
  5.2 1.2 %copy-start.1 = (bf16[4,4,64,128]{3,2,1,0:T(8,128)(2,1)S(1)}, bf16[4,4,64,128]{3,2,1,0:T(8,128)(2,1)}, u32[]{:S(2)}) copy-start(bf16[4,4,64,128]{3,2,1,0:T(8,128)(2,1)} %cells.5) | copy-start | bytes 786436
  5.3 4.3 %copy-start.2 = (bf16[32,2,32,64]{3,2,1,0:T(8,128)(2,1)S(1)}, bf16[32,2,32,64]{3,2,1,0:T(8,128)(2,1)}, u32[]{:S(2)}) copy-start(bf16[32,2,32,64]{3,2,1,0:T(8,128)(2,1)} %cot.1) | copy-start | bytes 786436
  5.4 0.6 %copy-start.3 = (bf16[128,3,3,6,4]{0,4,3,2,1:T(4,128)(2,1)}, bf16[128,3,3,6,4]{0,4,3,2,1:T(4,128)(2,1)S(1)}, u32[]{:S(2)}) copy-start(bf16[128,3,3,6,4]{0,4,3,2,1:T(4,128)(2,1)S(1)} %reshape.59) | copy-start | bytes 165892
  6.5 4.4 %collective-permute-start.1 = (bf16[272,128]{1,0:T(8,128)(2,1)S(1)}, bf16[272,128]{1,0:T(8,128)(2,1)S(1)}, u32[]{:S(2)}, u32[]{:S(2)}) collective-permute-start(bf16[272,128]{1,0:T(8,128)(2,1)S(1)} %get-tuple-element.40), channel_id=1, source_target_pairs={{0,8},{8,0},{16,24},{24,16},{1,9},{9,1},{17,25},{25,17},{2,10},{10... | collective-permute-start | bytes 208904 | tf_op jit(solution)/shard_map/ppermute | solution.py:39
  6.6 4.5 %collective-permute-start.2 = (bf16[272,128]{1,0:T(8,128)(2,1)S(1)}, bf16[272,128]{1,0:T(8,128)(2,1)S(1)}, u32[]{:S(2)}, u32[]{:S(2)}) collective-permute-start(bf16[272,128]{1,0:T(8,128)(2,1)S(1)} %get-tuple-element.41), channel_id=1, source_target_pairs={{0,24},{8,16},{16,8},{24,0},{1,25},{9,17},{17,9},{25,1},{2,26},{10... | collective-permute-start | bytes 208904 | tf_op jit(solution)/shard_map/ppermute | solution.py:39
  8.7 0.8 %slice-start = ((bf16[128,3,3,6,4]{0,4,3,2,1:T(4,128)(2,1)}), bf16[128,3,3,4,4]{0,4,3,2,1:T(4,128)(2,1)S(1)}, s32[]{:S(2)}) async-start(bf16[128,3,3,6,4]{0,4,3,2,1:T(4,128)(2,1)} %copy-done.3), calls=%async_computation | async-start | bytes 73728 | tf_op jit(solution)/shard_map/slice | solution.py:617
  11.1 7.7 %collective-permute-start.3 = (bf16[80,128]{1,0:T(8,128)(2,1)S(1)}, bf16[80,128]{1,0:T(8,128)(2,1)S(1)}, u32[]{:S(2)}, u32[]{:S(2)}) collective-permute-start(bf16[80,128]{1,0:T(8,128)(2,1)S(1)} %get-tuple-element.46), channel_id=1, source_target_pairs={{0,6},{2,4},{4,2},{6,0},{1,7},{3,5},{5,3},{7,1},{8,14},{10,12},{12... | collective-permute-start | bytes 61448 | tf_op jit(solution)/shard_map/ppermute | solution.py:39
  14.8 4.0 %collective-permute-start.4 = (bf16[80,128]{1,0:T(8,128)(2,1)S(1)}, bf16[80,128]{1,0:T(8,128)(2,1)S(1)}, u32[]{:S(2)}, u32[]{:S(2)}) collective-permute-start(bf16[80,128]{1,0:T(8,128)(2,1)S(1)} %get-tuple-element.47), channel_id=1, source_target_pairs={{0,2},{2,0},{4,6},{6,4},{1,3},{3,1},{5,7},{7,5},{8,10},{10,8},{12,... | collective-permute-start | bytes 61448 | tf_op jit(solution)/shard_map/ppermute | solution.py:39
  20.3 3.7 %collective-permute-start.8 = (bf16[80,128]{1,0:T(8,128)(2,1)S(1)}, bf16[80,128]{1,0:T(8,128)(2,1)S(1)}, u32[]{:S(2)}, u32[]{:S(2)}) collective-permute-start(bf16[80,128]{1,0:T(8,128)(2,1)S(1)} %get-tuple-element.62), channel_id=1, source_target_pairs={{0,24},{8,16},{16,8},{24,0},{1,25},{9,17},{17,9},{25,1},{2,26},{10... | collective-permute-start | bytes 61448 | tf_op jit(solution)/shard_map/ppermute | solution.py:39
  21.5 3.8 %collective-permute-start.9 = (bf16[80,128]{1,0:T(8,128)(2,1)S(1)}, bf16[80,128]{1,0:T(8,128)(2,1)S(1)}, u32[]{:S(2)}, u32[]{:S(2)}) collective-permute-start(bf16[80,128]{1,0:T(8,128)(2,1)S(1)} %get-tuple-element.61), channel_id=1, source_target_pairs={{0,16},{8,24},{16,0},{24,8},{1,17},{9,25},{17,1},{25,9},{2,18},{10... | collective-permute-start | bytes 61448 | tf_op jit(solution)/shard_map/ppermute | solution.py:39
  22.0 3.2 %collective-permute-start.7 = (bf16[80,128]{1,0:T(8,128)(2,1)S(1)}, bf16[80,128]{1,0:T(8,128)(2,1)S(1)}, u32[]{:S(2)}, u32[]{:S(2)}) collective-permute-start(bf16[80,128]{1,0:T(8,128)(2,1)S(1)} %get-tuple-element.61), channel_id=1, source_target_pairs={{0,8},{8,0},{16,24},{24,16},{1,9},{9,1},{17,25},{25,17},{2,10},{10... | collective-permute-start | bytes 61448 | tf_op jit(solution)/shard_map/ppermute | solution.py:39
  22.3 10.5 %collective-permute-start.5 = (bf16[256,128]{1,0:T(8,128)(2,1)S(1)}, bf16[256,128]{1,0:T(8,128)(2,1)S(1)}, u32[]{:S(2)}, u32[]{:S(2)}) collective-permute-start(bf16[256,128]{1,0:T(8,128)(2,1)S(1)} %get-tuple-element.55), channel_id=1, source_target_pairs={{0,8},{8,0},{16,24},{24,16},{1,9},{9,1},{17,25},{25,17},{2,10},{10... | collective-permute-start | bytes 196616 | tf_op jit(solution)/shard_map/ppermute | solution.py:39
  22.7 10.1 %collective-permute-start.6 = (bf16[256,128]{1,0:T(8,128)(2,1)S(1)}, bf16[256,128]{1,0:T(8,128)(2,1)S(1)}, u32[]{:S(2)}, u32[]{:S(2)}) collective-permute-start(bf16[256,128]{1,0:T(8,128)(2,1)S(1)} %get-tuple-element.56), channel_id=1, source_target_pairs={{0,24},{8,16},{16,8},{24,0},{1,25},{9,17},{17,9},{25,1},{2,26},{10... | collective-permute-start | bytes 196616 | tf_op jit(solution)/shard_map/ppermute | solution.py:39
  25.3 3.9 %collective-permute-start.10 = (bf16[96,128]{1,0:T(8,128)(2,1)S(1)}, bf16[96,128]{1,0:T(8,128)(2,1)S(1)}, u32[]{:S(2)}, u32[]{:S(2)}) collective-permute-start(bf16[96,128]{1,0:T(8,128)(2,1)S(1)} %get-tuple-element.63.mine), channel_id=1, source_target_pairs={{0,1},{1,0},{2,3},{3,2},{4,5},{5,4},{6,7},{7,6},{8,9},{9,8},{10,11... | collective-permute-start | bytes 73736 | tf_op jit(solution)/shard_map/ppermute | solution.py:39
  29.3 6.8 %collective-permute-start.11 = (bf16[80,128]{1,0:T(8,128)(2,1)S(1)}, bf16[80,128]{1,0:T(8,128)(2,1)S(1)}, u32[]{:S(2)}, u32[]{:S(2)}) collective-permute-start(bf16[80,128]{1,0:T(8,128)(2,1)S(1)} %get-tuple-element.69), channel_id=1, source_target_pairs={{0,2},{2,0},{4,6},{6,4},{1,3},{3,1},{5,7},{7,5},{8,10},{10,8},{12,... | collective-permute-start | bytes 61448 | tf_op jit(solution)/shard_map/ppermute | solution.py:39
  31.1 5.6 %collective-permute-start.12 = (bf16[80,128]{1,0:T(8,128)(2,1)S(1)}, bf16[80,128]{1,0:T(8,128)(2,1)S(1)}, u32[]{:S(2)}, u32[]{:S(2)}) collective-permute-start(bf16[80,128]{1,0:T(8,128)(2,1)S(1)} %get-tuple-element.70), channel_id=1, source_target_pairs={{0,6},{2,4},{4,2},{6,0},{1,7},{3,5},{5,3},{7,1},{8,14},{10,12},{12... | collective-permute-start | bytes 61448 | tf_op jit(solution)/shard_map/ppermute | solution.py:39
  31.4 4.6 %collective-permute-start.13 = (bf16[64,128]{1,0:T(8,128)(2,1)S(1)}, bf16[64,128]{1,0:T(8,128)(2,1)S(1)}, u32[]{:S(2)}, u32[]{:S(2)}) collective-permute-start(bf16[64,128]{1,0:T(8,128)(2,1)S(1)} %get-tuple-element.68.mine), channel_id=1, source_target_pairs={{0,4},{2,6},{4,0},{6,2},{1,5},{3,7},{5,1},{7,3},{8,12},{10,14},{12... | collective-permute-start | bytes 49160 | tf_op jit(solution)/shard_map/ppermute | solution.py:39

commit v15 on v14

--- a/solution.py
+++ b/solution.py
@@ -540,7 +540,7 @@
             ends[1, c, x] = plane[count_y - 8 : count_y]
 
 
-def final_kernel(whole, ends, mine, got_0, got_1, far, out, wout, bout, tiles, wtile, btile, sems):
+def final_kernel(whole, ends, mine, got_1, far, got_0, out, wout, bout, tiles, wtile, btile, sems):
     chan, count_x, count_y, _ = whole.shape
     own = chan * count_x
     chan_out = mine.shape[0] // 2
@@ -738,7 +738,7 @@
         in_specs=[anywhere] + [vmem] * 5,
         out_specs=[anywhere] * 3,
         input_output_aliases={0: 0},
-    )(grad, ends, mine, row_0, row_1, far)
+    )(grad, ends, mine, row_1, far, row_0)
     weight_grad = wsum.reshape(3, 3, 3, chan, chan_out).transpose(4, 3, 0, 1, 2)
     return (pooled, weight_grad, bias_grad.reshape(chan_out), input_grad)
 

time: 37.6 us -> 36.8 us (0.979)
  waiting for transfers between devices: 5.54 us -> 3.79 us
  starting transfers between devices: 17.6 us -> 18.5 us
    ppermute x14, waiting for transfers between devices: 5.54 us -> 3.79 us  [swapped(): return lax.ppermute(array, axis, pairs)]
    ppermute x14, starting transfers between devices: 17.6 us -> 18.5 us  [swapped(): return lax.ppermute(array, axis, pairs)]
  transfers between devices with their start and end apart: 14 -> 14, of which waited for: 6 -> 5; matrix products, arithmetic and copies ran while one was open for 3% -> 3% of each run, Pallas kernels for 20% -> 21%
where the time goes in v15:
time: 36.8 us; the launch traced here: 36.5 us
  starting transfers between devices  18.5 us (50%)
  Pallas kernels  10.2 us (28%)
  waiting for transfers between devices  3.79 us (10%)
  local copies, waits for them, and re-layouts  2.95 us (8%)
  between operations  0.84 us (2%)
    ppermute x14, starting transfers between devices, swapped(): return lax.ppermute(array, axis, pairs)  18.5 us
    ppermute x14, waiting for transfers between devices, swapped(): return lax.ppermute(array, axis, pairs)  3.79 us
    pallas_call x1, Pallas kernels, on_device(): call(functools.partial(inner_kernel, count_x), [pooled_rows, all_field, s...  3.7 us
    unnamed x12, local copies, waits for them, and re-layouts  1.52 us
    pallas_call x1, Pallas kernels, on_device(): call(functools.partial(main_kernel, count_x), [pooled_rows, all_field, bu...  1.5 us
    pallas_call x1, Pallas kernels, on_device(): call(functools.partial(pool_kernel, pairs), [shape(cotangent.shape, bf16)...  1.24 us
    pallas_call x1, Pallas kernels, on_device(): call(grad_kernel, [shape(cells.shape, f32), shape(tiles, f32)], cost=traf...  1.19 us
    pallas_call x1, Pallas kernels, on_device(): spread = call(spread_kernel, pooled_rows)(cotangent)  0.88 us
  transfers between devices with their start and end apart: 14, of which 5 were waited for; matrix products, arithmetic and copies ran while one was open for 3% of the time, Pallas kernels for 21%

profile of v15, /device:TPU:0, one launch (start us, length us, event | category | flops | bytes accessed | tf_op | source)
XLA Modules:
  0.0 36.5 jit_solution(8586849701995781413)
XLA Ops:
  0.6 0.9 %copy-done = bf16[4,4,64,128]{3,2,1,0:T(8,128)(2,1)S(1)} copy-done((bf16[4,4,64,128]{3,2,1,0:T(8,128)(2,1)S(1)}, bf16[4,4,64,128]{3,2,1,0:T(8,128)(2,1)}, u32[]{:S(2)}) %copy-start) | copy-done | bytes 262168
  1.8 3.0 %collective-permute-start = (bf16[32,128]{1,0:T(8,128)(2,1)S(1)}, bf16[32,128]{1,0:T(8,128)(2,1)S(1)}, u32[]{:S(2)}, u32[]{:S(2)}) collective-permute-start(bf16[32,128]{1,0:T(8,128)(2,1)S(1)} %get-tuple-element.39), channel_id=1, source_target_pairs={{0,1},{1,0},{2,3},{3,2},{4,5},{5,4},{6,7},{7,6},{8,9},{9,8},{10,11... | collective-permute-start | bytes 24584 | tf_op jit(solution)/shard_map/ppermute | solution.py:39
  5.5 0.6 %copy-done.3 = bf16[128,3,3,6,4]{0,4,3,2,1:T(4,128)(2,1)} copy-done((bf16[128,3,3,6,4]{0,4,3,2,1:T(4,128)(2,1)}, bf16[128,3,3,6,4]{0,4,3,2,1:T(4,128)(2,1)S(1)}, u32[]{:S(2)}) %copy-start.3) | copy-done | bytes 55320
  6.6 2.1 %collective-permute-start.2 = (bf16[272,128]{1,0:T(8,128)(2,1)S(1)}, bf16[272,128]{1,0:T(8,128)(2,1)S(1)}, u32[]{:S(2)}, u32[]{:S(2)}) collective-permute-start(bf16[272,128]{1,0:T(8,128)(2,1)S(1)} %get-tuple-element.41), channel_id=1, source_target_pairs={{0,24},{8,16},{16,8},{24,0},{1,25},{9,17},{17,9},{25,1},{2,26},{10... | collective-permute-start | bytes 208904 | tf_op jit(solution)/shard_map/ppermute | solution.py:39
  8.8 0.6 %slice-done = bf16[128,3,3,4,4]{0,4,3,2,1:T(4,128)(2,1)S(1)} async-done(((bf16[128,3,3,6,4]{0,4,3,2,1:T(4,128)(2,1)}), bf16[128,3,3,4,4]{0,4,3,2,1:T(4,128)(2,1)S(1)}, s32[]{:S(2)}) %slice-start) | async-done | bytes 36888 | tf_op jit(solution)/shard_map/slice | solution.py:617
  9.6 0.9 %shard_map.78.spread = f32[2048,128]{1,0:T(8,128)S(1)} custom-call(bf16[32,2,32,64]{3,2,1,0:T(8,128)(2,1)S(1)} %copy-done.2), custom_call_target="tpu_custom_call" | custom-call | tf_op jit(solution)/shard_map/pallas_call | solution.py:628
  10.5 0.4 %shard_map.77.inner = bf16[3168,128]{1,0:T(8,128)(2,1)S(1)} custom-call(bf16[4,4,64,128]{3,2,1,0:T(8,128)(2,1)S(1)} %copy-done.1, f32[16,128]{1,0:T(8,128)S(1)} %get-tuple-element.42.left, f32[16,128]{1,0:T(8,128)S(1)} %get-tuple-element.43.right), custom_call_target="tpu_custom_call" | custom-call | bytes 4194304 | tf_op jit(solution)/shard_map/pallas_call | solution.py:635
  11.1 3.7 %collective-permute-start.3 = (bf16[80,128]{1,0:T(8,128)(2,1)S(1)}, bf16[80,128]{1,0:T(8,128)(2,1)S(1)}, u32[]{:S(2)}, u32[]{:S(2)}) collective-permute-start(bf16[80,128]{1,0:T(8,128)(2,1)S(1)} %get-tuple-element.46), channel_id=1, source_target_pairs={{0,6},{2,4},{4,2},{6,0},{1,7},{3,5},{5,3},{7,1},{8,14},{10,12},{12... | collective-permute-start | bytes 61448 | tf_op jit(solution)/shard_map/ppermute | solution.py:39
  15.0 3.7 %shard_map.79 = (f32[2048,128]{1,0:T(8,128)S(1)}, f32[1584,128]{1,0:T(8,128)S(1)}, bf16[2112,128]{1,0:T(8,128)(2,1)S(1)}, f32[48,128]{1,0:T(8,128)S(1)}, f32[128,240]{1,0:T(8,128)S(1)}) custom-call(bf16[272,128]{1,0:T(8,128)(2,1)S(1)} %collective-permute-done.1.got_0, bf16[272,128]{1,0:T(8,128)(2,1)S(1)} %collective-permute-done.2.got_1, ...), custom_call_target="tpu_custom_call" | custom-call | bytes 16777216 | tf_op jit(solution)/shard_map/pallas_call | solution.py:654
  18.8 1.5 %shard_map.81 = (f32[2048,128]{1,0:T(8,128)S(1)}, f32[1584,128]{1,0:T(8,128)S(1)}, bf16[80,128]{1,0:T(8,128)(2,1)S(1)}, bf16[80,128]{1,0:T(8,128)(2,1)S(1)}, f32...) custom-call(bf16[80,128]{1,0:T(8,128)(2,1)S(1)} %collective-permute-done.3.row_, ...), custom_call_target="tpu_custom_call" | custom-call | tf_op jit(solution)/shard_map/pallas_call | solution.py:673
  20.3 1.2 %collective-permute-start.8 = (bf16[80,128]{1,0:T(8,128)(2,1)S(1)}, bf16[80,128]{1,0:T(8,128)(2,1)S(1)}, u32[]{:S(2)}, u32[]{:S(2)}) collective-permute-start(bf16[80,128]{1,0:T(8,128)(2,1)S(1)} %get-tuple-element.62), channel_id=1, source_target_pairs={{0,24},{8,16},{16,8},{24,0},{1,25},{9,17},{17,9},{25,1},{2,26},{10... | collective-permute-start | bytes 61448 | tf_op jit(solution)/shard_map/ppermute | solution.py:39
  21.5 0.5 %collective-permute-start.9 = (bf16[80,128]{1,0:T(8,128)(2,1)S(1)}, bf16[80,128]{1,0:T(8,128)(2,1)S(1)}, u32[]{:S(2)}, u32[]{:S(2)}) collective-permute-start(bf16[80,128]{1,0:T(8,128)(2,1)S(1)} %get-tuple-element.61), channel_id=1, source_target_pairs={{0,16},{8,24},{16,0},{24,8},{1,17},{9,25},{17,1},{25,9},{2,18},{10... | collective-permute-start | bytes 61448 | tf_op jit(solution)/shard_map/ppermute | solution.py:39
  22.3 0.4 %collective-permute-start.5 = (bf16[256,128]{1,0:T(8,128)(2,1)S(1)}, bf16[256,128]{1,0:T(8,128)(2,1)S(1)}, u32[]{:S(2)}, u32[]{:S(2)}) collective-permute-start(bf16[256,128]{1,0:T(8,128)(2,1)S(1)} %get-tuple-element.55), channel_id=1, source_target_pairs={{0,8},{8,0},{16,24},{24,16},{1,9},{9,1},{17,25},{25,17},{2,10},{10... | collective-permute-start | bytes 196616 | tf_op jit(solution)/shard_map/ppermute | solution.py:39
  22.7 1.3 %collective-permute-start.6 = (bf16[256,128]{1,0:T(8,128)(2,1)S(1)}, bf16[256,128]{1,0:T(8,128)(2,1)S(1)}, u32[]{:S(2)}, u32[]{:S(2)}) collective-permute-start(bf16[256,128]{1,0:T(8,128)(2,1)S(1)} %get-tuple-element.56), channel_id=1, source_target_pairs={{0,24},{8,16},{16,8},{24,0},{1,25},{9,17},{17,9},{25,1},{2,26},{10... | collective-permute-start | bytes 196616 | tf_op jit(solution)/shard_map/ppermute | solution.py:39
  24.0 1.3 %collective-permute-done.9.far = bf16[80,128]{1,0:T(8,128)(2,1)S(1)} collective-permute-done((bf16[80,128]{1,0:T(8,128)(2,1)S(1)}, bf16[80,128]{1,0:T(8,128)(2,1)S(1)}, u32[]{:S(2)}, u32[]{:S(2)}) %collective-permute-start.9) | collective-permute-done | bytes 20512 | tf_op jit(solution)/shard_map/ppermute | solution.py:39
  25.3 1.6 %collective-permute-start.10 = (bf16[96,128]{1,0:T(8,128)(2,1)S(1)}, bf16[96,128]{1,0:T(8,128)(2,1)S(1)}, u32[]{:S(2)}, u32[]{:S(2)}) collective-permute-start(bf16[96,128]{1,0:T(8,128)(2,1)S(1)} %get-tuple-element.63.mine), channel_id=1, source_target_pairs={{0,1},{1,0},{2,3},{3,2},{4,5},{5,4},{6,7},{7,6},{8,9},{9,8},{10,11... | collective-permute-start | bytes 73736 | tf_op jit(solution)/shard_map/ppermute | solution.py:39
  26.9 1.2 %shard_map.82 = (bf16[32,2,32,64]{3,2,1,0:T(8,128)(2,1)}, f32[8,128]{1,0:T(8,128)S(1)}) custom-call(f32[2048,128]{1,0:T(8,128)S(1)} %get-tuple-element.44.sums, f32[2048,128]{1,0:T(8,128)S(1)} %get-tuple-element.51.outer_sums), custom_call_target="tpu_custom_call" | custom-call | bytes 8388608 | tf_op jit(solution)/shard_map/pallas_call | solution.py:703
  28.1 1.1 %collective-permute-done.10.got = bf16[96,128]{1,0:T(8,128)(2,1)S(1)} collective-permute-done((bf16[96,128]{1,0:T(8,128)(2,1)S(1)}, bf16[96,128]{1,0:T(8,128)(2,1)S(1)}, u32[]{:S(2)}, u32[]{:S(2)}) %collective-permute-start.10) | collective-permute-done | bytes 24608 | tf_op jit(solution)/shard_map/ppermute | solution.py:39
  29.3 0.7 %collective-permute-start.11 = (bf16[80,128]{1,0:T(8,128)(2,1)S(1)}, bf16[80,128]{1,0:T(8,128)(2,1)S(1)}, u32[]{:S(2)}, u32[]{:S(2)}) collective-permute-start(bf16[80,128]{1,0:T(8,128)(2,1)S(1)} %get-tuple-element.69), channel_id=1, source_target_pairs={{0,6},{2,4},{4,2},{6,0},{1,7},{3,5},{5,3},{7,1},{8,14},{10,12},{12... | collective-permute-start | bytes 61448 | tf_op jit(solution)/shard_map/ppermute | solution.py:39
  30.0 1.1 %collective-permute-start.13 = (bf16[80,128]{1,0:T(8,128)(2,1)S(1)}, bf16[80,128]{1,0:T(8,128)(2,1)S(1)}, u32[]{:S(2)}, u32[]{:S(2)}) collective-permute-start(bf16[80,128]{1,0:T(8,128)(2,1)S(1)} %get-tuple-element.70), channel_id=1, source_target_pairs={{0,2},{2,0},{4,6},{6,4},{1,3},{3,1},{5,7},{7,5},{8,10},{10,8},{12,... | collective-permute-start | bytes 61448 | tf_op jit(solution)/shard_map/ppermute | solution.py:39
  31.1 2.6 %collective-permute-start.12 = (bf16[64,128]{1,0:T(8,128)(2,1)S(1)}, bf16[64,128]{1,0:T(8,128)(2,1)S(1)}, u32[]{:S(2)}, u32[]{:S(2)}) collective-permute-start(bf16[64,128]{1,0:T(8,128)(2,1)S(1)} %get-tuple-element.68.mine), channel_id=1, source_target_pairs={{0,4},{2,6},{4,0},{6,2},{1,5},{3,7},{5,1},{7,3},{8,12},{10,14},{12... | collective-permute-start | bytes 49160 | tf_op jit(solution)/shard_map/ppermute | solution.py:39
  33.7 1.2 %shard_map.85 = (f32[4,4,64,128]{3,2,1,0:T(8,128)}, f32[2,4,4,8,128]{4,3,2,1,0:T(8,128)S(1)}) custom-call(f32[1584,128]{1,0:T(8,128)S(1)} %get-tuple-element.53.field, f32[1584,128]{1,0:T(8,128)S(1)} %get-tuple-element.54.outer_field, bf16[256,128]{1,0:T(8,128)(2,1)S(1)} %collective-permute-done.5.face_0, ...), custom_call_target="tpu_custom_call" | custom-call | bytes 8388608 | tf_op jit(solution)/shard_map/pallas_call | solution.py:722
  34.9 0.9 %collective-permute-done.12.far = bf16[64,128]{1,0:T(8,128)(2,1)S(1)} collective-permute-done((bf16[64,128]{1,0:T(8,128)(2,1)S(1)}, bf16[64,128]{1,0:T(8,128)(2,1)S(1)}, u32[]{:S(2)}, u32[]{:S(2)}) %collective-permute-start.12) | collective-permute-done | bytes 16416 | tf_op jit(solution)/shard_map/ppermute | solution.py:39
  35.8 0.8 %shard_map.87 = (f32[4,4,64,128]{3,2,1,0:T(8,128)}, f32[27,4,32]{2,1,0:T(4,128)}, f32[1,32]{1,0:T(1,128)}) custom-call(f32[4,4,64,128]{3,2,1,0:T(8,128)} %get-tuple-element.64.whole, f32[2,4,4,8,128]{4,3,2,1,0:T(8,128)S(1)} %get-tuple-element.65.ends, bf16[64,128]{1,0:T(8,128)(2,1)S(1)} %get-tuple-element.68.mine, ...), custom_call_target="tpu_custom_call", output_to_operand_aliasing={{0}: (0, {})} | custom-call | tf_op jit(solution)/shard_map/pallas_call | solution.py:725
  (46 shorter events, 2.4 us)
Async XLA Ops:
  0.6 1.0 %copy-start = (bf16[4,4,64,128]{3,2,1,0:T(8,128)(2,1)S(1)}, bf16[4,4,64,128]{3,2,1,0:T(8,128)(2,1)}, u32[]{:S(2)}) copy-start(bf16[4,4,64,128]{3,2,1,0:T(8,128)(2,1)} %cells.5) | copy-start | bytes 786436
  1.6 3.3 %copy-start.4 = (bf16[32,4,3,3,3]{0,1,4,3,2:T(4,128)(2,1)S(1)}, bf16[32,4,3,3,3]{0,1,4,3,2:T(4,128)(2,1)}, u32[]{:S(2)}) copy-start(bf16[32,4,3,3,3]{0,1,4,3,2:T(4,128)(2,1)} %param.5) | copy-start | bytes 20740
  1.8 3.0 %copy-start.5 = (f32[32]{0:T(128)S(1)}, f32[32]{0:T(128)}, u32[]{:S(2)}) copy-start(f32[32]{0:T(128)} %param.6) | copy-start | bytes 388
  1.8 4.6 %collective-permute-start = (bf16[32,128]{1,0:T(8,128)(2,1)S(1)}, bf16[32,128]{1,0:T(8,128)(2,1)S(1)}, u32[]{:S(2)}, u32[]{:S(2)}) collective-permute-start(bf16[32,128]{1,0:T(8,128)(2,1)S(1)} %get-tuple-element.39), channel_id=1, source_target_pairs={{0,1},{1,0},{2,3},{3,2},{4,5},{5,4},{6,7},{7,6},{8,9},{9,8},{10,11... | collective-permute-start | bytes 24584 | tf_op jit(solution)/shard_map/ppermute | solution.py:39
  5.2 1.2 %copy-start.1 = (bf16[4,4,64,128]{3,2,1,0:T(8,128)(2,1)S(1)}, bf16[4,4,64,128]{3,2,1,0:T(8,128)(2,1)}, u32[]{:S(2)}) copy-start(bf16[4,4,64,128]{3,2,1,0:T(8,128)(2,1)} %cells.5) | copy-start | bytes 786436
  5.3 4.3 %copy-start.2 = (bf16[32,2,32,64]{3,2,1,0:T(8,128)(2,1)S(1)}, bf16[32,2,32,64]{3,2,1,0:T(8,128)(2,1)}, u32[]{:S(2)}) copy-start(bf16[32,2,32,64]{3,2,1,0:T(8,128)(2,1)} %cot.1) | copy-start | bytes 786436
  5.4 0.6 %copy-start.3 = (bf16[128,3,3,6,4]{0,4,3,2,1:T(4,128)(2,1)}, bf16[128,3,3,6,4]{0,4,3,2,1:T(4,128)(2,1)S(1)}, u32[]{:S(2)}) copy-start(bf16[128,3,3,6,4]{0,4,3,2,1:T(4,128)(2,1)S(1)} %reshape.59) | copy-start | bytes 165892
  6.5 4.4 %collective-permute-start.1 = (bf16[272,128]{1,0:T(8,128)(2,1)S(1)}, bf16[272,128]{1,0:T(8,128)(2,1)S(1)}, u32[]{:S(2)}, u32[]{:S(2)}) collective-permute-start(bf16[272,128]{1,0:T(8,128)(2,1)S(1)} %get-tuple-element.40), channel_id=1, source_target_pairs={{0,8},{8,0},{16,24},{24,16},{1,9},{9,1},{17,25},{25,17},{2,10},{10... | collective-permute-start | bytes 208904 | tf_op jit(solution)/shard_map/ppermute | solution.py:39
  6.6 4.5 %collective-permute-start.2 = (bf16[272,128]{1,0:T(8,128)(2,1)S(1)}, bf16[272,128]{1,0:T(8,128)(2,1)S(1)}, u32[]{:S(2)}, u32[]{:S(2)}) collective-permute-start(bf16[272,128]{1,0:T(8,128)(2,1)S(1)} %get-tuple-element.41), channel_id=1, source_target_pairs={{0,24},{8,16},{16,8},{24,0},{1,25},{9,17},{17,9},{25,1},{2,26},{10... | collective-permute-start | bytes 208904 | tf_op jit(solution)/shard_map/ppermute | solution.py:39
  8.7 0.8 %slice-start = ((bf16[128,3,3,6,4]{0,4,3,2,1:T(4,128)(2,1)}), bf16[128,3,3,4,4]{0,4,3,2,1:T(4,128)(2,1)S(1)}, s32[]{:S(2)}) async-start(bf16[128,3,3,6,4]{0,4,3,2,1:T(4,128)(2,1)} %copy-done.3), calls=%async_computation | async-start | bytes 73728 | tf_op jit(solution)/shard_map/slice | solution.py:617
  11.1 7.7 %collective-permute-start.3 = (bf16[80,128]{1,0:T(8,128)(2,1)S(1)}, bf16[80,128]{1,0:T(8,128)(2,1)S(1)}, u32[]{:S(2)}, u32[]{:S(2)}) collective-permute-start(bf16[80,128]{1,0:T(8,128)(2,1)S(1)} %get-tuple-element.46), channel_id=1, source_target_pairs={{0,6},{2,4},{4,2},{6,0},{1,7},{3,5},{5,3},{7,1},{8,14},{10,12},{12... | collective-permute-start | bytes 61448 | tf_op jit(solution)/shard_map/ppermute | solution.py:39
  14.8 4.0 %collective-permute-start.4 = (bf16[80,128]{1,0:T(8,128)(2,1)S(1)}, bf16[80,128]{1,0:T(8,128)(2,1)S(1)}, u32[]{:S(2)}, u32[]{:S(2)}) collective-permute-start(bf16[80,128]{1,0:T(8,128)(2,1)S(1)} %get-tuple-element.47), channel_id=1, source_target_pairs={{0,2},{2,0},{4,6},{6,4},{1,3},{3,1},{5,7},{7,5},{8,10},{10,8},{12,... | collective-permute-start | bytes 61448 | tf_op jit(solution)/shard_map/ppermute | solution.py:39
  20.3 3.7 %collective-permute-start.8 = (bf16[80,128]{1,0:T(8,128)(2,1)S(1)}, bf16[80,128]{1,0:T(8,128)(2,1)S(1)}, u32[]{:S(2)}, u32[]{:S(2)}) collective-permute-start(bf16[80,128]{1,0:T(8,128)(2,1)S(1)} %get-tuple-element.62), channel_id=1, source_target_pairs={{0,24},{8,16},{16,8},{24,0},{1,25},{9,17},{17,9},{25,1},{2,26},{10... | collective-permute-start | bytes 61448 | tf_op jit(solution)/shard_map/ppermute | solution.py:39
  21.5 3.8 %collective-permute-start.9 = (bf16[80,128]{1,0:T(8,128)(2,1)S(1)}, bf16[80,128]{1,0:T(8,128)(2,1)S(1)}, u32[]{:S(2)}, u32[]{:S(2)}) collective-permute-start(bf16[80,128]{1,0:T(8,128)(2,1)S(1)} %get-tuple-element.61), channel_id=1, source_target_pairs={{0,16},{8,24},{16,0},{24,8},{1,17},{9,25},{17,1},{25,9},{2,18},{10... | collective-permute-start | bytes 61448 | tf_op jit(solution)/shard_map/ppermute | solution.py:39
  22.0 3.2 %collective-permute-start.7 = (bf16[80,128]{1,0:T(8,128)(2,1)S(1)}, bf16[80,128]{1,0:T(8,128)(2,1)S(1)}, u32[]{:S(2)}, u32[]{:S(2)}) collective-permute-start(bf16[80,128]{1,0:T(8,128)(2,1)S(1)} %get-tuple-element.61), channel_id=1, source_target_pairs={{0,8},{8,0},{16,24},{24,16},{1,9},{9,1},{17,25},{25,17},{2,10},{10... | collective-permute-start | bytes 61448 | tf_op jit(solution)/shard_map/ppermute | solution.py:39
  22.3 11.4 %collective-permute-start.5 = (bf16[256,128]{1,0:T(8,128)(2,1)S(1)}, bf16[256,128]{1,0:T(8,128)(2,1)S(1)}, u32[]{:S(2)}, u32[]{:S(2)}) collective-permute-start(bf16[256,128]{1,0:T(8,128)(2,1)S(1)} %get-tuple-element.55), channel_id=1, source_target_pairs={{0,8},{8,0},{16,24},{24,16},{1,9},{9,1},{17,25},{25,17},{2,10},{10... | collective-permute-start | bytes 196616 | tf_op jit(solution)/shard_map/ppermute | solution.py:39
  22.7 11.0 %collective-permute-start.6 = (bf16[256,128]{1,0:T(8,128)(2,1)S(1)}, bf16[256,128]{1,0:T(8,128)(2,1)S(1)}, u32[]{:S(2)}, u32[]{:S(2)}) collective-permute-start(bf16[256,128]{1,0:T(8,128)(2,1)S(1)} %get-tuple-element.56), channel_id=1, source_target_pairs={{0,24},{8,16},{16,8},{24,0},{1,25},{9,17},{17,9},{25,1},{2,26},{10... | collective-permute-start | bytes 196616 | tf_op jit(solution)/shard_map/ppermute | solution.py:39
  25.3 3.9 %collective-permute-start.10 = (bf16[96,128]{1,0:T(8,128)(2,1)S(1)}, bf16[96,128]{1,0:T(8,128)(2,1)S(1)}, u32[]{:S(2)}, u32[]{:S(2)}) collective-permute-start(bf16[96,128]{1,0:T(8,128)(2,1)S(1)} %get-tuple-element.63.mine), channel_id=1, source_target_pairs={{0,1},{1,0},{2,3},{3,2},{4,5},{5,4},{6,7},{7,6},{8,9},{9,8},{10,11... | collective-permute-start | bytes 73736 | tf_op jit(solution)/shard_map/ppermute | solution.py:39
  29.3 6.5 %collective-permute-start.11 = (bf16[80,128]{1,0:T(8,128)(2,1)S(1)}, bf16[80,128]{1,0:T(8,128)(2,1)S(1)}, u32[]{:S(2)}, u32[]{:S(2)}) collective-permute-start(bf16[80,128]{1,0:T(8,128)(2,1)S(1)} %get-tuple-element.69), channel_id=1, source_target_pairs={{0,6},{2,4},{4,2},{6,0},{1,7},{3,5},{5,3},{7,1},{8,14},{10,12},{12... | collective-permute-start | bytes 61448 | tf_op jit(solution)/shard_map/ppermute | solution.py:39
  30.0 5.7 %collective-permute-start.13 = (bf16[80,128]{1,0:T(8,128)(2,1)S(1)}, bf16[80,128]{1,0:T(8,128)(2,1)S(1)}, u32[]{:S(2)}, u32[]{:S(2)}) collective-permute-start(bf16[80,128]{1,0:T(8,128)(2,1)S(1)} %get-tuple-element.70), channel_id=1, source_target_pairs={{0,2},{2,0},{4,6},{6,4},{1,3},{3,1},{5,7},{7,5},{8,10},{10,8},{12,... | collective-permute-start | bytes 61448 | tf_op jit(solution)/shard_map/ppermute | solution.py:39
  31.1 4.6 %collective-permute-start.12 = (bf16[64,128]{1,0:T(8,128)(2,1)S(1)}, bf16[64,128]{1,0:T(8,128)(2,1)S(1)}, u32[]{:S(2)}, u32[]{:S(2)}) collective-permute-start(bf16[64,128]{1,0:T(8,128)(2,1)S(1)} %get-tuple-element.68.mine), channel_id=1, source_target_pairs={{0,4},{2,6},{4,0},{6,2},{1,5},{3,7},{5,1},{7,3},{8,12},{10,14},{12... | collective-permute-start | bytes 49160 | tf_op jit(solution)/shard_map/ppermute | solution.py:39

commit v16 on v15

--- a/solution.py
+++ b/solution.py
@@ -102,7 +102,7 @@
     return pick("gx", two, one), pick("gx", one, two)
 
 
-def rows_kernel(chan, rows, left, right, got_0, got_1, inner, spread, sent_0, sent_1):
+def rows_kernel(chan, got_1, got_0, rows, left, right, inner, spread, sent_0, sent_1):
     own = rows.shape[0] // 2
     body = got_0.shape[0] - 16
     count_y = body // chan
@@ -644,7 +644,7 @@
         functools.partial(rows_kernel, chan),
         [bundle, bundle],
         in_specs=[vmem] * 5 + [anywhere] * 2,
-    )(rows, left, right, face_0, face_1, inner, spread)
+    )(face_1, face_0, rows, left, right, inner, spread)
     row_1, row_0 = swapped(row_1, "gy", 1), swapped(row_0, "gy", 0)
 
     tall = 2 * wide

time: 36.8 us -> 36.8 us (level)
  no operation moved by 1% of the time
where the time goes in v16:
time: 36.8 us; the launch traced here: 36.5 us
  starting transfers between devices  18.5 us (50%)
  Pallas kernels  10.2 us (28%)
  waiting for transfers between devices  3.79 us (10%)
  local copies, waits for them, and re-layouts  2.95 us (8%)
  between operations  0.84 us (2%)
    ppermute x14, starting transfers between devices, swapped(): return lax.ppermute(array, axis, pairs)  18.5 us
    ppermute x14, waiting for transfers between devices, swapped(): return lax.ppermute(array, axis, pairs)  3.79 us
    pallas_call x1, Pallas kernels, on_device(): call(functools.partial(inner_kernel, count_x), [pooled_rows, all_field, s...  3.7 us
    unnamed x12, local copies, waits for them, and re-layouts  1.52 us
    pallas_call x1, Pallas kernels, on_device(): call(functools.partial(main_kernel, count_x), [pooled_rows, all_field, bu...  1.5 us
    pallas_call x1, Pallas kernels, on_device(): call(functools.partial(pool_kernel, pairs), [shape(cotangent.shape, bf16)...  1.24 us
    pallas_call x1, Pallas kernels, on_device(): call(grad_kernel, [shape(cells.shape, f32), shape(tiles, f32)], cost=traf...  1.19 us
    pallas_call x1, Pallas kernels, on_device(): spread = call(spread_kernel, pooled_rows)(cotangent)  0.88 us
  transfers between devices with their start and end apart: 14, of which 5 were waited for; matrix products, arithmetic and copies ran while one was open for 3% of the time, Pallas kernels for 21%

profile of v16, /device:TPU:0, one launch (start us, length us, event | category | flops | bytes accessed | tf_op | source)
XLA Modules:
  0.0 36.5 jit_solution(16369092918096651675)
XLA Ops:
  0.6 0.9 %copy-done = bf16[4,4,64,128]{3,2,1,0:T(8,128)(2,1)S(1)} copy-done((bf16[4,4,64,128]{3,2,1,0:T(8,128)(2,1)S(1)}, bf16[4,4,64,128]{3,2,1,0:T(8,128)(2,1)}, u32[]{:S(2)}) %copy-start) | copy-done | bytes 262168
  1.8 3.0 %collective-permute-start = (bf16[32,128]{1,0:T(8,128)(2,1)S(1)}, bf16[32,128]{1,0:T(8,128)(2,1)S(1)}, u32[]{:S(2)}, u32[]{:S(2)}) collective-permute-start(bf16[32,128]{1,0:T(8,128)(2,1)S(1)} %get-tuple-element.39), channel_id=1, source_target_pairs={{0,1},{1,0},{2,3},{3,2},{4,5},{5,4},{6,7},{7,6},{8,9},{9,8},{10,11... | collective-permute-start | bytes 24584 | tf_op jit(solution)/shard_map/ppermute | solution.py:39
  5.5 0.6 %copy-done.3 = bf16[128,3,3,6,4]{0,4,3,2,1:T(4,128)(2,1)} copy-done((bf16[128,3,3,6,4]{0,4,3,2,1:T(4,128)(2,1)}, bf16[128,3,3,6,4]{0,4,3,2,1:T(4,128)(2,1)S(1)}, u32[]{:S(2)}) %copy-start.3) | copy-done | bytes 55320
  6.6 2.1 %collective-permute-start.2 = (bf16[272,128]{1,0:T(8,128)(2,1)S(1)}, bf16[272,128]{1,0:T(8,128)(2,1)S(1)}, u32[]{:S(2)}, u32[]{:S(2)}) collective-permute-start(bf16[272,128]{1,0:T(8,128)(2,1)S(1)} %get-tuple-element.41), channel_id=1, source_target_pairs={{0,24},{8,16},{16,8},{24,0},{1,25},{9,17},{17,9},{25,1},{2,26},{10... | collective-permute-start | bytes 208904 | tf_op jit(solution)/shard_map/ppermute | solution.py:39
  8.8 0.6 %slice-done = bf16[128,3,3,4,4]{0,4,3,2,1:T(4,128)(2,1)S(1)} async-done(((bf16[128,3,3,6,4]{0,4,3,2,1:T(4,128)(2,1)}), bf16[128,3,3,4,4]{0,4,3,2,1:T(4,128)(2,1)S(1)}, s32[]{:S(2)}) %slice-start) | async-done | bytes 36888 | tf_op jit(solution)/shard_map/slice | solution.py:617
  9.6 0.9 %shard_map.78.spread = f32[2048,128]{1,0:T(8,128)S(1)} custom-call(bf16[32,2,32,64]{3,2,1,0:T(8,128)(2,1)S(1)} %copy-done.2), custom_call_target="tpu_custom_call" | custom-call | tf_op jit(solution)/shard_map/pallas_call | solution.py:628
  10.5 0.4 %shard_map.77.inner = bf16[3168,128]{1,0:T(8,128)(2,1)S(1)} custom-call(bf16[4,4,64,128]{3,2,1,0:T(8,128)(2,1)S(1)} %copy-done.1, f32[16,128]{1,0:T(8,128)S(1)} %get-tuple-element.42.left, f32[16,128]{1,0:T(8,128)S(1)} %get-tuple-element.43.right), custom_call_target="tpu_custom_call" | custom-call | bytes 4194304 | tf_op jit(solution)/shard_map/pallas_call | solution.py:635
  11.1 3.7 %collective-permute-start.3 = (bf16[80,128]{1,0:T(8,128)(2,1)S(1)}, bf16[80,128]{1,0:T(8,128)(2,1)S(1)}, u32[]{:S(2)}, u32[]{:S(2)}) collective-permute-start(bf16[80,128]{1,0:T(8,128)(2,1)S(1)} %get-tuple-element.46), channel_id=1, source_target_pairs={{0,6},{2,4},{4,2},{6,0},{1,7},{3,5},{5,3},{7,1},{8,14},{10,12},{12... | collective-permute-start | bytes 61448 | tf_op jit(solution)/shard_map/ppermute | solution.py:39
  15.0 3.7 %shard_map.79 = (f32[2048,128]{1,0:T(8,128)S(1)}, f32[1584,128]{1,0:T(8,128)S(1)}, bf16[2112,128]{1,0:T(8,128)(2,1)S(1)}, f32[48,128]{1,0:T(8,128)S(1)}, f32[128,240]{1,0:T(8,128)S(1)}) custom-call(bf16[272,128]{1,0:T(8,128)(2,1)S(1)} %collective-permute-done.1.got_0, bf16[272,128]{1,0:T(8,128)(2,1)S(1)} %collective-permute-done.2.got_1, ...), custom_call_target="tpu_custom_call" | custom-call | bytes 16777216 | tf_op jit(solution)/shard_map/pallas_call | solution.py:654
  18.8 1.5 %shard_map.81 = (f32[2048,128]{1,0:T(8,128)S(1)}, f32[1584,128]{1,0:T(8,128)S(1)}, bf16[80,128]{1,0:T(8,128)(2,1)S(1)}, bf16[80,128]{1,0:T(8,128)(2,1)S(1)}, f32...) custom-call(bf16[80,128]{1,0:T(8,128)(2,1)S(1)} %collective-permute-done.3.row_, ...), custom_call_target="tpu_custom_call" | custom-call | tf_op jit(solution)/shard_map/pallas_call | solution.py:673
  20.3 1.2 %collective-permute-start.8 = (bf16[80,128]{1,0:T(8,128)(2,1)S(1)}, bf16[80,128]{1,0:T(8,128)(2,1)S(1)}, u32[]{:S(2)}, u32[]{:S(2)}) collective-permute-start(bf16[80,128]{1,0:T(8,128)(2,1)S(1)} %get-tuple-element.62), channel_id=1, source_target_pairs={{0,24},{8,16},{16,8},{24,0},{1,25},{9,17},{17,9},{25,1},{2,26},{10... | collective-permute-start | bytes 61448 | tf_op jit(solution)/shard_map/ppermute | solution.py:39
  21.5 0.5 %collective-permute-start.9 = (bf16[80,128]{1,0:T(8,128)(2,1)S(1)}, bf16[80,128]{1,0:T(8,128)(2,1)S(1)}, u32[]{:S(2)}, u32[]{:S(2)}) collective-permute-start(bf16[80,128]{1,0:T(8,128)(2,1)S(1)} %get-tuple-element.61), channel_id=1, source_target_pairs={{0,16},{8,24},{16,0},{24,8},{1,17},{9,25},{17,1},{25,9},{2,18},{10... | collective-permute-start | bytes 61448 | tf_op jit(solution)/shard_map/ppermute | solution.py:39
  22.3 0.4 %collective-permute-start.5 = (bf16[256,128]{1,0:T(8,128)(2,1)S(1)}, bf16[256,128]{1,0:T(8,128)(2,1)S(1)}, u32[]{:S(2)}, u32[]{:S(2)}) collective-permute-start(bf16[256,128]{1,0:T(8,128)(2,1)S(1)} %get-tuple-element.55), channel_id=1, source_target_pairs={{0,8},{8,0},{16,24},{24,16},{1,9},{9,1},{17,25},{25,17},{2,10},{10... | collective-permute-start | bytes 196616 | tf_op jit(solution)/shard_map/ppermute | solution.py:39
  22.7 1.3 %collective-permute-start.6 = (bf16[256,128]{1,0:T(8,128)(2,1)S(1)}, bf16[256,128]{1,0:T(8,128)(2,1)S(1)}, u32[]{:S(2)}, u32[]{:S(2)}) collective-permute-start(bf16[256,128]{1,0:T(8,128)(2,1)S(1)} %get-tuple-element.56), channel_id=1, source_target_pairs={{0,24},{8,16},{16,8},{24,0},{1,25},{9,17},{17,9},{25,1},{2,26},{10... | collective-permute-start | bytes 196616 | tf_op jit(solution)/shard_map/ppermute | solution.py:39
  24.0 1.3 %collective-permute-done.9.far = bf16[80,128]{1,0:T(8,128)(2,1)S(1)} collective-permute-done((bf16[80,128]{1,0:T(8,128)(2,1)S(1)}, bf16[80,128]{1,0:T(8,128)(2,1)S(1)}, u32[]{:S(2)}, u32[]{:S(2)}) %collective-permute-start.9) | collective-permute-done | bytes 20512 | tf_op jit(solution)/shard_map/ppermute | solution.py:39
  25.3 1.6 %collective-permute-start.10 = (bf16[96,128]{1,0:T(8,128)(2,1)S(1)}, bf16[96,128]{1,0:T(8,128)(2,1)S(1)}, u32[]{:S(2)}, u32[]{:S(2)}) collective-permute-start(bf16[96,128]{1,0:T(8,128)(2,1)S(1)} %get-tuple-element.63.mine), channel_id=1, source_target_pairs={{0,1},{1,0},{2,3},{3,2},{4,5},{5,4},{6,7},{7,6},{8,9},{9,8},{10,11... | collective-permute-start | bytes 73736 | tf_op jit(solution)/shard_map/ppermute | solution.py:39
  26.9 1.2 %shard_map.82 = (bf16[32,2,32,64]{3,2,1,0:T(8,128)(2,1)}, f32[8,128]{1,0:T(8,128)S(1)}) custom-call(f32[2048,128]{1,0:T(8,128)S(1)} %get-tuple-element.44.sums, f32[2048,128]{1,0:T(8,128)S(1)} %get-tuple-element.51.outer_sums), custom_call_target="tpu_custom_call" | custom-call | bytes 8388608 | tf_op jit(solution)/shard_map/pallas_call | solution.py:703
  28.1 1.1 %collective-permute-done.10.got = bf16[96,128]{1,0:T(8,128)(2,1)S(1)} collective-permute-done((bf16[96,128]{1,0:T(8,128)(2,1)S(1)}, bf16[96,128]{1,0:T(8,128)(2,1)S(1)}, u32[]{:S(2)}, u32[]{:S(2)}) %collective-permute-start.10) | collective-permute-done | bytes 24608 | tf_op jit(solution)/shard_map/ppermute | solution.py:39
  29.3 0.7 %collective-permute-start.11 = (bf16[80,128]{1,0:T(8,128)(2,1)S(1)}, bf16[80,128]{1,0:T(8,128)(2,1)S(1)}, u32[]{:S(2)}, u32[]{:S(2)}) collective-permute-start(bf16[80,128]{1,0:T(8,128)(2,1)S(1)} %get-tuple-element.69), channel_id=1, source_target_pairs={{0,6},{2,4},{4,2},{6,0},{1,7},{3,5},{5,3},{7,1},{8,14},{10,12},{12... | collective-permute-start | bytes 61448 | tf_op jit(solution)/shard_map/ppermute | solution.py:39
  30.0 1.1 %collective-permute-start.13 = (bf16[80,128]{1,0:T(8,128)(2,1)S(1)}, bf16[80,128]{1,0:T(8,128)(2,1)S(1)}, u32[]{:S(2)}, u32[]{:S(2)}) collective-permute-start(bf16[80,128]{1,0:T(8,128)(2,1)S(1)} %get-tuple-element.70), channel_id=1, source_target_pairs={{0,2},{2,0},{4,6},{6,4},{1,3},{3,1},{5,7},{7,5},{8,10},{10,8},{12,... | collective-permute-start | bytes 61448 | tf_op jit(solution)/shard_map/ppermute | solution.py:39
  31.1 2.6 %collective-permute-start.12 = (bf16[64,128]{1,0:T(8,128)(2,1)S(1)}, bf16[64,128]{1,0:T(8,128)(2,1)S(1)}, u32[]{:S(2)}, u32[]{:S(2)}) collective-permute-start(bf16[64,128]{1,0:T(8,128)(2,1)S(1)} %get-tuple-element.68.mine), channel_id=1, source_target_pairs={{0,4},{2,6},{4,0},{6,2},{1,5},{3,7},{5,1},{7,3},{8,12},{10,14},{12... | collective-permute-start | bytes 49160 | tf_op jit(solution)/shard_map/ppermute | solution.py:39
  33.7 1.2 %shard_map.85 = (f32[4,4,64,128]{3,2,1,0:T(8,128)}, f32[2,4,4,8,128]{4,3,2,1,0:T(8,128)S(1)}) custom-call(f32[1584,128]{1,0:T(8,128)S(1)} %get-tuple-element.53.field, f32[1584,128]{1,0:T(8,128)S(1)} %get-tuple-element.54.outer_field, bf16[256,128]{1,0:T(8,128)(2,1)S(1)} %collective-permute-done.5.face_0, ...), custom_call_target="tpu_custom_call" | custom-call | bytes 8388608 | tf_op jit(solution)/shard_map/pallas_call | solution.py:722
  34.9 0.9 %collective-permute-done.12.far = bf16[64,128]{1,0:T(8,128)(2,1)S(1)} collective-permute-done((bf16[64,128]{1,0:T(8,128)(2,1)S(1)}, bf16[64,128]{1,0:T(8,128)(2,1)S(1)}, u32[]{:S(2)}, u32[]{:S(2)}) %collective-permute-start.12) | collective-permute-done | bytes 16416 | tf_op jit(solution)/shard_map/ppermute | solution.py:39
  35.8 0.8 %shard_map.87 = (f32[4,4,64,128]{3,2,1,0:T(8,128)}, f32[27,4,32]{2,1,0:T(4,128)}, f32[1,32]{1,0:T(1,128)}) custom-call(f32[4,4,64,128]{3,2,1,0:T(8,128)} %get-tuple-element.64.whole, f32[2,4,4,8,128]{4,3,2,1,0:T(8,128)S(1)} %get-tuple-element.65.ends, bf16[64,128]{1,0:T(8,128)(2,1)S(1)} %get-tuple-element.68.mine, ...), custom_call_target="tpu_custom_call", output_to_operand_aliasing={{0}: (0, {})} | custom-call | tf_op jit(solution)/shard_map/pallas_call | solution.py:725
  (46 shorter events, 2.4 us)
Async XLA Ops:
  0.6 1.0 %copy-start = (bf16[4,4,64,128]{3,2,1,0:T(8,128)(2,1)S(1)}, bf16[4,4,64,128]{3,2,1,0:T(8,128)(2,1)}, u32[]{:S(2)}) copy-start(bf16[4,4,64,128]{3,2,1,0:T(8,128)(2,1)} %cells.5) | copy-start | bytes 786436
  1.6 3.3 %copy-start.4 = (bf16[32,4,3,3,3]{0,1,4,3,2:T(4,128)(2,1)S(1)}, bf16[32,4,3,3,3]{0,1,4,3,2:T(4,128)(2,1)}, u32[]{:S(2)}) copy-start(bf16[32,4,3,3,3]{0,1,4,3,2:T(4,128)(2,1)} %param.5) | copy-start | bytes 20740
  1.8 3.0 %copy-start.5 = (f32[32]{0:T(128)S(1)}, f32[32]{0:T(128)}, u32[]{:S(2)}) copy-start(f32[32]{0:T(128)} %param.6) | copy-start | bytes 388
  1.8 4.6 %collective-permute-start = (bf16[32,128]{1,0:T(8,128)(2,1)S(1)}, bf16[32,128]{1,0:T(8,128)(2,1)S(1)}, u32[]{:S(2)}, u32[]{:S(2)}) collective-permute-start(bf16[32,128]{1,0:T(8,128)(2,1)S(1)} %get-tuple-element.39), channel_id=1, source_target_pairs={{0,1},{1,0},{2,3},{3,2},{4,5},{5,4},{6,7},{7,6},{8,9},{9,8},{10,11... | collective-permute-start | bytes 24584 | tf_op jit(solution)/shard_map/ppermute | solution.py:39
  5.2 1.2 %copy-start.1 = (bf16[4,4,64,128]{3,2,1,0:T(8,128)(2,1)S(1)}, bf16[4,4,64,128]{3,2,1,0:T(8,128)(2,1)}, u32[]{:S(2)}) copy-start(bf16[4,4,64,128]{3,2,1,0:T(8,128)(2,1)} %cells.5) | copy-start | bytes 786436
  5.3 4.3 %copy-start.2 = (bf16[32,2,32,64]{3,2,1,0:T(8,128)(2,1)S(1)}, bf16[32,2,32,64]{3,2,1,0:T(8,128)(2,1)}, u32[]{:S(2)}) copy-start(bf16[32,2,32,64]{3,2,1,0:T(8,128)(2,1)} %cot.1) | copy-start | bytes 786436
  5.4 0.6 %copy-start.3 = (bf16[128,3,3,6,4]{0,4,3,2,1:T(4,128)(2,1)}, bf16[128,3,3,6,4]{0,4,3,2,1:T(4,128)(2,1)S(1)}, u32[]{:S(2)}) copy-start(bf16[128,3,3,6,4]{0,4,3,2,1:T(4,128)(2,1)S(1)} %reshape.59) | copy-start | bytes 165892
  6.5 4.4 %collective-permute-start.1 = (bf16[272,128]{1,0:T(8,128)(2,1)S(1)}, bf16[272,128]{1,0:T(8,128)(2,1)S(1)}, u32[]{:S(2)}, u32[]{:S(2)}) collective-permute-start(bf16[272,128]{1,0:T(8,128)(2,1)S(1)} %get-tuple-element.40), channel_id=1, source_target_pairs={{0,8},{8,0},{16,24},{24,16},{1,9},{9,1},{17,25},{25,17},{2,10},{10... | collective-permute-start | bytes 208904 | tf_op jit(solution)/shard_map/ppermute | solution.py:39
  6.6 4.5 %collective-permute-start.2 = (bf16[272,128]{1,0:T(8,128)(2,1)S(1)}, bf16[272,128]{1,0:T(8,128)(2,1)S(1)}, u32[]{:S(2)}, u32[]{:S(2)}) collective-permute-start(bf16[272,128]{1,0:T(8,128)(2,1)S(1)} %get-tuple-element.41), channel_id=1, source_target_pairs={{0,24},{8,16},{16,8},{24,0},{1,25},{9,17},{17,9},{25,1},{2,26},{10... | collective-permute-start | bytes 208904 | tf_op jit(solution)/shard_map/ppermute | solution.py:39
  8.7 0.8 %slice-start = ((bf16[128,3,3,6,4]{0,4,3,2,1:T(4,128)(2,1)}), bf16[128,3,3,4,4]{0,4,3,2,1:T(4,128)(2,1)S(1)}, s32[]{:S(2)}) async-start(bf16[128,3,3,6,4]{0,4,3,2,1:T(4,128)(2,1)} %copy-done.3), calls=%async_computation | async-start | bytes 73728 | tf_op jit(solution)/shard_map/slice | solution.py:617
  11.1 7.7 %collective-permute-start.3 = (bf16[80,128]{1,0:T(8,128)(2,1)S(1)}, bf16[80,128]{1,0:T(8,128)(2,1)S(1)}, u32[]{:S(2)}, u32[]{:S(2)}) collective-permute-start(bf16[80,128]{1,0:T(8,128)(2,1)S(1)} %get-tuple-element.46), channel_id=1, source_target_pairs={{0,6},{2,4},{4,2},{6,0},{1,7},{3,5},{5,3},{7,1},{8,14},{10,12},{12... | collective-permute-start | bytes 61448 | tf_op jit(solution)/shard_map/ppermute | solution.py:39
  14.8 4.0 %collective-permute-start.4 = (bf16[80,128]{1,0:T(8,128)(2,1)S(1)}, bf16[80,128]{1,0:T(8,128)(2,1)S(1)}, u32[]{:S(2)}, u32[]{:S(2)}) collective-permute-start(bf16[80,128]{1,0:T(8,128)(2,1)S(1)} %get-tuple-element.47), channel_id=1, source_target_pairs={{0,2},{2,0},{4,6},{6,4},{1,3},{3,1},{5,7},{7,5},{8,10},{10,8},{12,... | collective-permute-start | bytes 61448 | tf_op jit(solution)/shard_map/ppermute | solution.py:39
  20.3 3.7 %collective-permute-start.8 = (bf16[80,128]{1,0:T(8,128)(2,1)S(1)}, bf16[80,128]{1,0:T(8,128)(2,1)S(1)}, u32[]{:S(2)}, u32[]{:S(2)}) collective-permute-start(bf16[80,128]{1,0:T(8,128)(2,1)S(1)} %get-tuple-element.62), channel_id=1, source_target_pairs={{0,24},{8,16},{16,8},{24,0},{1,25},{9,17},{17,9},{25,1},{2,26},{10... | collective-permute-start | bytes 61448 | tf_op jit(solution)/shard_map/ppermute | solution.py:39
  21.5 3.8 %collective-permute-start.9 = (bf16[80,128]{1,0:T(8,128)(2,1)S(1)}, bf16[80,128]{1,0:T(8,128)(2,1)S(1)}, u32[]{:S(2)}, u32[]{:S(2)}) collective-permute-start(bf16[80,128]{1,0:T(8,128)(2,1)S(1)} %get-tuple-element.61), channel_id=1, source_target_pairs={{0,16},{8,24},{16,0},{24,8},{1,17},{9,25},{17,1},{25,9},{2,18},{10... | collective-permute-start | bytes 61448 | tf_op jit(solution)/shard_map/ppermute | solution.py:39
  22.0 3.2 %collective-permute-start.7 = (bf16[80,128]{1,0:T(8,128)(2,1)S(1)}, bf16[80,128]{1,0:T(8,128)(2,1)S(1)}, u32[]{:S(2)}, u32[]{:S(2)}) collective-permute-start(bf16[80,128]{1,0:T(8,128)(2,1)S(1)} %get-tuple-element.61), channel_id=1, source_target_pairs={{0,8},{8,0},{16,24},{24,16},{1,9},{9,1},{17,25},{25,17},{2,10},{10... | collective-permute-start | bytes 61448 | tf_op jit(solution)/shard_map/ppermute | solution.py:39
  22.3 11.4 %collective-permute-start.5 = (bf16[256,128]{1,0:T(8,128)(2,1)S(1)}, bf16[256,128]{1,0:T(8,128)(2,1)S(1)}, u32[]{:S(2)}, u32[]{:S(2)}) collective-permute-start(bf16[256,128]{1,0:T(8,128)(2,1)S(1)} %get-tuple-element.55), channel_id=1, source_target_pairs={{0,8},{8,0},{16,24},{24,16},{1,9},{9,1},{17,25},{25,17},{2,10},{10... | collective-permute-start | bytes 196616 | tf_op jit(solution)/shard_map/ppermute | solution.py:39
  22.7 11.0 %collective-permute-start.6 = (bf16[256,128]{1,0:T(8,128)(2,1)S(1)}, bf16[256,128]{1,0:T(8,128)(2,1)S(1)}, u32[]{:S(2)}, u32[]{:S(2)}) collective-permute-start(bf16[256,128]{1,0:T(8,128)(2,1)S(1)} %get-tuple-element.56), channel_id=1, source_target_pairs={{0,24},{8,16},{16,8},{24,0},{1,25},{9,17},{17,9},{25,1},{2,26},{10... | collective-permute-start | bytes 196616 | tf_op jit(solution)/shard_map/ppermute | solution.py:39
  25.3 3.9 %collective-permute-start.10 = (bf16[96,128]{1,0:T(8,128)(2,1)S(1)}, bf16[96,128]{1,0:T(8,128)(2,1)S(1)}, u32[]{:S(2)}, u32[]{:S(2)}) collective-permute-start(bf16[96,128]{1,0:T(8,128)(2,1)S(1)} %get-tuple-element.63.mine), channel_id=1, source_target_pairs={{0,1},{1,0},{2,3},{3,2},{4,5},{5,4},{6,7},{7,6},{8,9},{9,8},{10,11... | collective-permute-start | bytes 73736 | tf_op jit(solution)/shard_map/ppermute | solution.py:39
  29.3 6.5 %collective-permute-start.11 = (bf16[80,128]{1,0:T(8,128)(2,1)S(1)}, bf16[80,128]{1,0:T(8,128)(2,1)S(1)}, u32[]{:S(2)}, u32[]{:S(2)}) collective-permute-start(bf16[80,128]{1,0:T(8,128)(2,1)S(1)} %get-tuple-element.69), channel_id=1, source_target_pairs={{0,6},{2,4},{4,2},{6,0},{1,7},{3,5},{5,3},{7,1},{8,14},{10,12},{12... | collective-permute-start | bytes 61448 | tf_op jit(solution)/shard_map/ppermute | solution.py:39
  30.0 5.7 %collective-permute-start.13 = (bf16[80,128]{1,0:T(8,128)(2,1)S(1)}, bf16[80,128]{1,0:T(8,128)(2,1)S(1)}, u32[]{:S(2)}, u32[]{:S(2)}) collective-permute-start(bf16[80,128]{1,0:T(8,128)(2,1)S(1)} %get-tuple-element.70), channel_id=1, source_target_pairs={{0,2},{2,0},{4,6},{6,4},{1,3},{3,1},{5,7},{7,5},{8,10},{10,8},{12,... | collective-permute-start | bytes 61448 | tf_op jit(solution)/shard_map/ppermute | solution.py:39
  31.1 4.6 %collective-permute-start.12 = (bf16[64,128]{1,0:T(8,128)(2,1)S(1)}, bf16[64,128]{1,0:T(8,128)(2,1)S(1)}, u32[]{:S(2)}, u32[]{:S(2)}) collective-permute-start(bf16[64,128]{1,0:T(8,128)(2,1)S(1)} %get-tuple-element.68.mine), channel_id=1, source_target_pairs={{0,4},{2,6},{4,0},{6,2},{1,5},{3,7},{5,1},{7,3},{8,12},{10,14},{12... | collective-permute-start | bytes 49160 | tf_op jit(solution)/shard_map/ppermute | solution.py:39
